TPU v7x, 32 devices: a whole 2x2x4 slice. The times are simulated.
32 devices in a mesh: wide: 16 (over z, y, core), narrow: 2 (over x).
Axes of the slice: x: 2, y: 2, z: 4, core: 2. Of those that a mesh axis runs over, the one named last changes fastest.
Arguments:
- tokens: bfloat16 [64, 336, 768], P(('wide', 'narrow')), may hold values from -6 to 6
- skip: bfloat16 [64, 336, 768], P(('wide', 'narrow')), may hold values from -6 to 6
- flags: int32 [64], P(('wide', 'narrow')), may hold values from 0 to 1
- cotangent: bfloat16 [64, 336, 768], P(('wide', 'narrow')), may hold values from -6 to 6
- norm_gains: bfloat16 [2, 2, 768], P(None, None, 'narrow'), may hold values from 0.5 to 1.5
- norm_biases: bfloat16 [2, 2, 768], P(None, None, 'narrow'), may hold values from -2 to 2
- qkv_weight: bfloat16 [2, 768, 2304], P(None, 'narrow'), may hold values from -0.21875 to 0.21875
- out_weight: bfloat16 [2, 768, 768], P(None, 'narrow'), may hold values from -1.25 to 1.25
- out_bias: bfloat16 [2, 768], P(None, 'narrow'), may hold values from -2 to 2
- up_weight: bfloat16 [2, 768, 3072], P(None, 'narrow'), may hold values from -0.21875 to 0.21875
- up_bias: bfloat16 [2, 3072], P(None, 'narrow'), may hold values from -2 to 2
- down_weight: bfloat16 [2, 3072, 768], P(None, 'narrow'), may hold values from -0.109375 to 0.109375
- down_bias: bfloat16 [2, 768], P(None, 'narrow'), may hold values from -2 to 2
- skip_weight: bfloat16 [1536, 768], P('narrow'), may hold values from -0.15625 to 0.15625
- skip_bias: bfloat16 [768], P('narrow'), may hold values from -2 to 2
Outputs:
- output: bfloat16 [64, 336, 768], P(('wide', 'narrow'))
- tokens_grad: float32 [64, 336, 768], P(('wide', 'narrow'))
- skip_grad: float32 [64, 336, 768], P(('wide', 'narrow'))
- norm_gains_grad: float32 [2, 2, 768], P(None, None, 'narrow')
- norm_biases_grad: float32 [2, 2, 768], P(None, None, 'narrow')
- qkv_weight_grad: float32 [2, 768, 2304], P(None, 'narrow')
- out_weight_grad: float32 [2, 768, 768], P(None, 'narrow')
- out_bias_grad: float32 [2, 768], P(None, 'narrow')
- up_weight_grad: float32 [2, 768, 3072], P(None, 'narrow')
- up_bias_grad: float32 [2, 3072], P(None, 'narrow')
- down_weight_grad: float32 [2, 3072, 768], P(None, 'narrow')
- down_bias_grad: float32 [2, 768], P(None, 'narrow')
- skip_weight_grad: float32 [1536, 768], P('narrow')
- skip_bias_grad: float32 [768], P('narrow')
Inputs may be any that keep to these rules, and one draw needn't show every extreme that they name: `flags`: 1 where the item holds 77 caption tokens, 0 where it holds none.
All inputs are finite; a program needn't handle non-finite values.
Results may differ from a plain program's by a relative error of at most 0.02.
Values may be sent and summed in bfloat16 or wider, within the bound.
No kernel may reach another device: no remote copies, remote signals or barrier semaphores. Data moves between devices by JAX's collectives and lax.ppermute only.
A program may use at most 256 MiB of HBM per device.

v0:
```python
import copy
import math

import jax
import jax.numpy as jnp
from jax import lax
from jax.experimental import pallas as pl
from jax.experimental.pallas import tpu as pltpu
from jax.sharding import PartitionSpec as P

HEAD_DIM = 64
PATCHES = 256
CAPTION = 77
PAIR = 2 * HEAD_DIM


epsilon = 1e-05
masked_score = -1e30
low = jnp.bfloat16
full = jnp.float32
SPARE = 14
ANY = pl.BlockSpec(memory_space=pl.ANY)
SCALARS = pl.BlockSpec(memory_space=pltpu.SMEM)


def dot(left, right, contract=(1, 0)):
    dims = (((contract[0],), (contract[1],)), ((), ()))
    return lax.dot_general(left, right, dims, preferred_element_type=full)


def normalize(values):
    centred = values - jnp.mean(values, axis=-1, keepdims=True)
    factor = lax.rsqrt(jnp.mean(centred * centred, axis=-1, keepdims=True) + epsilon)
    return centred * factor, factor


def normalize_back(upstream, normed, factor):
    return factor * (
        upstream
        - jnp.mean(upstream, axis=-1, keepdims=True)
        - normed * jnp.mean(upstream * normed, axis=-1, keepdims=True)
    )


def column_sum(values):
    return jnp.sum(values.astype(full), axis=0, keepdims=True)


def whole(shape):
    return pl.BlockSpec(shape, lambda *grid: (0,) * len(shape))


def cost(micros):
    return pl.CostEstimate(flops=int(micros * 3 * 10**8), bytes_accessed=0, transcendentals=0)


def room(ins, outs, scratch, spare):
    total = spare * 2**20
    for shape, kind, spec in [(array.shape, array.dtype, spec) for array, spec in ins] + list(outs):
        if spec.block_shape is not None and spec.memory_space is None:
            total += 2 * math.prod(spec.block_shape) * jnp.dtype(kind).itemsize
    for piece in scratch:
        if piece.memory_space == pltpu.VMEM:
            total += math.prod(piece.shape) * jnp.dtype(piece.dtype).itemsize
    return total


def call(body, grid, ins, outs, name, micros, scratch=(), spare=6):
    return pl.pallas_call(
        body,
        grid=grid,
        in_specs=[spec for _, spec in ins],
        out_specs=[spec for _, _, spec in outs],
        out_shape=[jax.ShapeDtypeStruct(shape, kind) for shape, kind, _ in outs],
        scratch_shapes=list(scratch),
        name=name,
        cost_estimate=cost(micros),
        compiler_params=pltpu.CompilerParams(vmem_limit_bytes=room(ins, outs, scratch, spare)),
    )(*[array for array, _ in ins])


class Fetch:
    def __init__(self, arrays, sharing):
        self.arrays, self.sharing = arrays, list(sharing)
        self.rows = arrays[0][0].shape[-2]
        while self.rows % (16 << len(self.sharing)):
            self.sharing.pop()
        self.length = self.rows >> len(self.sharing)

    def quarter(self, place):
        return sum(((place // mask) & 1) << bit for bit, mask in enumerate(self.sharing))

    def fetch(self, *earlier):
        found = []
        for array, layer in self.arrays:
            array = after(array, *earlier)
            lead = () if layer is None else (layer,)
            begin = self.quarter(lax.axis_index("wide")) * self.length
            sizes = (1,) * len(lead) + (self.length, array.shape[-1])
            found.append(lax.dynamic_slice(array, lead + (begin, 0), sizes).reshape(self.length, -1))
        self.sent = (jnp.concatenate(found, axis=1) if len(found) > 1 else found[0])[None]
        held = self.sent
        for mask in masks("narrow"):
            held = jnp.concatenate([held, swap(held, "narrow", mask)])
        self.pieces = {0: held[1:]}

    def share(self, which, *earlier):
        if which < len(self.sharing):
            mask = self.sharing[which]
            got = {key ^ (1 << which): swap(after(piece, *earlier), "wide", mask) for key, piece in self.pieces.items()}
            self.pieces.update(got)

    def got(self):
        return list(self.pieces.values())


class Weight:
    def __init__(self, fetched, which, width, spots):
        self.fetched, self.spots, self.width = fetched, spots, width
        self.array, self.layer = fetched.arrays[which]
        self.begin = sum(array.shape[-1] for array, _ in fetched.arrays[:which])
        self.rows, columns = self.array.shape[-2:]
        self.shares = lax.axis_size("narrow")
        self.blocks = columns // width
        self.total = self.rows * self.shares

    def arrays(self):
        return [self.array] + self.fetched.got()

    def scratch(self):
        copies = 1 + len(self.fetched.pieces) * (self.shares - 1)
        return [pltpu.VMEM((self.blocks, self.total, self.width), low), pltpu.SemaphoreType.DMA((self.blocks, copies))]

    def copies(self, spots, refs, held, signals, block):
        own, pieces = refs[0], refs[1:]
        me, length = spots[0], self.fetched.length
        own = own if self.layer is None else own.at[self.layer]
        columns = pl.ds(block * self.width, self.width)
        begin = pl.multiple_of(me * self.rows, 16)
        found = [(own.at[:, columns], begin, self.rows)]
        columns = pl.ds(self.begin + block * self.width, self.width)
        for key, piece in zip(self.fetched.pieces, pieces):
            for offset in range(1, self.shares):
                begin = (me ^ offset) * self.rows + (self.fetched.quarter(spots[1]) ^ key) * length
                found.append((piece.at[offset - 1, :, columns], pl.multiple_of(begin, 16), length))
        return [
            pltpu.make_async_copy(source, held.at[block, pl.ds(begin, length)], signals.at[block, place])
            for place, (source, begin, length) in enumerate(found)
        ]

    def wait(self, *refs, block=0):
        for copy in self.copies(*refs, block):
            copy.wait()


def weighted(body, weights, grid, ins, outs, name, micros, scratch=(), first=((0, 0),), spare=SPARE):
    spots = weights[0].spots
    operands = [(spots, SCALARS)] + [(array, ANY) for weight in weights for array in weight.arrays()]
    counts = [len(weight.arrays()) for weight in weights]
    extra = [piece for weight in weights for piece in weight.scratch()]

    def wrapped(*refs):
        spots_ref, rest = refs[0], list(refs[1:])
        sources = []
        for count in counts:
            sources.append(rest[:count])
            rest = rest[count:]
        spare = rest[len(rest) - len(extra) :]
        rest = rest[: len(rest) - len(extra)]
        handles = []
        for place, weight in enumerate(weights):
            held, signals = spare[2 * place : 2 * place + 2]
            refs_of = (spots_ref, sources[place], held, signals)
            handles.append((weight, refs_of, held))

        everything = [(place, block) for place, weight in enumerate(weights) for block in range(weight.blocks)]

        def begin(wanted):
            for place, block in wanted:
                weight, refs_of, _ = handles[place]
                for copy in weight.copies(*refs_of, block):
                    copy.start()

        @pl.when(pl.program_id(0) == 0)
        def _():
            begin(first)

        def ready(place, block=0, then=False):
            weight, refs_of, held = handles[place]
            weight.wait(*refs_of, block=block)
            if then:
                begin([each for each in everything if each not in first])

        body(ready, [held for _, _, held in handles], *rest)

    return call(wrapped, grid, operands + ins, outs, name, micros, list(scratch) + extra, spare)


def pack_small(*small):
    part = small[0].shape[-1]
    counts = [piece.size // part for piece in small]

    def body(*refs):
        row = 0
        for ref in refs[:-1]:
            values = ref[...].reshape(-1, ref.shape[-1])
            for each in range(values.shape[0]):
                for begin in range(0, values.shape[1], part):
                    refs[-1][row : row + 1] = values[each : each + 1, begin : begin + part].astype(full)
                    row += 1
        refs[-1][row:] = jnp.zeros((refs[-1].shape[0] - row, part), full)

    flat = [piece.reshape((1,) * (2 - piece.ndim) + piece.shape) for piece in small]
    rows = -(-sum(counts) // 16) * 16
    out = ((rows, part), full, whole((rows, part)))
    return call(body, (1,), [(piece, whole(piece.shape)) for piece in flat], [out], "pack_small", 1)[0].astype(low)


def unpack_small(parts, me, small, width):
    shares, _, part = parts.shape
    lines = [(piece.size // piece.shape[-1], piece.shape[-1] // part) for piece in small]
    total = sum(count * many for count, many in lines)
    rows = -(-total // 8) * 8

    def body(me_ref, parts_ref, out_ref):
        values = parts_ref[...].astype(full)
        for mine in range(shares):

            @pl.when(me_ref[0] == mine)
            def _():
                for owner in range(shares):
                    source, target = 0, 0
                    for count, many in lines:
                        for each in range(count):
                            for piece in range(many):
                                at = owner * many * part + piece * part
                                row, column = target + at // width, at % width
                                line = values[owner ^ mine, source : source + 1]
                                out_ref[row : row + 1, column : column + part] = line
                                source += 1
                            target += many
        if rows > total:
            out_ref[total:] = jnp.zeros((rows - total, width), full)

    ins = [(parts, pl.BlockSpec(parts.shape, lambda g, me: (0, 0, 0)))]
    out = ((rows, width), full, pl.BlockSpec((rows, width), lambda g, me: (0, 0)))
    return picked(body, me, (1,), ins, [out], "unpack_small", 1)[0]


def project_qkv(inputs, gain, shift, weight):
    rows, width = inputs.shape

    def body(ready, held, x_ref, gain_ref, shift_ref, a_ref, out_ref):
        step = pl.program_id(0)

        @pl.when(step == 0)
        def _():
            normed, _ = normalize(x_ref[...].astype(full))
            a_ref[...] = (normed * gain_ref[...] + shift_ref[...]).astype(low)
            ready(0, 0, then=True)

        @pl.when(step > 0)
        def _():
            ready(0, step)

        scale = jnp.where(step == 0, HEAD_DIM ** (-0.5), 1.0)
        out_ref[0] = (dot(a_ref[...], held[0][step]).astype(low).astype(full) * scale).astype(low)

    return weighted(
        body,
        [weight],
        (3,),
        [
            (inputs, whole((rows, width))),
            (gain, whole((1, width))),
            (shift, whole((1, width))),
        ],
        [
            ((rows, width), low, whole((rows, width))),
            ((3, rows, width), low, pl.BlockSpec((1, rows, width), lambda j: (j, 0, 0))),
        ],
        "project_qkv",
        7,
    )


def join_qkv(middle, skip, join_weight, join_shift, gain, shift, weight):
    rows, width = middle.shape

    def body(ready, held, m_ref, s_ref, jb_ref, gain_ref, shift_ref, e_ref, a_ref, out_ref):
        step = pl.program_id(0)

        @pl.when(step == 0)
        def _():
            ready(0, then=True)
            entry = dot(m_ref[...], held[0][0, :width]) + dot(s_ref[...], held[0][0, width:]) + jb_ref[...]
            e_ref[...] = entry
            normed, _ = normalize(entry)
            a_ref[...] = (normed * gain_ref[...] + shift_ref[...]).astype(low)

        ready(1, step)
        scale = jnp.where(step == 0, HEAD_DIM ** (-0.5), 1.0)
        out_ref[0] = (dot(a_ref[...], held[1][step]).astype(low).astype(full) * scale).astype(low)

    return weighted(
        body,
        [join_weight, weight],
        (3,),
        [
            (middle, whole((rows, width))),
            (skip, whole((rows, width))),
            (join_shift, whole((1, width))),
            (gain, whole((1, width))),
            (shift, whole((1, width))),
        ],
        [
            ((rows, width), full, whole((rows, width))),
            ((rows, width), low, whole((rows, width))),
            ((3, rows, width), low, pl.BlockSpec((1, rows, width), lambda j: (j, 0, 0))),
        ],
        "join_qkv",
        11,
        first=((0, 0), (1, 0)),
    )


def head_masks(seq_rows):
    lane = lax.broadcasted_iota(jnp.int32, (seq_rows, PAIR), 1)
    return [lane < HEAD_DIM, lane >= HEAD_DIM]


def pairs_of(width):
    pairs = width // PAIR
    return pairs, max(group for group in (1, 2, 3) if pairs % group == 0)


def attend(packed, lengths, items, seq_rows):
    width = packed.shape[-1]
    pairs, group = pairs_of(width)

    def body(length_ref, q_ref, k_ref, v_ref, out_ref, total_ref):
        counts = lax.broadcasted_iota(jnp.int32, (seq_rows, seq_rows), 1) < length_ref[pl.program_id(0)]
        for pair in range(group):
            columns = slice(pair * PAIR, (pair + 1) * PAIR)
            queries, keys, values = q_ref[0, 0, :, columns], k_ref[0, 0, :, columns], v_ref[0, 0, :, columns]
            mixed = jnp.zeros((seq_rows, PAIR), full)
            for head, lanes in enumerate(head_masks(seq_rows)):
                scores = dot(jnp.where(lanes, queries, 0), keys, (1, 1))
                scores = jnp.where(counts, scores, masked_score)
                largest = jnp.max(scores, axis=1, keepdims=True)
                weights = jnp.exp(scores - largest)
                total = jnp.sum(weights, axis=1, keepdims=True)
                mixed += dot(weights.astype(low), jnp.where(lanes, values, 0)) * (1.0 / total)
                total_ref[0, pair, head : head + 1] = (largest + jnp.log(total)).T
            out_ref[0, :, columns] = mixed.astype(low)

    def block(which):
        return pl.BlockSpec((1, 1, seq_rows, group * PAIR), lambda n, h: (which, n, 0, h))

    return call(
        body,
        (items, pairs // group),
        [(lengths, SCALARS), (packed, block(0)), (packed, block(1)), (packed, block(2))],
        [
            (
                (items, seq_rows, width),
                low,
                pl.BlockSpec((1, seq_rows, group * PAIR), lambda n, h: (n, 0, h)),
            ),
            (
                (items, pairs, 8, seq_rows),
                full,
                pl.BlockSpec((1, group, 8, seq_rows), lambda n, h: (n, h, 0, 0)),
            ),
        ],
        "attend",
        10,
        spare=14,
    )


def attend_back(packed, grad_mixed, totals, lengths, items, seq_rows):
    width = packed.shape[-1]
    pairs, group = pairs_of(width)
    sides = [slice(0, PATCHES), slice(PATCHES, seq_rows)]

    def body(length_ref, q_ref, k_ref, v_ref, g_ref, total_ref, out_ref):
        row = PATCHES + lax.broadcasted_iota(jnp.int32, (seq_rows - PATCHES, seq_rows), 0)
        counts = row < length_ref[pl.program_id(0)]
        for pair in range(group):
            columns = slice(pair * PAIR, (pair + 1) * PAIR)
            queries, keys, values = q_ref[0, 0, :, columns], k_ref[0, 0, :, columns], v_ref[0, 0, :, columns]
            upstream = g_ref[0, :, columns]
            grad_queries = jnp.zeros((PAIR, seq_rows), full)
            grad_keys, grad_values = [0.0, 0.0], [0.0, 0.0]
            for head, lanes in enumerate(head_masks(seq_rows)):
                own_queries = jnp.where(lanes, queries, 0)
                own_upstream = jnp.where(lanes, upstream, 0)
                own_keys = jnp.where(lanes, keys, 0)
                parts, centre = [], 0.0
                for side, rows in enumerate(sides):
                    scores = dot(keys[rows], own_queries, (1, 1))
                    if side:
                        scores = jnp.where(counts, scores, masked_score)
                    probs = jnp.exp(scores - total_ref[0, pair, head : head + 1])
                    grad_probs = dot(values[rows], own_upstream, (1, 1))
                    centre += jnp.sum(grad_probs * probs, axis=0, keepdims=True)
                    parts.append((probs, grad_probs))
                for side, (probs, grad_probs) in enumerate(parts):
                    grad_scores = (probs * (grad_probs - centre)).astype(low)
                    grad_values[side] += dot(probs.astype(low), own_upstream)
                    grad_keys[side] += dot(grad_scores, own_queries)
                    grad_queries += dot(own_keys[sides[side]], grad_scores, (0, 0))
            out_ref[0, 0, :, columns] = (grad_queries.T * HEAD_DIM ** (-0.5)).astype(low)
            for side, rows in enumerate(sides):
                out_ref[1, 0, rows, columns] = grad_keys[side].astype(low)
                out_ref[2, 0, rows, columns] = grad_values[side].astype(low)

    def block(which):
        return pl.BlockSpec((1, 1, seq_rows, group * PAIR), lambda n, h: (which, n, 0, h))

    return call(
        body,
        (items, pairs // group),
        [
            (lengths, SCALARS),
            (packed, block(0)),
            (packed, block(1)),
            (packed, block(2)),
            (grad_mixed, pl.BlockSpec((1, seq_rows, group * PAIR), lambda n, h: (n, 0, h))),
            (totals, pl.BlockSpec((1, group, 8, seq_rows), lambda n, h: (n, h, 0, 0))),
        ],
        [
            (
                (3, items, seq_rows, width),
                low,
                pl.BlockSpec((3, 1, seq_rows, group * PAIR), lambda n, h: (0, n, 0, h)),
            ),
        ],
        "attend_back",
        15,
        spare=14,
    )[0]


def gelu_parts(before):
    decay = jnp.exp(before * before * -0.5)
    inverse = pl.reciprocal(1.0 + (0.3275911 * 0.5**0.5) * jnp.abs(before), approx=False)
    series = 1.061405429 * 0.5
    for term in (-1.453152027, 1.421413741, -0.284496736, 0.254829592):
        series = series * inverse + term * 0.5
    below = series * inverse * decay
    share = jnp.where(before >= 0, 1.0 - below, below)
    return before * share, share + before * decay * 0.3989422804014327


def feed_forward(inputs, mixed, out_weight, out_bias, gain, shift, up_weight, up_bias, down_weight, down_bias, keep=None):
    rows, width = inputs.shape
    steps = up_weight.blocks
    hidden = steps * width

    def body(ready, held, x_ref, o_ref, ob_ref, gain_ref, shift_ref, ub_ref, db_ref, *rest):
        m_ref, a_ref, g_ref, s_ref, y_ref, total = rest[-6:]
        step = pl.program_id(0)

        @pl.when(step == 0)
        def _():
            ready(0, then=True)
            middle = x_ref[...].astype(full) + dot(o_ref[...], held[0][0]) + ob_ref[...]
            m_ref[...] = middle
            normed, _ = normalize(middle)
            a_ref[...] = (normed * gain_ref[...] + shift_ref[...]).astype(low)
            total[...] = middle + db_ref[...]

        ready(1, step)
        before = dot(a_ref[...], held[1][step]) + ub_ref[...]
        value, slope = gelu_parts(before)
        g_ref[...] = value.astype(low)
        s_ref[...] = slope.astype(low)

        @pl.when(step == 0)
        def _():
            ready(2)

        total[...] += dot(g_ref[...], held[2][0, pl.ds(pl.multiple_of(step * width, width), width)])

        @pl.when(step == steps - 1)
        def _():
            value = total[...]
            if keep is not None:
                value = jnp.where(rest[0][...] > 0, value, 0.0)
            y_ref[...] = value.astype(low)

    return weighted(
        body,
        [out_weight, up_weight, down_weight],
        (steps,),
        [
            (inputs, whole((rows, width))),
            (mixed, whole((rows, width))),
            (out_bias, whole((1, width))),
            (gain, whole((1, width))),
            (shift, whole((1, width))),
            (up_bias, pl.BlockSpec((1, width), lambda j: (0, j))),
            (down_bias, whole((1, width))),
        ]
        + ([] if keep is None else [(keep, whole((rows, 1)))]),
        [
            ((rows, width), full, whole((rows, width))),
            ((rows, width), low, whole((rows, width))),
            ((rows, hidden), low, pl.BlockSpec((rows, width), lambda j: (0, j))),
            ((rows, hidden), low, pl.BlockSpec((rows, width), lambda j: (0, j))),
            ((rows, width), low, whole((rows, width))),
        ],
        "feed_forward",
        23,
        scratch=[pltpu.VMEM((rows, width), full)],
        first=((0, 0), (1, 0)),
    )


def feed_forward_back(upstream, rounded, slope, down_weight, up_weight, middle, gain, out_weight):
    rows, width = upstream.shape
    steps = up_weight.blocks
    hidden = steps * width

    def body(ready, held, y_ref, dz_ref, s_ref, m_ref, gain_ref, du_ref, dm_ref, db_ref, do_ref, sums_ref, total):
        step = pl.program_id(0)

        @pl.when(step == 0)
        def _():
            sums_ref[0:1] = column_sum(dz_ref[...])
            total[...] = jnp.zeros_like(total)
            ready(0, then=True)

        down = held[0][0, pl.ds(pl.multiple_of(step * width, width), width)]
        grad = (dot(dz_ref[...], down, (1, 1)) * s_ref[...].astype(full)).astype(low)
        du_ref[...] = grad
        sums_ref[pl.ds(4 + step, 1)] = column_sum(grad)
        ready(1, step)
        total[...] += dot(grad, held[1][step], (1, 1))

        @pl.when(step == steps - 1)
        def _():
            grad_second = total[...]
            normed, factor = normalize(m_ref[...])
            sums_ref[1:2] = column_sum(grad_second * normed)
            sums_ref[2:3] = column_sum(grad_second)
            grad_middle = y_ref[...].astype(full) + normalize_back(grad_second * gain_ref[...], normed, factor)
            dm_ref[...] = grad_middle
            branch = grad_middle.astype(low)
            db_ref[...] = branch
            sums_ref[3:4] = column_sum(branch)
            ready(2)
            do_ref[...] = dot(branch, held[2][0], (1, 1)).astype(low)

    return weighted(
        body,
        [down_weight, up_weight, out_weight],
        (steps,),
        [
            (upstream, whole((rows, width))),
            (rounded, whole((rows, width))),
            (slope, pl.BlockSpec((rows, width), lambda j: (0, j))),
            (middle, whole((rows, width))),
            (gain, whole((1, width))),
        ],
        [
            ((rows, hidden), low, pl.BlockSpec((rows, width), lambda j: (0, j))),
            ((rows, width), full, whole((rows, width))),
            ((rows, width), low, whole((rows, width))),
            ((rows, width), low, whole((rows, width))),
            ((4 + steps, width), full, whole((4 + steps, width))),
        ],
        "feed_forward_back",
        21,
        scratch=[pltpu.VMEM((rows, width), full)],
        first=((0, 0), (1, 0)),
    )


def project_back(grad_packed, weight, inputs, gain, grad_middle, join_weight=None):
    rows, width = inputs.shape
    joined = join_weight is not None

    def body(ready, held, g_ref, x_ref, gain_ref, dm_ref, *rest):
        if joined:
            de_ref, dx_ref, dz_ref, skip_ref, sums_ref, total = rest
        else:
            dx_ref, sums_ref, total = rest
        step = pl.program_id(0)

        @pl.when(step == 0)
        def _():
            total[...] = jnp.zeros_like(total)
            ready(0, 0, then=True)

        @pl.when(step > 0)
        def _():
            ready(0, step)

        total[...] += dot(g_ref[0], held[0][step], (1, 1))

        @pl.when(step == 2)
        def _():
            grad_first = total[...]
            normed, factor = normalize(x_ref[...].astype(full))
            sums_ref[0:1] = column_sum(grad_first * normed)
            sums_ref[1:2] = column_sum(grad_first)
            grad = dm_ref[...] + normalize_back(grad_first * gain_ref[...], normed, factor)
            if joined:
                entry = grad.astype(low)
                de_ref[...] = entry
                sums_ref[2:3] = column_sum(entry)
                ready(1)
                grad = dot(entry, held[1][0, :width], (1, 1))
                dx_ref[...] = grad
                dz_ref[...] = grad.astype(low)
                skip_ref[...] = dot(entry, held[1][0, width:], (1, 1))
            else:
                dx_ref[...] = grad

    ins = [
        (grad_packed, pl.BlockSpec((1, rows, width), lambda j: (j, 0, 0))),
        (inputs, whole((rows, width))),
        (gain, whole((1, width))),
        (grad_middle, whole((rows, width))),
    ]
    outs = [((rows, width), full, whole((rows, width))), ((8, width), full, whole((8, width)))]
    if joined:
        rounded = ((rows, width), low, whole((rows, width)))
        outs = [rounded, outs[0], rounded, outs[0], outs[1]]
    return weighted(
        body,
        [weight] + ([join_weight] if joined else []),
        (3,),
        ins,
        outs,
        "project_back",
        13 if joined else 9,
        scratch=[pltpu.VMEM((rows, width), full)],
    )


def picked(body, which, grid, ins, outs, name, micros, aliases=None, spare=4):
    return pl.pallas_call(
        body,
        grid_spec=pltpu.PrefetchScalarGridSpec(
            num_scalar_prefetch=1,
            grid=grid,
            in_specs=[spec for _, spec in ins],
            out_specs=[spec for _, _, spec in outs],
        ),
        out_shape=[jax.ShapeDtypeStruct(shape, kind) for shape, kind, _ in outs],
        name=name,
        input_output_aliases={place + 1: out for place, out in (aliases or {}).items()},
        cost_estimate=cost(micros),
        compiler_params=pltpu.CompilerParams(vmem_limit_bytes=room(ins, outs, (), spare)),
    )(which, *[array for array, _ in ins])


def quarters(rows, width, narrow_rows):
    shape = (lax.axis_size("narrow") // 2 * narrow_rows, width)
    return [(shape, low, pl.BlockSpec(shape, lambda g, core: (0, 0)))] * 4


def up_term(left, right, core):
    rows, width = left.shape
    part = width // lax.axis_size("narrow")
    half = width // 2

    def body(core_ref, l_ref, r_ref, *outs):
        value = dot(l_ref[...], r_ref[...], (0, 0)).astype(low)
        for block in range(2):

            @pl.when(pl.program_id(0) == block)
            def _():
                outs[block][...] = value[:half]
                outs[2 + block][...] = value[half:]

    return picked(
        body,
        core,
        (2,),
        [
            (left, pl.BlockSpec((rows, width), lambda g, core: (0, 0))),
            (right, pl.BlockSpec((rows, width), lambda g, core: (0, core[0] * 2 + g))),
        ],
        quarters(rows, width, part),
        "up_term",
        3.5,
    )


def qkv_out_term(first, packed, mixed, branch, core):
    rows, width = first.shape
    part = width // lax.axis_size("narrow")
    half = width // 2

    def body(core_ref, l_ref, r_ref, o_ref, b_ref, *outs):
        step = pl.program_id(0)
        last = core_ref[0] * 2 + step == 3

        def put(block, value):
            outs[block][...] = value[:half]
            outs[2 + block][...] = value[half:]

        @pl.when(last)
        def _():
            put(1, dot(o_ref[...], b_ref[...], (0, 0)).astype(low))

        @pl.when(jnp.logical_not(last))
        def _():
            value = dot(l_ref[...], r_ref[0], (0, 0)).astype(low)
            for block in range(2):

                @pl.when(step == block)
                def _():
                    put(block, value)

    flat = pl.BlockSpec((rows, width), lambda g, core: (0, 0))
    return picked(
        body,
        core,
        (2,),
        [
            (first, flat),
            (packed, pl.BlockSpec((1, rows, width), lambda g, core: (jnp.minimum(core[0] * 2 + g, 2), 0, 0))),
            (mixed, flat),
            (branch, flat),
        ],
        quarters(rows, width, part),
        "qkv_out_term",
        3.5,
    )


def down_term(left, right, core):
    rows, width = right.shape
    shares = lax.axis_size("narrow")
    part = left.shape[1] // (2 * shares)
    direct = part == width
    if not direct:
        left = left.reshape(rows, shares, 2, 2, part // 2)
        left = lax.dynamic_index_in_dim(left, core[0], 2, keepdims=False)
        left = left.reshape(rows, 2, shares // 2, 2, part // 2).swapaxes(2, 3).reshape(rows, 2 * width)
    half = width // 2

    def body(core_ref, l_ref, r_ref, *outs):
        value = dot(l_ref[...], r_ref[...], (0, 0)).astype(low)
        for owner in range(2):

            @pl.when(pl.program_id(0) == owner)
            def _():
                outs[2 * owner][...] = value[:half]
                outs[2 * owner + 1][...] = value[half:]

    return picked(
        body,
        core,
        (2,),
        [
            (left, pl.BlockSpec((rows, width), lambda g, core: (0, g * 2 + core[0] if direct else g))),
            (right, pl.BlockSpec((rows, width), lambda g, core: (0, 0))),
        ],
        quarters(rows, width, part // 2),
        "down_term",
        3.5,
    )


def join_term(middle, skip, right, core):
    rows, width = right.shape
    shares = lax.axis_size("narrow")
    part = width // shares
    half = width // 2
    if part != half:
        left = jnp.concatenate([middle, skip], axis=1).reshape(rows, shares, 2, 2, part // 2)
        left = lax.dynamic_index_in_dim(left, core[0], 2, keepdims=False)
        left = left.reshape(rows, 2, shares // 2, 2, part // 2).swapaxes(2, 3).reshape(rows, width)
        middle, skip = left[:, :half], left[:, half:]

    def body(core_ref, m_ref, s_ref, r_ref, *outs):
        for owner, left_ref in enumerate((m_ref, s_ref)):
            value = dot(left_ref[...], r_ref[...], (0, 0)).astype(low)
            outs[2 * owner][...] = value[: half // 2]
            outs[2 * owner + 1][...] = value[half // 2 :]

    side = pl.BlockSpec((rows, half), lambda g, core: (0, core[0] if part == half else 0))
    return picked(
        body,
        core,
        (1,),
        [(middle, side), (skip, side), (right, pl.BlockSpec((rows, width), lambda g, core: (0, 0)))],
        quarters(rows, width, part // 2),
        "join_term",
        2,
    )


def cross(bit, *pieces):
    kept, got = pieces[: len(pieces) // 2], pieces[len(pieces) // 2 :]
    rows, columns = kept[0].shape
    blocks = len(kept) // 2
    steps = 2 if rows % 32 == 0 else 1

    def body(bit_ref, *refs):
        sent_ref, left_ref = refs[-2:]

        def put(target, owner):
            for block in range(blocks):
                place = owner * blocks + block
                one, two = refs[place], refs[2 * blocks + place]
                target[block] = (one[...].astype(full) + two[...].astype(full)).astype(low)

        for mine in range(2):

            @pl.when(bit_ref[0] == mine)
            def _():
                put(sent_ref, 1 - mine)
                put(left_ref, mine)

    ins = [(piece, pl.BlockSpec((rows // steps, columns), lambda g, bit: (g, 0))) for piece in kept + got]
    out = ((blocks, rows, columns), low, pl.BlockSpec((blocks, rows // steps, columns), lambda g, bit: (0, g, 0)))
    return picked(body, bit, (steps,), ins, [out, out], "cross", 2)


def add_halve(bit, *pairs):
    lead, columns = pairs[0].shape[0], pairs[0].shape[-1]
    sizes = [pair.shape[2] for pair in pairs[::2]]
    total = sum(sizes)
    steps = 2 if len(sizes) == 1 and total % 32 == 0 and total >= 256 else 1

    def body(bit_ref, *refs):
        mine = bit_ref[0]
        for target, place in ((refs[-2], 1 - mine), (refs[-1], mine)):
            begin = 0
            for kept_ref, got_ref in zip(refs[:-2:2], refs[1:-2:2]):
                length = kept_ref.shape[2]
                for each in range(lead):
                    value = kept_ref[each, place].astype(full) + got_ref[each, place].astype(full)
                    target[each, begin : begin + length] = value.astype(low)
                begin += length

    ins = [
        (pair, pl.BlockSpec((lead, 2, pair.shape[2] // steps, columns), lambda g, bit: (0, 0, g, 0)))
        for pair in pairs
    ]
    out = (
        (lead, total, columns),
        low,
        pl.BlockSpec((lead, total // steps, columns), lambda g, bit: (0, g, 0)),
    )
    return picked(body, bit, (steps,), ins, [out, out], "add_halve", 2)


def add_into(target, place, count, one, two):
    rows, columns = one.shape[-2:]
    steps = 2 if rows % 32 == 0 else 1
    block = pl.BlockSpec((1, rows // steps, columns), lambda g: (0, g, 0))

    def body(one_ref, two_ref, *rest):
        rest[-1][...] = (one_ref[...].astype(full) + two_ref[...].astype(full)).astype(low)

    ins = [one.reshape(1, rows, columns), two.reshape(1, rows, columns)]
    return pl.pallas_call(
        body,
        grid=(steps,),
        in_specs=[block, block] + ([] if target is None else [ANY]),
        out_specs=pl.BlockSpec((1, rows // steps, columns), lambda g: (place, g, 0)),
        out_shape=jax.ShapeDtypeStruct((count, rows, columns), low),
        name="add_into",
        input_output_aliases={} if target is None else {2: 0},
        cost_estimate=cost(1.3),
    )(*ins, *([] if target is None else [target]))


def add(one, two):
    return (one.astype(full) + two.astype(full)).astype(low)


def pair_up(own, got, bit):
    rows, columns = own.shape

    def body(bit_ref, own_ref, got_ref, out_ref):
        mine = bit_ref[0]
        out_ref[mine] = own_ref[...]
        out_ref[1 - mine] = got_ref[...]

    flat = pl.BlockSpec((rows, columns), lambda g, bit: (0, 0))
    out = ((2, rows, columns), low, pl.BlockSpec((2, rows, columns), lambda g, bit: (0, 0, 0)))
    return picked(body, bit, (1,), [(own, flat), (got, flat)], [out], "pair_up", 1)[0]


def finish(kind, half, own, got, begin, length, core, layer, targets):
    pieces, _, columns = own.shape
    scale = 1.0 / lax.axis_size("wide")
    aliases = {place + 2: place for place in range(len(targets))}
    source = pl.BlockSpec((pieces, length, columns), lambda g, core: (0, begin // length, 0))
    ins = [(own, source), (got, source)] + [(target, ANY) for target in targets]
    rows = pieces * length

    def chosen(core_ref, which, own_ref, got_ref, place=None):
        sides = [own_ref, got_ref]
        if place is None:
            values = [side[...].reshape(pieces * length, columns) for side in sides]
        else:
            if pieces == 1:
                near = (0, pl.ds(place * (length // 2), length // 2))
            else:
                near = (pl.ds(place * (pieces // 2), pieces // 2),)
            values = [side[near].reshape(pieces * length // 2, columns) for side in sides]
        return jnp.where(core_ref[0] == which, values[0], values[1]).astype(full) * scale

    if kind in ("down", "join"):

        def body(core_ref, own_ref, got_ref, *rest):
            rest[-1][0] = chosen(core_ref, pl.program_id(0), own_ref, got_ref)

        place = layer if kind == "down" else 0
        shape = (2 if kind == "down" else 1, 2 * rows, columns)
        out = (shape, full, pl.BlockSpec((1, rows, columns), lambda g, core: (place, g, 0)))
        return picked(body, core, (2,), ins, [out], "finish_rows", 3, aliases)
    steps = 4 if half is None else 2
    rows = rows // 2 if half is None else rows

    def block(step):
        return step if half is None else 2 * step + half

    def values_of(core_ref, own_ref, got_ref):
        step = pl.program_id(0)
        if half is None:
            return chosen(core_ref, step // 2, own_ref, got_ref, step % 2)
        return chosen(core_ref, step, own_ref, got_ref)

    def body(core_ref, own_ref, got_ref, *rest):
        values = values_of(core_ref, own_ref, got_ref)
        if kind == "up":
            rest[-1][0] = values
            return
        if half == 0:
            rest[-1][0] = values
            return
        last = block(pl.program_id(0)) == 3

        @pl.when(jnp.logical_not(last))
        def _():
            rest[-2][0] = values

        @pl.when(last)
        def _():
            rest[-1][0] = values

    if kind == "up":
        outs = [((2, rows, 4 * columns), full, pl.BlockSpec((1, rows, columns), lambda g, core: (layer, 0, block(g))))]
        return picked(body, core, (steps,), ins, outs, "finish_columns", 3, aliases)

    def spot(step):
        return block(step if half == 0 else jnp.minimum(step, steps - 2))

    outs = [
        ((2, rows, 3 * columns), full, pl.BlockSpec((1, rows, columns), lambda g, core: (layer, 0, spot(g)))),
        ((2, rows, columns), full, pl.BlockSpec((1, rows, columns), lambda g, core: (layer, 0, 0))),
    ]
    if half == 0:
        kept = targets[1:]
        ins, outs, aliases = ins[:3] if targets else ins, outs[:1], {2: 0} if targets else {}
        return (picked(body, core, (steps,), ins, outs, "finish_qkv", 3, aliases)[0], *kept)
    return picked(body, core, (steps,), ins, outs, "finish_qkv_out", 3, aliases)


def small_gradients(total, me, width, shares, blocks):
    part = width // shares
    scale = 1.0 / lax.axis_size("wide")

    def body(me_ref, total_ref, gains_ref, shifts_ref, out_ref, up_ref, down_ref, join_ref):
        values = total_ref[...] * scale
        back = [values[0:8], values[8:16]]
        ahead = [values[16 : 20 + blocks], values[20 + blocks : 24 + 2 * blocks]]
        for place in range(shares):

            @pl.when(me_ref[0] == place)
            def _():
                columns = slice(place * part, place * part + part)
                for layer in range(2):
                    for row, target in ((0, gains_ref), (1, shifts_ref)):
                        target[layer, 0:1] = back[layer][row : row + 1, columns]
                        target[layer, 1:2] = ahead[layer][row + 1 : row + 2, columns]
                    out_ref[layer : layer + 1] = ahead[layer][3:4, columns]
                    down_ref[layer : layer + 1] = ahead[layer][0:1, columns]
                    begin = place * part * blocks
                    while begin < (place + 1) * part * blocks:
                        row, column = begin // width, begin % width
                        length = min(width - column, (place + 1) * part * blocks - begin)
                        at = begin - place * part * blocks
                        piece = ahead[layer][4 + row : 5 + row, column : column + length]
                        up_ref[layer : layer + 1, at : at + length] = piece
                        begin += length
                join_ref[...] = back[1][2:3, columns]

    shapes = [(2, 2, part), (2, 2, part), (2, part), (2, part * blocks), (2, part), (1, part)]
    outs = [(shape, full, pl.BlockSpec(shape, lambda g, me, n=len(shape): (0,) * n)) for shape in shapes]
    ins = [(total, pl.BlockSpec(total.shape, lambda g, me: (0, 0)))]
    return picked(body, me, (1,), ins, outs, "small_gradients", 1)


def after(value, *earlier):
    return lax.optimization_barrier((value,) + earlier)[0] if earlier else value


def swap(values, axis, mask):
    size = lax.axis_size(axis)
    return lax.ppermute(values, axis, [(source, source ^ mask) for source in range(size)])


def masks(axis):
    return [1 << bit for bit in range(lax.axis_size(axis).bit_length() - 1)]


class Order:
    def __init__(self):
        self.last = ()

    def run(self, function, *arrays):
        held = lax.optimization_barrier(tuple(arrays) + self.last)[: len(arrays)]
        out = function(*held)
        self.last = (jax.tree.leaves(out)[0],)
        return out

    def hold(self, *arrays):
        self.last += arrays


def place_bit(axis, mask):
    return ((lax.axis_index(axis) & mask) // mask).astype(jnp.int32).reshape(1)


class Term:
    def __init__(self, order, kind, layer, function, *arrays):
        self.order, self.kind, self.layer, self.half = order, kind, layer, None
        self.core = place_bit("wide", 1)
        sent = order.run(lambda *x: function(*x, 1 - self.core), *arrays)
        self.got = [swap(each, "wide", 1) for each in sent]
        self.columns = sent[0].shape[-1]
        self.keep = lambda: order.run(lambda *x: function(*x, self.core), *arrays)

    def stay(self):
        self.kept, self.keep = self.keep(), None

    def part(self, half):
        other = copy.copy(self)
        other.kept, other.got, other.half = self.kept[half::2], self.got[half::2], half
        return other

    def pass_narrow(self):
        stages = list(reversed(masks("narrow")))
        if isinstance(self.kept, (list, tuple)):
            bit = place_bit("narrow", stages[0])
            blocks = len(self.kept) // 2
            sent, self.kept = self.order.run(lambda *x: cross(bit, *x), *self.kept, *self.got)
            self.got = swap(sent, "narrow", stages.pop(0))
        else:
            blocks = 1
        for mask in stages:
            pairs = [(self.kept, self.got)]
            self.kept, self.got = halve(self.order, "narrow", mask, blocks, pairs, self.columns)

    def pass_first(self, mask):
        swapped = [self.kept[owner * 2 + block] for block in range(2) for owner in range(2)]
        brought = [self.got[owner * 2 + block] for block in range(2) for owner in range(2)]
        bit = place_bit("wide", mask)
        sent, self.kept = self.order.run(lambda *x: cross(bit, *x), *swapped, *brought)
        self.got = swap(sent, "wide", mask)

    def pass_wide(self, mask):
        pairs = list(zip(self.kept, self.got)) if isinstance(self.kept, (list, tuple)) else [(self.kept, self.got)]
        self.kept, self.got = halve(self.order, "wide", mask, 1, pairs, self.columns)

    def add_into(self, target, place, count):
        kept, got = [side.reshape(-1, self.columns) for side in (self.kept, self.got)]
        if target is None:
            return self.order.run(lambda one, two: add_into(None, place, count, one, two), kept, got)
        return self.order.run(lambda target, one, two: add_into(target, place, count, one, two), target, kept, got)

    def finish(self, done, own, got, begin, length):
        targets = done.get(self.kind, ())

        def last(own, got, core, *targets):
            return finish(self.kind, self.half, own, got, begin, length, core, self.layer, targets)

        done[self.kind] = self.order.run(last, own, got, self.core, *targets)


def halve(order, axis, mask, lead, pairs, columns):
    shaped = [array.reshape(lead, 2, -1, columns) for pair in pairs for array in pair]
    bit = place_bit(axis, mask)
    sent, kept = order.run(lambda *x: add_halve(bit, *x), *shaped)
    return kept, swap(sent, axis, mask)


class Reduce:
    def __init__(self, order, terms, passed=(), late=()):
        self.order, self.terms = order, terms
        rest = [mask for mask in masks("wide")[1:] if mask not in passed]
        self.down = [mask for mask in rest if mask not in late] + [mask for mask in rest if mask in late]
        self.up = list(reversed(passed))
        self.pieces, self.columns = 2 ** len(passed), terms[0].columns
        self.parts = [(term.kept, term.got) for term in terms]
        self.lengths, self.first = [each.size // self.columns for each, _ in self.parts], True
        self.joining, self.closed = None, False

    def step(self):
        if self.closed:
            return
        if self.down:
            mask = self.down.pop(0)
            rows = [kept.size // self.columns for kept, _ in self.parts]
            even = all(each % 32 == 0 for each in rows)
            if self.first and even:
                self.pieces, self.lengths = 2 * self.pieces, [each // 2 for each in rows]
            self.first = False
            if even:
                self.up.insert(0, mask)
                self.parts = [halve(self.order, "wide", mask, 1, self.parts, self.columns)]
            else:
                flat = [[side.reshape(-1, self.columns) for side in pair] for pair in self.parts]
                pair = [jnp.concatenate(sides) for sides in zip(*flat)]
                total = self.order.run(add, *pair)
                self.parts = [(total, swap(total, "wide", mask))]
            return
        kept, got = [array.reshape(-1, self.columns) for array in self.parts[0]]
        if self.joining is None:
            total = self.order.run(add, kept, got)
        else:
            bit = place_bit("wide", self.joining)
            total = self.order.run(lambda *x: pair_up(*x, bit), kept, got).reshape(-1, self.columns)
        if self.up:
            self.joining = self.up.pop(0)
            self.parts = [(total, swap(total, "wide", self.joining))]
        else:
            self.parts = [(total, swap(total, "wide", 1))]
            self.closed = True

    def finish(self, done):
        own, got = [array.reshape(self.pieces, -1, self.columns) for array in self.parts[0]]
        begin = 0
        for term, length in zip(self.terms, self.lengths):
            term.finish(done, own, got, begin, length)
            begin += length


def on_device(
    tokens,
    skip,
    flags,
    cotangent,
    norm_gains,
    norm_biases,
    qkv_weight,
    out_weight,
    out_bias,
    up_weight,
    up_bias,
    down_weight,
    down_bias,
    skip_weight,
    skip_bias,
):
    items, seq_rows, width = tokens.shape
    rows = items * seq_rows
    me = lax.axis_index("narrow")
    shares = lax.axis_size("narrow")
    spots = jnp.stack([me, lax.axis_index("wide")]).astype(jnp.int32)
    order = Order()

    def fetches(layer):
        return (
            Fetch([(qkv_weight, layer)], (1, 2)),
            Fetch([(out_weight, layer), (up_weight, layer)], (1, 2)),
            Fetch([(down_weight, layer)], (1, 4)),
        )

    fetch_qkv0, fetch_up0, fetch_down0 = fetches(0)
    fetch_qkv1, fetch_up1, fetch_down1 = fetches(1)
    fetch_join = Fetch([(skip_weight, None)], (1, 4))
    qkv0, qkv1 = [Weight(each, 0, width, spots) for each in (fetch_qkv0, fetch_qkv1)]
    out0, out1 = [Weight(each, 0, width, spots) for each in (fetch_up0, fetch_up1)]
    up0, up1 = [Weight(each, 1, width, spots) for each in (fetch_up0, fetch_up1)]
    down0, down1 = [Weight(each, 0, width, spots) for each in (fetch_down0, fetch_down1)]
    join = Weight(fetch_join, 0, width, spots)

    small = (norm_gains, norm_biases, out_bias, down_bias, skip_bias, up_bias)
    held = order.run(pack_small, *small)[None]
    for mask in masks("narrow"):
        held = jnp.concatenate([held, swap(held, "narrow", mask)])
    fetch_qkv0.fetch(*order.last)
    fetch_up0.fetch(held)
    fetch_down0.fetch(fetch_up0.sent)
    fetch_join.fetch(fetch_down0.sent)
    fetch_qkv1.fetch(fetch_join.sent)
    place = me.astype(jnp.int32).reshape(1)
    lines = order.run(lambda x: unpack_small(x, place, small, width), held)

    def line(row):
        return lines[row : row + 1]

    gains, shifts = [[line(2 * layer + each) for each in range(2)] for layer in range(2)], None
    shifts = [[line(4 + 2 * layer + each) for each in range(2)] for layer in range(2)]
    out_biases, down_biases, join_shift = [line(8), line(9)], [line(10), line(11)], line(12)
    blocks = up0.blocks
    up_biases = [lines[13 + layer * blocks : 13 + (layer + 1) * blocks].reshape(1, -1) for layer in range(2)]

    tokens_flat, skip_flat, cotangent_flat = [array.reshape(rows, width) for array in (tokens, skip, cotangent)]
    lengths = PATCHES + 1 + CAPTION * flags
    valid = lax.broadcasted_iota(jnp.int32, (items, seq_rows), 1) < lengths[:, None]
    keep = valid.reshape(rows, 1).astype(full)
    dz1 = jnp.where(keep > 0, cotangent_flat, 0)

    fetch_qkv0.share(1)
    fetch_qkv0.share(0)
    order.hold(*fetch_up0.got())
    fetch_up0.share(1)
    a0, packed0 = order.run(lambda *x: project_qkv(*x, qkv0), tokens_flat, gains[0][0], shifts[0][0])
    order.hold(*fetch_down0.got())
    fetch_down0.share(1, a0)
    fetch_up1.fetch(a0)
    fetch_down1.fetch(fetch_up1.sent)
    packed0 = packed0.reshape(3, items, seq_rows, width)
    mixed0, totals0 = order.run(lambda *x: attend(*x, items, seq_rows), packed0, lengths)
    fetch_up0.share(0, mixed0)
    fetch_down0.share(0, mixed0)
    order.hold(*fetch_join.got(), *fetch_qkv1.got())
    fetch_join.share(1, mixed0)
    fetch_qkv1.share(1, mixed0)
    mixed0 = mixed0.reshape(rows, width)
    m0, second0, hidden0, slope0, middle = order.run(
        lambda x, o, ob, g, s, ub, db: feed_forward(x, o, out0, ob, g, s, up0, ub, down0, db),
        tokens_flat, mixed0, out_biases[0], gains[0][1], shifts[0][1], up_biases[0], down_biases[0],
    )
    fetch_join.share(0, middle)
    fetch_qkv1.share(0, middle)
    order.hold(*fetch_up1.got(), *fetch_down1.got())
    fetch_up1.share(1, middle)
    fetch_down1.share(1, middle)
    entry, a1, packed1 = order.run(
        lambda m, s, jb, g, sh: join_qkv(m, s, join, jb, g, sh, qkv1),
        middle, skip_flat, join_shift, gains[1][0], shifts[1][0],
    )
    packed1 = packed1.reshape(3, items, seq_rows, width)
    mixed1, totals1 = order.run(lambda *x: attend(*x, items, seq_rows), packed1, lengths)
    fetch_up1.share(0, mixed1)
    fetch_down1.share(0, mixed1)
    mixed1 = mixed1.reshape(rows, width)
    m1, second1, hidden1, slope1, output = order.run(
        lambda x, o, ob, g, s, ub, db, k: feed_forward(x, o, out1, ob, g, s, up1, ub, down1, db, k),
        entry, mixed1, out_biases[1], gains[1][1], shifts[1][1], up_biases[1], down_biases[1], keep,
    )

    done = {}
    term_down1 = Term(order, "down", 1, down_term, hidden1, dz1)
    term_down1.stay()
    term_down1.pass_narrow()
    du, dm, db, do, sums1 = order.run(
        lambda y, z, s, m, g: feed_forward_back(y, z, s, down1, up1, m, g, out1),
        dz1, dz1, slope1, m1, gains[1][1],
    )
    term_up1 = Term(order, "up", 1, up_term, second1, du)
    term_up1.stay()
    term_up1.pass_narrow()
    total = term_down1.add_into(None, 0, 3)
    dpacked = order.run(
        lambda *x: attend_back(*x, items, seq_rows), packed1, do.reshape(items, seq_rows, width), totals1, lengths
    )
    flat_packed = dpacked.reshape(3, rows, width)
    term_qkv1 = Term(order, "qkv", 1, qkv_out_term, a1, flat_packed, mixed1, db)
    term_qkv1.stay()
    term_qkv1.pass_narrow()
    total = term_up1.add_into(total, 1, 3)
    dentry, dmiddle, dz0, skip_grad, sums3 = order.run(
        lambda gp, x, g, dm: project_back(gp, qkv1, x, g, dm, join), flat_packed, entry, gains[1][0], dm
    )
    term_join = Term(order, "join", 1, join_term, middle, skip_flat, dentry)
    term_join.stay()
    term_join.pass_narrow()
    term_down0 = Term(order, "down", 0, down_term, hidden0, dz0)
    term_down0.stay()
    total = term_qkv1.add_into(total, 2, 3)
    size = lax.axis_size("wide")
    groups = [[device + core for device in range(0, size, 2)] for core in range(2)]
    flat_total = total.reshape(-1, width)
    part = lax.psum_scatter(flat_total, "wide", axis_index_groups=groups, scatter_dimension=0, tiled=True)
    term_down0.pass_first(2)

    du, dm, db, do, sums0 = order.run(
        lambda y, z, s, m, g: feed_forward_back(y, z, s, down0, up0, m, g, out0),
        dmiddle, dz0, slope0, m0, gains[0][1],
    )
    term_join.pass_wide(2)
    term_up0 = Term(order, "up", 0, up_term, second0, du)
    term_up0.stay()
    term_down0.pass_narrow()
    term_up0.pass_narrow()
    dpacked = order.run(
        lambda *x: attend_back(*x, items, seq_rows), packed0, do.reshape(items, seq_rows, width), totals0, lengths
    )
    order.hold(term_down0.got, term_join.got)
    flat_packed = dpacked.reshape(3, rows, width)
    term_qkv0 = Term(order, "qkv", 0, qkv_out_term, a0, flat_packed, mixed0, db)
    term_qkv0.stay()
    one, two = term_qkv0.part(0), term_qkv0.part(1)
    one.pass_narrow()
    two.pass_narrow()
    order.hold(term_up0.got, part)
    first = Reduce(order, [term_down0, term_join], (2,))
    first.step()
    gathered = lax.all_gather(after(part, *order.last), "wide", axis_index_groups=groups, tiled=True)
    second = Reduce(order, [term_up0])
    second.step()
    tokens_grad, sums2 = order.run(
        lambda gp, x, g, dm: project_back(gp, qkv0, x, g, dm), flat_packed, tokens_flat, gains[0][0], dm
    )
    minor = jnp.concatenate([sums2, sums3, sums0, sums1])
    places = masks("wide")
    minor_stages = [("narrow", mask) for mask in masks("narrow")]
    minor_stages += [("wide", mask) for mask in places if mask != 2] + [("wide", mask) for mask in places if mask == 2]
    minor_got = swap(minor, *minor_stages[0])

    def minor_step():
        nonlocal minor, minor_got
        if minor_stages:
            minor_stages.pop(0)
            minor = order.run(lambda one, two: one + two, minor, minor_got)
            if minor_stages:
                minor_got = swap(minor, *minor_stages[0])

    first.step()
    third = Reduce(order, [one])
    third.step()
    second.step()
    fourth = Reduce(order, [two], late=(2,))
    fourth.step()
    first.step()
    third.step()
    minor_step()
    second.step()
    fourth.step()
    minor_step()
    fourth.step()
    first.step()
    third.step()
    minor_step()
    second.step()
    fourth.step()
    order.hold(gathered)
    other = swap(after(gathered, *order.last), "wide", 1)
    first.step()
    third.step()
    own, got = gathered.reshape(1, -1, width), other.reshape(1, -1, width)
    for which, term in enumerate((term_down1, term_up1, term_qkv1)):
        term.finish(done, own, got, which * (own.shape[1] // 3), own.shape[1] // 3)
    second.step()
    fourth.step()
    third.step()
    minor_step()
    first.step()
    fourth.step()
    second.step()
    third.step()
    first.finish(done)
    fourth.step()
    second.step()
    third.step()
    for each in (first, second, third, fourth):
        while not each.closed:
            each.step()
    while minor_stages:
        minor_step()
    fourth.finish(done)
    second.finish(done)
    third.finish(done)
    small = order.run(lambda x: small_gradients(x, place, width, shares, up1.blocks), minor)

    return (
        output.reshape(tokens.shape),
        tokens_grad.reshape(tokens.shape),
        skip_grad.reshape(tokens.shape),
        small[0],
        small[1],
        done["qkv"][0],
        done["qkv"][1],
        small[2],
        done["up"][0],
        small[3],
        done["down"][0],
        small[4],
        done["join"][0][0],
        small[5].reshape(-1),
    )


def solution(mesh):
    placed = (
        P(("wide", "narrow"), None, None),
        P(("wide", "narrow"), None, None),
        P(("wide", "narrow")),
        P(("wide", "narrow"), None, None),
        P(None, None, "narrow"),
        P(None, None, "narrow"),
        P(None, "narrow", None),
        P(None, "narrow", None),
        P(None, "narrow"),
        P(None, "narrow", None),
        P(None, "narrow"),
        P(None, "narrow", None),
        P(None, "narrow"),
        P("narrow", None),
        P("narrow"),
    )
    return jax.shard_map(
        on_device,
        mesh=mesh,
        in_specs=placed,
        out_specs=(
            P(("wide", "narrow"), None, None),
            P(("wide", "narrow"), None, None),
            P(("wide", "narrow"), None, None),
            P(None, None, "narrow"),
            P(None, None, "narrow"),
            P(None, "narrow", None),
            P(None, "narrow", None),
            P(None, "narrow"),
            P(None, "narrow", None),
            P(None, "narrow"),
            P(None, "narrow", None),
            P(None, "narrow"),
            P("narrow", None),
            P("narrow"),
        ),
        check_vma=False,
    )
```

profile of v0, /device:TPU:1, one launch (start us, length us, event | category | flops | bytes accessed | tf_op | source)
XLA Modules:
  0.0 551.4 jit_solution(11711366089372693957)
XLA Ops:
  19.1 6.3 %collective-permute-done.refs_2_ = bf16[1,96,2304]{2,1,0:T(8,128)(2,1)S(1)} collective-permute-done((bf16[1,96,2304]{2,1,0:T(8,128)(2,1)S(1)}, bf16[1,96,2304]{2,1,0:T(8,128)(2,1)S(1)}, u32[]{:S(2)}, u32[]{:S(2)}) %collective-permute-start) | collective-permute-done | bytes 442400 | tf_op jit(solution)/shard_map/ppermute | solution.py:1013
  27.1 3.9 collective-permute-start.2
  31.0 10.2 %collective-permute-done.5.refs_2_.refs_7_.refs_12_ = bf16[1,96,3840]{2,1,0:T(8,128)(2,1)S(1)} collective-permute-done((bf16[1,96,3840]{2,1,0:T(8,128)(2,1)S(1)}, bf16[1,96,3840]{2,1,0:T(8,128)(2,1)S(1)}, u32[]{:S(2)}, u32[]{:S(2)}) %collective-permute-start.5) | collective-permute-done | bytes 737312 | tf_op jit(solution)/shard_map/ppermute | solution.py:1013
  42.4 3.6 collective-permute-start.3
  47.5 4.8 project_qkv.1
  55.1 8.7 %attend.2 = (bf16[2,336,768]{2,1,0:T(8,128)(2,1)S(1)}, f32[2,6,8,336]{3,2,1,0:T(8,128)S(1)}) custom-call(s32[2]{0:T(128)S(1)} %multiply_add_fusion.length_ref, bf16[3,2,336,768]{3,2,1,0:T(8,128)(2,1)S(1)} %bitcast.197, bf16[3,2,336,768]{3,2,1,0:T(8,128)(2,1)S(1)} %bitcast.198, bf16[3,2,336,768]{3,2,1,0:T(8,128)(2,1)S(1)} %bitcast.199), custom_call_target="tpu_custom_call" | custom-call | flops 3000000000 | tf_op jit(solution)/shard_map/attend/pallas_call | solution.py:69
  63.9 3.7 collective-permute-start.9
  75.1 20.4 %feed_forward.2 = (f32[672,768]{1,0:T(8,128)}, bf16[672,768]{1,0:T(8,128)(2,1)S(1)}, bf16[672,3072]{1,0:T(8,128)(2,1)}, bf16[672,3072]{1,0:T(8,128)(2,1)}, bf16[672,768]{1,0:T(8,128)(2,1)S(1)}) custom-call(s32[2]{0:T(128)S(1)} %pad_add_fusion.refs_0_, bf16[2,384,768]{2,1,0:T(8,128)(2,1)S(1)} %copy-done.11, ...), custom_call_target="tpu_custom_call" | custom-call | flops 6899999744 | tf_op jit(solution)/shard_map/feed_forward/pallas_call | solution.py:69
  95.6 2.9 collective-permute-start.22
  101.4 7.5 %join_qkv.1 = (f32[672,768]{1,0:T(8,128)S(1)}, bf16[672,768]{1,0:T(8,128)(2,1)S(1)}, bf16[3,672,768]{2,1,0:T(8,128)(2,1)S(1)}) custom-call(s32[2]{0:T(128)S(1)} %pad_add_fusion.refs_0_, bf16[768,768]{1,0:T(8,128)(2,1)S(1)} %copy-done.46, bf16[1,192,768]{2,1,0:T(8,128)(2,1)S(1)} %collective-permute-done.14.refs_2_.refs_7_, ...), custom_call_target="tpu_custom_call" | custom-call | flops 3300000000 | tf_op jit(solution)/shard_map/join_qkv/pallas_call | solution.py:69
  109.1 8.7 %attend.3 = (bf16[2,336,768]{2,1,0:T(8,128)(2,1)S(1)}, f32[2,6,8,336]{3,2,1,0:T(8,128)S(1)}) custom-call(s32[2]{0:T(128)S(1)} %multiply_add_fusion.length_ref, bf16[3,2,336,768]{3,2,1,0:T(8,128)(2,1)S(1)} %bitcast.203, bf16[3,2,336,768]{3,2,1,0:T(8,128)(2,1)S(1)} %bitcast.204, bf16[3,2,336,768]{3,2,1,0:T(8,128)(2,1)S(1)} %bitcast.205), custom_call_target="tpu_custom_call" | custom-call | flops 3000000000 | tf_op jit(solution)/shard_map/attend/pallas_call | solution.py:69
  117.8 3.2 collective-permute-start.24
  127.0 22.8 %feed_forward.3 = (f32[672,768]{1,0:T(8,128)}, bf16[672,768]{1,0:T(8,128)(2,1)S(1)}, bf16[672,3072]{1,0:T(8,128)(2,1)}, bf16[672,3072]{1,0:T(8,128)(2,1)}, bf16[672,768]{1,0:T(8,128)(2,1)}) custom-call(s32[2]{0:T(128)S(1)} %pad_add_fusion.refs_0_, bf16[2,384,768]{2,1,0:T(8,128)(2,1)S(1)} %copy-done.11, ...), custom_call_target="tpu_custom_call" | custom-call | flops 6899999744 | tf_op jit(solution)/shard_map/feed_forward/pallas_call | solution.py:69
  152.4 4.1 down_term.4
  159.7 2.8 down_term.5
  164.7 19.6 %feed_forward_back.2 = (bf16[672,3072]{1,0:T(8,128)(2,1)}, f32[672,768]{1,0:T(8,128)}, bf16[672,768]{1,0:T(8,128)(2,1)S(1)}, bf16[672,768]{1,0:T(8,128)(2,1)S(1)}, f32[8,768]{1,0:T(8,128)S(1)}) custom-call(s32[2]{0:T(128)S(1)} %pad_add_fusion.refs_0_, bf16[2,1536,768]{2,1,0:T(8,128)(2,1)} %refs_1_.15, ...), custom_call_target="tpu_custom_call" | custom-call | flops 6300000256 | tf_op jit(solution)/shard_map/feed_forward_back/pallas_call | solution.py:69
  184.4 2.9 copy-done.7
  187.3 2.7 up_term.4
  191.3 2.7 up_term.5
  205.3 14.0 %attend_back.2 = bf16[3,2,336,768]{3,2,1,0:T(8,128)(2,1)S(1)} custom-call(s32[2]{0:T(128)S(1)} %multiply_add_fusion.length_ref, bf16[3,2,336,768]{3,2,1,0:T(8,128)(2,1)S(1)} %bitcast.206, bf16[3,2,336,768]{3,2,1,0:T(8,128)(2,1)S(1)} %bitcast.207, bf16[3,2,336,768]{3,2,1,0:T(8,128)(2,1)S(1)} %bitcast.208, bf16[2,336,768]{2,1,0:T(8,128)(2,1)S(1)} %bitcast.175, ...), custom_call_target="tpu_custom_call" | custom-call | flops 4499999744 | tf_op jit(solution)/shard_map/attend_back/pallas_call | solution.py:69
  229.4 2.7 add_into.4.rest_0_
  240.3 12.5 %project_back.2 = (bf16[672,768]{1,0:T(8,128)(2,1)S(1)}, f32[672,768]{1,0:T(8,128)S(1)}, bf16[672,768]{1,0:T(8,128)(2,1)S(1)}, f32[672,768]{1,0:T(8,128)}, f32[8,768]{1,0:T(8,128)S(1)}) custom-call(s32[2]{0:T(128)S(1)} %pad_add_fusion.refs_0_, bf16[2,384,2304]{2,1,0:T(8,128)(2,1)} %refs_1_.16, bf16[1,96,2304]{2,1,0:T(8,128)(2,1)S(1)} %copy-done.72, ...), custom_call_target="tpu_custom_call" | custom-call | flops 3900000000 | tf_op jit(solution)/shard_map/project_back/pallas_call | solution.py:69
  257.6 2.7 down_term.6
  261.2 2.7 down_term.7
  275.4 20.3 %feed_forward_back.3 = (bf16[672,3072]{1,0:T(8,128)(2,1)}, f32[672,768]{1,0:T(8,128)}, bf16[672,768]{1,0:T(8,128)(2,1)S(1)}, bf16[672,768]{1,0:T(8,128)(2,1)}, f32[8,768]{1,0:T(8,128)S(1)}) custom-call(s32[2]{0:T(128)S(1)} %pad_add_fusion.refs_0_, bf16[2,1536,768]{2,1,0:T(8,128)(2,1)} %refs_1_.15, bf16[1,384,768]{2,1,0:T(8,128)(2,1)S(1)} %copy-done.56, ...), custom_call_target="tpu_custom_call" | custom-call | flops 6300000256 | tf_op jit(solution)/shard_map/feed_forward_back/pallas_call | solution.py:69
  299.6 2.7 up_term.6
  303.9 2.7 up_term.7
  306.6 4.9 collective-permute-done.57
  317.2 13.9 %attend_back.3 = bf16[3,2,336,768]{3,2,1,0:T(8,128)(2,1)S(1)} custom-call(s32[2]{0:T(128)S(1)} %copy-done.95, bf16[3,2,336,768]{3,2,1,0:T(8,128)(2,1)S(1)} %bitcast.200, bf16[3,2,336,768]{3,2,1,0:T(8,128)(2,1)S(1)} %bitcast.201, bf16[3,2,336,768]{3,2,1,0:T(8,128)(2,1)S(1)} %bitcast.202, bf16[2,336,768]{2,1,0:T(8,128)(2,1)S(1)} %bitcast.174, ...), custom_call_target="tpu_custom_call" | custom-call | flops 4499999744 | tf_op jit(solution)/shard_map/attend_back/pallas_call | solution.py:69
  331.2 4.0 qkv_out_term.6
  351.9 3.6 reduce-scatter.2.cloned.1.call-done
  374.8 7.4 %project_back.3 = (f32[672,768]{1,0:T(8,128)}, f32[8,768]{1,0:T(8,128)S(1)}) custom-call(s32[2]{0:T(128)S(1)} %pad_add_fusion.refs_0_, bf16[2,384,2304]{2,1,0:T(8,128)(2,1)S(1)} %copy-done.4, bf16[1,96,2304]{2,1,0:T(8,128)(2,1)S(1)} %copy-done.64, bf16[1,96,2304]{2,1,0:T(8,128)(2,1)S(1)} %copy-done.66, bf16[1,96,2304]{2,1,0:T(8,128)(2,1)S(1)} %copy-done.68, ...), custom_call_target="tpu_custom_call" | custom-call | flops 2700000000 | tf_op jit(solution)/shard_map/project_back/pallas_call | solution.py:69
  390.0 10.9 %collective-permute-done.69 = bf16[1,144,768]{2,1,0:T(8,128)(2,1)S(1)} collective-permute-done((bf16[1,144,768]{2,1,0:T(8,128)(2,1)S(1)}, bf16[1,144,768]{2,1,0:T(8,128)(2,1)S(1)}, u32[]{:S(2)}, u32[]{:S(2)}) %collective-permute-start.69) | collective-permute-done | bytes 221216 | tf_op jit(solution)/shard_map/ppermute | solution.py:1013
  401.3 13.6 %collective-permute-done.73 = bf16[1,192,768]{2,1,0:T(8,128)(2,1)S(1)} collective-permute-done((bf16[1,192,768]{2,1,0:T(8,128)(2,1)S(1)}, bf16[1,192,768]{2,1,0:T(8,128)(2,1)S(1)}, u32[]{:S(2)}, u32[]{:S(2)}) %collective-permute-start.73) | collective-permute-done | bytes 294944 | tf_op jit(solution)/shard_map/ppermute | solution.py:1013
  416.6 6.1 %collective-permute-start.72 = (f32[32,768]{1,0:T(8,128)S(1)}, f32[32,768]{1,0:T(8,128)S(1)}, u32[]{:S(2)}, u32[]{:S(2)}) collective-permute-start(f32[32,768]{1,0:T(8,128)S(1)} %add.75), channel_id=1, source_target_pairs={{0,2},{2,0},{4,6},{6,4},{8,10},{10,8},{12,14},{14,12},{16,18},{18,... | collective-permute-start | bytes 294920 | tf_op jit(solution)/shard_map/ppermute | solution.py:1013
  422.7 2.6 collective-permute-start.76
  426.8 6.2 %collective-permute-done.78 = bf16[1,96,768]{2,1,0:T(8,128)(2,1)S(1)} collective-permute-done((bf16[1,96,768]{2,1,0:T(8,128)(2,1)S(1)}, bf16[1,96,768]{2,1,0:T(8,128)(2,1)S(1)}, u32[]{:S(2)}, u32[]{:S(2)}) %collective-permute-start.78) | collective-permute-done | bytes 147488 | tf_op jit(solution)/shard_map/ppermute | solution.py:1013
  433.2 6.1 %collective-permute-done.76 = bf16[1,96,768]{2,1,0:T(8,128)(2,1)S(1)} collective-permute-done((bf16[1,96,768]{2,1,0:T(8,128)(2,1)S(1)}, bf16[1,96,768]{2,1,0:T(8,128)(2,1)S(1)}, u32[]{:S(2)}, u32[]{:S(2)}) %collective-permute-start.76) | collective-permute-done | bytes 147488 | tf_op jit(solution)/shard_map/ppermute | solution.py:1013
  439.4 8.6 %collective-permute-done.75 = f32[32,768]{1,0:T(8,128)S(1)} collective-permute-done((f32[32,768]{1,0:T(8,128)S(1)}, f32[32,768]{1,0:T(8,128)S(1)}, u32[]{:S(2)}, u32[]{:S(2)}) %collective-permute-start.75) | collective-permute-done | bytes 98336 | tf_op jit(solution)/shard_map/ppermute | solution.py:1013
  448.1 7.5 %all-gather.2.cloned.1.call-done = bf16[2304,768]{1,0:T(8,128)(2,1)} async-done(((bf16[288,768]{1,0:T(8,128)(2,1)}), bf16[2304,768]{1,0:T(8,128)(2,1)}) %all-gather.2.cloned.1.call-update) | async-done | bytes 3538960 | tf_op jit(solution)/shard_map/all_gather | solution.py:1316
  456.1 11.7 %collective-permute-done.81.got_ref = bf16[288,768]{1,0:T(8,128)(2,1)S(1)} collective-permute-done((bf16[288,768]{1,0:T(8,128)(2,1)S(1)}, bf16[288,768]{1,0:T(8,128)(2,1)S(1)}, u32[]{:S(2)}, u32[]{:S(2)}) %collective-permute-start.81) | collective-permute-done | bytes 442400 | tf_op jit(solution)/shard_map/ppermute | solution.py:1013
  471.0 8.3 %collective-permute-done.80 = bf16[1,48,768]{2,1,0:T(8,128)(2,1)S(1)} collective-permute-done((bf16[1,48,768]{2,1,0:T(8,128)(2,1)S(1)}, bf16[1,48,768]{2,1,0:T(8,128)(2,1)S(1)}, u32[]{:S(2)}, u32[]{:S(2)}) %collective-permute-start.80) | collective-permute-done | bytes 73760 | tf_op jit(solution)/shard_map/ppermute | solution.py:1013
  483.2 2.7 finish_rows.3.rest_0_
  489.5 3.3 finish_qkv_out.2
  497.1 8.9 %collective-permute-done.91.got_ref = bf16[96,768]{1,0:T(8,128)(2,1)S(1)} collective-permute-done((bf16[96,768]{1,0:T(8,128)(2,1)S(1)}, bf16[96,768]{1,0:T(8,128)(2,1)S(1)}, u32[]{:S(2)}, u32[]{:S(2)}) %collective-permute-start.91) | collective-permute-done | bytes 147488 | tf_op jit(solution)/shard_map/ppermute | solution.py:1013
  509.5 3.0 collective-permute-done.89.got_ref
  523.9 7.6 %collective-permute-done.93.got_ref = bf16[192,768]{1,0:T(8,128)(2,1)S(1)} collective-permute-done((bf16[192,768]{1,0:T(8,128)(2,1)S(1)}, bf16[192,768]{1,0:T(8,128)(2,1)S(1)}, u32[]{:S(2)}, u32[]{:S(2)}) %collective-permute-start.93) | collective-permute-done | bytes 294944 | tf_op jit(solution)/shard_map/ppermute | solution.py:1013
  533.1 3.7 collective-permute-done.88
  (546 shorter events, 188.3 us)
Async XLA Ops:
  7.2 348.3 %reduce-scatter.2.cloned.1.call-start = ((), (), s32[]{:S(2)}) async-start(), calls=%async_computation.1 | async-start | bytes 3981312 | tf_op jit(solution)/shard_map/reduce_scatter | solution.py:1291
  16.1 25.1 %collective-permute-start.5 = (bf16[1,96,3840]{2,1,0:T(8,128)(2,1)S(1)}, bf16[1,96,3840]{2,1,0:T(8,128)(2,1)S(1)}, u32[]{:S(2)}, u32[]{:S(2)}) collective-permute-start(bf16[1,96,3840]{2,1,0:T(8,128)(2,1)S(1)} %maximum_bitcast_fusion), channel_id=1, source_target_pairs={{0,1},{1,0},{2,3},{3,2},{4,5},{5,4},{6,7},{7,6},{8,9},{9,8},{10,11... | collective-permute-start | bytes 2211848 | tf_op jit(solution)/shard_map/ppermute | solution.py:1013
  18.8 35.0 %collective-permute-start.8 = (bf16[1,384,768]{2,1,0:T(8,128)(2,1)S(1)}, bf16[1,384,768]{2,1,0:T(8,128)(2,1)S(1)}, u32[]{:S(2)}, u32[]{:S(2)}) collective-permute-start(bf16[1,384,768]{2,1,0:T(8,128)(2,1)S(1)} %constant_dynamic-slice_fusion.2), channel_id=1, source_target_pairs={{0,1},{1,0},{2,3},{3,2},{4,5},{5,4},{6,7},{7,6},{8,9},{9,8},{10,11... | collective-permute-start | bytes 1769480 | tf_op jit(solution)/shard_map/ppermute | solution.py:1013
  25.4 17.0 %collective-permute-start.1 = (bf16[1,96,2304]{2,1,0:T(8,128)(2,1)S(1)}, bf16[1,96,2304]{2,1,0:T(8,128)(2,1)S(1)}, u32[]{:S(2)}, u32[]{:S(2)}) collective-permute-start(bf16[1,96,2304]{2,1,0:T(8,128)(2,1)S(1)} %collective-permute-done.refs_2_), channel_id=1, source_target_pairs={{0,4},{2,6},{4,0},{6,2},{8,12},{10,14},{12,8},{14,10},{16,20},{18,... | collective-permute-start | bytes 1327112 | tf_op jit(solution)/shard_map/ppermute | solution.py:1013
  26.7 42.9 %collective-permute-start.14 = (bf16[1,192,768]{2,1,0:T(8,128)(2,1)S(1)}, bf16[1,192,768]{2,1,0:T(8,128)(2,1)S(1)}, u32[]{:S(2)}, u32[]{:S(2)}) collective-permute-start(bf16[1,192,768]{2,1,0:T(8,128)(2,1)S(1)} %dynamic-slice_bitcast_fusion.2), channel_id=1, source_target_pairs={{0,1},{1,0},{2,3},{3,2},{4,5},{5,4},{6,7},{7,6},{8,9},{9,8},{10,11... | collective-permute-start | bytes 884744 | tf_op jit(solution)/shard_map/ppermute | solution.py:1013
  27.1 19.0 %collective-permute-start.2 = (bf16[1,96,2304]{2,1,0:T(8,128)(2,1)S(1)}, bf16[1,96,2304]{2,1,0:T(8,128)(2,1)S(1)}, u32[]{:S(2)}, u32[]{:S(2)}) collective-permute-start(bf16[1,96,2304]{2,1,0:T(8,128)(2,1)S(1)} %collective-permute-done.refs_2_), channel_id=1, source_target_pairs={{0,2},{2,0},{4,6},{6,4},{8,10},{10,8},{12,14},{14,12},{16,18},{18,... | collective-permute-start | bytes 1327112 | tf_op jit(solution)/shard_map/ppermute | solution.py:1013
  41.2 26.4 %collective-permute-start.7 = (bf16[1,96,3840]{2,1,0:T(8,128)(2,1)S(1)}, bf16[1,96,3840]{2,1,0:T(8,128)(2,1)S(1)}, u32[]{:S(2)}, u32[]{:S(2)}) collective-permute-start(bf16[1,96,3840]{2,1,0:T(8,128)(2,1)S(1)} %collective-permute-done.5.refs_2_.refs_7_.refs_12_), channel_id=1, source_target_pairs={{0,4},{2,6},{4,0},{6,2},{8,12},{10,14},{12,8},{14,10},{16,20},{18,... | collective-permute-start | bytes 2211848 | tf_op jit(solution)/shard_map/ppermute | solution.py:1013
  46.1 23.6 %collective-permute-start.15 = (bf16[1,96,2304]{2,1,0:T(8,128)(2,1)S(1)}, bf16[1,96,2304]{2,1,0:T(8,128)(2,1)S(1)}, u32[]{:S(2)}, u32[]{:S(2)}) collective-permute-start(bf16[1,96,2304]{2,1,0:T(8,128)(2,1)S(1)} %constant_dynamic-slice_fusion.1), channel_id=1, source_target_pairs={{0,1},{1,0},{2,3},{3,2},{4,5},{5,4},{6,7},{7,6},{8,9},{9,8},{10,11... | collective-permute-start | bytes 1327112 | tf_op jit(solution)/shard_map/ppermute | solution.py:1013
  53.8 15.1 %collective-permute-start.11 = (bf16[1,384,768]{2,1,0:T(8,128)(2,1)S(1)}, bf16[1,384,768]{2,1,0:T(8,128)(2,1)S(1)}, u32[]{:S(2)}, u32[]{:S(2)}) collective-permute-start(bf16[1,384,768]{2,1,0:T(8,128)(2,1)S(1)} %collective-permute-done.8.refs_12_.refs_2_), channel_id=1, source_target_pairs={{0,8},{2,10},{4,12},{6,14},{8,0},{10,2},{12,4},{14,6},{16,24},{18,... | collective-permute-start | bytes 1769480 | tf_op jit(solution)/shard_map/ppermute | solution.py:1013
  69.7 29.2 %collective-permute-start.6 = (bf16[1,96,3840]{2,1,0:T(8,128)(2,1)S(1)}, bf16[1,96,3840]{2,1,0:T(8,128)(2,1)}, u32[]{:S(2)}, u32[]{:S(2)}) collective-permute-start(bf16[1,96,3840]{2,1,0:T(8,128)(2,1)S(1)} %maximum_bitcast_fusion.1), channel_id=1, source_target_pairs={{0,1},{1,0},{2,3},{3,2},{4,5},{5,4},{6,7},{7,6},{8,9},{9,8},{10,11... | collective-permute-start | bytes 2211848 | tf_op jit(solution)/shard_map/ppermute | solution.py:1013
  71.8 27.3 %collective-permute-start.23 = (bf16[1,384,768]{2,1,0:T(8,128)(2,1)S(1)}, bf16[1,384,768]{2,1,0:T(8,128)(2,1)}, u32[]{:S(2)}, u32[]{:S(2)}) collective-permute-start(bf16[1,384,768]{2,1,0:T(8,128)(2,1)S(1)} %constant_dynamic-slice_fusion), channel_id=1, source_target_pairs={{0,1},{1,0},{2,3},{3,2},{4,5},{5,4},{6,7},{7,6},{8,9},{9,8},{10,11... | collective-permute-start | bytes 1769480 | tf_op jit(solution)/shard_map/ppermute | solution.py:1013
  72.5 23.1 %collective-permute-start.20 = (bf16[1,96,2304]{2,1,0:T(8,128)(2,1)S(1)}, bf16[1,96,2304]{2,1,0:T(8,128)(2,1)S(1)}, u32[]{:S(2)}, u32[]{:S(2)}) collective-permute-start(bf16[1,96,2304]{2,1,0:T(8,128)(2,1)S(1)} %collective-permute-done.15.refs_7_.refs_2_), channel_id=1, source_target_pairs={{0,4},{2,6},{4,0},{6,2},{8,12},{10,14},{12,8},{14,10},{16,20},{18,... | collective-permute-start | bytes 1327112 | tf_op jit(solution)/shard_map/ppermute | solution.py:1013
  73.7 24.8 %collective-permute-start.17 = (bf16[1,192,768]{2,1,0:T(8,128)(2,1)S(1)}, bf16[1,192,768]{2,1,0:T(8,128)(2,1)S(1)}, u32[]{:S(2)}, u32[]{:S(2)}) collective-permute-start(bf16[1,192,768]{2,1,0:T(8,128)(2,1)S(1)} %collective-permute-done.14.refs_2_.refs_7_), channel_id=1, source_target_pairs={{0,8},{2,10},{4,12},{6,14},{8,0},{10,2},{12,4},{14,6},{16,24},{18,... | collective-permute-start | bytes 884744 | tf_op jit(solution)/shard_map/ppermute | solution.py:1013
  99.1 22.0 %collective-permute-start.16 = (bf16[1,96,3840]{2,1,0:T(8,128)(2,1)}, bf16[1,96,3840]{2,1,0:T(8,128)(2,1)}, u32[]{:S(2)}, u32[]{:S(2)}) collective-permute-start(bf16[1,96,3840]{2,1,0:T(8,128)(2,1)} %collective-permute-done.6.refs_2_.refs_7_.refs_12_), channel_id=1, source_target_pairs={{0,4},{2,6},{4,0},{6,2},{8,12},{10,14},{12,8},{14,10},{16,20},{18,... | collective-permute-start | bytes 2211848 | tf_op jit(solution)/shard_map/ppermute | solution.py:1013
  100.9 20.7 %collective-permute-start.26 = (bf16[1,384,768]{2,1,0:T(8,128)(2,1)}, bf16[1,384,768]{2,1,0:T(8,128)(2,1)}, u32[]{:S(2)}, u32[]{:S(2)}) collective-permute-start(bf16[1,384,768]{2,1,0:T(8,128)(2,1)} %collective-permute-done.23.refs_12_.refs_2_), channel_id=1, source_target_pairs={{0,8},{2,10},{4,12},{6,14},{8,0},{10,2},{12,4},{14,6},{16,24},{18,... | collective-permute-start | bytes 1769480 | tf_op jit(solution)/shard_map/ppermute | solution.py:1013
  164.4 34.1 %collective-permute-start.33 = (bf16[2,384,768]{2,1,0:T(8,128)(2,1)S(1)}, bf16[2,384,768]{2,1,0:T(8,128)(2,1)S(1)}, u32[]{:S(2)}, u32[]{:S(2)}) collective-permute-start(bf16[2,384,768]{2,1,0:T(8,128)(2,1)S(1)} %get-tuple-element.541), channel_id=1, source_target_pairs={{0,1},{1,0},{2,3},{3,2},{4,5},{5,4},{6,7},{7,6},{8,9},{9,8},{10,11... | collective-permute-start | bytes 3538952 | tf_op jit(solution)/shard_map/ppermute | solution.py:1013
  197.4 32.1 %collective-permute-start.38 = (bf16[2,384,768]{2,1,0:T(8,128)(2,1)}, bf16[2,384,768]{2,1,0:T(8,128)(2,1)}, u32[]{:S(2)}, u32[]{:S(2)}) collective-permute-start(bf16[2,384,768]{2,1,0:T(8,128)(2,1)} %get-tuple-element.572), channel_id=1, source_target_pairs={{0,1},{1,0},{2,3},{3,2},{4,5},{5,4},{6,7},{7,6},{8,9},{9,8},{10,11... | collective-permute-start | bytes 3538952 | tf_op jit(solution)/shard_map/ppermute | solution.py:1013
  229.1 34.8 %collective-permute-start.51 = (bf16[2,384,768]{2,1,0:T(8,128)(2,1)}, bf16[2,384,768]{2,1,0:T(8,128)(2,1)}, u32[]{:S(2)}, u32[]{:S(2)}) collective-permute-start(bf16[2,384,768]{2,1,0:T(8,128)(2,1)} %get-tuple-element.607), channel_id=1, source_target_pairs={{0,1},{1,0},{2,3},{3,2},{4,5},{5,4},{6,7},{7,6},{8,9},{9,8},{10,11... | collective-permute-start | bytes 3538952 | tf_op jit(solution)/shard_map/ppermute | solution.py:1013
  266.5 189.1 %all-gather.2.cloned.1.call-start = ((), (), s32[]{:S(2)}) async-start(), calls=%async_computation.2 | async-start | bytes 3981312 | tf_op jit(solution)/shard_map/all_gather | solution.py:1316
  274.1 37.4 %collective-permute-start.57 = (bf16[2,384,768]{2,1,0:T(8,128)(2,1)S(1)}, bf16[2,384,768]{2,1,0:T(8,128)(2,1)S(1)}, u32[]{:S(2)}, u32[]{:S(2)}) collective-permute-start(bf16[2,384,768]{2,1,0:T(8,128)(2,1)S(1)} %get-tuple-element.667), channel_id=1, source_target_pairs={{0,4},{2,6},{4,0},{6,2},{8,12},{10,14},{12,8},{14,10},{16,20},{18,... | collective-permute-start | bytes 3538952 | tf_op jit(solution)/shard_map/ppermute | solution.py:1013
  274.2 21.6 %collective-permute-start.52 = (bf16[2,192,768]{2,1,0:T(8,128)(2,1)}, bf16[2,192,768]{2,1,0:T(8,128)(2,1)S(1)}, u32[]{:S(2)}, u32[]{:S(2)}) collective-permute-start(bf16[2,192,768]{2,1,0:T(8,128)(2,1)} %copy-done.111), channel_id=1, source_target_pairs={{0,1},{1,0},{2,3},{3,2},{4,5},{5,4},{6,7},{7,6},{8,9},{9,8},{10,11... | collective-permute-start | bytes 1769480 | tf_op jit(solution)/shard_map/ppermute | solution.py:1013
  312.8 18.3 %collective-permute-start.59 = (bf16[1,384,768]{2,1,0:T(8,128)(2,1)S(1)}, bf16[1,384,768]{2,1,0:T(8,128)(2,1)S(1)}, u32[]{:S(2)}, u32[]{:S(2)}) collective-permute-start(bf16[1,384,768]{2,1,0:T(8,128)(2,1)S(1)} %get-tuple-element.696), channel_id=1, source_target_pairs={{0,1},{1,0},{2,3},{3,2},{4,5},{5,4},{6,7},{7,6},{8,9},{9,8},{10,11... | collective-permute-start | bytes 1769480 | tf_op jit(solution)/shard_map/ppermute | solution.py:1013
  313.6 17.5 %collective-permute-start.60 = (bf16[1,192,768]{2,1,0:T(8,128)(2,1)S(1)}, bf16[1,192,768]{2,1,0:T(8,128)(2,1)S(1)}, u32[]{:S(2)}, u32[]{:S(2)}) collective-permute-start(bf16[1,192,768]{2,1,0:T(8,128)(2,1)S(1)} %get-tuple-element.680), channel_id=1, source_target_pairs={{0,4},{2,6},{4,0},{6,2},{8,12},{10,14},{12,8},{14,10},{16,20},{18,... | collective-permute-start | bytes 884744 | tf_op jit(solution)/shard_map/ppermute | solution.py:1013
  316.7 35.2 %collective-permute-start.58 = (bf16[2,384,768]{2,1,0:T(8,128)(2,1)}, bf16[2,384,768]{2,1,0:T(8,128)(2,1)}, u32[]{:S(2)}, u32[]{:S(2)}) collective-permute-start(bf16[2,384,768]{2,1,0:T(8,128)(2,1)} %get-tuple-element.705), channel_id=1, source_target_pairs={{0,1},{1,0},{2,3},{3,2},{4,5},{5,4},{6,7},{7,6},{8,9},{9,8},{10,11... | collective-permute-start | bytes 3538952 | tf_op jit(solution)/shard_map/ppermute | solution.py:1013
  361.3 22.9 %collective-permute-start.66 = (bf16[1,384,768]{2,1,0:T(8,128)(2,1)}, bf16[1,384,768]{2,1,0:T(8,128)(2,1)S(1)}, u32[]{:S(2)}, u32[]{:S(2)}) collective-permute-start(bf16[1,384,768]{2,1,0:T(8,128)(2,1)} %copy-done.108), channel_id=1, source_target_pairs={{0,1},{1,0},{2,3},{3,2},{4,5},{5,4},{6,7},{7,6},{8,9},{9,8},{10,11... | collective-permute-start | bytes 1769480 | tf_op jit(solution)/shard_map/ppermute | solution.py:1013
  362.6 25.7 %collective-permute-start.70 = (bf16[1,384,768]{2,1,0:T(8,128)(2,1)}, bf16[1,384,768]{2,1,0:T(8,128)(2,1)S(1)}, u32[]{:S(2)}, u32[]{:S(2)}) collective-permute-start(bf16[1,384,768]{2,1,0:T(8,128)(2,1)} %copy-done.105), channel_id=1, source_target_pairs={{0,1},{1,0},{2,3},{3,2},{4,5},{5,4},{6,7},{7,6},{8,9},{9,8},{10,11... | collective-permute-start | bytes 1769480 | tf_op jit(solution)/shard_map/ppermute | solution.py:1013
  362.8 19.4 %collective-permute-start.67 = (bf16[1,288,768]{2,1,0:T(8,128)(2,1)}, bf16[1,288,768]{2,1,0:T(8,128)(2,1)S(1)}, u32[]{:S(2)}, u32[]{:S(2)}) collective-permute-start(bf16[1,288,768]{2,1,0:T(8,128)(2,1)} %copy-done.116), channel_id=1, source_target_pairs={{0,8},{2,10},{4,12},{6,14},{8,0},{10,2},{12,4},{14,6},{16,24},{18,... | collective-permute-start | bytes 1327112 | tf_op jit(solution)/shard_map/ppermute | solution.py:1013
  367.0 18.0 %collective-permute-start.71 = (bf16[1,384,768]{2,1,0:T(8,128)(2,1)S(1)}, bf16[1,384,768]{2,1,0:T(8,128)(2,1)S(1)}, u32[]{:S(2)}, u32[]{:S(2)}) collective-permute-start(bf16[1,384,768]{2,1,0:T(8,128)(2,1)S(1)} %get-tuple-element.748), channel_id=1, source_target_pairs={{0,4},{2,6},{4,0},{6,2},{8,12},{10,14},{12,8},{14,10},{16,20},{18,... | collective-permute-start | bytes 1769480 | tf_op jit(solution)/shard_map/ppermute | solution.py:1013
  382.4 18.5 %collective-permute-start.69 = (bf16[1,144,768]{2,1,0:T(8,128)(2,1)S(1)}, bf16[1,144,768]{2,1,0:T(8,128)(2,1)S(1)}, u32[]{:S(2)}, u32[]{:S(2)}) collective-permute-start(bf16[1,144,768]{2,1,0:T(8,128)(2,1)S(1)} %get-tuple-element.763), channel_id=1, source_target_pairs={{0,16},{2,18},{4,20},{6,22},{8,24},{10,26},{12,28},{14,30},{16,0},... | collective-permute-start | bytes 663560 | tf_op jit(solution)/shard_map/ppermute | solution.py:1013
  382.9 18.2 %collective-permute-start.65 = (f32[32,768]{1,0:T(8,128)S(1)}, f32[32,768]{1,0:T(8,128)S(1)}, u32[]{:S(2)}, u32[]{:S(2)}) collective-permute-start(f32[32,768]{1,0:T(8,128)S(1)} %constant_dynamic-update-slice_fusion), channel_id=1, source_target_pairs={{0,1},{1,0},{2,3},{3,2},{4,5},{5,4},{6,7},{7,6},{8,9},{9,8},{10,11... | collective-permute-start | bytes 294920 | tf_op jit(solution)/shard_map/ppermute | solution.py:1013
  384.4 16.7 %collective-permute-start.68 = (bf16[1,192,768]{2,1,0:T(8,128)(2,1)S(1)}, bf16[1,192,768]{2,1,0:T(8,128)(2,1)S(1)}, u32[]{:S(2)}, u32[]{:S(2)}) collective-permute-start(bf16[1,192,768]{2,1,0:T(8,128)(2,1)S(1)} %get-tuple-element.767), channel_id=1, source_target_pairs={{0,4},{2,6},{4,0},{6,2},{8,12},{10,14},{12,8},{14,10},{16,20},{18,... | collective-permute-start | bytes 884744 | tf_op jit(solution)/shard_map/ppermute | solution.py:1013
  385.1 16.0 %collective-permute-start.74 = (bf16[1,192,768]{2,1,0:T(8,128)(2,1)S(1)}, bf16[1,192,768]{2,1,0:T(8,128)(2,1)S(1)}, u32[]{:S(2)}, u32[]{:S(2)}) collective-permute-start(bf16[1,192,768]{2,1,0:T(8,128)(2,1)S(1)} %get-tuple-element.773), channel_id=1, source_target_pairs={{0,8},{2,10},{4,12},{6,14},{8,0},{10,2},{12,4},{14,6},{16,24},{18,... | collective-permute-start | bytes 884744 | tf_op jit(solution)/shard_map/ppermute | solution.py:1013
  388.4 26.5 %collective-permute-start.73 = (bf16[1,192,768]{2,1,0:T(8,128)(2,1)S(1)}, bf16[1,192,768]{2,1,0:T(8,128)(2,1)S(1)}, u32[]{:S(2)}, u32[]{:S(2)}) collective-permute-start(bf16[1,192,768]{2,1,0:T(8,128)(2,1)S(1)} %get-tuple-element.776), channel_id=1, source_target_pairs={{0,8},{2,10},{4,12},{6,14},{8,0},{10,2},{12,4},{14,6},{16,24},{18,... | collective-permute-start | bytes 884744 | tf_op jit(solution)/shard_map/ppermute | solution.py:1013
  401.0 32.2 %collective-permute-start.77 = (bf16[144,768]{1,0:T(8,128)(2,1)S(1)}, bf16[144,768]{1,0:T(8,128)(2,1)S(1)}, u32[]{:S(2)}, u32[]{:S(2)}) collective-permute-start(bf16[144,768]{1,0:T(8,128)(2,1)S(1)} %add_convert_fusion.own_ref), channel_id=1, source_target_pairs={{0,16},{2,18},{4,20},{6,22},{8,24},{10,26},{12,28},{14,30},{16,0},... | collective-permute-start | bytes 663560 | tf_op jit(solution)/shard_map/ppermute | solution.py:1013
  415.0 18.0 %collective-permute-start.78 = (bf16[1,96,768]{2,1,0:T(8,128)(2,1)S(1)}, bf16[1,96,768]{2,1,0:T(8,128)(2,1)S(1)}, u32[]{:S(2)}, u32[]{:S(2)}) collective-permute-start(bf16[1,96,768]{2,1,0:T(8,128)(2,1)S(1)} %get-tuple-element.791), channel_id=1, source_target_pairs={{0,16},{2,18},{4,20},{6,22},{8,24},{10,26},{12,28},{14,30},{16,0},... | collective-permute-start | bytes 442376 | tf_op jit(solution)/shard_map/ppermute | solution.py:1013
  422.7 16.6 %collective-permute-start.76 = (bf16[1,96,768]{2,1,0:T(8,128)(2,1)S(1)}, bf16[1,96,768]{2,1,0:T(8,128)(2,1)S(1)}, u32[]{:S(2)}, u32[]{:S(2)}) collective-permute-start(bf16[1,96,768]{2,1,0:T(8,128)(2,1)S(1)} %get-tuple-element.781), channel_id=1, source_target_pairs={{0,8},{2,10},{4,12},{6,14},{8,0},{10,2},{12,4},{14,6},{16,24},{18,... | collective-permute-start | bytes 442376 | tf_op jit(solution)/shard_map/ppermute | solution.py:1013
  425.3 22.7 %collective-permute-start.83 = (bf16[1,96,768]{2,1,0:T(8,128)(2,1)S(1)}, bf16[1,96,768]{2,1,0:T(8,128)(2,1)S(1)}, u32[]{:S(2)}, u32[]{:S(2)}) collective-permute-start(bf16[1,96,768]{2,1,0:T(8,128)(2,1)S(1)} %get-tuple-element.788), channel_id=1, source_target_pairs={{0,16},{2,18},{4,20},{6,22},{8,24},{10,26},{12,28},{14,30},{16,0},... | collective-permute-start | bytes 442376 | tf_op jit(solution)/shard_map/ppermute | solution.py:1013
  425.3 22.7 %collective-permute-start.75 = (f32[32,768]{1,0:T(8,128)S(1)}, f32[32,768]{1,0:T(8,128)S(1)}, u32[]{:S(2)}, u32[]{:S(2)}) collective-permute-start(f32[32,768]{1,0:T(8,128)S(1)} %add.76), channel_id=1, source_target_pairs={{0,8},{2,10},{4,12},{6,14},{8,0},{10,2},{12,4},{14,6},{16,24},{18,... | collective-permute-start | bytes 294920 | tf_op jit(solution)/shard_map/ppermute | solution.py:1013
  433.0 15.1 %collective-permute-start.82 = (bf16[1,48,768]{2,1,0:T(8,128)(2,1)S(1)}, bf16[1,48,768]{2,1,0:T(8,128)(2,1)S(1)}, u32[]{:S(2)}, u32[]{:S(2)}) collective-permute-start(bf16[1,48,768]{2,1,0:T(8,128)(2,1)S(1)} %get-tuple-element.798), channel_id=1, source_target_pairs={{0,4},{2,6},{4,0},{6,2},{8,12},{10,14},{12,8},{14,10},{16,20},{18,... | collective-permute-start | bytes 221192 | tf_op jit(solution)/shard_map/ppermute | solution.py:1013
  455.6 25.5 %collective-permute-start.87 = (bf16[2304,768]{1,0:T(8,128)(2,1)}, bf16[2304,768]{1,0:T(8,128)(2,1)S(1)}, u32[]{:S(2)}, u32[]{:S(2)}) collective-permute-start(bf16[2304,768]{1,0:T(8,128)(2,1)} %all-gather.2.cloned.1.call-done), channel_id=1, source_target_pairs={{0,2},{2,0},{4,6},{6,4},{8,10},{10,8},{12,14},{14,12},{16,18},{18,... | collective-permute-start | bytes 10616840 | tf_op jit(solution)/shard_map/ppermute | solution.py:1013
  467.9 25.0 %collective-permute-start.92 = (bf16[576,768]{1,0:T(8,128)(2,1)S(1)}, bf16[576,768]{1,0:T(8,128)(2,1)S(1)}, u32[]{:S(2)}, u32[]{:S(2)}) collective-permute-start(bf16[576,768]{1,0:T(8,128)(2,1)S(1)} %bitcast.142), channel_id=1, source_target_pairs={{0,4},{2,6},{4,0},{6,2},{8,12},{10,14},{12,8},{14,10},{16,20},{18,... | collective-permute-start | bytes 2654216 | tf_op jit(solution)/shard_map/ppermute | solution.py:1013
  468.7 24.1 %collective-permute-start.86 = (bf16[96,768]{1,0:T(8,128)(2,1)S(1)}, bf16[96,768]{1,0:T(8,128)(2,1)S(1)}, u32[]{:S(2)}, u32[]{:S(2)}) collective-permute-start(bf16[96,768]{1,0:T(8,128)(2,1)S(1)} %add_convert_fusion.1.own_ref), channel_id=1, source_target_pairs={{0,16},{2,18},{4,20},{6,22},{8,24},{10,26},{12,28},{14,30},{16,0},... | collective-permute-start | bytes 442376 | tf_op jit(solution)/shard_map/ppermute | solution.py:1013
  470.5 22.4 %collective-permute-start.79 = (f32[32,768]{1,0:T(8,128)S(1)}, f32[32,768]{1,0:T(8,128)S(1)}, u32[]{:S(2)}, u32[]{:S(2)}) collective-permute-start(f32[32,768]{1,0:T(8,128)S(1)} %add.77), channel_id=1, source_target_pairs={{0,16},{2,18},{4,20},{6,22},{8,24},{10,26},{12,28},{14,30},{16,0},... | collective-permute-start | bytes 294920 | tf_op jit(solution)/shard_map/ppermute | solution.py:1013
  479.4 13.5 %collective-permute-start.85 = (bf16[48,768]{1,0:T(8,128)(2,1)S(1)}, bf16[48,768]{1,0:T(8,128)(2,1)S(1)}, u32[]{:S(2)}, u32[]{:S(2)}) collective-permute-start(bf16[48,768]{1,0:T(8,128)(2,1)S(1)} %add_convert_fusion.3.own_ref), channel_id=1, source_target_pairs={{0,4},{2,6},{4,0},{6,2},{8,12},{10,14},{12,8},{14,10},{16,20},{18,... | collective-permute-start | bytes 221192 | tf_op jit(solution)/shard_map/ppermute | solution.py:1013
  493.1 19.5 %collective-permute-start.96 = (bf16[1152,768]{1,0:T(8,128)(2,1)S(1)}, bf16[1152,768]{1,0:T(8,128)(2,1)S(1)}, u32[]{:S(2)}, u32[]{:S(2)}) collective-permute-start(bf16[1152,768]{1,0:T(8,128)(2,1)S(1)} %bitcast.127), channel_id=1, source_target_pairs={{0,2},{2,0},{4,6},{6,4},{8,10},{10,8},{12,14},{14,12},{16,18},{18,... | collective-permute-start | bytes 5308424 | tf_op jit(solution)/shard_map/ppermute | solution.py:1013
  507.0 14.3 %collective-permute-start.94 = (bf16[384,768]{1,0:T(8,128)(2,1)S(1)}, bf16[384,768]{1,0:T(8,128)(2,1)S(1)}, u32[]{:S(2)}, u32[]{:S(2)}) collective-permute-start(bf16[384,768]{1,0:T(8,128)(2,1)S(1)} %bitcast.145), channel_id=1, source_target_pairs={{0,4},{2,6},{4,0},{6,2},{8,12},{10,14},{12,8},{14,10},{16,20},{18,... | collective-permute-start | bytes 1769480 | tf_op jit(solution)/shard_map/ppermute | solution.py:1013
  521.3 17.5 %collective-permute-start.99 = (bf16[768,768]{1,0:T(8,128)(2,1)S(1)}, bf16[768,768]{1,0:T(8,128)(2,1)S(1)}, u32[]{:S(2)}, u32[]{:S(2)}) collective-permute-start(bf16[768,768]{1,0:T(8,128)(2,1)S(1)} %bitcast.132), channel_id=1, source_target_pairs={{0,2},{2,0},{4,6},{6,4},{8,10},{10,8},{12,14},{14,12},{16,18},{18,... | collective-permute-start | bytes 3538952 | tf_op jit(solution)/shard_map/ppermute | solution.py:1013
  523.6 13.3 %collective-permute-start.98 = (bf16[384,768]{1,0:T(8,128)(2,1)S(1)}, bf16[384,768]{1,0:T(8,128)(2,1)S(1)}, u32[]{:S(2)}, u32[]{:S(2)}) collective-permute-start(bf16[384,768]{1,0:T(8,128)(2,1)S(1)} %bitcast.147), channel_id=1, source_target_pairs={{0,2},{2,0},{4,6},{6,4},{8,10},{10,8},{12,14},{14,12},{16,18},{18,... | collective-permute-start | bytes 1769480 | tf_op jit(solution)/shard_map/ppermute | solution.py:1013
  (192 other events, 1528.1 us)
Sparse Core Ops, SparseCore 0:
  266.6 88.7 reduce-scatter.1
  361.4 94.1 all-gather.1
where the time goes:
time: 562 us; the launch traced here: 551 us
  Pallas kernels  239 us (43%)
  waiting for transfers between devices  143 us (25%)
  starting transfers between devices  84.7 us (15%)
  local copies, waits for them, and re-layouts  65.6 us (12%)
  between operations  16.5 us (3%)
    pallas_call x13, Pallas kernels, call(): pl.pallas_call(body, grid=grid, in_specs=[spec for _, spec in ins], out_s...  161 us
    ppermute x100, waiting for transfers between devices, swap(): lax.ppermute(values, axis, [(source, source ^ mask) for source in range(s...  132 us
    ppermute x100, starting transfers between devices, swap(): lax.ppermute(values, axis, [(source, source ^ mask) for source in range(s...  84.6 us
    pallas_call x57, Pallas kernels, picked(): pl.pallas_call(body, grid_spec=pltpu.PrefetchScalarGridSpec(num_scalar_pr...  70.8 us
    unnamed x282, local copies, waits for them, and re-layouts  57.9 us
  transfers between devices with their start and end apart: 102, of which 36 were waited for; matrix products, arithmetic and copies ran while one was open for 2% of the time, Pallas kernels for 37%

commit v1 on v0

--- a/solution.py
+++ b/solution.py
@@ -19,7 +19,7 @@
 low = jnp.bfloat16
 full = jnp.float32
 SPARE = 14
-ANY = pl.BlockSpec(memory_space=pl.ANY)
+ANY = pl.BlockSpec(memory_space=pltpu.HBM)
 SCALARS = pl.BlockSpec(memory_space=pltpu.SMEM)
 
 
@@ -1310,10 +1310,8 @@
     one, two = term_qkv0.part(0), term_qkv0.part(1)
     one.pass_narrow()
     two.pass_narrow()
-    order.hold(term_up0.got, part)
     first = Reduce(order, [term_down0, term_join], (2,))
     first.step()
-    gathered = lax.all_gather(after(part, *order.last), "wide", axis_index_groups=groups, tiled=True)
     second = Reduce(order, [term_up0])
     second.step()
     tokens_grad, sums2 = order.run(
@@ -1333,51 +1331,54 @@
             if minor_stages:
                 minor_got = swap(minor, *minor_stages[0])
 
+    third = Reduce(order, [one], late=(2,))
+    third.step()
     first.step()
-    third = Reduce(order, [one])
-    third.step()
     second.step()
-    fourth = Reduce(order, [two], late=(2,))
-    fourth.step()
-    first.step()
-    third.step()
-    minor_step()
-    second.step()
-    fourth.step()
-    minor_step()
-    fourth.step()
-    first.step()
-    third.step()
-    minor_step()
-    second.step()
-    fourth.step()
-    order.hold(gathered)
-    other = swap(after(gathered, *order.last), "wide", 1)
-    first.step()
-    third.step()
-    own, got = gathered.reshape(1, -1, width), other.reshape(1, -1, width)
-    for which, term in enumerate((term_down1, term_up1, term_qkv1)):
-        term.finish(done, own, got, which * (own.shape[1] // 3), own.shape[1] // 3)
-    second.step()
+    order.hold(part)
+    gathered = lax.all_gather(after(part, *order.last), "wide", axis_index_groups=groups, tiled=True)
+    fourth = Reduce(order, [two])
     fourth.step()
     third.step()
     minor_step()
     first.step()
     fourth.step()
     second.step()
+    minor_step()
     third.step()
-    first.finish(done)
+    first.step()
+    minor_step()
     fourth.step()
     second.step()
     third.step()
+    minor_step()
+    first.step()
+    fourth.step()
+    second.step()
+    third.step()
+    order.hold(gathered)
+    other = swap(after(gathered, *order.last), "wide", 1)
+    fourth.step()
+    minor_step()
+    second.step()
+    first.step()
+    own, got = gathered.reshape(1, -1, width), other.reshape(1, -1, width)
+    for which, term in enumerate((term_down1, term_up1, term_qkv1)):
+        term.finish(done, own, got, which * (own.shape[1] // 3), own.shape[1] // 3)
+    third.step()
+    fourth.step()
+    first.finish(done)
+    second.step()
+    third.step()
+    fourth.step()
     for each in (first, second, third, fourth):
         while not each.closed:
             each.step()
     while minor_stages:
         minor_step()
-    fourth.finish(done)
     second.finish(done)
     third.finish(done)
+    fourth.finish(done)
     small = order.run(lambda x: small_gradients(x, place, width, shares, up1.blocks), minor)
 
     return (

time: 562 us -> 552 us (0.982)
  waiting for transfers between devices: 143 us -> 123 us
  starting transfers between devices: 84.7 us -> 97 us
  local copies, waits for them, and re-layouts: 65.6 us -> 57.9 us
  Pallas kernels: 239 us -> 245 us
    ppermute x100, waiting for transfers between devices: 132 us -> 111 us  [swap(): lax.ppermute(values, axis, [(source, source ^ mask) for source in range(s...]
    ppermute x100, starting transfers between devices: 84.6 us -> 97 us  [swap(): lax.ppermute(values, axis, [(source, source ^ mask) for source in range(s...]
    unnamed x282 -> x286, local copies, waits for them, and re-layouts: 57.9 us -> 50.2 us
  transfers between devices with their start and end apart: 102 -> 102, of which waited for: 36 -> 28; matrix products, arithmetic and copies ran while one was open for 2% -> 2% of each run, Pallas kernels for 37% -> 39%
where the time goes in v1:
time: 552 us; the launch traced here: 542 us
  Pallas kernels  245 us (44%)
  waiting for transfers between devices  123 us (22%)
  starting transfers between devices  97 us (18%)
  local copies, waits for them, and re-layouts  57.9 us (10%)
  between operations  16.6 us (3%)
    pallas_call x13, Pallas kernels, call(): pl.pallas_call(body, grid=grid, in_specs=[spec for _, spec in ins], out_s...  161 us
    ppermute x100, waiting for transfers between devices, swap(): lax.ppermute(values, axis, [(source, source ^ mask) for source in range(s...  111 us
    ppermute x100, starting transfers between devices, swap(): lax.ppermute(values, axis, [(source, source ^ mask) for source in range(s...  97 us
    pallas_call x57, Pallas kernels, picked(): pl.pallas_call(body, grid_spec=pltpu.PrefetchScalarGridSpec(num_scalar_pr...  76.1 us
    unnamed x286, local copies, waits for them, and re-layouts  50.2 us
    all_gather x1, waiting for transfers between devices, on_device(): lax.all_gather(after(part, *order.last), 'wide', axis_index_groups=groups...  12 us
  transfers between devices with their start and end apart: 102, of which 28 were waited for; matrix products, arithmetic and copies ran while one was open for 2% of the time, Pallas kernels for 39%

profile of v1, /device:TPU:1, one launch (start us, length us, event | category | flops | bytes accessed | tf_op | source)
XLA Modules:
  0.0 541.6 jit_solution(2987327845517806452)
XLA Ops:
  19.1 6.3 %collective-permute-done.refs_2_ = bf16[1,96,2304]{2,1,0:T(8,128)(2,1)S(1)} collective-permute-done((bf16[1,96,2304]{2,1,0:T(8,128)(2,1)S(1)}, bf16[1,96,2304]{2,1,0:T(8,128)(2,1)S(1)}, u32[]{:S(2)}, u32[]{:S(2)}) %collective-permute-start) | collective-permute-done | bytes 442400 | tf_op jit(solution)/shard_map/ppermute | solution.py:1013
  27.1 3.9 collective-permute-start.2
  31.0 10.2 %collective-permute-done.5.refs_2_.refs_7_.refs_12_ = bf16[1,96,3840]{2,1,0:T(8,128)(2,1)S(1)} collective-permute-done((bf16[1,96,3840]{2,1,0:T(8,128)(2,1)S(1)}, bf16[1,96,3840]{2,1,0:T(8,128)(2,1)S(1)}, u32[]{:S(2)}, u32[]{:S(2)}) %collective-permute-start.5) | collective-permute-done | bytes 737312 | tf_op jit(solution)/shard_map/ppermute | solution.py:1013
  42.4 3.6 collective-permute-start.3
  47.5 4.8 project_qkv.1
  55.1 8.7 %attend.2 = (bf16[2,336,768]{2,1,0:T(8,128)(2,1)S(1)}, f32[2,6,8,336]{3,2,1,0:T(8,128)S(1)}) custom-call(s32[2]{0:T(128)S(1)} %multiply_add_fusion.length_ref, bf16[3,2,336,768]{3,2,1,0:T(8,128)(2,1)S(1)} %bitcast.194, bf16[3,2,336,768]{3,2,1,0:T(8,128)(2,1)S(1)} %bitcast.195, bf16[3,2,336,768]{3,2,1,0:T(8,128)(2,1)S(1)} %bitcast.196), custom_call_target="tpu_custom_call" | custom-call | flops 3000000000 | tf_op jit(solution)/shard_map/attend/pallas_call | solution.py:69
  63.9 3.7 collective-permute-start.9
  75.1 20.4 %feed_forward.2 = (f32[672,768]{1,0:T(8,128)}, bf16[672,768]{1,0:T(8,128)(2,1)S(1)}, bf16[672,3072]{1,0:T(8,128)(2,1)}, bf16[672,3072]{1,0:T(8,128)(2,1)}, bf16[672,768]{1,0:T(8,128)(2,1)S(1)}) custom-call(s32[2]{0:T(128)S(1)} %pad_add_fusion.refs_0_, bf16[2,384,768]{2,1,0:T(8,128)(2,1)S(1)} %copy-done.10, ...), custom_call_target="tpu_custom_call" | custom-call | flops 6899999744 | tf_op jit(solution)/shard_map/feed_forward/pallas_call | solution.py:69
  95.6 2.9 collective-permute-start.22
  101.4 7.5 %join_qkv.1 = (f32[672,768]{1,0:T(8,128)S(1)}, bf16[672,768]{1,0:T(8,128)(2,1)S(1)}, bf16[3,672,768]{2,1,0:T(8,128)(2,1)S(1)}) custom-call(s32[2]{0:T(128)S(1)} %pad_add_fusion.refs_0_, bf16[768,768]{1,0:T(8,128)(2,1)S(1)} %copy-done.45, bf16[1,192,768]{2,1,0:T(8,128)(2,1)S(1)} %collective-permute-done.14.refs_2_.refs_7_, ...), custom_call_target="tpu_custom_call" | custom-call | flops 3300000000 | tf_op jit(solution)/shard_map/join_qkv/pallas_call | solution.py:69
  109.1 8.7 %attend.3 = (bf16[2,336,768]{2,1,0:T(8,128)(2,1)S(1)}, f32[2,6,8,336]{3,2,1,0:T(8,128)S(1)}) custom-call(s32[2]{0:T(128)S(1)} %multiply_add_fusion.length_ref, bf16[3,2,336,768]{3,2,1,0:T(8,128)(2,1)S(1)} %bitcast.200, bf16[3,2,336,768]{3,2,1,0:T(8,128)(2,1)S(1)} %bitcast.201, bf16[3,2,336,768]{3,2,1,0:T(8,128)(2,1)S(1)} %bitcast.202), custom_call_target="tpu_custom_call" | custom-call | flops 3000000000 | tf_op jit(solution)/shard_map/attend/pallas_call | solution.py:69
  117.8 3.2 collective-permute-start.24
  127.0 22.8 %feed_forward.3 = (f32[672,768]{1,0:T(8,128)}, bf16[672,768]{1,0:T(8,128)(2,1)S(1)}, bf16[672,3072]{1,0:T(8,128)(2,1)}, bf16[672,3072]{1,0:T(8,128)(2,1)}, bf16[672,768]{1,0:T(8,128)(2,1)}) custom-call(s32[2]{0:T(128)S(1)} %pad_add_fusion.refs_0_, bf16[2,384,768]{2,1,0:T(8,128)(2,1)S(1)} %copy-done.10, ...), custom_call_target="tpu_custom_call" | custom-call | flops 6899999744 | tf_op jit(solution)/shard_map/feed_forward/pallas_call | solution.py:69
  152.4 4.1 down_term.4
  159.7 2.8 down_term.5
  164.7 19.6 %feed_forward_back.2 = (bf16[672,3072]{1,0:T(8,128)(2,1)}, f32[672,768]{1,0:T(8,128)}, bf16[672,768]{1,0:T(8,128)(2,1)S(1)}, bf16[672,768]{1,0:T(8,128)(2,1)S(1)}, f32[8,768]{1,0:T(8,128)S(1)}) custom-call(s32[2]{0:T(128)S(1)} %pad_add_fusion.refs_0_, bf16[2,1536,768]{2,1,0:T(8,128)(2,1)} %refs_1_.15, ...), custom_call_target="tpu_custom_call" | custom-call | flops 6300000256 | tf_op jit(solution)/shard_map/feed_forward_back/pallas_call | solution.py:69
  184.4 2.9 copy-done.6
  187.3 2.7 up_term.4
  191.3 2.7 up_term.5
  205.3 14.0 %attend_back.2 = bf16[3,2,336,768]{3,2,1,0:T(8,128)(2,1)S(1)} custom-call(s32[2]{0:T(128)S(1)} %multiply_add_fusion.length_ref, bf16[3,2,336,768]{3,2,1,0:T(8,128)(2,1)S(1)} %bitcast.203, bf16[3,2,336,768]{3,2,1,0:T(8,128)(2,1)S(1)} %bitcast.204, bf16[3,2,336,768]{3,2,1,0:T(8,128)(2,1)S(1)} %bitcast.205, bf16[2,336,768]{2,1,0:T(8,128)(2,1)S(1)} %bitcast.175, ...), custom_call_target="tpu_custom_call" | custom-call | flops 4499999744 | tf_op jit(solution)/shard_map/attend_back/pallas_call | solution.py:69
  229.5 2.7 add_into.4.rest_0_
  240.4 12.5 %project_back.2 = (bf16[672,768]{1,0:T(8,128)(2,1)S(1)}, f32[672,768]{1,0:T(8,128)S(1)}, bf16[672,768]{1,0:T(8,128)(2,1)S(1)}, f32[672,768]{1,0:T(8,128)}, f32[8,768]{1,0:T(8,128)S(1)}) custom-call(s32[2]{0:T(128)S(1)} %pad_add_fusion.refs_0_, bf16[2,384,2304]{2,1,0:T(8,128)(2,1)} %refs_1_.16, bf16[1,96,2304]{2,1,0:T(8,128)(2,1)S(1)} %copy-done.71, ...), custom_call_target="tpu_custom_call" | custom-call | flops 3900000000 | tf_op jit(solution)/shard_map/project_back/pallas_call | solution.py:69
  257.7 2.7 down_term.6
  261.2 2.7 down_term.7
  275.4 20.3 %feed_forward_back.3 = (bf16[672,3072]{1,0:T(8,128)(2,1)}, f32[672,768]{1,0:T(8,128)}, bf16[672,768]{1,0:T(8,128)(2,1)S(1)}, bf16[672,768]{1,0:T(8,128)(2,1)}, f32[8,768]{1,0:T(8,128)S(1)}) custom-call(s32[2]{0:T(128)S(1)} %pad_add_fusion.refs_0_, bf16[2,1536,768]{2,1,0:T(8,128)(2,1)} %refs_1_.15, bf16[1,384,768]{2,1,0:T(8,128)(2,1)S(1)} %copy-done.55, ...), custom_call_target="tpu_custom_call" | custom-call | flops 6300000256 | tf_op jit(solution)/shard_map/feed_forward_back/pallas_call | solution.py:69
  299.7 2.7 up_term.6
  304.0 2.7 up_term.7
  306.7 4.9 collective-permute-done.57
  317.2 14.0 %attend_back.3 = bf16[3,2,336,768]{3,2,1,0:T(8,128)(2,1)S(1)} custom-call(s32[2]{0:T(128)S(1)} %copy-done.96, bf16[3,2,336,768]{3,2,1,0:T(8,128)(2,1)S(1)} %bitcast.197, bf16[3,2,336,768]{3,2,1,0:T(8,128)(2,1)S(1)} %bitcast.198, bf16[3,2,336,768]{3,2,1,0:T(8,128)(2,1)S(1)} %bitcast.199, bf16[2,336,768]{2,1,0:T(8,128)(2,1)S(1)} %bitcast.174, ...), custom_call_target="tpu_custom_call" | custom-call | flops 4499999744 | tf_op jit(solution)/shard_map/attend_back/pallas_call | solution.py:69
  331.3 4.0 qkv_out_term.6
  367.1 7.4 %project_back.3 = (f32[672,768]{1,0:T(8,128)}, f32[8,768]{1,0:T(8,128)S(1)}) custom-call(s32[2]{0:T(128)S(1)} %pad_add_fusion.refs_0_, bf16[2,384,2304]{2,1,0:T(8,128)(2,1)S(1)} %copy-done.3, bf16[1,96,2304]{2,1,0:T(8,128)(2,1)S(1)} %copy-done.63, bf16[1,96,2304]{2,1,0:T(8,128)(2,1)S(1)} %copy-done.65, bf16[1,96,2304]{2,1,0:T(8,128)(2,1)S(1)} %copy-done.67, ...), custom_call_target="tpu_custom_call" | custom-call | flops 2700000000 | tf_op jit(solution)/shard_map/project_back/pallas_call | solution.py:69
  378.9 2.8 collective-permute-start.74
  384.0 7.3 %collective-permute-done.68 = bf16[1,384,768]{2,1,0:T(8,128)(2,1)S(1)} collective-permute-done((bf16[1,384,768]{2,1,0:T(8,128)(2,1)S(1)}, bf16[1,384,768]{2,1,0:T(8,128)(2,1)S(1)}, u32[]{:S(2)}, u32[]{:S(2)}) %collective-permute-start.68) | collective-permute-done | bytes 589856 | tf_op jit(solution)/shard_map/ppermute | solution.py:1013
  396.0 11.5 %collective-permute-start.71 = (f32[32,768]{1,0:T(8,128)S(1)}, f32[32,768]{1,0:T(8,128)S(1)}, u32[]{:S(2)}, u32[]{:S(2)}) collective-permute-start(f32[32,768]{1,0:T(8,128)S(1)} %add.74), channel_id=1, source_target_pairs={{0,2},{2,0},{4,6},{6,4},{8,10},{10,8},{12,14},{14,12},{16,18},{18,... | collective-permute-start | bytes 294920 | tf_op jit(solution)/shard_map/ppermute | solution.py:1013
  407.5 3.0 collective-permute-start.81
  414.0 5.2 collective-permute-done.77
  419.2 2.8 collective-permute-start.79
  422.1 3.2 collective-permute-done.75
  429.9 14.7 %collective-permute-done.78 = f32[32,768]{1,0:T(8,128)S(1)} collective-permute-done((f32[32,768]{1,0:T(8,128)S(1)}, f32[32,768]{1,0:T(8,128)S(1)}, u32[]{:S(2)}, u32[]{:S(2)}) %collective-permute-start.78) | collective-permute-done | bytes 98336 | tf_op jit(solution)/shard_map/ppermute | solution.py:1013
  444.6 17.9 %collective-permute-done.84.got_ref = bf16[288,768]{1,0:T(8,128)(2,1)S(1)} collective-permute-done((bf16[288,768]{1,0:T(8,128)(2,1)S(1)}, bf16[288,768]{1,0:T(8,128)(2,1)S(1)}, u32[]{:S(2)}, u32[]{:S(2)}) %collective-permute-start.84) | collective-permute-done | bytes 442400 | tf_op jit(solution)/shard_map/ppermute | solution.py:1013
  462.7 12.0 %all-gather.2.cloned.1.call-done = bf16[2304,768]{1,0:T(8,128)(2,1)} async-done(((bf16[288,768]{1,0:T(8,128)(2,1)}), bf16[2304,768]{1,0:T(8,128)(2,1)}) %all-gather.2.cloned.1.call-update) | async-done | bytes 3538960 | tf_op jit(solution)/shard_map/all_gather | solution.py:1339
  479.3 5.1 collective-permute-done.85.got_ref
  484.5 14.0 %collective-permute-done.82 = f32[32,768]{1,0:T(8,128)S(1)} collective-permute-done((f32[32,768]{1,0:T(8,128)S(1)}, f32[32,768]{1,0:T(8,128)S(1)}, u32[]{:S(2)}, u32[]{:S(2)}) %collective-permute-start.82) | collective-permute-done | bytes 98336 | tf_op jit(solution)/shard_map/ppermute | solution.py:1013
  499.7 2.8 collective-permute-start.89
  505.0 2.6 finish_columns.2.rest_0_
  507.6 3.3 finish_qkv_out.2
  518.6 6.2 %collective-permute-done.94.got_ref = bf16[192,768]{1,0:T(8,128)(2,1)S(1)} collective-permute-done((bf16[192,768]{1,0:T(8,128)(2,1)S(1)}, bf16[192,768]{1,0:T(8,128)(2,1)S(1)}, u32[]{:S(2)}, u32[]{:S(2)}) %collective-permute-start.94) | collective-permute-done | bytes 294944 | tf_op jit(solution)/shard_map/ppermute | solution.py:1013
  527.1 2.6 finish_columns.3
  (550 shorter events, 176.1 us)
Async XLA Ops:
  7.2 371.2 %reduce-scatter.2.cloned.1.call-start = ((), (), s32[]{:S(2)}) async-start(), calls=%async_computation.1 | async-start | bytes 3981312 | tf_op jit(solution)/shard_map/reduce_scatter | solution.py:1291
  16.1 25.1 %collective-permute-start.5 = (bf16[1,96,3840]{2,1,0:T(8,128)(2,1)S(1)}, bf16[1,96,3840]{2,1,0:T(8,128)(2,1)S(1)}, u32[]{:S(2)}, u32[]{:S(2)}) collective-permute-start(bf16[1,96,3840]{2,1,0:T(8,128)(2,1)S(1)} %maximum_bitcast_fusion), channel_id=1, source_target_pairs={{0,1},{1,0},{2,3},{3,2},{4,5},{5,4},{6,7},{7,6},{8,9},{9,8},{10,11... | collective-permute-start | bytes 2211848 | tf_op jit(solution)/shard_map/ppermute | solution.py:1013
  18.8 35.0 %collective-permute-start.8 = (bf16[1,384,768]{2,1,0:T(8,128)(2,1)S(1)}, bf16[1,384,768]{2,1,0:T(8,128)(2,1)S(1)}, u32[]{:S(2)}, u32[]{:S(2)}) collective-permute-start(bf16[1,384,768]{2,1,0:T(8,128)(2,1)S(1)} %constant_dynamic-slice_fusion.2), channel_id=1, source_target_pairs={{0,1},{1,0},{2,3},{3,2},{4,5},{5,4},{6,7},{7,6},{8,9},{9,8},{10,11... | collective-permute-start | bytes 1769480 | tf_op jit(solution)/shard_map/ppermute | solution.py:1013
  25.4 17.0 %collective-permute-start.1 = (bf16[1,96,2304]{2,1,0:T(8,128)(2,1)S(1)}, bf16[1,96,2304]{2,1,0:T(8,128)(2,1)S(1)}, u32[]{:S(2)}, u32[]{:S(2)}) collective-permute-start(bf16[1,96,2304]{2,1,0:T(8,128)(2,1)S(1)} %collective-permute-done.refs_2_), channel_id=1, source_target_pairs={{0,4},{2,6},{4,0},{6,2},{8,12},{10,14},{12,8},{14,10},{16,20},{18,... | collective-permute-start | bytes 1327112 | tf_op jit(solution)/shard_map/ppermute | solution.py:1013
  26.7 42.9 %collective-permute-start.14 = (bf16[1,192,768]{2,1,0:T(8,128)(2,1)S(1)}, bf16[1,192,768]{2,1,0:T(8,128)(2,1)S(1)}, u32[]{:S(2)}, u32[]{:S(2)}) collective-permute-start(bf16[1,192,768]{2,1,0:T(8,128)(2,1)S(1)} %dynamic-slice_bitcast_fusion.2), channel_id=1, source_target_pairs={{0,1},{1,0},{2,3},{3,2},{4,5},{5,4},{6,7},{7,6},{8,9},{9,8},{10,11... | collective-permute-start | bytes 884744 | tf_op jit(solution)/shard_map/ppermute | solution.py:1013
  27.1 19.0 %collective-permute-start.2 = (bf16[1,96,2304]{2,1,0:T(8,128)(2,1)S(1)}, bf16[1,96,2304]{2,1,0:T(8,128)(2,1)S(1)}, u32[]{:S(2)}, u32[]{:S(2)}) collective-permute-start(bf16[1,96,2304]{2,1,0:T(8,128)(2,1)S(1)} %collective-permute-done.refs_2_), channel_id=1, source_target_pairs={{0,2},{2,0},{4,6},{6,4},{8,10},{10,8},{12,14},{14,12},{16,18},{18,... | collective-permute-start | bytes 1327112 | tf_op jit(solution)/shard_map/ppermute | solution.py:1013
  41.2 26.4 %collective-permute-start.7 = (bf16[1,96,3840]{2,1,0:T(8,128)(2,1)S(1)}, bf16[1,96,3840]{2,1,0:T(8,128)(2,1)S(1)}, u32[]{:S(2)}, u32[]{:S(2)}) collective-permute-start(bf16[1,96,3840]{2,1,0:T(8,128)(2,1)S(1)} %collective-permute-done.5.refs_2_.refs_7_.refs_12_), channel_id=1, source_target_pairs={{0,4},{2,6},{4,0},{6,2},{8,12},{10,14},{12,8},{14,10},{16,20},{18,... | collective-permute-start | bytes 2211848 | tf_op jit(solution)/shard_map/ppermute | solution.py:1013
  46.1 23.6 %collective-permute-start.15 = (bf16[1,96,2304]{2,1,0:T(8,128)(2,1)S(1)}, bf16[1,96,2304]{2,1,0:T(8,128)(2,1)S(1)}, u32[]{:S(2)}, u32[]{:S(2)}) collective-permute-start(bf16[1,96,2304]{2,1,0:T(8,128)(2,1)S(1)} %constant_dynamic-slice_fusion.1), channel_id=1, source_target_pairs={{0,1},{1,0},{2,3},{3,2},{4,5},{5,4},{6,7},{7,6},{8,9},{9,8},{10,11... | collective-permute-start | bytes 1327112 | tf_op jit(solution)/shard_map/ppermute | solution.py:1013
  53.8 15.1 %collective-permute-start.11 = (bf16[1,384,768]{2,1,0:T(8,128)(2,1)S(1)}, bf16[1,384,768]{2,1,0:T(8,128)(2,1)S(1)}, u32[]{:S(2)}, u32[]{:S(2)}) collective-permute-start(bf16[1,384,768]{2,1,0:T(8,128)(2,1)S(1)} %collective-permute-done.8.refs_12_.refs_2_), channel_id=1, source_target_pairs={{0,8},{2,10},{4,12},{6,14},{8,0},{10,2},{12,4},{14,6},{16,24},{18,... | collective-permute-start | bytes 1769480 | tf_op jit(solution)/shard_map/ppermute | solution.py:1013
  69.7 29.2 %collective-permute-start.6 = (bf16[1,96,3840]{2,1,0:T(8,128)(2,1)S(1)}, bf16[1,96,3840]{2,1,0:T(8,128)(2,1)}, u32[]{:S(2)}, u32[]{:S(2)}) collective-permute-start(bf16[1,96,3840]{2,1,0:T(8,128)(2,1)S(1)} %maximum_bitcast_fusion.1), channel_id=1, source_target_pairs={{0,1},{1,0},{2,3},{3,2},{4,5},{5,4},{6,7},{7,6},{8,9},{9,8},{10,11... | collective-permute-start | bytes 2211848 | tf_op jit(solution)/shard_map/ppermute | solution.py:1013
  71.8 27.3 %collective-permute-start.23 = (bf16[1,384,768]{2,1,0:T(8,128)(2,1)S(1)}, bf16[1,384,768]{2,1,0:T(8,128)(2,1)}, u32[]{:S(2)}, u32[]{:S(2)}) collective-permute-start(bf16[1,384,768]{2,1,0:T(8,128)(2,1)S(1)} %constant_dynamic-slice_fusion), channel_id=1, source_target_pairs={{0,1},{1,0},{2,3},{3,2},{4,5},{5,4},{6,7},{7,6},{8,9},{9,8},{10,11... | collective-permute-start | bytes 1769480 | tf_op jit(solution)/shard_map/ppermute | solution.py:1013
  72.5 23.1 %collective-permute-start.20 = (bf16[1,96,2304]{2,1,0:T(8,128)(2,1)S(1)}, bf16[1,96,2304]{2,1,0:T(8,128)(2,1)S(1)}, u32[]{:S(2)}, u32[]{:S(2)}) collective-permute-start(bf16[1,96,2304]{2,1,0:T(8,128)(2,1)S(1)} %collective-permute-done.15.refs_7_.refs_2_), channel_id=1, source_target_pairs={{0,4},{2,6},{4,0},{6,2},{8,12},{10,14},{12,8},{14,10},{16,20},{18,... | collective-permute-start | bytes 1327112 | tf_op jit(solution)/shard_map/ppermute | solution.py:1013
  73.7 24.8 %collective-permute-start.17 = (bf16[1,192,768]{2,1,0:T(8,128)(2,1)S(1)}, bf16[1,192,768]{2,1,0:T(8,128)(2,1)S(1)}, u32[]{:S(2)}, u32[]{:S(2)}) collective-permute-start(bf16[1,192,768]{2,1,0:T(8,128)(2,1)S(1)} %collective-permute-done.14.refs_2_.refs_7_), channel_id=1, source_target_pairs={{0,8},{2,10},{4,12},{6,14},{8,0},{10,2},{12,4},{14,6},{16,24},{18,... | collective-permute-start | bytes 884744 | tf_op jit(solution)/shard_map/ppermute | solution.py:1013
  99.1 22.0 %collective-permute-start.16 = (bf16[1,96,3840]{2,1,0:T(8,128)(2,1)}, bf16[1,96,3840]{2,1,0:T(8,128)(2,1)}, u32[]{:S(2)}, u32[]{:S(2)}) collective-permute-start(bf16[1,96,3840]{2,1,0:T(8,128)(2,1)} %collective-permute-done.6.refs_2_.refs_7_.refs_12_), channel_id=1, source_target_pairs={{0,4},{2,6},{4,0},{6,2},{8,12},{10,14},{12,8},{14,10},{16,20},{18,... | collective-permute-start | bytes 2211848 | tf_op jit(solution)/shard_map/ppermute | solution.py:1013
  100.9 20.7 %collective-permute-start.26 = (bf16[1,384,768]{2,1,0:T(8,128)(2,1)}, bf16[1,384,768]{2,1,0:T(8,128)(2,1)}, u32[]{:S(2)}, u32[]{:S(2)}) collective-permute-start(bf16[1,384,768]{2,1,0:T(8,128)(2,1)} %collective-permute-done.23.refs_12_.refs_2_), channel_id=1, source_target_pairs={{0,8},{2,10},{4,12},{6,14},{8,0},{10,2},{12,4},{14,6},{16,24},{18,... | collective-permute-start | bytes 1769480 | tf_op jit(solution)/shard_map/ppermute | solution.py:1013
  164.4 34.1 %collective-permute-start.33 = (bf16[2,384,768]{2,1,0:T(8,128)(2,1)S(1)}, bf16[2,384,768]{2,1,0:T(8,128)(2,1)S(1)}, u32[]{:S(2)}, u32[]{:S(2)}) collective-permute-start(bf16[2,384,768]{2,1,0:T(8,128)(2,1)S(1)} %get-tuple-element.541), channel_id=1, source_target_pairs={{0,1},{1,0},{2,3},{3,2},{4,5},{5,4},{6,7},{7,6},{8,9},{9,8},{10,11... | collective-permute-start | bytes 3538952 | tf_op jit(solution)/shard_map/ppermute | solution.py:1013
  197.4 32.1 %collective-permute-start.38 = (bf16[2,384,768]{2,1,0:T(8,128)(2,1)}, bf16[2,384,768]{2,1,0:T(8,128)(2,1)}, u32[]{:S(2)}, u32[]{:S(2)}) collective-permute-start(bf16[2,384,768]{2,1,0:T(8,128)(2,1)} %get-tuple-element.572), channel_id=1, source_target_pairs={{0,1},{1,0},{2,3},{3,2},{4,5},{5,4},{6,7},{7,6},{8,9},{9,8},{10,11... | collective-permute-start | bytes 3538952 | tf_op jit(solution)/shard_map/ppermute | solution.py:1013
  229.2 34.8 %collective-permute-start.51 = (bf16[2,384,768]{2,1,0:T(8,128)(2,1)}, bf16[2,384,768]{2,1,0:T(8,128)(2,1)}, u32[]{:S(2)}, u32[]{:S(2)}) collective-permute-start(bf16[2,384,768]{2,1,0:T(8,128)(2,1)} %get-tuple-element.607), channel_id=1, source_target_pairs={{0,1},{1,0},{2,3},{3,2},{4,5},{5,4},{6,7},{7,6},{8,9},{9,8},{10,11... | collective-permute-start | bytes 3538952 | tf_op jit(solution)/shard_map/ppermute | solution.py:1013
  266.6 208.1 %all-gather.2.cloned.1.call-start = ((), (), s32[]{:S(2)}) async-start(), calls=%async_computation.2 | async-start | bytes 3981312 | tf_op jit(solution)/shard_map/all_gather | solution.py:1339
  274.2 37.4 %collective-permute-start.57 = (bf16[2,384,768]{2,1,0:T(8,128)(2,1)S(1)}, bf16[2,384,768]{2,1,0:T(8,128)(2,1)S(1)}, u32[]{:S(2)}, u32[]{:S(2)}) collective-permute-start(bf16[2,384,768]{2,1,0:T(8,128)(2,1)S(1)} %get-tuple-element.667), channel_id=1, source_target_pairs={{0,4},{2,6},{4,0},{6,2},{8,12},{10,14},{12,8},{14,10},{16,20},{18,... | collective-permute-start | bytes 3538952 | tf_op jit(solution)/shard_map/ppermute | solution.py:1013
  274.2 21.6 %collective-permute-start.52 = (bf16[2,192,768]{2,1,0:T(8,128)(2,1)}, bf16[2,192,768]{2,1,0:T(8,128)(2,1)S(1)}, u32[]{:S(2)}, u32[]{:S(2)}) collective-permute-start(bf16[2,192,768]{2,1,0:T(8,128)(2,1)} %copy-done.110), channel_id=1, source_target_pairs={{0,1},{1,0},{2,3},{3,2},{4,5},{5,4},{6,7},{7,6},{8,9},{9,8},{10,11... | collective-permute-start | bytes 1769480 | tf_op jit(solution)/shard_map/ppermute | solution.py:1013
  312.9 18.4 %collective-permute-start.59 = (bf16[1,384,768]{2,1,0:T(8,128)(2,1)S(1)}, bf16[1,384,768]{2,1,0:T(8,128)(2,1)S(1)}, u32[]{:S(2)}, u32[]{:S(2)}) collective-permute-start(bf16[1,384,768]{2,1,0:T(8,128)(2,1)S(1)} %get-tuple-element.696), channel_id=1, source_target_pairs={{0,1},{1,0},{2,3},{3,2},{4,5},{5,4},{6,7},{7,6},{8,9},{9,8},{10,11... | collective-permute-start | bytes 1769480 | tf_op jit(solution)/shard_map/ppermute | solution.py:1013
  313.9 17.3 %collective-permute-start.60 = (bf16[1,192,768]{2,1,0:T(8,128)(2,1)S(1)}, bf16[1,192,768]{2,1,0:T(8,128)(2,1)S(1)}, u32[]{:S(2)}, u32[]{:S(2)}) collective-permute-start(bf16[1,192,768]{2,1,0:T(8,128)(2,1)S(1)} %get-tuple-element.680), channel_id=1, source_target_pairs={{0,4},{2,6},{4,0},{6,2},{8,12},{10,14},{12,8},{14,10},{16,20},{18,... | collective-permute-start | bytes 884744 | tf_op jit(solution)/shard_map/ppermute | solution.py:1013
  316.7 36.3 %collective-permute-start.58 = (bf16[2,384,768]{2,1,0:T(8,128)(2,1)}, bf16[2,384,768]{2,1,0:T(8,128)(2,1)}, u32[]{:S(2)}, u32[]{:S(2)}) collective-permute-start(bf16[2,384,768]{2,1,0:T(8,128)(2,1)} %get-tuple-element.705), channel_id=1, source_target_pairs={{0,1},{1,0},{2,3},{3,2},{4,5},{5,4},{6,7},{7,6},{8,9},{9,8},{10,11... | collective-permute-start | bytes 3538952 | tf_op jit(solution)/shard_map/ppermute | solution.py:1013
  346.9 27.6 %collective-permute-start.66 = (bf16[1,384,768]{2,1,0:T(8,128)(2,1)}, bf16[1,384,768]{2,1,0:T(8,128)(2,1)}, u32[]{:S(2)}, u32[]{:S(2)}) collective-permute-start(bf16[1,384,768]{2,1,0:T(8,128)(2,1)} %get-tuple-element.735), channel_id=1, source_target_pairs={{0,1},{1,0},{2,3},{3,2},{4,5},{5,4},{6,7},{7,6},{8,9},{9,8},{10,11... | collective-permute-start | bytes 1769480 | tf_op jit(solution)/shard_map/ppermute | solution.py:1013
  355.9 21.2 %collective-permute-start.69 = (bf16[1,384,768]{2,1,0:T(8,128)(2,1)}, bf16[1,384,768]{2,1,0:T(8,128)(2,1)}, u32[]{:S(2)}, u32[]{:S(2)}) collective-permute-start(bf16[1,384,768]{2,1,0:T(8,128)(2,1)} %get-tuple-element.748), channel_id=1, source_target_pairs={{0,4},{2,6},{4,0},{6,2},{8,12},{10,14},{12,8},{14,10},{16,20},{18,... | collective-permute-start | bytes 1769480 | tf_op jit(solution)/shard_map/ppermute | solution.py:1013
  357.3 18.6 %collective-permute-start.70 = (bf16[1,288,768]{2,1,0:T(8,128)(2,1)}, bf16[1,288,768]{2,1,0:T(8,128)(2,1)}, u32[]{:S(2)}, u32[]{:S(2)}) collective-permute-start(bf16[1,288,768]{2,1,0:T(8,128)(2,1)} %get-tuple-element.745), channel_id=1, source_target_pairs={{0,8},{2,10},{4,12},{6,14},{8,0},{10,2},{12,4},{14,6},{16,24},{18,... | collective-permute-start | bytes 1327112 | tf_op jit(solution)/shard_map/ppermute | solution.py:1013
  378.5 12.8 %collective-permute-start.68 = (bf16[1,384,768]{2,1,0:T(8,128)(2,1)S(1)}, bf16[1,384,768]{2,1,0:T(8,128)(2,1)S(1)}, u32[]{:S(2)}, u32[]{:S(2)}) collective-permute-start(bf16[1,384,768]{2,1,0:T(8,128)(2,1)S(1)} %copy-done.105), channel_id=1, source_target_pairs={{0,1},{1,0},{2,3},{3,2},{4,5},{5,4},{6,7},{7,6},{8,9},{9,8},{10,11... | collective-permute-start | bytes 1769480 | tf_op jit(solution)/shard_map/ppermute | solution.py:1013
  378.8 12.6 %collective-permute-start.67 = (bf16[1,192,768]{2,1,0:T(8,128)(2,1)S(1)}, bf16[1,192,768]{2,1,0:T(8,128)(2,1)S(1)}, u32[]{:S(2)}, u32[]{:S(2)}) collective-permute-start(bf16[1,192,768]{2,1,0:T(8,128)(2,1)S(1)} %get-tuple-element.763), channel_id=1, source_target_pairs={{0,8},{2,10},{4,12},{6,14},{8,0},{10,2},{12,4},{14,6},{16,24},{18,... | collective-permute-start | bytes 884744 | tf_op jit(solution)/shard_map/ppermute | solution.py:1013
  378.9 14.6 %collective-permute-start.74 = (bf16[1,144,768]{2,1,0:T(8,128)(2,1)S(1)}, bf16[1,144,768]{2,1,0:T(8,128)(2,1)S(1)}, u32[]{:S(2)}, u32[]{:S(2)}) collective-permute-start(bf16[1,144,768]{2,1,0:T(8,128)(2,1)S(1)} %get-tuple-element.769), channel_id=1, source_target_pairs={{0,16},{2,18},{4,20},{6,22},{8,24},{10,26},{12,28},{14,30},{16,0},... | collective-permute-start | bytes 663560 | tf_op jit(solution)/shard_map/ppermute | solution.py:1013
  382.7 30.0 %collective-permute-start.72 = (bf16[1,192,768]{2,1,0:T(8,128)(2,1)S(1)}, bf16[1,192,768]{2,1,0:T(8,128)(2,1)S(1)}, u32[]{:S(2)}, u32[]{:S(2)}) collective-permute-start(bf16[1,192,768]{2,1,0:T(8,128)(2,1)S(1)} %get-tuple-element.772), channel_id=1, source_target_pairs={{0,8},{2,10},{4,12},{6,14},{8,0},{10,2},{12,4},{14,6},{16,24},{18,... | collective-permute-start | bytes 884744 | tf_op jit(solution)/shard_map/ppermute | solution.py:1013
  391.4 16.1 %collective-permute-start.73 = (bf16[1,192,768]{2,1,0:T(8,128)(2,1)S(1)}, bf16[1,192,768]{2,1,0:T(8,128)(2,1)S(1)}, u32[]{:S(2)}, u32[]{:S(2)}) collective-permute-start(bf16[1,192,768]{2,1,0:T(8,128)(2,1)S(1)} %get-tuple-element.775), channel_id=1, source_target_pairs={{0,4},{2,6},{4,0},{6,2},{8,12},{10,14},{12,8},{14,10},{16,20},{18,... | collective-permute-start | bytes 884744 | tf_op jit(solution)/shard_map/ppermute | solution.py:1013
  393.6 28.4 %collective-permute-start.76 = (bf16[144,768]{1,0:T(8,128)(2,1)S(1)}, bf16[144,768]{1,0:T(8,128)(2,1)S(1)}, u32[]{:S(2)}, u32[]{:S(2)}) collective-permute-start(bf16[144,768]{1,0:T(8,128)(2,1)S(1)} %add_convert_fusion.own_ref), channel_id=1, source_target_pairs={{0,16},{2,18},{4,20},{6,22},{8,24},{10,26},{12,28},{14,30},{16,0},... | collective-permute-start | bytes 663560 | tf_op jit(solution)/shard_map/ppermute | solution.py:1013
  395.9 23.3 %collective-permute-start.77 = (bf16[1,96,768]{2,1,0:T(8,128)(2,1)S(1)}, bf16[1,96,768]{2,1,0:T(8,128)(2,1)S(1)}, u32[]{:S(2)}, u32[]{:S(2)}) collective-permute-start(bf16[1,96,768]{2,1,0:T(8,128)(2,1)S(1)} %get-tuple-element.778), channel_id=1, source_target_pairs={{0,16},{2,18},{4,20},{6,22},{8,24},{10,26},{12,28},{14,30},{16,0},... | collective-permute-start | bytes 442376 | tf_op jit(solution)/shard_map/ppermute | solution.py:1013
  396.0 16.9 %collective-permute-start.71 = (f32[32,768]{1,0:T(8,128)S(1)}, f32[32,768]{1,0:T(8,128)S(1)}, u32[]{:S(2)}, u32[]{:S(2)}) collective-permute-start(f32[32,768]{1,0:T(8,128)S(1)} %add.74), channel_id=1, source_target_pairs={{0,2},{2,0},{4,6},{6,4},{8,10},{10,8},{12,14},{14,12},{16,18},{18,... | collective-permute-start | bytes 294920 | tf_op jit(solution)/shard_map/ppermute | solution.py:1013
  407.5 17.9 %collective-permute-start.81 = (bf16[1,96,768]{2,1,0:T(8,128)(2,1)S(1)}, bf16[1,96,768]{2,1,0:T(8,128)(2,1)S(1)}, u32[]{:S(2)}, u32[]{:S(2)}) collective-permute-start(bf16[1,96,768]{2,1,0:T(8,128)(2,1)S(1)} %get-tuple-element.788), channel_id=1, source_target_pairs={{0,8},{2,10},{4,12},{6,14},{8,0},{10,2},{12,4},{14,6},{16,24},{18,... | collective-permute-start | bytes 442376 | tf_op jit(solution)/shard_map/ppermute | solution.py:1013
  412.9 12.5 %collective-permute-start.75 = (f32[32,768]{1,0:T(8,128)S(1)}, f32[32,768]{1,0:T(8,128)S(1)}, u32[]{:S(2)}, u32[]{:S(2)}) collective-permute-start(f32[32,768]{1,0:T(8,128)S(1)} %add.76), channel_id=1, source_target_pairs={{0,8},{2,10},{4,12},{6,14},{8,0},{10,2},{12,4},{14,6},{16,24},{18,... | collective-permute-start | bytes 294920 | tf_op jit(solution)/shard_map/ppermute | solution.py:1013
  413.0 15.0 %collective-permute-start.80 = (bf16[1,96,768]{2,1,0:T(8,128)(2,1)S(1)}, bf16[1,96,768]{2,1,0:T(8,128)(2,1)S(1)}, u32[]{:S(2)}, u32[]{:S(2)}) collective-permute-start(bf16[1,96,768]{2,1,0:T(8,128)(2,1)S(1)} %get-tuple-element.791), channel_id=1, source_target_pairs={{0,16},{2,18},{4,20},{6,22},{8,24},{10,26},{12,28},{14,30},{16,0},... | collective-permute-start | bytes 442376 | tf_op jit(solution)/shard_map/ppermute | solution.py:1013
  422.0 40.5 %collective-permute-start.84 = (bf16[288,768]{1,0:T(8,128)(2,1)S(1)}, bf16[288,768]{1,0:T(8,128)(2,1)S(1)}, u32[]{:S(2)}, u32[]{:S(2)}) collective-permute-start(bf16[288,768]{1,0:T(8,128)(2,1)S(1)} %bitcast.160), channel_id=1, source_target_pairs={{0,8},{2,10},{4,12},{6,14},{8,0},{10,2},{12,4},{14,6},{16,24},{18,... | collective-permute-start | bytes 1327112 | tf_op jit(solution)/shard_map/ppermute | solution.py:1013
  425.4 19.2 %collective-permute-start.78 = (f32[32,768]{1,0:T(8,128)S(1)}, f32[32,768]{1,0:T(8,128)S(1)}, u32[]{:S(2)}, u32[]{:S(2)}) collective-permute-start(f32[32,768]{1,0:T(8,128)S(1)} %add.77), channel_id=1, source_target_pairs={{0,16},{2,18},{4,20},{6,22},{8,24},{10,26},{12,28},{14,30},{16,0},... | collective-permute-start | bytes 294920 | tf_op jit(solution)/shard_map/ppermute | solution.py:1013
  425.5 37.1 %collective-permute-start.83 = (bf16[1,48,768]{2,1,0:T(8,128)(2,1)S(1)}, bf16[1,48,768]{2,1,0:T(8,128)(2,1)S(1)}, u32[]{:S(2)}, u32[]{:S(2)}) collective-permute-start(bf16[1,48,768]{2,1,0:T(8,128)(2,1)S(1)} %get-tuple-element.807), channel_id=1, source_target_pairs={{0,16},{2,18},{4,20},{6,22},{8,24},{10,26},{12,28},{14,30},{16,0},... | collective-permute-start | bytes 221192 | tf_op jit(solution)/shard_map/ppermute | solution.py:1013
  427.9 34.6 %collective-permute-start.87 = (bf16[96,768]{1,0:T(8,128)(2,1)S(1)}, bf16[96,768]{1,0:T(8,128)(2,1)S(1)}, u32[]{:S(2)}, u32[]{:S(2)}) collective-permute-start(bf16[96,768]{1,0:T(8,128)(2,1)S(1)} %add_convert_fusion.1.own_ref), channel_id=1, source_target_pairs={{0,16},{2,18},{4,20},{6,22},{8,24},{10,26},{12,28},{14,30},{16,0},... | collective-permute-start | bytes 442376 | tf_op jit(solution)/shard_map/ppermute | solution.py:1013
  428.1 34.6 %collective-permute-start.86 = (bf16[48,768]{1,0:T(8,128)(2,1)S(1)}, bf16[48,768]{1,0:T(8,128)(2,1)S(1)}, u32[]{:S(2)}, u32[]{:S(2)}) collective-permute-start(bf16[48,768]{1,0:T(8,128)(2,1)S(1)} %add_convert_fusion.3.own_ref), channel_id=1, source_target_pairs={{0,4},{2,6},{4,0},{6,2},{8,12},{10,14},{12,8},{14,10},{16,20},{18,... | collective-permute-start | bytes 221192 | tf_op jit(solution)/shard_map/ppermute | solution.py:1013
  474.7 28.0 %collective-permute-start.90 = (bf16[2304,768]{1,0:T(8,128)(2,1)}, bf16[2304,768]{1,0:T(8,128)(2,1)S(1)}, u32[]{:S(2)}, u32[]{:S(2)}) collective-permute-start(bf16[2304,768]{1,0:T(8,128)(2,1)} %all-gather.2.cloned.1.call-done), channel_id=1, source_target_pairs={{0,2},{2,0},{4,6},{6,4},{8,10},{10,8},{12,14},{14,12},{16,18},{18,... | collective-permute-start | bytes 10616840 | tf_op jit(solution)/shard_map/ppermute | solution.py:1013
  475.1 23.4 %collective-permute-start.91 = (bf16[576,768]{1,0:T(8,128)(2,1)S(1)}, bf16[576,768]{1,0:T(8,128)(2,1)S(1)}, u32[]{:S(2)}, u32[]{:S(2)}) collective-permute-start(bf16[576,768]{1,0:T(8,128)(2,1)S(1)} %bitcast.142), channel_id=1, source_target_pairs={{0,4},{2,6},{4,0},{6,2},{8,12},{10,14},{12,8},{14,10},{16,20},{18,... | collective-permute-start | bytes 2654216 | tf_op jit(solution)/shard_map/ppermute | solution.py:1013
  475.3 23.2 %collective-permute-start.92 = (bf16[192,768]{1,0:T(8,128)(2,1)S(1)}, bf16[192,768]{1,0:T(8,128)(2,1)S(1)}, u32[]{:S(2)}, u32[]{:S(2)}) collective-permute-start(bf16[192,768]{1,0:T(8,128)(2,1)S(1)} %bitcast.162), channel_id=1, source_target_pairs={{0,8},{2,10},{4,12},{6,14},{8,0},{10,2},{12,4},{14,6},{16,24},{18,... | collective-permute-start | bytes 884744 | tf_op jit(solution)/shard_map/ppermute | solution.py:1013
  478.2 20.3 %collective-permute-start.82 = (f32[32,768]{1,0:T(8,128)S(1)}, f32[32,768]{1,0:T(8,128)S(1)}, u32[]{:S(2)}, u32[]{:S(2)}) collective-permute-start(f32[32,768]{1,0:T(8,128)S(1)} %add.80), channel_id=1, source_target_pairs={{0,4},{2,6},{4,0},{6,2},{8,12},{10,14},{12,8},{14,10},{16,20},{18,... | collective-permute-start | bytes 294920 | tf_op jit(solution)/shard_map/ppermute | solution.py:1013
  499.6 15.6 %collective-permute-start.95 = (bf16[384,768]{1,0:T(8,128)(2,1)S(1)}, bf16[384,768]{1,0:T(8,128)(2,1)S(1)}, u32[]{:S(2)}, u32[]{:S(2)}) collective-permute-start(bf16[384,768]{1,0:T(8,128)(2,1)S(1)} %bitcast.145), channel_id=1, source_target_pairs={{0,4},{2,6},{4,0},{6,2},{8,12},{10,14},{12,8},{14,10},{16,20},{18,... | collective-permute-start | bytes 1769480 | tf_op jit(solution)/shard_map/ppermute | solution.py:1013
  (194 other events, 1566.0 us)
Sparse Core Ops, SparseCore 0:
  266.7 88.8 reduce-scatter.1
  378.6 96.0 all-gather.1

commit v2 on v1

--- a/solution.py
+++ b/solution.py
@@ -90,7 +90,7 @@
     def quarter(self, place):
         return sum(((place // mask) & 1) << bit for bit, mask in enumerate(self.sharing))
 
-    def fetch(self, *earlier):
+    def cut(self, *earlier):
         found = []
         for array, layer in self.arrays:
             array = after(array, *earlier)
@@ -99,7 +99,9 @@
             sizes = (1,) * len(lead) + (self.length, array.shape[-1])
             found.append(lax.dynamic_slice(array, lead + (begin, 0), sizes).reshape(self.length, -1))
         self.sent = (jnp.concatenate(found, axis=1) if len(found) > 1 else found[0])[None]
-        held = self.sent
+
+    def fetch(self, *earlier):
+        held = after(self.sent, *earlier)
         for mask in masks("narrow"):
             held = jnp.concatenate([held, swap(held, "narrow", mask)])
         self.pieces = {0: held[1:]}
@@ -155,7 +157,9 @@
 
 def weighted(body, weights, grid, ins, outs, name, micros, scratch=(), first=((0, 0),), spare=SPARE):
     spots = weights[0].spots
-    operands = [(spots, SCALARS)] + [(array, ANY) for weight in weights for array in weight.arrays()]
+    operands = [(spots, SCALARS)]
+    for weight in weights:
+        operands += [(pltpu.with_memory_space_constraint(array, pltpu.HBM), ANY) for array in weight.arrays()]
     counts = [len(weight.arrays()) for weight in weights]
     extra = [piece for weight in weights for piece in weight.scratch()]
 
@@ -454,7 +458,7 @@
     return before * share, share + before * decay * 0.3989422804014327
 
 
-def feed_forward(inputs, mixed, out_weight, out_bias, gain, shift, up_weight, up_bias, down_weight, down_bias, keep=None):
+def feed_forward(inputs, mixed, out_weight, out_bias, gain, shift, up_weight, up_bias, down_weight, down_bias, lengths=None):
     rows, width = inputs.shape
     steps = up_weight.blocks
     hidden = steps * width
@@ -486,10 +490,14 @@
 
         @pl.when(step == steps - 1)
         def _():
-            value = total[...]
-            if keep is not None:
-                value = jnp.where(rest[0][...] > 0, value, 0.0)
-            y_ref[...] = value.astype(low)
+            if lengths is None:
+                y_ref[...] = total[...].astype(low)
+            else:
+                length = rows // lengths.shape[0]
+                row = lax.broadcasted_iota(jnp.int32, (length, width), 0)
+                for item in range(lengths.shape[0]):
+                    at = slice(item * length, (item + 1) * length)
+                    y_ref[at] = jnp.where(row < rest[0][item], total[at], 0.0).astype(low)
 
     return weighted(
         body,
@@ -504,7 +512,7 @@
             (up_bias, pl.BlockSpec((1, width), lambda j: (0, j))),
             (down_bias, whole((1, width))),
         ]
-        + ([] if keep is None else [(keep, whole((rows, 1)))]),
+        + ([] if lengths is None else [(lengths, SCALARS)]),
         [
             ((rows, width), full, whole((rows, width))),
             ((rows, width), low, whole((rows, width))),
@@ -1027,6 +1035,9 @@
         self.last = (jax.tree.leaves(out)[0],)
         return out
 
+    def mark(self, value):
+        return self.run(lambda x: x + 1, value)
+
     def hold(self, *arrays):
         self.last += arrays
 
@@ -1115,7 +1126,7 @@
         if self.down:
             mask = self.down.pop(0)
             rows = [kept.size // self.columns for kept, _ in self.parts]
-            even = all(each % 32 == 0 for each in rows)
+            even = all(each % 32 == 0 for each in rows) and bool(self.down)
             if self.first and even:
                 self.pieces, self.lengths = 2 * self.pieces, [each // 2 for each in rows]
             self.first = False
@@ -1190,11 +1201,16 @@
     join = Weight(fetch_join, 0, width, spots)
 
     small = (norm_gains, norm_biases, out_bias, down_bias, skip_bias, up_bias)
-    held = order.run(pack_small, *small)[None]
+    fetch_qkv0.cut()
+    fetch_qkv0.fetch()
+    held = order.run(pack_small, *[after(piece, fetch_qkv0.sent) for piece in small])[None]
     for mask in masks("narrow"):
         held = jnp.concatenate([held, swap(held, "narrow", mask)])
-    fetch_qkv0.fetch(*order.last)
-    fetch_up0.fetch(held)
+    last = order.last
+    for each in (fetch_up0, fetch_down0, fetch_join, fetch_qkv1, fetch_up1, fetch_down1):
+        each.cut(*last)
+        last = (each.sent,)
+    fetch_up0.fetch()
     fetch_down0.fetch(fetch_up0.sent)
     fetch_join.fetch(fetch_down0.sent)
     fetch_qkv1.fetch(fetch_join.sent)
@@ -1213,8 +1229,7 @@
     tokens_flat, skip_flat, cotangent_flat = [array.reshape(rows, width) for array in (tokens, skip, cotangent)]
     lengths = PATCHES + 1 + CAPTION * flags
     valid = lax.broadcasted_iota(jnp.int32, (items, seq_rows), 1) < lengths[:, None]
-    keep = valid.reshape(rows, 1).astype(full)
-    dz1 = jnp.where(keep > 0, cotangent_flat, 0)
+    dz1 = order.run(lambda x: jnp.where(valid.reshape(rows, 1), x, 0), after(cotangent_flat, fetch_down1.sent))
 
     fetch_qkv0.share(1)
     fetch_qkv0.share(0)
@@ -1224,14 +1239,15 @@
     order.hold(*fetch_down0.got())
     fetch_down0.share(1, a0)
     fetch_up1.fetch(a0)
-    fetch_down1.fetch(fetch_up1.sent)
+    fetch_down1.fetch(a0)
     packed0 = packed0.reshape(3, items, seq_rows, width)
     mixed0, totals0 = order.run(lambda *x: attend(*x, items, seq_rows), packed0, lengths)
-    fetch_up0.share(0, mixed0)
-    fetch_down0.share(0, mixed0)
     order.hold(*fetch_join.got(), *fetch_qkv1.got())
-    fetch_join.share(1, mixed0)
-    fetch_qkv1.share(1, mixed0)
+    there = order.mark(spots)
+    fetch_up0.share(0, there)
+    fetch_down0.share(0, there)
+    fetch_join.share(1, there)
+    fetch_qkv1.share(1, there)
     mixed0 = mixed0.reshape(rows, width)
     m0, second0, hidden0, slope0, middle = order.run(
         lambda x, o, ob, g, s, ub, db: feed_forward(x, o, out0, ob, g, s, up0, ub, down0, db),
@@ -1253,7 +1269,7 @@
     mixed1 = mixed1.reshape(rows, width)
     m1, second1, hidden1, slope1, output = order.run(
         lambda x, o, ob, g, s, ub, db, k: feed_forward(x, o, out1, ob, g, s, up1, ub, down1, db, k),
-        entry, mixed1, out_biases[1], gains[1][1], shifts[1][1], up_biases[1], down_biases[1], keep,
+        entry, mixed1, out_biases[1], gains[1][1], shifts[1][1], up_biases[1], down_biases[1], lengths,
     )
 
     done = {}
@@ -1331,54 +1347,50 @@
             if minor_stages:
                 minor_got = swap(minor, *minor_stages[0])
 
-    third = Reduce(order, [one], late=(2,))
+    third = Reduce(order, [one])
     third.step()
     first.step()
     second.step()
     order.hold(part)
     gathered = lax.all_gather(after(part, *order.last), "wide", axis_index_groups=groups, tiled=True)
-    fourth = Reduce(order, [two])
+    fourth = Reduce(order, [two], late=(2,))
     fourth.step()
+    minor_step()
     third.step()
+    first.step()
+    second.step()
     minor_step()
+    fourth.step()
+    minor_step()
+    third.step()
     first.step()
     fourth.step()
     second.step()
     minor_step()
+    first.step()
     third.step()
-    first.step()
-    minor_step()
     fourth.step()
-    second.step()
-    third.step()
-    minor_step()
-    first.step()
-    fourth.step()
-    second.step()
-    third.step()
     order.hold(gathered)
     other = swap(after(gathered, *order.last), "wide", 1)
-    fourth.step()
-    minor_step()
-    second.step()
-    first.step()
-    own, got = gathered.reshape(1, -1, width), other.reshape(1, -1, width)
-    for which, term in enumerate((term_down1, term_up1, term_qkv1)):
-        term.finish(done, own, got, which * (own.shape[1] // 3), own.shape[1] // 3)
-    third.step()
-    fourth.step()
     first.finish(done)
     second.step()
     third.step()
     fourth.step()
+    minor_step()
+    own, got = gathered.reshape(1, -1, width), other.reshape(1, -1, width)
+    for which, term in enumerate((term_down1, term_up1, term_qkv1)):
+        term.finish(done, own, got, which * (own.shape[1] // 3), own.shape[1] // 3)
+    fourth.step()
+    second.step()
+    third.step()
     for each in (first, second, third, fourth):
         while not each.closed:
             each.step()
     while minor_stages:
         minor_step()
+    fourth.finish(done)
     second.finish(done)
     third.finish(done)
-    fourth.finish(done)
     small = order.run(lambda x: small_gradients(x, place, width, shares, up1.blocks), minor)
 
     return (

time: 552 us -> 546 us (0.989)
  waiting for transfers between devices: 123 us -> 137 us
  starting transfers between devices: 97 us -> 87.1 us
  Pallas kernels: 245 us -> 238 us
    ppermute x100 -> x96, waiting for transfers between devices: 111 us -> 137 us  [swap(): lax.ppermute(values, axis, [(source, source ^ mask) for source in range(s...]
    all_gather x1, waiting for transfers between devices: 12 us -> 0.02 us  [on_device(): lax.all_gather(after(part, *order.last), 'wide', axis_index_groups=groups...]
    unnamed x286 -> x226, local copies, waits for them, and re-layouts: 50.2 us -> 39.4 us
    ppermute x100 -> x96, starting transfers between devices: 97 us -> 87 us  [swap(): lax.ppermute(values, axis, [(source, source ^ mask) for source in range(s...]
    pallas_call x57 -> x49, Pallas kernels: 76.1 us -> 71.8 us  [picked(): pl.pallas_call(body, grid_spec=pltpu.PrefetchScalarGridSpec(num_scalar_pr...]
  transfers between devices with their start and end apart: 102 -> 98, of which waited for: 28 -> 29; matrix products, arithmetic and copies ran while one was open for 2% -> 3% of each run, Pallas kernels for 39% -> 38%
where the time goes in v2:
time: 546 us; the launch traced here: 537 us
  Pallas kernels  238 us (44%)
  waiting for transfers between devices  137 us (25%)
  starting transfers between devices  87.1 us (16%)
  local copies, waits for them, and re-layouts  52.7 us (10%)
  between operations  15.9 us (3%)
    pallas_call x13, Pallas kernels, call(): pl.pallas_call(body, grid=grid, in_specs=[spec for _, spec in ins], out_s...  159 us
    ppermute x96, waiting for transfers between devices, swap(): lax.ppermute(values, axis, [(source, source ^ mask) for source in range(s...  137 us
    ppermute x96, starting transfers between devices, swap(): lax.ppermute(values, axis, [(source, source ^ mask) for source in range(s...  87 us
    pallas_call x49, Pallas kernels, picked(): pl.pallas_call(body, grid_spec=pltpu.PrefetchScalarGridSpec(num_scalar_pr...  71.8 us
    unnamed x226, local copies, waits for them, and re-layouts  39.4 us
  transfers between devices with their start and end apart: 98, of which 29 were waited for; matrix products, arithmetic and copies ran while one was open for 3% of the time, Pallas kernels for 38%

profile of v2, /device:TPU:1, one launch (start us, length us, event | category | flops | bytes accessed | tf_op | source)
XLA Modules:
  0.0 536.7 jit_solution(1125624207347655527)
XLA Ops:
  34.9 5.9 %collective-permute-done.1.refs_3_ = bf16[1,96,2304]{2,1,0:T(8,128)(2,1)} collective-permute-done((bf16[1,96,2304]{2,1,0:T(8,128)(2,1)}, bf16[1,96,2304]{2,1,0:T(8,128)(2,1)}, u32[]{:S(2)}, u32[]{:S(2)}) %collective-permute-start.1) | collective-permute-done | bytes 442400 | tf_op jit(solution)/shard_map/ppermute | solution.py:1021
  40.8 3.0 collective-permute-start.3
  48.1 5.1 project_qkv.1
  54.7 8.7 %attend.2 = (bf16[2,336,768]{2,1,0:T(8,128)(2,1)S(1)}, f32[2,6,8,336]{3,2,1,0:T(8,128)S(1)}) custom-call(s32[2]{0:T(128)S(1)} %multiply_add_fusion.length_ref.refs_23_, bf16[3,2,336,768]{3,2,1,0:T(8,128)(2,1)S(1)} %bitcast.171, bf16[3,2,336,768]{3,2,1,0:T(8,128)(2,1)S(1)} %bitcast.172, bf16[3,2,336,768]{3,2,1,0:T(8,128)(2,1)S(1)} %bitcast.173), custom_call_target="tpu_custom_call" | custom-call | flops 3000000000 | tf_op jit(solution)/shard_map/attend/pallas_call | solution.py:69
  75.0 20.7 %feed_forward.2 = (f32[672,768]{1,0:T(8,128)S(1)}, bf16[672,768]{1,0:T(8,128)(2,1)S(1)}, bf16[672,3072]{1,0:T(8,128)(2,1)S(1)}, bf16[672,3072]{1,0:T(8,128)(2,1)}, bf16[672,768]{1,0:T(8,128)(2,1)S(1)}) custom-call(s32[2]{0:T(128)S(1)} %pad_add_fusion.refs_0_, bf16[2,384,768]{2,1,0:T(8,128)(2,1)} %refs_11_.7, bf16[1,96,3840]{2,1,0:T(8,128)(2,1)} %copy-done.80, ...), custom_call_target="tpu_custom_call" | custom-call | flops 6899999744 | tf_op jit(solution)/shard_map/feed_forward/pallas_call | solution.py:69
  104.0 8.2 %join_qkv.1 = (f32[672,768]{1,0:T(8,128)S(1)}, bf16[672,768]{1,0:T(8,128)(2,1)S(1)}, bf16[3,672,768]{2,1,0:T(8,128)(2,1)S(1)}) custom-call(s32[2]{0:T(128)S(1)} %pad_add_fusion.refs_0_, bf16[768,768]{1,0:T(8,128)(2,1)} %refs_6_.10, bf16[1,192,768]{2,1,0:T(8,128)(2,1)} %copy-done.105, bf16[1,192,768]{2,1,0:T(8,128)(2,1)} %copy-done.106, ...), custom_call_target="tpu_custom_call" | custom-call | flops 3300000000 | tf_op jit(solution)/shard_map/join_qkv/pallas_call | solution.py:69
  112.3 8.7 %attend.3 = (bf16[2,336,768]{2,1,0:T(8,128)(2,1)S(1)}, f32[2,6,8,336]{3,2,1,0:T(8,128)S(1)}) custom-call(s32[2]{0:T(128)S(1)} %multiply_add_fusion.length_ref.refs_23_, bf16[3,2,336,768]{3,2,1,0:T(8,128)(2,1)S(1)} %bitcast.177, bf16[3,2,336,768]{3,2,1,0:T(8,128)(2,1)S(1)} %bitcast.178, bf16[3,2,336,768]{3,2,1,0:T(8,128)(2,1)S(1)} %bitcast.179), custom_call_target="tpu_custom_call" | custom-call | flops 3000000000 | tf_op jit(solution)/shard_map/attend/pallas_call | solution.py:69
  122.4 3.1 collective-permute-done.27.refs_14_.refs_4_
  128.4 21.2 %feed_forward.3 = (f32[672,768]{1,0:T(8,128)S(1)}, bf16[672,768]{1,0:T(8,128)(2,1)S(1)}, bf16[672,3072]{1,0:T(8,128)(2,1)S(1)}, bf16[672,3072]{1,0:T(8,128)(2,1)}, bf16[672,768]{1,0:T(8,128)(2,1)}) custom-call(s32[2]{0:T(128)S(1)} %pad_add_fusion.refs_0_, bf16[2,384,768]{2,1,0:T(8,128)(2,1)} %refs_11_.7, bf16[1,96,3840]{2,1,0:T(8,128)(2,1)} %copy-done.84, ...), custom_call_target="tpu_custom_call" | custom-call | flops 6899999744 | tf_op jit(solution)/shard_map/feed_forward/pallas_call | solution.py:69
  150.9 4.1 down_term.4
  158.2 3.1 down_term.5
  165.2 18.3 %feed_forward_back.2 = (bf16[672,3072]{1,0:T(8,128)(2,1)}, f32[672,768]{1,0:T(8,128)S(1)}, bf16[672,768]{1,0:T(8,128)(2,1)S(1)}, bf16[672,768]{1,0:T(8,128)(2,1)S(1)}, f32[8,768]{1,0:T(8,128)S(1)}) custom-call(s32[2]{0:T(128)S(1)} %pad_add_fusion.refs_0_, bf16[2,1536,768]{2,1,0:T(8,128)(2,1)} %refs_1_.15, bf16[1,384,768]{2,1,0:T(8,128)(2,1)} %copy-done.95, ...), custom_call_target="tpu_custom_call" | custom-call | flops 6300000256 | tf_op jit(solution)/shard_map/feed_forward_back/pallas_call | solution.py:69
  183.6 3.6 copy-done.5
  187.2 2.7 up_term.4
  191.2 2.7 up_term.5
  199.0 2.7 add_into.3.rest_0_
  203.0 13.9 %attend_back.2 = bf16[3,2,336,768]{3,2,1,0:T(8,128)(2,1)S(1)} custom-call(s32[2]{0:T(128)S(1)} %multiply_add_fusion.length_ref.refs_23_, bf16[3,2,336,768]{3,2,1,0:T(8,128)(2,1)S(1)} %bitcast.180, bf16[3,2,336,768]{3,2,1,0:T(8,128)(2,1)S(1)} %bitcast.181, bf16[3,2,336,768]{3,2,1,0:T(8,128)(2,1)S(1)} %bitcast.182, bf16[2,336,768]{2,1,0:T(8,128)(2,1)S(1)} %bitcast.158, ...), custom_call_target="tpu_custom_call" | custom-call | flops 4499999744 | tf_op jit(solution)/shard_map/attend_back/pallas_call | solution.py:69
  227.6 2.7 add_into.4.rest_0_
  231.9 11.9 %project_back.2 = (bf16[672,768]{1,0:T(8,128)(2,1)S(1)}, f32[672,768]{1,0:T(8,128)S(1)}, bf16[672,768]{1,0:T(8,128)(2,1)S(1)}, f32[672,768]{1,0:T(8,128)}, f32[8,768]{1,0:T(8,128)S(1)}) custom-call(s32[2]{0:T(128)S(1)} %pad_add_fusion.refs_0_, bf16[2,384,2304]{2,1,0:T(8,128)(2,1)} %refs_1_.16, bf16[1,96,2304]{2,1,0:T(8,128)(2,1)} %collective-permute-done.10.refs_7_.refs_2_, ...), custom_call_target="tpu_custom_call" | custom-call | flops 3900000000 | tf_op jit(solution)/shard_map/project_back/pallas_call | solution.py:69
  250.2 2.7 down_term.6
  253.0 2.7 down_term.7
  255.8 2.6 add_into.5
  267.7 19.6 %feed_forward_back.3 = (bf16[672,3072]{1,0:T(8,128)(2,1)}, f32[672,768]{1,0:T(8,128)S(1)}, bf16[672,768]{1,0:T(8,128)(2,1)S(1)}, bf16[672,768]{1,0:T(8,128)(2,1)S(1)}, f32[8,768]{1,0:T(8,128)S(1)}) custom-call(s32[2]{0:T(128)S(1)} %pad_add_fusion.refs_0_, bf16[2,1536,768]{2,1,0:T(8,128)(2,1)} %refs_1_.15, bf16[1,384,768]{2,1,0:T(8,128)(2,1)} %copy-done.91, ...), custom_call_target="tpu_custom_call" | custom-call | flops 6300000256 | tf_op jit(solution)/shard_map/feed_forward_back/pallas_call | solution.py:69
  291.5 2.7 up_term.6
  295.7 2.7 up_term.7
  298.4 5.2 collective-permute-done.57
  309.3 13.9 %attend_back.3 = bf16[3,2,336,768]{3,2,1,0:T(8,128)(2,1)S(1)} custom-call(s32[2]{0:T(128)S(1)} %multiply_add_fusion.length_ref.refs_23_, bf16[3,2,336,768]{3,2,1,0:T(8,128)(2,1)S(1)} %bitcast.174, bf16[3,2,336,768]{3,2,1,0:T(8,128)(2,1)S(1)} %bitcast.175, bf16[3,2,336,768]{3,2,1,0:T(8,128)(2,1)S(1)} %bitcast.176, bf16[2,336,768]{2,1,0:T(8,128)(2,1)S(1)} %bitcast.157, ...), custom_call_target="tpu_custom_call" | custom-call | flops 4499999744 | tf_op jit(solution)/shard_map/attend_back/pallas_call | solution.py:69
  323.3 3.6 qkv_out_term.6
  346.1 8.3 %project_back.3 = (f32[672,768]{1,0:T(8,128)}, f32[8,768]{1,0:T(8,128)S(1)}) custom-call(s32[2]{0:T(128)S(1)} %pad_add_fusion.refs_0_, bf16[2,384,2304]{2,1,0:T(8,128)(2,1)} %refs_1_.16, bf16[1,96,2304]{2,1,0:T(8,128)(2,1)} %collective-permute-done.refs_2_, bf16[1,96,2304]{2,1,0:T(8,128)(2,1)} %collective-permute-done.1.refs_3_, ...), custom_call_target="tpu_custom_call" | custom-call | flops 2700000000 | tf_op jit(solution)/shard_map/project_back/pallas_call | solution.py:69
  359.5 2.7 collective-permute-start.72
  366.4 4.4 collective-permute-done.66
  370.9 2.7 collective-permute-start.75
  373.7 4.7 collective-permute-start.70
  380.1 8.6 %collective-permute-done.72 = bf16[288,768]{1,0:T(8,128)(2,1)S(1)} collective-permute-done((bf16[288,768]{1,0:T(8,128)(2,1)}, bf16[288,768]{1,0:T(8,128)(2,1)S(1)}, u32[]{:S(2)}, u32[]{:S(2)}) %collective-permute-start.72) | collective-permute-done | bytes 442400 | tf_op jit(solution)/shard_map/ppermute | solution.py:1021
  388.7 6.5 %collective-permute-start.79 = (bf16[288,768]{1,0:T(8,128)(2,1)S(1)}, bf16[288,768]{1,0:T(8,128)(2,1)S(1)}, u32[]{:S(2)}, u32[]{:S(2)}) collective-permute-start(bf16[288,768]{1,0:T(8,128)(2,1)S(1)} %add_convert_fusion.own_ref), channel_id=1, source_target_pairs={{0,8},{2,10},{4,12},{6,14},{8,0},{10,2},{12,4},{14,6},{16,24},{18,... | collective-permute-start | bytes 1327112 | tf_op jit(solution)/shard_map/ppermute | solution.py:1021
  395.4 5.2 collective-permute-done.75
  400.7 28.7 %collective-permute-done.74 = f32[32,768]{1,0:T(8,128)S(1)} collective-permute-done((f32[32,768]{1,0:T(8,128)S(1)}, f32[32,768]{1,0:T(8,128)S(1)}, u32[]{:S(2)}, u32[]{:S(2)}) %collective-permute-start.74) | collective-permute-done | bytes 98336 | tf_op jit(solution)/shard_map/ppermute | solution.py:1021
  429.5 4.3 collective-permute-start.84
  438.5 13.2 %collective-permute-done.78 = bf16[1,96,768]{2,1,0:T(8,128)(2,1)S(1)} collective-permute-done((bf16[1,96,768]{2,1,0:T(8,128)(2,1)S(1)}, bf16[1,96,768]{2,1,0:T(8,128)(2,1)S(1)}, u32[]{:S(2)}, u32[]{:S(2)}) %collective-permute-start.78) | collective-permute-done | bytes 147488 | tf_op jit(solution)/shard_map/ppermute | solution.py:1021
  451.9 15.1 %collective-permute-done.77 = bf16[192,768]{1,0:T(8,128)(2,1)S(1)} collective-permute-done((bf16[192,768]{1,0:T(8,128)(2,1)S(1)}, bf16[192,768]{1,0:T(8,128)(2,1)S(1)}, u32[]{:S(2)}, u32[]{:S(2)}) %collective-permute-start.77) | collective-permute-done | bytes 294944 | tf_op jit(solution)/shard_map/ppermute | solution.py:1021
  469.2 3.0 collective-permute-done.83
  474.0 8.2 %collective-permute-done.88 = bf16[1152,768]{1,0:T(8,128)(2,1)S(1)} collective-permute-done((bf16[1152,768]{1,0:T(8,128)(2,1)S(1)}, bf16[1152,768]{1,0:T(8,128)(2,1)S(1)}, u32[]{:S(2)}, u32[]{:S(2)}) %collective-permute-start.88) | collective-permute-done | bytes 1769504 | tf_op jit(solution)/shard_map/ppermute | solution.py:1021
  489.3 5.3 collective-permute-done.86.got_ref
  496.3 7.1 %collective-permute-done.81 = f32[32,768]{1,0:T(8,128)S(1)} collective-permute-done((f32[32,768]{1,0:T(8,128)S(1)}, f32[32,768]{1,0:T(8,128)S(1)}, u32[]{:S(2)}, u32[]{:S(2)}) %collective-permute-start.81) | collective-permute-done | bytes 98336 | tf_op jit(solution)/shard_map/ppermute | solution.py:1021
  505.8 2.6 finish_columns.2.rest_0_
  508.4 3.3 finish_qkv_out.2
  513.5 8.0 %collective-permute-done.89.got_ref = bf16[192,768]{1,0:T(8,128)(2,1)S(1)} collective-permute-done((bf16[192,768]{1,0:T(8,128)(2,1)S(1)}, bf16[192,768]{1,0:T(8,128)(2,1)S(1)}, u32[]{:S(2)}, u32[]{:S(2)}) %collective-permute-start.89) | collective-permute-done | bytes 294944 | tf_op jit(solution)/shard_map/ppermute | solution.py:1021
  524.3 2.6 finish_columns.3
  (476 shorter events, 170.3 us)
Async XLA Ops:
  7.2 351.6 %reduce-scatter.2.cloned.1.call-start = ((), (), s32[]{:S(2)}) async-start(), calls=%async_computation.1 | async-start | bytes 3981312 | tf_op jit(solution)/shard_map/reduce_scatter | solution.py:1307
  8.3 22.6 %collective-permute-start = (bf16[1,96,2304]{2,1,0:T(8,128)(2,1)S(1)}, bf16[1,96,2304]{2,1,0:T(8,128)(2,1)}, u32[]{:S(2)}, u32[]{:S(2)}) collective-permute-start(bf16[1,96,2304]{2,1,0:T(8,128)(2,1)S(1)} %constant_dynamic-slice_fusion.3), channel_id=1, source_target_pairs={{0,1},{1,0},{2,3},{3,2},{4,5},{5,4},{6,7},{7,6},{8,9},{9,8},{10,11... | collective-permute-start | bytes 1327112 | tf_op jit(solution)/shard_map/ppermute | solution.py:1021
  14.5 17.9 %collective-permute-start.4 = (bf16[1,32,384]{2,1,0:T(8,128)(2,1)S(1)}, bf16[1,32,384]{2,1,0:T(8,128)(2,1)S(1)}, u32[]{:S(2)}, u32[]{:S(2)}) collective-permute-start(bf16[1,32,384]{2,1,0:T(8,128)(2,1)S(1)} %convert_bitcast_fusion), channel_id=1, source_target_pairs={{0,1},{1,0},{2,3},{3,2},{4,5},{5,4},{6,7},{7,6},{8,9},{9,8},{10,11... | collective-permute-start | bytes 73736 | tf_op jit(solution)/shard_map/ppermute | solution.py:1021
  17.6 27.6 %collective-permute-start.5 = (bf16[1,96,3840]{2,1,0:T(8,128)(2,1)}, bf16[1,96,3840]{2,1,0:T(8,128)(2,1)S(1)}, u32[]{:S(2)}, u32[]{:S(2)}) collective-permute-start(bf16[1,96,3840]{2,1,0:T(8,128)(2,1)} %maximum_bitcast_fusion), channel_id=1, source_target_pairs={{0,1},{1,0},{2,3},{3,2},{4,5},{5,4},{6,7},{7,6},{8,9},{9,8},{10,11... | collective-permute-start | bytes 2211848 | tf_op jit(solution)/shard_map/ppermute | solution.py:1021
  20.9 32.4 %collective-permute-start.8 = (bf16[1,384,768]{2,1,0:T(8,128)(2,1)}, bf16[1,384,768]{2,1,0:T(8,128)(2,1)S(1)}, u32[]{:S(2)}, u32[]{:S(2)}) collective-permute-start(bf16[1,384,768]{2,1,0:T(8,128)(2,1)} %constant_dynamic-slice_fusion.2), channel_id=1, source_target_pairs={{0,1},{1,0},{2,3},{3,2},{4,5},{5,4},{6,7},{7,6},{8,9},{9,8},{10,11... | collective-permute-start | bytes 1769480 | tf_op jit(solution)/shard_map/ppermute | solution.py:1021
  24.5 40.6 %collective-permute-start.10 = (bf16[1,96,2304]{2,1,0:T(8,128)(2,1)}, bf16[1,96,2304]{2,1,0:T(8,128)(2,1)}, u32[]{:S(2)}, u32[]{:S(2)}) collective-permute-start(bf16[1,96,2304]{2,1,0:T(8,128)(2,1)} %constant_dynamic-slice_fusion.1), channel_id=1, source_target_pairs={{0,1},{1,0},{2,3},{3,2},{4,5},{5,4},{6,7},{7,6},{8,9},{9,8},{10,11... | collective-permute-start | bytes 1327112 | tf_op jit(solution)/shard_map/ppermute | solution.py:1021
  32.5 14.1 %collective-permute-start.2 = (bf16[1,96,2304]{2,1,0:T(8,128)(2,1)}, bf16[1,96,2304]{2,1,0:T(8,128)(2,1)S(1)}, u32[]{:S(2)}, u32[]{:S(2)}) collective-permute-start(bf16[1,96,2304]{2,1,0:T(8,128)(2,1)} %collective-permute-done.refs_2_), channel_id=1, source_target_pairs={{0,2},{2,0},{4,6},{6,4},{8,10},{10,8},{12,14},{14,12},{16,18},{18,... | collective-permute-start | bytes 1327112 | tf_op jit(solution)/shard_map/ppermute | solution.py:1021
  45.2 21.1 %collective-permute-start.7 = (bf16[1,96,3840]{2,1,0:T(8,128)(2,1)S(1)}, bf16[1,96,3840]{2,1,0:T(8,128)(2,1)S(1)}, u32[]{:S(2)}, u32[]{:S(2)}) collective-permute-start(bf16[1,96,3840]{2,1,0:T(8,128)(2,1)S(1)} %collective-permute-done.5.refs_2_.refs_7_.refs_12_), channel_id=1, source_target_pairs={{0,4},{2,6},{4,0},{6,2},{8,12},{10,14},{12,8},{14,10},{16,20},{18,... | collective-permute-start | bytes 2211848 | tf_op jit(solution)/shard_map/ppermute | solution.py:1021
  46.6 18.5 %collective-permute-start.9 = (bf16[1,192,768]{2,1,0:T(8,128)(2,1)}, bf16[1,192,768]{2,1,0:T(8,128)(2,1)S(1)}, u32[]{:S(2)}, u32[]{:S(2)}) collective-permute-start(bf16[1,192,768]{2,1,0:T(8,128)(2,1)} %dynamic-slice_bitcast_fusion.2), channel_id=1, source_target_pairs={{0,1},{1,0},{2,3},{3,2},{4,5},{5,4},{6,7},{7,6},{8,9},{9,8},{10,11... | collective-permute-start | bytes 884744 | tf_op jit(solution)/shard_map/ppermute | solution.py:1021
  53.4 14.7 %collective-permute-start.13 = (bf16[1,384,768]{2,1,0:T(8,128)(2,1)S(1)}, bf16[1,384,768]{2,1,0:T(8,128)(2,1)S(1)}, u32[]{:S(2)}, u32[]{:S(2)}) collective-permute-start(bf16[1,384,768]{2,1,0:T(8,128)(2,1)S(1)} %collective-permute-done.8.refs_12_.refs_2_), channel_id=1, source_target_pairs={{0,8},{2,10},{4,12},{6,14},{8,0},{10,2},{12,4},{14,6},{16,24},{18,... | collective-permute-start | bytes 1769480 | tf_op jit(solution)/shard_map/ppermute | solution.py:1021
  69.2 31.6 %collective-permute-start.23 = (bf16[1,384,768]{2,1,0:T(8,128)(2,1)S(1)}, bf16[1,384,768]{2,1,0:T(8,128)(2,1)S(1)}, u32[]{:S(2)}, u32[]{:S(2)}) collective-permute-start(bf16[1,384,768]{2,1,0:T(8,128)(2,1)S(1)} %copy-done.99), channel_id=1, source_target_pairs={{0,1},{1,0},{2,3},{3,2},{4,5},{5,4},{6,7},{7,6},{8,9},{9,8},{10,11... | collective-permute-start | bytes 1769480 | tf_op jit(solution)/shard_map/ppermute | solution.py:1021
  70.1 29.9 %collective-permute-start.6 = (bf16[1,96,3840]{2,1,0:T(8,128)(2,1)S(1)}, bf16[1,96,3840]{2,1,0:T(8,128)(2,1)S(1)}, u32[]{:S(2)}, u32[]{:S(2)}) collective-permute-start(bf16[1,96,3840]{2,1,0:T(8,128)(2,1)S(1)} %copy-done.90), channel_id=1, source_target_pairs={{0,1},{1,0},{2,3},{3,2},{4,5},{5,4},{6,7},{7,6},{8,9},{9,8},{10,11... | collective-permute-start | bytes 2211848 | tf_op jit(solution)/shard_map/ppermute | solution.py:1021
  71.6 24.2 %collective-permute-start.20 = (bf16[1,96,2304]{2,1,0:T(8,128)(2,1)}, bf16[1,96,2304]{2,1,0:T(8,128)(2,1)S(1)}, u32[]{:S(2)}, u32[]{:S(2)}) collective-permute-start(bf16[1,96,2304]{2,1,0:T(8,128)(2,1)} %collective-permute-done.10.refs_7_.refs_2_), channel_id=1, source_target_pairs={{0,4},{2,6},{4,0},{6,2},{8,12},{10,14},{12,8},{14,10},{16,20},{18,... | collective-permute-start | bytes 1327112 | tf_op jit(solution)/shard_map/ppermute | solution.py:1021
  72.8 24.4 %collective-permute-start.17 = (bf16[1,192,768]{2,1,0:T(8,128)(2,1)S(1)}, bf16[1,192,768]{2,1,0:T(8,128)(2,1)S(1)}, u32[]{:S(2)}, u32[]{:S(2)}) collective-permute-start(bf16[1,192,768]{2,1,0:T(8,128)(2,1)S(1)} %collective-permute-done.9.refs_2_.refs_7_), channel_id=1, source_target_pairs={{0,8},{2,10},{4,12},{6,14},{8,0},{10,2},{12,4},{14,6},{16,24},{18,... | collective-permute-start | bytes 884744 | tf_op jit(solution)/shard_map/ppermute | solution.py:1021
  100.8 20.9 %collective-permute-start.16 = (bf16[1,96,3840]{2,1,0:T(8,128)(2,1)S(1)}, bf16[1,96,3840]{2,1,0:T(8,128)(2,1)S(1)}, u32[]{:S(2)}, u32[]{:S(2)}) collective-permute-start(bf16[1,96,3840]{2,1,0:T(8,128)(2,1)S(1)} %collective-permute-done.6.refs_2_.refs_7_.refs_12_), channel_id=1, source_target_pairs={{0,4},{2,6},{4,0},{6,2},{8,12},{10,14},{12,8},{14,10},{16,20},{18,... | collective-permute-start | bytes 2211848 | tf_op jit(solution)/shard_map/ppermute | solution.py:1021
  101.1 21.2 %collective-permute-start.26 = (bf16[1,384,768]{2,1,0:T(8,128)(2,1)S(1)}, bf16[1,384,768]{2,1,0:T(8,128)(2,1)S(1)}, u32[]{:S(2)}, u32[]{:S(2)}) collective-permute-start(bf16[1,384,768]{2,1,0:T(8,128)(2,1)S(1)} %collective-permute-done.23.refs_12_.refs_2_), channel_id=1, source_target_pairs={{0,8},{2,10},{4,12},{6,14},{8,0},{10,2},{12,4},{14,6},{16,24},{18,... | collective-permute-start | bytes 1769480 | tf_op jit(solution)/shard_map/ppermute | solution.py:1021
  164.4 33.6 %collective-permute-start.33 = (bf16[2,384,768]{2,1,0:T(8,128)(2,1)S(1)}, bf16[2,384,768]{2,1,0:T(8,128)(2,1)S(1)}, u32[]{:S(2)}, u32[]{:S(2)}) collective-permute-start(bf16[2,384,768]{2,1,0:T(8,128)(2,1)S(1)} %get-tuple-element.551), channel_id=1, source_target_pairs={{0,1},{1,0},{2,3},{3,2},{4,5},{5,4},{6,7},{7,6},{8,9},{9,8},{10,11... | collective-permute-start | bytes 3538952 | tf_op jit(solution)/shard_map/ppermute | solution.py:1021
  197.3 30.3 %collective-permute-start.38 = (bf16[2,384,768]{2,1,0:T(8,128)(2,1)}, bf16[2,384,768]{2,1,0:T(8,128)(2,1)}, u32[]{:S(2)}, u32[]{:S(2)}) collective-permute-start(bf16[2,384,768]{2,1,0:T(8,128)(2,1)} %get-tuple-element.582), channel_id=1, source_target_pairs={{0,1},{1,0},{2,3},{3,2},{4,5},{5,4},{6,7},{7,6},{8,9},{9,8},{10,11... | collective-permute-start | bytes 3538952 | tf_op jit(solution)/shard_map/ppermute | solution.py:1021
  226.8 28.9 %collective-permute-start.51 = (bf16[2,384,768]{2,1,0:T(8,128)(2,1)}, bf16[2,384,768]{2,1,0:T(8,128)(2,1)}, u32[]{:S(2)}, u32[]{:S(2)}) collective-permute-start(bf16[2,384,768]{2,1,0:T(8,128)(2,1)} %get-tuple-element.617), channel_id=1, source_target_pairs={{0,1},{1,0},{2,3},{3,2},{4,5},{5,4},{6,7},{7,6},{8,9},{9,8},{10,11... | collective-permute-start | bytes 3538952 | tf_op jit(solution)/shard_map/ppermute | solution.py:1021
  258.4 214.0 %all-gather.2.cloned.1.call-start = ((), (), s32[]{:S(2)}) async-start(), calls=%async_computation.2 | async-start | bytes 3981312 | tf_op jit(solution)/shard_map/all_gather | solution.py:1355
  265.6 37.9 %collective-permute-start.57 = (bf16[2,384,768]{2,1,0:T(8,128)(2,1)S(1)}, bf16[2,384,768]{2,1,0:T(8,128)(2,1)S(1)}, u32[]{:S(2)}, u32[]{:S(2)}) collective-permute-start(bf16[2,384,768]{2,1,0:T(8,128)(2,1)S(1)} %get-tuple-element.677), channel_id=1, source_target_pairs={{0,4},{2,6},{4,0},{6,2},{8,12},{10,14},{12,8},{14,10},{16,20},{18,... | collective-permute-start | bytes 3538952 | tf_op jit(solution)/shard_map/ppermute | solution.py:1021
  267.0 20.3 %collective-permute-start.52 = (bf16[2,192,768]{2,1,0:T(8,128)(2,1)S(1)}, bf16[2,192,768]{2,1,0:T(8,128)(2,1)S(1)}, u32[]{:S(2)}, u32[]{:S(2)}) collective-permute-start(bf16[2,192,768]{2,1,0:T(8,128)(2,1)S(1)} %copy-done.54), channel_id=1, source_target_pairs={{0,1},{1,0},{2,3},{3,2},{4,5},{5,4},{6,7},{7,6},{8,9},{9,8},{10,11... | collective-permute-start | bytes 1769480 | tf_op jit(solution)/shard_map/ppermute | solution.py:1021
  304.9 18.3 %collective-permute-start.59 = (bf16[1,384,768]{2,1,0:T(8,128)(2,1)S(1)}, bf16[1,384,768]{2,1,0:T(8,128)(2,1)S(1)}, u32[]{:S(2)}, u32[]{:S(2)}) collective-permute-start(bf16[1,384,768]{2,1,0:T(8,128)(2,1)S(1)} %get-tuple-element.706), channel_id=1, source_target_pairs={{0,1},{1,0},{2,3},{3,2},{4,5},{5,4},{6,7},{7,6},{8,9},{9,8},{10,11... | collective-permute-start | bytes 1769480 | tf_op jit(solution)/shard_map/ppermute | solution.py:1021
  304.9 18.3 %collective-permute-start.60 = (bf16[1,192,768]{2,1,0:T(8,128)(2,1)S(1)}, bf16[1,192,768]{2,1,0:T(8,128)(2,1)S(1)}, u32[]{:S(2)}, u32[]{:S(2)}) collective-permute-start(bf16[1,192,768]{2,1,0:T(8,128)(2,1)S(1)} %get-tuple-element.690), channel_id=1, source_target_pairs={{0,4},{2,6},{4,0},{6,2},{8,12},{10,14},{12,8},{14,10},{16,20},{18,... | collective-permute-start | bytes 884744 | tf_op jit(solution)/shard_map/ppermute | solution.py:1021
  308.9 35.6 %collective-permute-start.58 = (bf16[2,384,768]{2,1,0:T(8,128)(2,1)}, bf16[2,384,768]{2,1,0:T(8,128)(2,1)}, u32[]{:S(2)}, u32[]{:S(2)}) collective-permute-start(bf16[2,384,768]{2,1,0:T(8,128)(2,1)} %get-tuple-element.715), channel_id=1, source_target_pairs={{0,1},{1,0},{2,3},{3,2},{4,5},{5,4},{6,7},{7,6},{8,9},{9,8},{10,11... | collective-permute-start | bytes 3538952 | tf_op jit(solution)/shard_map/ppermute | solution.py:1021
  335.1 21.3 %collective-permute-start.69 = (bf16[1,384,768]{2,1,0:T(8,128)(2,1)}, bf16[1,384,768]{2,1,0:T(8,128)(2,1)}, u32[]{:S(2)}, u32[]{:S(2)}) collective-permute-start(bf16[1,384,768]{2,1,0:T(8,128)(2,1)} %get-tuple-element.745), channel_id=1, source_target_pairs={{0,1},{1,0},{2,3},{3,2},{4,5},{5,4},{6,7},{7,6},{8,9},{9,8},{10,11... | collective-permute-start | bytes 1769480 | tf_op jit(solution)/shard_map/ppermute | solution.py:1021
  342.4 15.3 %collective-permute-start.68 = (bf16[1,288,768]{2,1,0:T(8,128)(2,1)S(1)}, bf16[1,288,768]{2,1,0:T(8,128)(2,1)S(1)}, u32[]{:S(2)}, u32[]{:S(2)}) collective-permute-start(bf16[1,288,768]{2,1,0:T(8,128)(2,1)S(1)} %get-tuple-element.755), channel_id=1, source_target_pairs={{0,8},{2,10},{4,12},{6,14},{8,0},{10,2},{12,4},{14,6},{16,24},{18,... | collective-permute-start | bytes 1327112 | tf_op jit(solution)/shard_map/ppermute | solution.py:1021
  346.0 12.6 %collective-permute-start.67 = (bf16[1,384,768]{2,1,0:T(8,128)(2,1)S(1)}, bf16[1,384,768]{2,1,0:T(8,128)(2,1)S(1)}, u32[]{:S(2)}, u32[]{:S(2)}) collective-permute-start(bf16[1,384,768]{2,1,0:T(8,128)(2,1)S(1)} %get-tuple-element.758), channel_id=1, source_target_pairs={{0,4},{2,6},{4,0},{6,2},{8,12},{10,14},{12,8},{14,10},{16,20},{18,... | collective-permute-start | bytes 1769480 | tf_op jit(solution)/shard_map/ppermute | solution.py:1021
  359.5 29.1 %collective-permute-start.72 = (bf16[288,768]{1,0:T(8,128)(2,1)}, bf16[288,768]{1,0:T(8,128)(2,1)S(1)}, u32[]{:S(2)}, u32[]{:S(2)}) collective-permute-start(bf16[288,768]{1,0:T(8,128)(2,1)} %add_convert_fusion.1), channel_id=1, source_target_pairs={{0,16},{2,18},{4,20},{6,22},{8,24},{10,26},{12,28},{14,30},{16,0},... | collective-permute-start | bytes 1327112 | tf_op jit(solution)/shard_map/ppermute | solution.py:1021
  362.2 16.2 %collective-permute-start.73 = (bf16[1,192,768]{2,1,0:T(8,128)(2,1)S(1)}, bf16[1,192,768]{2,1,0:T(8,128)(2,1)S(1)}, u32[]{:S(2)}, u32[]{:S(2)}) collective-permute-start(bf16[1,192,768]{2,1,0:T(8,128)(2,1)S(1)} %get-tuple-element.775), channel_id=1, source_target_pairs={{0,4},{2,6},{4,0},{6,2},{8,12},{10,14},{12,8},{14,10},{16,20},{18,... | collective-permute-start | bytes 884744 | tf_op jit(solution)/shard_map/ppermute | solution.py:1021
  365.4 29.9 %collective-permute-start.71 = (bf16[1,192,768]{2,1,0:T(8,128)(2,1)S(1)}, bf16[1,192,768]{2,1,0:T(8,128)(2,1)S(1)}, u32[]{:S(2)}, u32[]{:S(2)}) collective-permute-start(bf16[1,192,768]{2,1,0:T(8,128)(2,1)S(1)} %get-tuple-element.780), channel_id=1, source_target_pairs={{0,8},{2,10},{4,12},{6,14},{8,0},{10,2},{12,4},{14,6},{16,24},{18,... | collective-permute-start | bytes 884744 | tf_op jit(solution)/shard_map/ppermute | solution.py:1021
  370.9 29.7 %collective-permute-start.75 = (bf16[1,192,768]{2,1,0:T(8,128)(2,1)S(1)}, bf16[1,192,768]{2,1,0:T(8,128)(2,1)S(1)}, u32[]{:S(2)}, u32[]{:S(2)}) collective-permute-start(bf16[1,192,768]{2,1,0:T(8,128)(2,1)S(1)} %get-tuple-element.783), channel_id=1, source_target_pairs={{0,8},{2,10},{4,12},{6,14},{8,0},{10,2},{12,4},{14,6},{16,24},{18,... | collective-permute-start | bytes 884744 | tf_op jit(solution)/shard_map/ppermute | solution.py:1021
  373.7 21.6 %collective-permute-start.70 = (f32[32,768]{1,0:T(8,128)S(1)}, f32[32,768]{1,0:T(8,128)S(1)}, u32[]{:S(2)}, u32[]{:S(2)}) collective-permute-start(f32[32,768]{1,0:T(8,128)S(1)} %add.91), channel_id=1, source_target_pairs={{0,2},{2,0},{4,6},{6,4},{8,10},{10,8},{12,14},{14,12},{16,18},{18,... | collective-permute-start | bytes 294920 | tf_op jit(solution)/shard_map/ppermute | solution.py:1021
  379.4 49.9 %collective-permute-start.80 = (bf16[1,96,768]{2,1,0:T(8,128)(2,1)S(1)}, bf16[1,96,768]{2,1,0:T(8,128)(2,1)S(1)}, u32[]{:S(2)}, u32[]{:S(2)}) collective-permute-start(bf16[1,96,768]{2,1,0:T(8,128)(2,1)S(1)} %get-tuple-element.790), channel_id=1, source_target_pairs={{0,8},{2,10},{4,12},{6,14},{8,0},{10,2},{12,4},{14,6},{16,24},{18,... | collective-permute-start | bytes 442376 | tf_op jit(solution)/shard_map/ppermute | solution.py:1021
  388.7 40.7 %collective-permute-start.79 = (bf16[288,768]{1,0:T(8,128)(2,1)S(1)}, bf16[288,768]{1,0:T(8,128)(2,1)S(1)}, u32[]{:S(2)}, u32[]{:S(2)}) collective-permute-start(bf16[288,768]{1,0:T(8,128)(2,1)S(1)} %add_convert_fusion.own_ref), channel_id=1, source_target_pairs={{0,8},{2,10},{4,12},{6,14},{8,0},{10,2},{12,4},{14,6},{16,24},{18,... | collective-permute-start | bytes 1327112 | tf_op jit(solution)/shard_map/ppermute | solution.py:1021
  395.3 34.0 %collective-permute-start.74 = (f32[32,768]{1,0:T(8,128)S(1)}, f32[32,768]{1,0:T(8,128)S(1)}, u32[]{:S(2)}, u32[]{:S(2)}) collective-permute-start(f32[32,768]{1,0:T(8,128)S(1)} %add.94), channel_id=1, source_target_pairs={{0,8},{2,10},{4,12},{6,14},{8,0},{10,2},{12,4},{14,6},{16,24},{18,... | collective-permute-start | bytes 294920 | tf_op jit(solution)/shard_map/ppermute | solution.py:1021
  429.5 39.6 %collective-permute-start.84 = (bf16[576,768]{1,0:T(8,128)(2,1)S(1)}, bf16[576,768]{1,0:T(8,128)(2,1)S(1)}, u32[]{:S(2)}, u32[]{:S(2)}) collective-permute-start(bf16[576,768]{1,0:T(8,128)(2,1)S(1)} %bitcast.129), channel_id=1, source_target_pairs={{0,4},{2,6},{4,0},{6,2},{8,12},{10,14},{12,8},{14,10},{16,20},{18,... | collective-permute-start | bytes 2654216 | tf_op jit(solution)/shard_map/ppermute | solution.py:1021
  433.8 18.0 %collective-permute-start.78 = (bf16[1,96,768]{2,1,0:T(8,128)(2,1)S(1)}, bf16[1,96,768]{2,1,0:T(8,128)(2,1)S(1)}, u32[]{:S(2)}, u32[]{:S(2)}) collective-permute-start(bf16[1,96,768]{2,1,0:T(8,128)(2,1)S(1)} %get-tuple-element.800), channel_id=1, source_target_pairs={{0,16},{2,18},{4,20},{6,22},{8,24},{10,26},{12,28},{14,30},{16,0},... | collective-permute-start | bytes 442376 | tf_op jit(solution)/shard_map/ppermute | solution.py:1021
  434.5 32.5 %collective-permute-start.77 = (bf16[192,768]{1,0:T(8,128)(2,1)S(1)}, bf16[192,768]{1,0:T(8,128)(2,1)S(1)}, u32[]{:S(2)}, u32[]{:S(2)}) collective-permute-start(bf16[192,768]{1,0:T(8,128)(2,1)S(1)} %add_convert_fusion.3), channel_id=1, source_target_pairs={{0,16},{2,18},{4,20},{6,22},{8,24},{10,26},{12,28},{14,30},{16,0},... | collective-permute-start | bytes 884744 | tf_op jit(solution)/shard_map/ppermute | solution.py:1021
  436.1 32.9 %collective-permute-start.76 = (f32[32,768]{1,0:T(8,128)S(1)}, f32[32,768]{1,0:T(8,128)S(1)}, u32[]{:S(2)}, u32[]{:S(2)}) collective-permute-start(f32[32,768]{1,0:T(8,128)S(1)} %add.95), channel_id=1, source_target_pairs={{0,16},{2,18},{4,20},{6,22},{8,24},{10,26},{12,28},{14,30},{16,0},... | collective-permute-start | bytes 294920 | tf_op jit(solution)/shard_map/ppermute | solution.py:1021
  436.8 35.4 %collective-permute-start.83 = (bf16[96,768]{1,0:T(8,128)(2,1)S(1)}, bf16[96,768]{1,0:T(8,128)(2,1)S(1)}, u32[]{:S(2)}, u32[]{:S(2)}) collective-permute-start(bf16[96,768]{1,0:T(8,128)(2,1)S(1)} %add_convert_fusion.7), channel_id=1, source_target_pairs={{0,16},{2,18},{4,20},{6,22},{8,24},{10,26},{12,28},{14,30},{16,0},... | collective-permute-start | bytes 442376 | tf_op jit(solution)/shard_map/ppermute | solution.py:1021
  451.8 20.5 %collective-permute-start.82 = (bf16[96,768]{1,0:T(8,128)(2,1)S(1)}, bf16[96,768]{1,0:T(8,128)(2,1)S(1)}, u32[]{:S(2)}, u32[]{:S(2)}) collective-permute-start(bf16[96,768]{1,0:T(8,128)(2,1)S(1)} %add_convert_fusion.6), channel_id=1, source_target_pairs={{0,4},{2,6},{4,0},{6,2},{8,12},{10,14},{12,8},{14,10},{16,20},{18,... | collective-permute-start | bytes 442376 | tf_op jit(solution)/shard_map/ppermute | solution.py:1021
  472.4 31.0 %collective-permute-start.92 = (bf16[2304,768]{1,0:T(8,128)(2,1)}, bf16[2304,768]{1,0:T(8,128)(2,1)S(1)}, u32[]{:S(2)}, u32[]{:S(2)}) collective-permute-start(bf16[2304,768]{1,0:T(8,128)(2,1)} %all-gather.2.cloned.1.call-done), channel_id=1, source_target_pairs={{0,2},{2,0},{4,6},{6,4},{8,10},{10,8},{12,14},{14,12},{16,18},{18,... | collective-permute-start | bytes 10616840 | tf_op jit(solution)/shard_map/ppermute | solution.py:1021
  474.0 12.3 %collective-permute-start.87 = (bf16[192,768]{1,0:T(8,128)(2,1)S(1)}, bf16[192,768]{1,0:T(8,128)(2,1)S(1)}, u32[]{:S(2)}, u32[]{:S(2)}) collective-permute-start(bf16[192,768]{1,0:T(8,128)(2,1)S(1)} %add_convert_fusion.2.own_ref), channel_id=1, source_target_pairs={{0,8},{2,10},{4,12},{6,14},{8,0},{10,2},{12,4},{14,6},{16,24},{18,... | collective-permute-start | bytes 884744 | tf_op jit(solution)/shard_map/ppermute | solution.py:1021
  486.4 25.4 %collective-permute-start.90 = (bf16[384,768]{1,0:T(8,128)(2,1)S(1)}, bf16[384,768]{1,0:T(8,128)(2,1)S(1)}, u32[]{:S(2)}, u32[]{:S(2)}) collective-permute-start(bf16[384,768]{1,0:T(8,128)(2,1)S(1)} %bitcast.132), channel_id=1, source_target_pairs={{0,4},{2,6},{4,0},{6,2},{8,12},{10,14},{12,8},{14,10},{16,20},{18,... | collective-permute-start | bytes 1769480 | tf_op jit(solution)/shard_map/ppermute | solution.py:1021
  489.1 14.2 %collective-permute-start.81 = (f32[32,768]{1,0:T(8,128)S(1)}, f32[32,768]{1,0:T(8,128)S(1)}, u32[]{:S(2)}, u32[]{:S(2)}) collective-permute-start(f32[32,768]{1,0:T(8,128)S(1)} %add.99), channel_id=1, source_target_pairs={{0,4},{2,6},{4,0},{6,2},{8,12},{10,14},{12,8},{14,10},{16,20},{18,... | collective-permute-start | bytes 294920 | tf_op jit(solution)/shard_map/ppermute | solution.py:1021
  494.7 17.0 %collective-permute-start.91 = (bf16[192,768]{1,0:T(8,128)(2,1)S(1)}, bf16[192,768]{1,0:T(8,128)(2,1)S(1)}, u32[]{:S(2)}, u32[]{:S(2)}) collective-permute-start(bf16[192,768]{1,0:T(8,128)(2,1)S(1)} %bitcast.151), channel_id=1, source_target_pairs={{0,8},{2,10},{4,12},{6,14},{8,0},{10,2},{12,4},{14,6},{16,24},{18,... | collective-permute-start | bytes 884744 | tf_op jit(solution)/shard_map/ppermute | solution.py:1021
  511.8 12.5 %collective-permute-start.95 = (bf16[768,768]{1,0:T(8,128)(2,1)S(1)}, bf16[768,768]{1,0:T(8,128)(2,1)S(1)}, u32[]{:S(2)}, u32[]{:S(2)}) collective-permute-start(bf16[768,768]{1,0:T(8,128)(2,1)S(1)} %bitcast.119), channel_id=1, source_target_pairs={{0,2},{2,0},{4,6},{6,4},{8,10},{10,8},{12,14},{14,12},{16,18},{18,... | collective-permute-start | bytes 3538952 | tf_op jit(solution)/shard_map/ppermute | solution.py:1021
  (160 other events, 1027.2 us)
Sparse Core Ops, SparseCore 0:
  258.5 89.5 reduce-scatter.1
  358.9 92.5 all-gather.1

commit v3 on v2

--- a/solution.py
+++ b/solution.py
@@ -1046,6 +1046,44 @@
     return ((lax.axis_index(axis) & mask) // mask).astype(jnp.int32).reshape(1)
 
 
+class Spread:
+    def __init__(self, order, total):
+        self.order = order
+        self.count, rows, self.columns = total.shape
+        self.masks = list(reversed(masks("wide")[1:]))
+        places = 1 << len(self.masks)
+        ranks = [sum(((place >> bit) & 1) << (len(self.masks) - 1 - bit) for bit in range(len(self.masks))) for place in range(places)]
+        groups = [[2 * rank + core for rank in ranks] for core in range(2)]
+        self.length = rows // places
+        part = lax.psum_scatter(total, "wide", axis_index_groups=groups, scatter_dimension=1, tiled=True)
+        self.part = part.reshape(-1, self.columns)
+        self.mask, self.closed = None, False
+
+    def step(self):
+        if self.mask is not None:
+            bit = place_bit("wide", self.mask)
+            self.part = self.order.run(lambda *x: pair_up(*x, bit), self.part, self.got).reshape(-1, self.columns)
+        if self.masks:
+            self.mask = self.masks.pop(0)
+            self.got = swap(self.part, "wide", self.mask)
+        else:
+            self.got, self.closed = swap(self.part, "wide", 1), True
+
+    def finish(self, done, terms):
+        while not self.closed:
+            self.step()
+        own, got = [side.reshape(-1, self.count * self.length, self.columns) for side in (self.part, self.got)]
+        if self.length % 16:
+            pieces = own.shape[0]
+            own, got = [
+                side.reshape(pieces, self.count, -1, self.columns).swapaxes(0, 1).reshape(1, -1, self.columns)
+                for side in (own, got)
+            ]
+            self.length *= pieces
+        for which, term in enumerate(terms):
+            term.finish(done, own, got, which * self.length, self.length)
+
+
 class Term:
     def __init__(self, order, kind, layer, function, *arrays):
         self.order, self.kind, self.layer, self.half = order, kind, layer, None
@@ -1301,10 +1339,7 @@
     term_down0 = Term(order, "down", 0, down_term, hidden0, dz0)
     term_down0.stay()
     total = term_qkv1.add_into(total, 2, 3)
-    size = lax.axis_size("wide")
-    groups = [[device + core for device in range(0, size, 2)] for core in range(2)]
-    flat_total = total.reshape(-1, width)
-    part = lax.psum_scatter(flat_total, "wide", axis_index_groups=groups, scatter_dimension=0, tiled=True)
+    spread = Spread(order, total)
     term_down0.pass_first(2)
 
     du, dm, db, do, sums0 = order.run(
@@ -1351,46 +1386,44 @@
     third.step()
     first.step()
     second.step()
-    order.hold(part)
-    gathered = lax.all_gather(after(part, *order.last), "wide", axis_index_groups=groups, tiled=True)
-    fourth = Reduce(order, [two], late=(2,))
+    spread.step()
+    fourth = Reduce(order, [two])
     fourth.step()
     minor_step()
     third.step()
     first.step()
     second.step()
-    minor_step()
+    spread.step()
     fourth.step()
     minor_step()
     third.step()
     first.step()
+    minor_step()
+    spread.step()
     fourth.step()
     second.step()
     minor_step()
     first.step()
     third.step()
     fourth.step()
-    order.hold(gathered)
-    other = swap(after(gathered, *order.last), "wide", 1)
+    second.step()
+    spread.step()
     first.finish(done)
-    second.step()
     third.step()
     fourth.step()
     minor_step()
-    own, got = gathered.reshape(1, -1, width), other.reshape(1, -1, width)
-    for which, term in enumerate((term_down1, term_up1, term_qkv1)):
-        term.finish(done, own, got, which * (own.shape[1] // 3), own.shape[1] // 3)
+    second.step()
+    spread.finish(done, (term_down1, term_up1, term_qkv1))
+    third.step()
     fourth.step()
-    second.step()
-    third.step()
     for each in (first, second, third, fourth):
         while not each.closed:
             each.step()
     while minor_stages:
         minor_step()
-    fourth.finish(done)
     second.finish(done)
     third.finish(done)
+    fourth.finish(done)
     small = order.run(lambda x: small_gradients(x, place, width, shares, up1.blocks), minor)
 
     return (

time: 546 us -> 599 us (1.097)
  waiting for transfers between devices: 137 us -> 210 us
  starting transfers between devices: 87.1 us -> 68.9 us
    ppermute x96 -> x99, waiting for transfers between devices: 137 us -> 196 us  [swap(): lax.ppermute(values, axis, [(source, source ^ mask) for source in range(s...]
    ppermute x96 -> x99, starting transfers between devices: 87 us -> 68.8 us  [swap(): lax.ppermute(values, axis, [(source, source ^ mask) for source in range(s...]
    reduce_scatter x1, waiting for transfers between devices: 0.02 us -> 13.8 us  [__init__(): lax.psum_scatter(total, 'wide', axis_index_groups=groups, scatter_dimensi...]
    unnamed x226 -> x212, local copies, waits for them, and re-layouts: 39.4 us -> 37.2 us
    pallas_call x49 -> x52, Pallas kernels: 71.8 us -> 72.9 us  [picked(): pl.pallas_call(body, grid_spec=pltpu.PrefetchScalarGridSpec(num_scalar_pr...]
  transfers between devices with their start and end apart: 98 -> 100, of which waited for: 29 -> 36; matrix products, arithmetic and copies ran while one was open for 3% -> 3% of each run, Pallas kernels for 38% -> 35%
where the time goes in v3:
time: 599 us; the launch traced here: 590 us
  Pallas kernels  239 us (40%)
  waiting for transfers between devices  210 us (35%)
  starting transfers between devices  68.9 us (12%)
  local copies, waits for them, and re-layouts  50.5 us (8%)
  between operations  16.1 us (3%)
    ppermute x99, waiting for transfers between devices, swap(): lax.ppermute(values, axis, [(source, source ^ mask) for source in range(s...  196 us
    pallas_call x13, Pallas kernels, call(): pl.pallas_call(body, grid=grid, in_specs=[spec for _, spec in ins], out_s...  159 us
    pallas_call x52, Pallas kernels, picked(): pl.pallas_call(body, grid_spec=pltpu.PrefetchScalarGridSpec(num_scalar_pr...  72.9 us
    ppermute x99, starting transfers between devices, swap(): lax.ppermute(values, axis, [(source, source ^ mask) for source in range(s...  68.8 us
    unnamed x212, local copies, waits for them, and re-layouts  37.2 us
    reduce_scatter x1, waiting for transfers between devices, __init__(): lax.psum_scatter(total, 'wide', axis_index_groups=groups, scatter_dimensi...  13.8 us
  transfers between devices with their start and end apart: 100, of which 36 were waited for; matrix products, arithmetic and copies ran while one was open for 3% of the time, Pallas kernels for 35%

profile of v3, /device:TPU:1, one launch (start us, length us, event | category | flops | bytes accessed | tf_op | source)
XLA Modules:
  0.0 589.6 jit_solution(4469877608723376561)
XLA Ops:
  34.9 5.9 %collective-permute-done.1.refs_3_ = bf16[1,96,2304]{2,1,0:T(8,128)(2,1)} collective-permute-done((bf16[1,96,2304]{2,1,0:T(8,128)(2,1)}, bf16[1,96,2304]{2,1,0:T(8,128)(2,1)}, u32[]{:S(2)}, u32[]{:S(2)}) %collective-permute-start.1) | collective-permute-done | bytes 442400 | tf_op jit(solution)/shard_map/ppermute | solution.py:1021
  40.8 3.0 collective-permute-start.3
  48.1 5.1 project_qkv.1
  54.7 8.7 %attend.2 = (bf16[2,336,768]{2,1,0:T(8,128)(2,1)S(1)}, f32[2,6,8,336]{3,2,1,0:T(8,128)S(1)}) custom-call(s32[2]{0:T(128)S(1)} %multiply_add_fusion.length_ref.refs_23_, bf16[3,2,336,768]{3,2,1,0:T(8,128)(2,1)S(1)} %bitcast.181, bf16[3,2,336,768]{3,2,1,0:T(8,128)(2,1)S(1)} %bitcast.182, bf16[3,2,336,768]{3,2,1,0:T(8,128)(2,1)S(1)} %bitcast.183), custom_call_target="tpu_custom_call" | custom-call | flops 3000000000 | tf_op jit(solution)/shard_map/attend/pallas_call | solution.py:69
  75.0 20.7 %feed_forward.2 = (f32[672,768]{1,0:T(8,128)S(1)}, bf16[672,768]{1,0:T(8,128)(2,1)S(1)}, bf16[672,3072]{1,0:T(8,128)(2,1)S(1)}, bf16[672,3072]{1,0:T(8,128)(2,1)}, bf16[672,768]{1,0:T(8,128)(2,1)S(1)}) custom-call(s32[2]{0:T(128)S(1)} %pad_add_fusion.refs_0_, bf16[2,384,768]{2,1,0:T(8,128)(2,1)} %refs_11_.7, bf16[1,96,3840]{2,1,0:T(8,128)(2,1)} %copy-done.74, ...), custom_call_target="tpu_custom_call" | custom-call | flops 6899999744 | tf_op jit(solution)/shard_map/feed_forward/pallas_call | solution.py:69
  104.1 8.2 %join_qkv.1 = (f32[672,768]{1,0:T(8,128)S(1)}, bf16[672,768]{1,0:T(8,128)(2,1)S(1)}, bf16[3,672,768]{2,1,0:T(8,128)(2,1)S(1)}) custom-call(s32[2]{0:T(128)S(1)} %pad_add_fusion.refs_0_, bf16[768,768]{1,0:T(8,128)(2,1)} %refs_6_.10, bf16[1,192,768]{2,1,0:T(8,128)(2,1)} %copy-done.98, bf16[1,192,768]{2,1,0:T(8,128)(2,1)} %copy-done.99, ...), custom_call_target="tpu_custom_call" | custom-call | flops 3300000000 | tf_op jit(solution)/shard_map/join_qkv/pallas_call | solution.py:69
  112.4 8.7 %attend.3 = (bf16[2,336,768]{2,1,0:T(8,128)(2,1)S(1)}, f32[2,6,8,336]{3,2,1,0:T(8,128)S(1)}) custom-call(s32[2]{0:T(128)S(1)} %multiply_add_fusion.length_ref.refs_23_, bf16[3,2,336,768]{3,2,1,0:T(8,128)(2,1)S(1)} %bitcast.187, bf16[3,2,336,768]{3,2,1,0:T(8,128)(2,1)S(1)} %bitcast.188, bf16[3,2,336,768]{3,2,1,0:T(8,128)(2,1)S(1)} %bitcast.189), custom_call_target="tpu_custom_call" | custom-call | flops 3000000000 | tf_op jit(solution)/shard_map/attend/pallas_call | solution.py:69
  122.5 3.1 collective-permute-done.27.refs_14_.refs_4_
  128.4 21.2 %feed_forward.3 = (f32[672,768]{1,0:T(8,128)S(1)}, bf16[672,768]{1,0:T(8,128)(2,1)S(1)}, bf16[672,3072]{1,0:T(8,128)(2,1)S(1)}, bf16[672,3072]{1,0:T(8,128)(2,1)}, bf16[672,768]{1,0:T(8,128)(2,1)}) custom-call(s32[2]{0:T(128)S(1)} %pad_add_fusion.refs_0_, bf16[2,384,768]{2,1,0:T(8,128)(2,1)} %refs_11_.7, bf16[1,96,3840]{2,1,0:T(8,128)(2,1)} %copy-done.78, ...), custom_call_target="tpu_custom_call" | custom-call | flops 6899999744 | tf_op jit(solution)/shard_map/feed_forward/pallas_call | solution.py:69
  150.9 4.1 down_term.4
  158.2 2.9 down_term.5
  165.0 18.3 %feed_forward_back.2 = (bf16[672,3072]{1,0:T(8,128)(2,1)}, f32[672,768]{1,0:T(8,128)S(1)}, bf16[672,768]{1,0:T(8,128)(2,1)S(1)}, bf16[672,768]{1,0:T(8,128)(2,1)S(1)}, f32[8,768]{1,0:T(8,128)S(1)}) custom-call(s32[2]{0:T(128)S(1)} %pad_add_fusion.refs_0_, bf16[2,1536,768]{2,1,0:T(8,128)(2,1)} %refs_1_.15, bf16[1,384,768]{2,1,0:T(8,128)(2,1)} %copy-done.88, ...), custom_call_target="tpu_custom_call" | custom-call | flops 6300000256 | tf_op jit(solution)/shard_map/feed_forward_back/pallas_call | solution.py:69
  183.4 3.6 copy-done.4
  187.0 2.7 up_term.4
  191.1 2.7 up_term.5
  198.8 2.7 add_into.3.rest_0_
  202.9 14.1 %attend_back.2 = bf16[3,2,336,768]{3,2,1,0:T(8,128)(2,1)S(1)} custom-call(s32[2]{0:T(128)S(1)} %multiply_add_fusion.length_ref.refs_23_, bf16[3,2,336,768]{3,2,1,0:T(8,128)(2,1)S(1)} %bitcast.190, bf16[3,2,336,768]{3,2,1,0:T(8,128)(2,1)S(1)} %bitcast.191, bf16[3,2,336,768]{3,2,1,0:T(8,128)(2,1)S(1)} %bitcast.192, bf16[2,336,768]{2,1,0:T(8,128)(2,1)S(1)} %bitcast.168, ...), custom_call_target="tpu_custom_call" | custom-call | flops 4499999744 | tf_op jit(solution)/shard_map/attend_back/pallas_call | solution.py:69
  217.1 2.6 qkv_out_term.4
  227.7 2.7 add_into.4.rest_0_
  232.0 11.6 %project_back.2 = (bf16[672,768]{1,0:T(8,128)(2,1)S(1)}, f32[672,768]{1,0:T(8,128)S(1)}, bf16[672,768]{1,0:T(8,128)(2,1)S(1)}, f32[672,768]{1,0:T(8,128)}, f32[8,768]{1,0:T(8,128)S(1)}) custom-call(s32[2]{0:T(128)S(1)} %pad_add_fusion.refs_0_, bf16[2,384,2304]{2,1,0:T(8,128)(2,1)} %refs_1_.16, bf16[1,96,2304]{2,1,0:T(8,128)(2,1)} %collective-permute-done.10.refs_7_.refs_2_, ...), custom_call_target="tpu_custom_call" | custom-call | flops 3900000000 | tf_op jit(solution)/shard_map/project_back/pallas_call | solution.py:69
  250.1 2.7 down_term.6
  252.8 2.7 down_term.7
  255.6 2.6 add_into.5
  267.5 19.6 %feed_forward_back.3 = (bf16[672,3072]{1,0:T(8,128)(2,1)}, f32[672,768]{1,0:T(8,128)S(1)}, bf16[672,768]{1,0:T(8,128)(2,1)S(1)}, bf16[672,768]{1,0:T(8,128)(2,1)S(1)}, f32[8,768]{1,0:T(8,128)S(1)}) custom-call(s32[2]{0:T(128)S(1)} %pad_add_fusion.refs_0_, bf16[2,1536,768]{2,1,0:T(8,128)(2,1)} %refs_1_.15, bf16[1,384,768]{2,1,0:T(8,128)(2,1)} %copy-done.84, ...), custom_call_target="tpu_custom_call" | custom-call | flops 6300000256 | tf_op jit(solution)/shard_map/feed_forward_back/pallas_call | solution.py:69
  291.2 2.9 up_term.6
  295.7 2.7 up_term.7
  298.4 7.1 %collective-permute-done.57 = bf16[2,384,768]{2,1,0:T(8,128)(2,1)S(1)} collective-permute-done((bf16[2,384,768]{2,1,0:T(8,128)(2,1)S(1)}, bf16[2,384,768]{2,1,0:T(8,128)(2,1)S(1)}, u32[]{:S(2)}, u32[]{:S(2)}) %collective-permute-start.57) | collective-permute-done | bytes 1179680 | tf_op jit(solution)/shard_map/ppermute | solution.py:1021
  312.8 13.8 %attend_back.3 = bf16[3,2,336,768]{3,2,1,0:T(8,128)(2,1)S(1)} custom-call(s32[2]{0:T(128)S(1)} %multiply_add_fusion.length_ref.refs_23_, bf16[3,2,336,768]{3,2,1,0:T(8,128)(2,1)S(1)} %bitcast.184, bf16[3,2,336,768]{3,2,1,0:T(8,128)(2,1)S(1)} %bitcast.185, bf16[3,2,336,768]{3,2,1,0:T(8,128)(2,1)S(1)} %bitcast.186, bf16[2,336,768]{2,1,0:T(8,128)(2,1)S(1)} %bitcast.167, ...), custom_call_target="tpu_custom_call" | custom-call | flops 4499999744 | tf_op jit(solution)/shard_map/attend_back/pallas_call | solution.py:69
  326.6 3.6 qkv_out_term.6
  347.6 2.5 collective-permute-start.67
  350.2 8.4 %project_back.3 = (f32[672,768]{1,0:T(8,128)}, f32[8,768]{1,0:T(8,128)S(1)}) custom-call(s32[2]{0:T(128)S(1)} %pad_add_fusion.refs_0_, bf16[2,384,2304]{2,1,0:T(8,128)(2,1)} %refs_1_.16, bf16[1,96,2304]{2,1,0:T(8,128)(2,1)} %collective-permute-done.refs_2_, bf16[1,96,2304]{2,1,0:T(8,128)(2,1)} %collective-permute-done.1.refs_3_, ...), custom_call_target="tpu_custom_call" | custom-call | flops 2700000000 | tf_op jit(solution)/shard_map/project_back/pallas_call | solution.py:69
  362.4 2.6 collective-permute-start.75
  367.2 4.1 collective-permute-done.66
  373.5 35.8 %collective-permute-done.74 = bf16[288,768]{1,0:T(8,128)(2,1)S(1)} collective-permute-done((bf16[288,768]{1,0:T(8,128)(2,1)S(1)}, bf16[288,768]{1,0:T(8,128)(2,1)S(1)}, u32[]{:S(2)}, u32[]{:S(2)}) %collective-permute-start.74) | collective-permute-done | bytes 442400 | tf_op jit(solution)/shard_map/ppermute | solution.py:1021
  409.3 13.8 %reduce-scatter.2.cloned.1.call-done = bf16[3,96,768]{2,1,0:T(8,128)(2,1)} async-done(((bf16[3,768,768]{2,1,0:T(8,128)(2,1)}), bf16[3,96,768]{2,1,0:T(8,128)(2,1)}) %reduce-scatter.2.cloned.1.call-update) | async-done | bytes 442384 | tf_op jit(solution)/shard_map/reduce_scatter | solution.py:1058
  423.3 21.3 %collective-permute-done.72.got_ref = bf16[288,768]{1,0:T(8,128)(2,1)S(1)} collective-permute-done((bf16[288,768]{1,0:T(8,128)(2,1)}, bf16[288,768]{1,0:T(8,128)(2,1)S(1)}, u32[]{:S(2)}, u32[]{:S(2)}) %collective-permute-start.72) | collective-permute-done | bytes 442400 | tf_op jit(solution)/shard_map/ppermute | solution.py:1021
  447.4 5.5 collective-permute-done.71
  454.1 24.0 %collective-permute-done.78 = bf16[1,96,768]{2,1,0:T(8,128)(2,1)S(1)} collective-permute-done((bf16[1,96,768]{2,1,0:T(8,128)(2,1)S(1)}, bf16[1,96,768]{2,1,0:T(8,128)(2,1)S(1)}, u32[]{:S(2)}, u32[]{:S(2)}) %collective-permute-start.78) | collective-permute-done | bytes 147488 | tf_op jit(solution)/shard_map/ppermute | solution.py:1021
  484.6 3.0 collective-permute-done.81
  487.6 14.5 %collective-permute-done.80 = bf16[192,768]{1,0:T(8,128)(2,1)S(1)} collective-permute-done((bf16[192,768]{1,0:T(8,128)(2,1)S(1)}, bf16[192,768]{1,0:T(8,128)(2,1)S(1)}, u32[]{:S(2)}, u32[]{:S(2)}) %collective-permute-start.80) | collective-permute-done | bytes 294944 | tf_op jit(solution)/shard_map/ppermute | solution.py:1021
  502.2 8.3 %collective-permute-done.79 = f32[32,768]{1,0:T(8,128)S(1)} collective-permute-done((f32[32,768]{1,0:T(8,128)S(1)}, f32[32,768]{1,0:T(8,128)S(1)}, u32[]{:S(2)}, u32[]{:S(2)}) %collective-permute-start.79) | collective-permute-done | bytes 98336 | tf_op jit(solution)/shard_map/ppermute | solution.py:1021
  510.6 27.6 %collective-permute-done.86.got_ref = bf16[576,768]{1,0:T(8,128)(2,1)S(1)} collective-permute-done((bf16[576,768]{1,0:T(8,128)(2,1)S(1)}, bf16[576,768]{1,0:T(8,128)(2,1)S(1)}, u32[]{:S(2)}, u32[]{:S(2)}) %collective-permute-start.86) | collective-permute-done | bytes 884768 | tf_op jit(solution)/shard_map/ppermute | solution.py:1021
  542.9 6.5 %collective-permute-done.89 = bf16[1152,768]{1,0:T(8,128)(2,1)S(1)} collective-permute-done((bf16[1152,768]{1,0:T(8,128)(2,1)S(1)}, bf16[1152,768]{1,0:T(8,128)(2,1)S(1)}, u32[]{:S(2)}, u32[]{:S(2)}) %collective-permute-start.89) | collective-permute-done | bytes 1769504 | tf_op jit(solution)/shard_map/ppermute | solution.py:1021
  554.5 3.2 collective-permute-done.83
  563.2 2.8 finish_columns.2.rest_0_
  565.9 3.5 finish_qkv_out.2
  570.1 3.9 collective-permute-done.92.got_ref
  575.0 2.6 finish_columns.3
  (468 shorter events, 169.3 us)
Async XLA Ops:
  7.2 415.9 %reduce-scatter.2.cloned.1.call-start = ((), (), s32[]{:S(2)}) async-start(), calls=%async_computation.1 | async-start | bytes 3981312 | tf_op jit(solution)/shard_map/reduce_scatter | solution.py:1058
  8.3 22.6 %collective-permute-start = (bf16[1,96,2304]{2,1,0:T(8,128)(2,1)S(1)}, bf16[1,96,2304]{2,1,0:T(8,128)(2,1)}, u32[]{:S(2)}, u32[]{:S(2)}) collective-permute-start(bf16[1,96,2304]{2,1,0:T(8,128)(2,1)S(1)} %constant_dynamic-slice_fusion.3), channel_id=1, source_target_pairs={{0,1},{1,0},{2,3},{3,2},{4,5},{5,4},{6,7},{7,6},{8,9},{9,8},{10,11... | collective-permute-start | bytes 1327112 | tf_op jit(solution)/shard_map/ppermute | solution.py:1021
  14.5 17.9 %collective-permute-start.4 = (bf16[1,32,384]{2,1,0:T(8,128)(2,1)S(1)}, bf16[1,32,384]{2,1,0:T(8,128)(2,1)S(1)}, u32[]{:S(2)}, u32[]{:S(2)}) collective-permute-start(bf16[1,32,384]{2,1,0:T(8,128)(2,1)S(1)} %convert_bitcast_fusion), channel_id=1, source_target_pairs={{0,1},{1,0},{2,3},{3,2},{4,5},{5,4},{6,7},{7,6},{8,9},{9,8},{10,11... | collective-permute-start | bytes 73736 | tf_op jit(solution)/shard_map/ppermute | solution.py:1021
  17.6 27.6 %collective-permute-start.5 = (bf16[1,96,3840]{2,1,0:T(8,128)(2,1)}, bf16[1,96,3840]{2,1,0:T(8,128)(2,1)S(1)}, u32[]{:S(2)}, u32[]{:S(2)}) collective-permute-start(bf16[1,96,3840]{2,1,0:T(8,128)(2,1)} %maximum_bitcast_fusion), channel_id=1, source_target_pairs={{0,1},{1,0},{2,3},{3,2},{4,5},{5,4},{6,7},{7,6},{8,9},{9,8},{10,11... | collective-permute-start | bytes 2211848 | tf_op jit(solution)/shard_map/ppermute | solution.py:1021
  20.9 32.4 %collective-permute-start.8 = (bf16[1,384,768]{2,1,0:T(8,128)(2,1)}, bf16[1,384,768]{2,1,0:T(8,128)(2,1)S(1)}, u32[]{:S(2)}, u32[]{:S(2)}) collective-permute-start(bf16[1,384,768]{2,1,0:T(8,128)(2,1)} %constant_dynamic-slice_fusion.2), channel_id=1, source_target_pairs={{0,1},{1,0},{2,3},{3,2},{4,5},{5,4},{6,7},{7,6},{8,9},{9,8},{10,11... | collective-permute-start | bytes 1769480 | tf_op jit(solution)/shard_map/ppermute | solution.py:1021
  24.5 40.6 %collective-permute-start.10 = (bf16[1,96,2304]{2,1,0:T(8,128)(2,1)}, bf16[1,96,2304]{2,1,0:T(8,128)(2,1)}, u32[]{:S(2)}, u32[]{:S(2)}) collective-permute-start(bf16[1,96,2304]{2,1,0:T(8,128)(2,1)} %constant_dynamic-slice_fusion.1), channel_id=1, source_target_pairs={{0,1},{1,0},{2,3},{3,2},{4,5},{5,4},{6,7},{7,6},{8,9},{9,8},{10,11... | collective-permute-start | bytes 1327112 | tf_op jit(solution)/shard_map/ppermute | solution.py:1021
  45.2 21.1 %collective-permute-start.7 = (bf16[1,96,3840]{2,1,0:T(8,128)(2,1)S(1)}, bf16[1,96,3840]{2,1,0:T(8,128)(2,1)S(1)}, u32[]{:S(2)}, u32[]{:S(2)}) collective-permute-start(bf16[1,96,3840]{2,1,0:T(8,128)(2,1)S(1)} %collective-permute-done.5.refs_2_.refs_7_.refs_12_), channel_id=1, source_target_pairs={{0,4},{2,6},{4,0},{6,2},{8,12},{10,14},{12,8},{14,10},{16,20},{18,... | collective-permute-start | bytes 2211848 | tf_op jit(solution)/shard_map/ppermute | solution.py:1021
  46.6 18.5 %collective-permute-start.9 = (bf16[1,192,768]{2,1,0:T(8,128)(2,1)}, bf16[1,192,768]{2,1,0:T(8,128)(2,1)S(1)}, u32[]{:S(2)}, u32[]{:S(2)}) collective-permute-start(bf16[1,192,768]{2,1,0:T(8,128)(2,1)} %dynamic-slice_bitcast_fusion.2), channel_id=1, source_target_pairs={{0,1},{1,0},{2,3},{3,2},{4,5},{5,4},{6,7},{7,6},{8,9},{9,8},{10,11... | collective-permute-start | bytes 884744 | tf_op jit(solution)/shard_map/ppermute | solution.py:1021
  53.4 14.7 %collective-permute-start.13 = (bf16[1,384,768]{2,1,0:T(8,128)(2,1)S(1)}, bf16[1,384,768]{2,1,0:T(8,128)(2,1)S(1)}, u32[]{:S(2)}, u32[]{:S(2)}) collective-permute-start(bf16[1,384,768]{2,1,0:T(8,128)(2,1)S(1)} %collective-permute-done.8.refs_12_.refs_2_), channel_id=1, source_target_pairs={{0,8},{2,10},{4,12},{6,14},{8,0},{10,2},{12,4},{14,6},{16,24},{18,... | collective-permute-start | bytes 1769480 | tf_op jit(solution)/shard_map/ppermute | solution.py:1021
  69.2 31.6 %collective-permute-start.23 = (bf16[1,384,768]{2,1,0:T(8,128)(2,1)S(1)}, bf16[1,384,768]{2,1,0:T(8,128)(2,1)S(1)}, u32[]{:S(2)}, u32[]{:S(2)}) collective-permute-start(bf16[1,384,768]{2,1,0:T(8,128)(2,1)S(1)} %copy-done.92), channel_id=1, source_target_pairs={{0,1},{1,0},{2,3},{3,2},{4,5},{5,4},{6,7},{7,6},{8,9},{9,8},{10,11... | collective-permute-start | bytes 1769480 | tf_op jit(solution)/shard_map/ppermute | solution.py:1021
  70.1 29.9 %collective-permute-start.6 = (bf16[1,96,3840]{2,1,0:T(8,128)(2,1)S(1)}, bf16[1,96,3840]{2,1,0:T(8,128)(2,1)S(1)}, u32[]{:S(2)}, u32[]{:S(2)}) collective-permute-start(bf16[1,96,3840]{2,1,0:T(8,128)(2,1)S(1)} %copy-done.83), channel_id=1, source_target_pairs={{0,1},{1,0},{2,3},{3,2},{4,5},{5,4},{6,7},{7,6},{8,9},{9,8},{10,11... | collective-permute-start | bytes 2211848 | tf_op jit(solution)/shard_map/ppermute | solution.py:1021
  71.6 24.2 %collective-permute-start.20 = (bf16[1,96,2304]{2,1,0:T(8,128)(2,1)}, bf16[1,96,2304]{2,1,0:T(8,128)(2,1)S(1)}, u32[]{:S(2)}, u32[]{:S(2)}) collective-permute-start(bf16[1,96,2304]{2,1,0:T(8,128)(2,1)} %collective-permute-done.10.refs_7_.refs_2_), channel_id=1, source_target_pairs={{0,4},{2,6},{4,0},{6,2},{8,12},{10,14},{12,8},{14,10},{16,20},{18,... | collective-permute-start | bytes 1327112 | tf_op jit(solution)/shard_map/ppermute | solution.py:1021
  72.8 24.4 %collective-permute-start.17 = (bf16[1,192,768]{2,1,0:T(8,128)(2,1)S(1)}, bf16[1,192,768]{2,1,0:T(8,128)(2,1)S(1)}, u32[]{:S(2)}, u32[]{:S(2)}) collective-permute-start(bf16[1,192,768]{2,1,0:T(8,128)(2,1)S(1)} %collective-permute-done.9.refs_2_.refs_7_), channel_id=1, source_target_pairs={{0,8},{2,10},{4,12},{6,14},{8,0},{10,2},{12,4},{14,6},{16,24},{18,... | collective-permute-start | bytes 884744 | tf_op jit(solution)/shard_map/ppermute | solution.py:1021
  100.8 21.0 %collective-permute-start.16 = (bf16[1,96,3840]{2,1,0:T(8,128)(2,1)S(1)}, bf16[1,96,3840]{2,1,0:T(8,128)(2,1)S(1)}, u32[]{:S(2)}, u32[]{:S(2)}) collective-permute-start(bf16[1,96,3840]{2,1,0:T(8,128)(2,1)S(1)} %collective-permute-done.6.refs_2_.refs_7_.refs_12_), channel_id=1, source_target_pairs={{0,4},{2,6},{4,0},{6,2},{8,12},{10,14},{12,8},{14,10},{16,20},{18,... | collective-permute-start | bytes 2211848 | tf_op jit(solution)/shard_map/ppermute | solution.py:1021
  101.1 21.3 %collective-permute-start.26 = (bf16[1,384,768]{2,1,0:T(8,128)(2,1)S(1)}, bf16[1,384,768]{2,1,0:T(8,128)(2,1)S(1)}, u32[]{:S(2)}, u32[]{:S(2)}) collective-permute-start(bf16[1,384,768]{2,1,0:T(8,128)(2,1)S(1)} %collective-permute-done.23.refs_12_.refs_2_), channel_id=1, source_target_pairs={{0,8},{2,10},{4,12},{6,14},{8,0},{10,2},{12,4},{14,6},{16,24},{18,... | collective-permute-start | bytes 1769480 | tf_op jit(solution)/shard_map/ppermute | solution.py:1021
  164.2 33.6 %collective-permute-start.33 = (bf16[2,384,768]{2,1,0:T(8,128)(2,1)S(1)}, bf16[2,384,768]{2,1,0:T(8,128)(2,1)S(1)}, u32[]{:S(2)}, u32[]{:S(2)}) collective-permute-start(bf16[2,384,768]{2,1,0:T(8,128)(2,1)S(1)} %get-tuple-element.555), channel_id=1, source_target_pairs={{0,1},{1,0},{2,3},{3,2},{4,5},{5,4},{6,7},{7,6},{8,9},{9,8},{10,11... | collective-permute-start | bytes 3538952 | tf_op jit(solution)/shard_map/ppermute | solution.py:1021
  197.1 30.6 %collective-permute-start.38 = (bf16[2,384,768]{2,1,0:T(8,128)(2,1)}, bf16[2,384,768]{2,1,0:T(8,128)(2,1)}, u32[]{:S(2)}, u32[]{:S(2)}) collective-permute-start(bf16[2,384,768]{2,1,0:T(8,128)(2,1)} %get-tuple-element.586), channel_id=1, source_target_pairs={{0,1},{1,0},{2,3},{3,2},{4,5},{5,4},{6,7},{7,6},{8,9},{9,8},{10,11... | collective-permute-start | bytes 3538952 | tf_op jit(solution)/shard_map/ppermute | solution.py:1021
  226.9 28.7 %collective-permute-start.51 = (bf16[2,384,768]{2,1,0:T(8,128)(2,1)}, bf16[2,384,768]{2,1,0:T(8,128)(2,1)}, u32[]{:S(2)}, u32[]{:S(2)}) collective-permute-start(bf16[2,384,768]{2,1,0:T(8,128)(2,1)} %get-tuple-element.621), channel_id=1, source_target_pairs={{0,1},{1,0},{2,3},{3,2},{4,5},{5,4},{6,7},{7,6},{8,9},{9,8},{10,11... | collective-permute-start | bytes 3538952 | tf_op jit(solution)/shard_map/ppermute | solution.py:1021
  265.6 39.9 %collective-permute-start.57 = (bf16[2,384,768]{2,1,0:T(8,128)(2,1)S(1)}, bf16[2,384,768]{2,1,0:T(8,128)(2,1)S(1)}, u32[]{:S(2)}, u32[]{:S(2)}) collective-permute-start(bf16[2,384,768]{2,1,0:T(8,128)(2,1)S(1)} %get-tuple-element.681), channel_id=1, source_target_pairs={{0,4},{2,6},{4,0},{6,2},{8,12},{10,14},{12,8},{14,10},{16,20},{18,... | collective-permute-start | bytes 3538952 | tf_op jit(solution)/shard_map/ppermute | solution.py:1021
  266.9 20.2 %collective-permute-start.52 = (bf16[2,192,768]{2,1,0:T(8,128)(2,1)S(1)}, bf16[2,192,768]{2,1,0:T(8,128)(2,1)S(1)}, u32[]{:S(2)}, u32[]{:S(2)}) collective-permute-start(bf16[2,192,768]{2,1,0:T(8,128)(2,1)S(1)} %copy-done.56), channel_id=1, source_target_pairs={{0,1},{1,0},{2,3},{3,2},{4,5},{5,4},{6,7},{7,6},{8,9},{9,8},{10,11... | collective-permute-start | bytes 1769480 | tf_op jit(solution)/shard_map/ppermute | solution.py:1021
  295.1 14.4 %collective-permute-start.54 = (bf16[384,768]{1,0:T(8,128)(2,1)S(1)}, bf16[384,768]{1,0:T(8,128)(2,1)S(1)}, u32[]{:S(2)}, u32[]{:S(2)}) collective-permute-start(bf16[384,768]{1,0:T(8,128)(2,1)S(1)} %get-tuple-element.704), channel_id=1, source_target_pairs={{0,2},{2,0},{4,6},{6,4},{8,10},{10,8},{12,14},{14,12},{16,18},{18,... | collective-permute-start | bytes 1769480 | tf_op jit(solution)/shard_map/ppermute | solution.py:1021
  295.2 14.4 %collective-permute-start.55 = (bf16[384,768]{1,0:T(8,128)(2,1)S(1)}, bf16[384,768]{1,0:T(8,128)(2,1)S(1)}, u32[]{:S(2)}, u32[]{:S(2)}) collective-permute-start(bf16[384,768]{1,0:T(8,128)(2,1)S(1)} %get-tuple-element.705), channel_id=1, source_target_pairs={{0,2},{2,0},{4,6},{6,4},{8,10},{10,8},{12,14},{14,12},{16,18},{18,... | collective-permute-start | bytes 1769480 | tf_op jit(solution)/shard_map/ppermute | solution.py:1021
  306.9 19.7 %collective-permute-start.59 = (bf16[1,384,768]{2,1,0:T(8,128)(2,1)S(1)}, bf16[1,384,768]{2,1,0:T(8,128)(2,1)S(1)}, u32[]{:S(2)}, u32[]{:S(2)}) collective-permute-start(bf16[1,384,768]{2,1,0:T(8,128)(2,1)S(1)} %get-tuple-element.710), channel_id=1, source_target_pairs={{0,1},{1,0},{2,3},{3,2},{4,5},{5,4},{6,7},{7,6},{8,9},{9,8},{10,11... | collective-permute-start | bytes 1769480 | tf_op jit(solution)/shard_map/ppermute | solution.py:1021
  307.8 18.8 %collective-permute-start.60 = (bf16[1,192,768]{2,1,0:T(8,128)(2,1)S(1)}, bf16[1,192,768]{2,1,0:T(8,128)(2,1)S(1)}, u32[]{:S(2)}, u32[]{:S(2)}) collective-permute-start(bf16[1,192,768]{2,1,0:T(8,128)(2,1)S(1)} %get-tuple-element.694), channel_id=1, source_target_pairs={{0,4},{2,6},{4,0},{6,2},{8,12},{10,14},{12,8},{14,10},{16,20},{18,... | collective-permute-start | bytes 884744 | tf_op jit(solution)/shard_map/ppermute | solution.py:1021
  312.1 34.0 %collective-permute-start.58 = (bf16[2,384,768]{2,1,0:T(8,128)(2,1)}, bf16[2,384,768]{2,1,0:T(8,128)(2,1)}, u32[]{:S(2)}, u32[]{:S(2)}) collective-permute-start(bf16[2,384,768]{2,1,0:T(8,128)(2,1)} %get-tuple-element.719), channel_id=1, source_target_pairs={{0,1},{1,0},{2,3},{3,2},{4,5},{5,4},{6,7},{7,6},{8,9},{9,8},{10,11... | collective-permute-start | bytes 3538952 | tf_op jit(solution)/shard_map/ppermute | solution.py:1021
  337.8 21.0 %collective-permute-start.69 = (bf16[1,384,768]{2,1,0:T(8,128)(2,1)}, bf16[1,384,768]{2,1,0:T(8,128)(2,1)}, u32[]{:S(2)}, u32[]{:S(2)}) collective-permute-start(bf16[1,384,768]{2,1,0:T(8,128)(2,1)} %get-tuple-element.749), channel_id=1, source_target_pairs={{0,1},{1,0},{2,3},{3,2},{4,5},{5,4},{6,7},{7,6},{8,9},{9,8},{10,11... | collective-permute-start | bytes 1769480 | tf_op jit(solution)/shard_map/ppermute | solution.py:1021
  342.6 28.7 %collective-permute-start.66 = (bf16[1,384,768]{2,1,0:T(8,128)(2,1)S(1)}, bf16[1,384,768]{2,1,0:T(8,128)(2,1)S(1)}, u32[]{:S(2)}, u32[]{:S(2)}) collective-permute-start(bf16[1,384,768]{2,1,0:T(8,128)(2,1)S(1)} %get-tuple-element.754), channel_id=1, source_target_pairs={{0,1},{1,0},{2,3},{3,2},{4,5},{5,4},{6,7},{7,6},{8,9},{9,8},{10,11... | collective-permute-start | bytes 1769480 | tf_op jit(solution)/shard_map/ppermute | solution.py:1021
  344.3 17.8 %collective-permute-start.68 = (bf16[1,288,768]{2,1,0:T(8,128)(2,1)S(1)}, bf16[1,288,768]{2,1,0:T(8,128)(2,1)S(1)}, u32[]{:S(2)}, u32[]{:S(2)}) collective-permute-start(bf16[1,288,768]{2,1,0:T(8,128)(2,1)S(1)} %get-tuple-element.759), channel_id=1, source_target_pairs={{0,8},{2,10},{4,12},{6,14},{8,0},{10,2},{12,4},{14,6},{16,24},{18,... | collective-permute-start | bytes 1327112 | tf_op jit(solution)/shard_map/ppermute | solution.py:1021
  347.6 19.4 %collective-permute-start.67 = (bf16[1,384,768]{2,1,0:T(8,128)(2,1)S(1)}, bf16[1,384,768]{2,1,0:T(8,128)(2,1)S(1)}, u32[]{:S(2)}, u32[]{:S(2)}) collective-permute-start(bf16[1,384,768]{2,1,0:T(8,128)(2,1)S(1)} %get-tuple-element.762), channel_id=1, source_target_pairs={{0,4},{2,6},{4,0},{6,2},{8,12},{10,14},{12,8},{14,10},{16,20},{18,... | collective-permute-start | bytes 1769480 | tf_op jit(solution)/shard_map/ppermute | solution.py:1021
  362.3 47.0 %collective-permute-start.74 = (bf16[288,768]{1,0:T(8,128)(2,1)S(1)}, bf16[288,768]{1,0:T(8,128)(2,1)S(1)}, u32[]{:S(2)}, u32[]{:S(2)}) collective-permute-start(bf16[288,768]{1,0:T(8,128)(2,1)S(1)} %add_convert_fusion.1), channel_id=1, source_target_pairs={{0,16},{2,18},{4,20},{6,22},{8,24},{10,26},{12,28},{14,30},{16,0},... | collective-permute-start | bytes 1327112 | tf_op jit(solution)/shard_map/ppermute | solution.py:1021
  367.2 56.1 %collective-permute-start.73 = (bf16[1,192,768]{2,1,0:T(8,128)(2,1)S(1)}, bf16[1,192,768]{2,1,0:T(8,128)(2,1)S(1)}, u32[]{:S(2)}, u32[]{:S(2)}) collective-permute-start(bf16[1,192,768]{2,1,0:T(8,128)(2,1)S(1)} %get-tuple-element.784), channel_id=1, source_target_pairs={{0,8},{2,10},{4,12},{6,14},{8,0},{10,2},{12,4},{14,6},{16,24},{18,... | collective-permute-start | bytes 884744 | tf_op jit(solution)/shard_map/ppermute | solution.py:1021
  423.1 21.5 %collective-permute-start.72 = (bf16[288,768]{1,0:T(8,128)(2,1)}, bf16[288,768]{1,0:T(8,128)(2,1)S(1)}, u32[]{:S(2)}, u32[]{:S(2)}) collective-permute-start(bf16[288,768]{1,0:T(8,128)(2,1)} %bitcast.155), channel_id=1, source_target_pairs={{0,16},{2,18},{4,20},{6,22},{8,24},{10,26},{12,28},{14,30},{16,0},... | collective-permute-start | bytes 1327112 | tf_op jit(solution)/shard_map/ppermute | solution.py:1021
  444.7 35.6 %collective-permute-start.82 = (bf16[576,768]{1,0:T(8,128)(2,1)S(1)}, bf16[576,768]{1,0:T(8,128)(2,1)S(1)}, u32[]{:S(2)}, u32[]{:S(2)}) collective-permute-start(bf16[576,768]{1,0:T(8,128)(2,1)S(1)} %bitcast.137), channel_id=1, source_target_pairs={{0,8},{2,10},{4,12},{6,14},{8,0},{10,2},{12,4},{14,6},{16,24},{18,... | collective-permute-start | bytes 2654216 | tf_op jit(solution)/shard_map/ppermute | solution.py:1021
  444.8 33.3 %collective-permute-start.77 = (bf16[288,768]{1,0:T(8,128)(2,1)S(1)}, bf16[288,768]{1,0:T(8,128)(2,1)S(1)}, u32[]{:S(2)}, u32[]{:S(2)}) collective-permute-start(bf16[288,768]{1,0:T(8,128)(2,1)S(1)} %add_convert_fusion.own_ref), channel_id=1, source_target_pairs={{0,8},{2,10},{4,12},{6,14},{8,0},{10,2},{12,4},{14,6},{16,24},{18,... | collective-permute-start | bytes 1327112 | tf_op jit(solution)/shard_map/ppermute | solution.py:1021
  446.2 31.9 %collective-permute-start.78 = (bf16[1,96,768]{2,1,0:T(8,128)(2,1)S(1)}, bf16[1,96,768]{2,1,0:T(8,128)(2,1)S(1)}, u32[]{:S(2)}, u32[]{:S(2)}) collective-permute-start(bf16[1,96,768]{2,1,0:T(8,128)(2,1)S(1)} %get-tuple-element.795), channel_id=1, source_target_pairs={{0,8},{2,10},{4,12},{6,14},{8,0},{10,2},{12,4},{14,6},{16,24},{18,... | collective-permute-start | bytes 442376 | tf_op jit(solution)/shard_map/ppermute | solution.py:1021
  453.0 27.2 %collective-permute-start.76 = (f32[32,768]{1,0:T(8,128)S(1)}, f32[32,768]{1,0:T(8,128)S(1)}, u32[]{:S(2)}, u32[]{:S(2)}) collective-permute-start(f32[32,768]{1,0:T(8,128)S(1)} %add.94), channel_id=1, source_target_pairs={{0,8},{2,10},{4,12},{6,14},{8,0},{10,2},{12,4},{14,6},{16,24},{18,... | collective-permute-start | bytes 294920 | tf_op jit(solution)/shard_map/ppermute | solution.py:1021
  480.4 58.1 %collective-permute-start.90 = (bf16[1152,768]{1,0:T(8,128)(2,1)S(1)}, bf16[1152,768]{1,0:T(8,128)(2,1)S(1)}, u32[]{:S(2)}, u32[]{:S(2)}) collective-permute-start(bf16[1152,768]{1,0:T(8,128)(2,1)S(1)} %bitcast.121), channel_id=1, source_target_pairs={{0,4},{2,6},{4,0},{6,2},{8,12},{10,14},{12,8},{14,10},{16,20},{18,... | collective-permute-start | bytes 5308424 | tf_op jit(solution)/shard_map/ppermute | solution.py:1021
  480.5 57.7 %collective-permute-start.86 = (bf16[576,768]{1,0:T(8,128)(2,1)S(1)}, bf16[576,768]{1,0:T(8,128)(2,1)S(1)}, u32[]{:S(2)}, u32[]{:S(2)}) collective-permute-start(bf16[576,768]{1,0:T(8,128)(2,1)S(1)} %bitcast.135), channel_id=1, source_target_pairs={{0,4},{2,6},{4,0},{6,2},{8,12},{10,14},{12,8},{14,10},{16,20},{18,... | collective-permute-start | bytes 2654216 | tf_op jit(solution)/shard_map/ppermute | solution.py:1021
  482.2 19.9 %collective-permute-start.80 = (bf16[192,768]{1,0:T(8,128)(2,1)S(1)}, bf16[192,768]{1,0:T(8,128)(2,1)S(1)}, u32[]{:S(2)}, u32[]{:S(2)}) collective-permute-start(bf16[192,768]{1,0:T(8,128)(2,1)S(1)} %add_convert_fusion.3), channel_id=1, source_target_pairs={{0,16},{2,18},{4,20},{6,22},{8,24},{10,26},{12,28},{14,30},{16,0},... | collective-permute-start | bytes 884744 | tf_op jit(solution)/shard_map/ppermute | solution.py:1021
  482.2 56.1 %collective-permute-start.85 = (bf16[96,768]{1,0:T(8,128)(2,1)S(1)}, bf16[96,768]{1,0:T(8,128)(2,1)S(1)}, u32[]{:S(2)}, u32[]{:S(2)}) collective-permute-start(bf16[96,768]{1,0:T(8,128)(2,1)S(1)} %add_convert_fusion.7), channel_id=1, source_target_pairs={{0,16},{2,18},{4,20},{6,22},{8,24},{10,26},{12,28},{14,30},{16,0},... | collective-permute-start | bytes 442376 | tf_op jit(solution)/shard_map/ppermute | solution.py:1021
  487.6 23.0 %collective-permute-start.79 = (f32[32,768]{1,0:T(8,128)S(1)}, f32[32,768]{1,0:T(8,128)S(1)}, u32[]{:S(2)}, u32[]{:S(2)}) collective-permute-start(f32[32,768]{1,0:T(8,128)S(1)} %add.96), channel_id=1, source_target_pairs={{0,16},{2,18},{4,20},{6,22},{8,24},{10,26},{12,28},{14,30},{16,0},... | collective-permute-start | bytes 294920 | tf_op jit(solution)/shard_map/ppermute | solution.py:1021
  502.1 36.2 %collective-permute-start.84 = (bf16[96,768]{1,0:T(8,128)(2,1)S(1)}, bf16[96,768]{1,0:T(8,128)(2,1)S(1)}, u32[]{:S(2)}, u32[]{:S(2)}) collective-permute-start(bf16[96,768]{1,0:T(8,128)(2,1)S(1)} %add_convert_fusion.6), channel_id=1, source_target_pairs={{0,16},{2,18},{4,20},{6,22},{8,24},{10,26},{12,28},{14,30},{16,0},... | collective-permute-start | bytes 442376 | tf_op jit(solution)/shard_map/ppermute | solution.py:1021
  510.5 27.9 %collective-permute-start.91 = (bf16[192,768]{1,0:T(8,128)(2,1)S(1)}, bf16[192,768]{1,0:T(8,128)(2,1)S(1)}, u32[]{:S(2)}, u32[]{:S(2)}) collective-permute-start(bf16[192,768]{1,0:T(8,128)(2,1)S(1)} %add_convert_fusion.2.own_ref), channel_id=1, source_target_pairs={{0,8},{2,10},{4,12},{6,14},{8,0},{10,2},{12,4},{14,6},{16,24},{18,... | collective-permute-start | bytes 884744 | tf_op jit(solution)/shard_map/ppermute | solution.py:1021
  538.7 21.9 %collective-permute-start.94 = (bf16[2304,768]{1,0:T(8,128)(2,1)S(1)}, bf16[2304,768]{1,0:T(8,128)(2,1)S(1)}, u32[]{:S(2)}, u32[]{:S(2)}) collective-permute-start(bf16[2304,768]{1,0:T(8,128)(2,1)S(1)} %bitcast.105), channel_id=1, source_target_pairs={{0,2},{2,0},{4,6},{6,4},{8,10},{10,8},{12,14},{14,12},{16,18},{18,... | collective-permute-start | bytes 10616840 | tf_op jit(solution)/shard_map/ppermute | solution.py:1021
  541.1 16.6 %collective-permute-start.95 = (bf16[384,768]{1,0:T(8,128)(2,1)S(1)}, bf16[384,768]{1,0:T(8,128)(2,1)S(1)}, u32[]{:S(2)}, u32[]{:S(2)}) collective-permute-start(bf16[384,768]{1,0:T(8,128)(2,1)S(1)} %bitcast.140), channel_id=1, source_target_pairs={{0,4},{2,6},{4,0},{6,2},{8,12},{10,14},{12,8},{14,10},{16,20},{18,... | collective-permute-start | bytes 1769480 | tf_op jit(solution)/shard_map/ppermute | solution.py:1021
  541.4 16.2 %collective-permute-start.83 = (f32[32,768]{1,0:T(8,128)S(1)}, f32[32,768]{1,0:T(8,128)S(1)}, u32[]{:S(2)}, u32[]{:S(2)}) collective-permute-start(f32[32,768]{1,0:T(8,128)S(1)} %add.99), channel_id=1, source_target_pairs={{0,4},{2,6},{4,0},{6,2},{8,12},{10,14},{12,8},{14,10},{16,20},{18,... | collective-permute-start | bytes 294920 | tf_op jit(solution)/shard_map/ppermute | solution.py:1021
  557.8 17.2 %collective-permute-start.98 = (bf16[768,768]{1,0:T(8,128)(2,1)S(1)}, bf16[768,768]{1,0:T(8,128)(2,1)S(1)}, u32[]{:S(2)}, u32[]{:S(2)}) collective-permute-start(bf16[768,768]{1,0:T(8,128)(2,1)S(1)} %bitcast.125), channel_id=1, source_target_pairs={{0,2},{2,0},{4,6},{6,4},{8,10},{10,8},{12,14},{14,12},{16,18},{18,... | collective-permute-start | bytes 3538952 | tf_op jit(solution)/shard_map/ppermute | solution.py:1021
  559.2 14.9 %collective-permute-start.92 = (bf16[192,768]{1,0:T(8,128)(2,1)S(1)}, bf16[192,768]{1,0:T(8,128)(2,1)S(1)}, u32[]{:S(2)}, u32[]{:S(2)}) collective-permute-start(bf16[192,768]{1,0:T(8,128)(2,1)S(1)} %bitcast.159), channel_id=1, source_target_pairs={{0,4},{2,6},{4,0},{6,2},{8,12},{10,14},{12,8},{14,10},{16,20},{18,... | collective-permute-start | bytes 884744 | tf_op jit(solution)/shard_map/ppermute | solution.py:1021
  (155 other events, 1014.5 us)
Sparse Core Ops, SparseCore 0:
  258.3 164.7 reduce-scatter.1

commit v4 on v3

--- a/solution.py
+++ b/solution.py
@@ -900,7 +900,7 @@
     return picked(body, bit, (1,), [(own, flat), (got, flat)], [out], "pair_up", 1)[0]
 
 
-def finish(kind, half, own, got, begin, length, core, layer, targets):
+def finish(kind, half, own, got, begin, length, core, layer, targets, ranks=None):
     pieces, _, columns = own.shape
     scale = 1.0 / lax.axis_size("wide")
     aliases = {place + 2: place for place in range(len(targets))}
@@ -910,7 +910,10 @@
 
     def chosen(core_ref, which, own_ref, got_ref, place=None):
         sides = [own_ref, got_ref]
-        if place is None:
+        if ranks is not None:
+            wanted = ranks if place is None else ranks[place * pieces // 2 : (place + 1) * pieces // 2]
+            values = [jnp.concatenate([side[rank] for rank in wanted]) for side in sides]
+        elif place is None:
             values = [side[...].reshape(pieces * length, columns) for side in sides]
         else:
             if pieces == 1:
@@ -937,6 +940,9 @@
 
     def values_of(core_ref, own_ref, got_ref):
         step = pl.program_id(0)
+        if half is None and ranks is not None:
+            both = [chosen(core_ref, step // 2, own_ref, got_ref, place) for place in range(2)]
+            return jnp.where(step % 2 == 0, both[0], both[1])
         if half is None:
             return chosen(core_ref, step // 2, own_ref, got_ref, step % 2)
         return chosen(core_ref, step, own_ref, got_ref)
@@ -1052,8 +1058,9 @@
         self.count, rows, self.columns = total.shape
         self.masks = list(reversed(masks("wide")[1:]))
         places = 1 << len(self.masks)
-        ranks = [sum(((place >> bit) & 1) << (len(self.masks) - 1 - bit) for bit in range(len(self.masks))) for place in range(places)]
-        groups = [[2 * rank + core for rank in ranks] for core in range(2)]
+        last = len(self.masks) - 1
+        self.ranks = [sum(((place >> bit) & 1) << (last - bit) for bit in range(last + 1)) for place in range(places)]
+        groups = [[2 * place + core for place in range(places)] for core in range(2)]
         self.length = rows // places
         part = lax.psum_scatter(total, "wide", axis_index_groups=groups, scatter_dimension=1, tiled=True)
         self.part = part.reshape(-1, self.columns)
@@ -1076,12 +1083,13 @@
         if self.length % 16:
             pieces = own.shape[0]
             own, got = [
-                side.reshape(pieces, self.count, -1, self.columns).swapaxes(0, 1).reshape(1, -1, self.columns)
+                jnp.stack([side.reshape(pieces, self.count, -1, self.columns)[rank] for rank in self.ranks], axis=1)
+                .reshape(1, -1, self.columns)
                 for side in (own, got)
             ]
-            self.length *= pieces
+            self.length, self.ranks = self.length * pieces, None
         for which, term in enumerate(terms):
-            term.finish(done, own, got, which * self.length, self.length)
+            term.finish(done, own, got, which * self.length, self.length, self.ranks)
 
 
 class Term:
@@ -1131,11 +1139,11 @@
             return self.order.run(lambda one, two: add_into(None, place, count, one, two), kept, got)
         return self.order.run(lambda target, one, two: add_into(target, place, count, one, two), target, kept, got)
 
-    def finish(self, done, own, got, begin, length):
+    def finish(self, done, own, got, begin, length, ranks=None):
         targets = done.get(self.kind, ())
 
         def last(own, got, core, *targets):
-            return finish(self.kind, self.half, own, got, begin, length, core, self.layer, targets)
+            return finish(self.kind, self.half, own, got, begin, length, core, self.layer, targets, ranks)
 
         done[self.kind] = self.order.run(last, own, got, self.core, *targets)
 

time: 599 us -> 556 us (0.928)
  waiting for transfers between devices: 210 us -> 145 us
  starting transfers between devices: 68.9 us -> 90.8 us
    ppermute x99, waiting for transfers between devices: 196 us -> 145 us  [swap(): lax.ppermute(values, axis, [(source, source ^ mask) for source in range(s...]
    ppermute x99, starting transfers between devices: 68.8 us -> 90.8 us  [swap(): lax.ppermute(values, axis, [(source, source ^ mask) for source in range(s...]
    reduce_scatter x1, waiting for transfers between devices: 13.8 us -> 0.01 us  [__init__(): lax.psum_scatter(total, 'wide', axis_index_groups=groups, scatter_dimensi...]
  transfers between devices with their start and end apart: 100 -> 100, of which waited for: 36 -> 31; matrix products, arithmetic and copies ran while one was open for 3% -> 3% of each run, Pallas kernels for 35% -> 38%
where the time goes in v4:
time: 556 us; the launch traced here: 547 us
  Pallas kernels  240 us (43%)
  waiting for transfers between devices  145 us (26%)
  starting transfers between devices  90.8 us (16%)
  local copies, waits for them, and re-layouts  50.5 us (9%)
  between operations  16 us (3%)
    pallas_call x13, Pallas kernels, call(): pl.pallas_call(body, grid=grid, in_specs=[spec for _, spec in ins], out_s...  159 us
    ppermute x99, waiting for transfers between devices, swap(): lax.ppermute(values, axis, [(source, source ^ mask) for source in range(s...  145 us
    ppermute x99, starting transfers between devices, swap(): lax.ppermute(values, axis, [(source, source ^ mask) for source in range(s...  90.8 us
    pallas_call x52, Pallas kernels, picked(): pl.pallas_call(body, grid_spec=pltpu.PrefetchScalarGridSpec(num_scalar_pr...  73.7 us
    unnamed x212, local copies, waits for them, and re-layouts  37.2 us
  transfers between devices with their start and end apart: 100, of which 31 were waited for; matrix products, arithmetic and copies ran while one was open for 3% of the time, Pallas kernels for 38%

profile of v4, /device:TPU:1, one launch (start us, length us, event | category | flops | bytes accessed | tf_op | source)
XLA Modules:
  0.0 547.3 jit_solution(5738970171983907485)
XLA Ops:
  34.9 5.9 %collective-permute-done.1.refs_3_ = bf16[1,96,2304]{2,1,0:T(8,128)(2,1)} collective-permute-done((bf16[1,96,2304]{2,1,0:T(8,128)(2,1)}, bf16[1,96,2304]{2,1,0:T(8,128)(2,1)}, u32[]{:S(2)}, u32[]{:S(2)}) %collective-permute-start.1) | collective-permute-done | bytes 442400 | tf_op jit(solution)/shard_map/ppermute | solution.py:1027
  40.8 3.0 collective-permute-start.3
  48.1 5.1 project_qkv.1
  54.7 8.7 %attend.2 = (bf16[2,336,768]{2,1,0:T(8,128)(2,1)S(1)}, f32[2,6,8,336]{3,2,1,0:T(8,128)S(1)}) custom-call(s32[2]{0:T(128)S(1)} %multiply_add_fusion.length_ref.refs_23_, bf16[3,2,336,768]{3,2,1,0:T(8,128)(2,1)S(1)} %bitcast.181, bf16[3,2,336,768]{3,2,1,0:T(8,128)(2,1)S(1)} %bitcast.182, bf16[3,2,336,768]{3,2,1,0:T(8,128)(2,1)S(1)} %bitcast.183), custom_call_target="tpu_custom_call" | custom-call | flops 3000000000 | tf_op jit(solution)/shard_map/attend/pallas_call | solution.py:69
  75.0 20.7 %feed_forward.2 = (f32[672,768]{1,0:T(8,128)S(1)}, bf16[672,768]{1,0:T(8,128)(2,1)S(1)}, bf16[672,3072]{1,0:T(8,128)(2,1)S(1)}, bf16[672,3072]{1,0:T(8,128)(2,1)}, bf16[672,768]{1,0:T(8,128)(2,1)S(1)}) custom-call(s32[2]{0:T(128)S(1)} %pad_add_fusion.refs_0_, bf16[2,384,768]{2,1,0:T(8,128)(2,1)} %refs_11_.7, bf16[1,96,3840]{2,1,0:T(8,128)(2,1)} %copy-done.74, ...), custom_call_target="tpu_custom_call" | custom-call | flops 6899999744 | tf_op jit(solution)/shard_map/feed_forward/pallas_call | solution.py:69
  104.1 8.2 %join_qkv.1 = (f32[672,768]{1,0:T(8,128)S(1)}, bf16[672,768]{1,0:T(8,128)(2,1)S(1)}, bf16[3,672,768]{2,1,0:T(8,128)(2,1)S(1)}) custom-call(s32[2]{0:T(128)S(1)} %pad_add_fusion.refs_0_, bf16[768,768]{1,0:T(8,128)(2,1)} %refs_6_.10, bf16[1,192,768]{2,1,0:T(8,128)(2,1)} %copy-done.98, bf16[1,192,768]{2,1,0:T(8,128)(2,1)} %copy-done.99, ...), custom_call_target="tpu_custom_call" | custom-call | flops 3300000000 | tf_op jit(solution)/shard_map/join_qkv/pallas_call | solution.py:69
  112.4 8.7 %attend.3 = (bf16[2,336,768]{2,1,0:T(8,128)(2,1)S(1)}, f32[2,6,8,336]{3,2,1,0:T(8,128)S(1)}) custom-call(s32[2]{0:T(128)S(1)} %multiply_add_fusion.length_ref.refs_23_, bf16[3,2,336,768]{3,2,1,0:T(8,128)(2,1)S(1)} %bitcast.187, bf16[3,2,336,768]{3,2,1,0:T(8,128)(2,1)S(1)} %bitcast.188, bf16[3,2,336,768]{3,2,1,0:T(8,128)(2,1)S(1)} %bitcast.189), custom_call_target="tpu_custom_call" | custom-call | flops 3000000000 | tf_op jit(solution)/shard_map/attend/pallas_call | solution.py:69
  122.5 3.1 collective-permute-done.27.refs_14_.refs_4_
  128.4 21.2 %feed_forward.3 = (f32[672,768]{1,0:T(8,128)S(1)}, bf16[672,768]{1,0:T(8,128)(2,1)S(1)}, bf16[672,3072]{1,0:T(8,128)(2,1)S(1)}, bf16[672,3072]{1,0:T(8,128)(2,1)}, bf16[672,768]{1,0:T(8,128)(2,1)}) custom-call(s32[2]{0:T(128)S(1)} %pad_add_fusion.refs_0_, bf16[2,384,768]{2,1,0:T(8,128)(2,1)} %refs_11_.7, bf16[1,96,3840]{2,1,0:T(8,128)(2,1)} %copy-done.78, ...), custom_call_target="tpu_custom_call" | custom-call | flops 6899999744 | tf_op jit(solution)/shard_map/feed_forward/pallas_call | solution.py:69
  150.9 4.1 down_term.4
  158.2 2.9 down_term.5
  165.0 18.3 %feed_forward_back.2 = (bf16[672,3072]{1,0:T(8,128)(2,1)}, f32[672,768]{1,0:T(8,128)S(1)}, bf16[672,768]{1,0:T(8,128)(2,1)S(1)}, bf16[672,768]{1,0:T(8,128)(2,1)S(1)}, f32[8,768]{1,0:T(8,128)S(1)}) custom-call(s32[2]{0:T(128)S(1)} %pad_add_fusion.refs_0_, bf16[2,1536,768]{2,1,0:T(8,128)(2,1)} %refs_1_.15, bf16[1,384,768]{2,1,0:T(8,128)(2,1)} %copy-done.88, ...), custom_call_target="tpu_custom_call" | custom-call | flops 6300000256 | tf_op jit(solution)/shard_map/feed_forward_back/pallas_call | solution.py:69
  183.4 3.6 copy-done.4
  187.0 2.7 up_term.4
  191.1 2.7 up_term.5
  198.8 2.7 add_into.3.rest_0_
  202.9 14.1 %attend_back.2 = bf16[3,2,336,768]{3,2,1,0:T(8,128)(2,1)S(1)} custom-call(s32[2]{0:T(128)S(1)} %multiply_add_fusion.length_ref.refs_23_, bf16[3,2,336,768]{3,2,1,0:T(8,128)(2,1)S(1)} %bitcast.190, bf16[3,2,336,768]{3,2,1,0:T(8,128)(2,1)S(1)} %bitcast.191, bf16[3,2,336,768]{3,2,1,0:T(8,128)(2,1)S(1)} %bitcast.192, bf16[2,336,768]{2,1,0:T(8,128)(2,1)S(1)} %bitcast.168, ...), custom_call_target="tpu_custom_call" | custom-call | flops 4499999744 | tf_op jit(solution)/shard_map/attend_back/pallas_call | solution.py:69
  217.1 2.6 qkv_out_term.4
  227.7 2.7 add_into.4.rest_0_
  232.0 11.6 %project_back.2 = (bf16[672,768]{1,0:T(8,128)(2,1)S(1)}, f32[672,768]{1,0:T(8,128)S(1)}, bf16[672,768]{1,0:T(8,128)(2,1)S(1)}, f32[672,768]{1,0:T(8,128)}, f32[8,768]{1,0:T(8,128)S(1)}) custom-call(s32[2]{0:T(128)S(1)} %pad_add_fusion.refs_0_, bf16[2,384,2304]{2,1,0:T(8,128)(2,1)} %refs_1_.16, bf16[1,96,2304]{2,1,0:T(8,128)(2,1)} %collective-permute-done.10.refs_7_.refs_2_, ...), custom_call_target="tpu_custom_call" | custom-call | flops 3900000000 | tf_op jit(solution)/shard_map/project_back/pallas_call | solution.py:69
  250.1 2.7 down_term.6
  252.8 2.7 down_term.7
  255.6 2.6 add_into.5
  267.5 19.6 %feed_forward_back.3 = (bf16[672,3072]{1,0:T(8,128)(2,1)}, f32[672,768]{1,0:T(8,128)S(1)}, bf16[672,768]{1,0:T(8,128)(2,1)S(1)}, bf16[672,768]{1,0:T(8,128)(2,1)S(1)}, f32[8,768]{1,0:T(8,128)S(1)}) custom-call(s32[2]{0:T(128)S(1)} %pad_add_fusion.refs_0_, bf16[2,1536,768]{2,1,0:T(8,128)(2,1)} %refs_1_.15, bf16[1,384,768]{2,1,0:T(8,128)(2,1)} %copy-done.84, ...), custom_call_target="tpu_custom_call" | custom-call | flops 6300000256 | tf_op jit(solution)/shard_map/feed_forward_back/pallas_call | solution.py:69
  291.3 2.9 up_term.6
  295.8 2.7 up_term.7
  298.4 5.0 collective-permute-done.57
  309.3 13.8 %attend_back.3 = bf16[3,2,336,768]{3,2,1,0:T(8,128)(2,1)S(1)} custom-call(s32[2]{0:T(128)S(1)} %multiply_add_fusion.length_ref.refs_23_, bf16[3,2,336,768]{3,2,1,0:T(8,128)(2,1)S(1)} %bitcast.184, bf16[3,2,336,768]{3,2,1,0:T(8,128)(2,1)S(1)} %bitcast.185, bf16[3,2,336,768]{3,2,1,0:T(8,128)(2,1)S(1)} %bitcast.186, bf16[2,336,768]{2,1,0:T(8,128)(2,1)S(1)} %bitcast.167, ...), custom_call_target="tpu_custom_call" | custom-call | flops 4499999744 | tf_op jit(solution)/shard_map/attend_back/pallas_call | solution.py:69
  323.1 3.6 qkv_out_term.6
  345.9 8.4 %project_back.3 = (f32[672,768]{1,0:T(8,128)}, f32[8,768]{1,0:T(8,128)S(1)}) custom-call(s32[2]{0:T(128)S(1)} %pad_add_fusion.refs_0_, bf16[2,384,2304]{2,1,0:T(8,128)(2,1)} %refs_1_.16, bf16[1,96,2304]{2,1,0:T(8,128)(2,1)} %collective-permute-done.refs_2_, bf16[1,96,2304]{2,1,0:T(8,128)(2,1)} %collective-permute-done.1.refs_3_, ...), custom_call_target="tpu_custom_call" | custom-call | flops 2700000000 | tf_op jit(solution)/shard_map/project_back/pallas_call | solution.py:69
  357.6 3.0 collective-permute-start.74
  364.0 4.8 collective-permute-done.66
  371.0 7.9 %collective-permute-done.74 = bf16[288,768]{1,0:T(8,128)(2,1)S(1)} collective-permute-done((bf16[288,768]{1,0:T(8,128)(2,1)S(1)}, bf16[288,768]{1,0:T(8,128)(2,1)S(1)}, u32[]{:S(2)}, u32[]{:S(2)}) %collective-permute-start.74) | collective-permute-done | bytes 442400 | tf_op jit(solution)/shard_map/ppermute | solution.py:1027
  379.1 10.3 %collective-permute-done.72.got_ref = bf16[288,768]{1,0:T(8,128)(2,1)S(1)} collective-permute-done((bf16[288,768]{1,0:T(8,128)(2,1)}, bf16[288,768]{1,0:T(8,128)(2,1)S(1)}, u32[]{:S(2)}, u32[]{:S(2)}) %collective-permute-start.72) | collective-permute-done | bytes 442400 | tf_op jit(solution)/shard_map/ppermute | solution.py:1027
  389.5 14.7 %collective-permute-start.82 = (bf16[576,768]{1,0:T(8,128)(2,1)S(1)}, bf16[576,768]{1,0:T(8,128)(2,1)S(1)}, u32[]{:S(2)}, u32[]{:S(2)}) collective-permute-start(bf16[576,768]{1,0:T(8,128)(2,1)S(1)} %bitcast.137), channel_id=1, source_target_pairs={{0,8},{2,10},{4,12},{6,14},{8,0},{10,2},{12,4},{14,6},{16,24},{18,... | collective-permute-start | bytes 2654216 | tf_op jit(solution)/shard_map/ppermute | solution.py:1027
  407.6 3.8 collective-permute-done.71
  411.9 23.9 %collective-permute-done.78 = bf16[1,96,768]{2,1,0:T(8,128)(2,1)S(1)} collective-permute-done((bf16[1,96,768]{2,1,0:T(8,128)(2,1)S(1)}, bf16[1,96,768]{2,1,0:T(8,128)(2,1)S(1)}, u32[]{:S(2)}, u32[]{:S(2)}) %collective-permute-start.78) | collective-permute-done | bytes 147488 | tf_op jit(solution)/shard_map/ppermute | solution.py:1027
  445.6 15.3 %collective-permute-done.80 = bf16[192,768]{1,0:T(8,128)(2,1)S(1)} collective-permute-done((bf16[192,768]{1,0:T(8,128)(2,1)S(1)}, bf16[192,768]{1,0:T(8,128)(2,1)S(1)}, u32[]{:S(2)}, u32[]{:S(2)}) %collective-permute-start.80) | collective-permute-done | bytes 294944 | tf_op jit(solution)/shard_map/ppermute | solution.py:1027
  460.9 8.3 %collective-permute-done.79 = f32[32,768]{1,0:T(8,128)S(1)} collective-permute-done((f32[32,768]{1,0:T(8,128)S(1)}, f32[32,768]{1,0:T(8,128)S(1)}, u32[]{:S(2)}, u32[]{:S(2)}) %collective-permute-start.79) | collective-permute-done | bytes 98336 | tf_op jit(solution)/shard_map/ppermute | solution.py:1027
  469.3 26.3 %collective-permute-done.86.got_ref = bf16[576,768]{1,0:T(8,128)(2,1)S(1)} collective-permute-done((bf16[576,768]{1,0:T(8,128)(2,1)S(1)}, bf16[576,768]{1,0:T(8,128)(2,1)S(1)}, u32[]{:S(2)}, u32[]{:S(2)}) %collective-permute-start.86) | collective-permute-done | bytes 884768 | tf_op jit(solution)/shard_map/ppermute | solution.py:1027
  496.1 2.6 collective-permute-start.94
  501.4 5.7 %collective-permute-done.89 = bf16[1152,768]{1,0:T(8,128)(2,1)S(1)} collective-permute-done((bf16[1152,768]{1,0:T(8,128)(2,1)S(1)}, bf16[1152,768]{1,0:T(8,128)(2,1)S(1)}, u32[]{:S(2)}, u32[]{:S(2)}) %collective-permute-start.89) | collective-permute-done | bytes 1769504 | tf_op jit(solution)/shard_map/ppermute | solution.py:1027
  512.4 2.9 collective-permute-done.83
  518.3 2.6 finish_rows.5
  520.9 3.0 finish_columns.2.rest_0_
  523.9 4.1 finish_qkv_out.2
  528.8 3.0 collective-permute-done.92.got_ref
  532.7 2.6 finish_columns.3
  (468 shorter events, 169.7 us)
Async XLA Ops:
  7.2 371.7 %reduce-scatter.2.cloned.1.call-start = ((), (), s32[]{:S(2)}) async-start(), calls=%async_computation.1 | async-start | bytes 3981312 | tf_op jit(solution)/shard_map/reduce_scatter | solution.py:1065
  8.3 22.6 %collective-permute-start = (bf16[1,96,2304]{2,1,0:T(8,128)(2,1)S(1)}, bf16[1,96,2304]{2,1,0:T(8,128)(2,1)}, u32[]{:S(2)}, u32[]{:S(2)}) collective-permute-start(bf16[1,96,2304]{2,1,0:T(8,128)(2,1)S(1)} %constant_dynamic-slice_fusion.3), channel_id=1, source_target_pairs={{0,1},{1,0},{2,3},{3,2},{4,5},{5,4},{6,7},{7,6},{8,9},{9,8},{10,11... | collective-permute-start | bytes 1327112 | tf_op jit(solution)/shard_map/ppermute | solution.py:1027
  14.5 17.9 %collective-permute-start.4 = (bf16[1,32,384]{2,1,0:T(8,128)(2,1)S(1)}, bf16[1,32,384]{2,1,0:T(8,128)(2,1)S(1)}, u32[]{:S(2)}, u32[]{:S(2)}) collective-permute-start(bf16[1,32,384]{2,1,0:T(8,128)(2,1)S(1)} %convert_bitcast_fusion), channel_id=1, source_target_pairs={{0,1},{1,0},{2,3},{3,2},{4,5},{5,4},{6,7},{7,6},{8,9},{9,8},{10,11... | collective-permute-start | bytes 73736 | tf_op jit(solution)/shard_map/ppermute | solution.py:1027
  17.6 27.6 %collective-permute-start.5 = (bf16[1,96,3840]{2,1,0:T(8,128)(2,1)}, bf16[1,96,3840]{2,1,0:T(8,128)(2,1)S(1)}, u32[]{:S(2)}, u32[]{:S(2)}) collective-permute-start(bf16[1,96,3840]{2,1,0:T(8,128)(2,1)} %maximum_bitcast_fusion), channel_id=1, source_target_pairs={{0,1},{1,0},{2,3},{3,2},{4,5},{5,4},{6,7},{7,6},{8,9},{9,8},{10,11... | collective-permute-start | bytes 2211848 | tf_op jit(solution)/shard_map/ppermute | solution.py:1027
  20.9 32.4 %collective-permute-start.8 = (bf16[1,384,768]{2,1,0:T(8,128)(2,1)}, bf16[1,384,768]{2,1,0:T(8,128)(2,1)S(1)}, u32[]{:S(2)}, u32[]{:S(2)}) collective-permute-start(bf16[1,384,768]{2,1,0:T(8,128)(2,1)} %constant_dynamic-slice_fusion.2), channel_id=1, source_target_pairs={{0,1},{1,0},{2,3},{3,2},{4,5},{5,4},{6,7},{7,6},{8,9},{9,8},{10,11... | collective-permute-start | bytes 1769480 | tf_op jit(solution)/shard_map/ppermute | solution.py:1027
  24.5 40.6 %collective-permute-start.10 = (bf16[1,96,2304]{2,1,0:T(8,128)(2,1)}, bf16[1,96,2304]{2,1,0:T(8,128)(2,1)}, u32[]{:S(2)}, u32[]{:S(2)}) collective-permute-start(bf16[1,96,2304]{2,1,0:T(8,128)(2,1)} %constant_dynamic-slice_fusion.1), channel_id=1, source_target_pairs={{0,1},{1,0},{2,3},{3,2},{4,5},{5,4},{6,7},{7,6},{8,9},{9,8},{10,11... | collective-permute-start | bytes 1327112 | tf_op jit(solution)/shard_map/ppermute | solution.py:1027
  32.5 14.1 %collective-permute-start.2 = (bf16[1,96,2304]{2,1,0:T(8,128)(2,1)}, bf16[1,96,2304]{2,1,0:T(8,128)(2,1)S(1)}, u32[]{:S(2)}, u32[]{:S(2)}) collective-permute-start(bf16[1,96,2304]{2,1,0:T(8,128)(2,1)} %collective-permute-done.refs_2_), channel_id=1, source_target_pairs={{0,2},{2,0},{4,6},{6,4},{8,10},{10,8},{12,14},{14,12},{16,18},{18,... | collective-permute-start | bytes 1327112 | tf_op jit(solution)/shard_map/ppermute | solution.py:1027
  45.2 21.1 %collective-permute-start.7 = (bf16[1,96,3840]{2,1,0:T(8,128)(2,1)S(1)}, bf16[1,96,3840]{2,1,0:T(8,128)(2,1)S(1)}, u32[]{:S(2)}, u32[]{:S(2)}) collective-permute-start(bf16[1,96,3840]{2,1,0:T(8,128)(2,1)S(1)} %collective-permute-done.5.refs_2_.refs_7_.refs_12_), channel_id=1, source_target_pairs={{0,4},{2,6},{4,0},{6,2},{8,12},{10,14},{12,8},{14,10},{16,20},{18,... | collective-permute-start | bytes 2211848 | tf_op jit(solution)/shard_map/ppermute | solution.py:1027
  46.6 18.5 %collective-permute-start.9 = (bf16[1,192,768]{2,1,0:T(8,128)(2,1)}, bf16[1,192,768]{2,1,0:T(8,128)(2,1)S(1)}, u32[]{:S(2)}, u32[]{:S(2)}) collective-permute-start(bf16[1,192,768]{2,1,0:T(8,128)(2,1)} %dynamic-slice_bitcast_fusion.2), channel_id=1, source_target_pairs={{0,1},{1,0},{2,3},{3,2},{4,5},{5,4},{6,7},{7,6},{8,9},{9,8},{10,11... | collective-permute-start | bytes 884744 | tf_op jit(solution)/shard_map/ppermute | solution.py:1027
  53.4 14.7 %collective-permute-start.13 = (bf16[1,384,768]{2,1,0:T(8,128)(2,1)S(1)}, bf16[1,384,768]{2,1,0:T(8,128)(2,1)S(1)}, u32[]{:S(2)}, u32[]{:S(2)}) collective-permute-start(bf16[1,384,768]{2,1,0:T(8,128)(2,1)S(1)} %collective-permute-done.8.refs_12_.refs_2_), channel_id=1, source_target_pairs={{0,8},{2,10},{4,12},{6,14},{8,0},{10,2},{12,4},{14,6},{16,24},{18,... | collective-permute-start | bytes 1769480 | tf_op jit(solution)/shard_map/ppermute | solution.py:1027
  69.2 31.6 %collective-permute-start.23 = (bf16[1,384,768]{2,1,0:T(8,128)(2,1)S(1)}, bf16[1,384,768]{2,1,0:T(8,128)(2,1)S(1)}, u32[]{:S(2)}, u32[]{:S(2)}) collective-permute-start(bf16[1,384,768]{2,1,0:T(8,128)(2,1)S(1)} %copy-done.92), channel_id=1, source_target_pairs={{0,1},{1,0},{2,3},{3,2},{4,5},{5,4},{6,7},{7,6},{8,9},{9,8},{10,11... | collective-permute-start | bytes 1769480 | tf_op jit(solution)/shard_map/ppermute | solution.py:1027
  70.1 29.9 %collective-permute-start.6 = (bf16[1,96,3840]{2,1,0:T(8,128)(2,1)S(1)}, bf16[1,96,3840]{2,1,0:T(8,128)(2,1)S(1)}, u32[]{:S(2)}, u32[]{:S(2)}) collective-permute-start(bf16[1,96,3840]{2,1,0:T(8,128)(2,1)S(1)} %copy-done.83), channel_id=1, source_target_pairs={{0,1},{1,0},{2,3},{3,2},{4,5},{5,4},{6,7},{7,6},{8,9},{9,8},{10,11... | collective-permute-start | bytes 2211848 | tf_op jit(solution)/shard_map/ppermute | solution.py:1027
  71.6 24.2 %collective-permute-start.20 = (bf16[1,96,2304]{2,1,0:T(8,128)(2,1)}, bf16[1,96,2304]{2,1,0:T(8,128)(2,1)S(1)}, u32[]{:S(2)}, u32[]{:S(2)}) collective-permute-start(bf16[1,96,2304]{2,1,0:T(8,128)(2,1)} %collective-permute-done.10.refs_7_.refs_2_), channel_id=1, source_target_pairs={{0,4},{2,6},{4,0},{6,2},{8,12},{10,14},{12,8},{14,10},{16,20},{18,... | collective-permute-start | bytes 1327112 | tf_op jit(solution)/shard_map/ppermute | solution.py:1027
  72.8 24.4 %collective-permute-start.17 = (bf16[1,192,768]{2,1,0:T(8,128)(2,1)S(1)}, bf16[1,192,768]{2,1,0:T(8,128)(2,1)S(1)}, u32[]{:S(2)}, u32[]{:S(2)}) collective-permute-start(bf16[1,192,768]{2,1,0:T(8,128)(2,1)S(1)} %collective-permute-done.9.refs_2_.refs_7_), channel_id=1, source_target_pairs={{0,8},{2,10},{4,12},{6,14},{8,0},{10,2},{12,4},{14,6},{16,24},{18,... | collective-permute-start | bytes 884744 | tf_op jit(solution)/shard_map/ppermute | solution.py:1027
  100.8 21.0 %collective-permute-start.16 = (bf16[1,96,3840]{2,1,0:T(8,128)(2,1)S(1)}, bf16[1,96,3840]{2,1,0:T(8,128)(2,1)S(1)}, u32[]{:S(2)}, u32[]{:S(2)}) collective-permute-start(bf16[1,96,3840]{2,1,0:T(8,128)(2,1)S(1)} %collective-permute-done.6.refs_2_.refs_7_.refs_12_), channel_id=1, source_target_pairs={{0,4},{2,6},{4,0},{6,2},{8,12},{10,14},{12,8},{14,10},{16,20},{18,... | collective-permute-start | bytes 2211848 | tf_op jit(solution)/shard_map/ppermute | solution.py:1027
  101.1 21.3 %collective-permute-start.26 = (bf16[1,384,768]{2,1,0:T(8,128)(2,1)S(1)}, bf16[1,384,768]{2,1,0:T(8,128)(2,1)S(1)}, u32[]{:S(2)}, u32[]{:S(2)}) collective-permute-start(bf16[1,384,768]{2,1,0:T(8,128)(2,1)S(1)} %collective-permute-done.23.refs_12_.refs_2_), channel_id=1, source_target_pairs={{0,8},{2,10},{4,12},{6,14},{8,0},{10,2},{12,4},{14,6},{16,24},{18,... | collective-permute-start | bytes 1769480 | tf_op jit(solution)/shard_map/ppermute | solution.py:1027
  164.2 33.6 %collective-permute-start.33 = (bf16[2,384,768]{2,1,0:T(8,128)(2,1)S(1)}, bf16[2,384,768]{2,1,0:T(8,128)(2,1)S(1)}, u32[]{:S(2)}, u32[]{:S(2)}) collective-permute-start(bf16[2,384,768]{2,1,0:T(8,128)(2,1)S(1)} %get-tuple-element.555), channel_id=1, source_target_pairs={{0,1},{1,0},{2,3},{3,2},{4,5},{5,4},{6,7},{7,6},{8,9},{9,8},{10,11... | collective-permute-start | bytes 3538952 | tf_op jit(solution)/shard_map/ppermute | solution.py:1027
  197.1 30.6 %collective-permute-start.38 = (bf16[2,384,768]{2,1,0:T(8,128)(2,1)}, bf16[2,384,768]{2,1,0:T(8,128)(2,1)}, u32[]{:S(2)}, u32[]{:S(2)}) collective-permute-start(bf16[2,384,768]{2,1,0:T(8,128)(2,1)} %get-tuple-element.586), channel_id=1, source_target_pairs={{0,1},{1,0},{2,3},{3,2},{4,5},{5,4},{6,7},{7,6},{8,9},{9,8},{10,11... | collective-permute-start | bytes 3538952 | tf_op jit(solution)/shard_map/ppermute | solution.py:1027
  226.9 28.7 %collective-permute-start.51 = (bf16[2,384,768]{2,1,0:T(8,128)(2,1)}, bf16[2,384,768]{2,1,0:T(8,128)(2,1)}, u32[]{:S(2)}, u32[]{:S(2)}) collective-permute-start(bf16[2,384,768]{2,1,0:T(8,128)(2,1)} %get-tuple-element.621), channel_id=1, source_target_pairs={{0,1},{1,0},{2,3},{3,2},{4,5},{5,4},{6,7},{7,6},{8,9},{9,8},{10,11... | collective-permute-start | bytes 3538952 | tf_op jit(solution)/shard_map/ppermute | solution.py:1027
  265.4 38.0 %collective-permute-start.57 = (bf16[2,384,768]{2,1,0:T(8,128)(2,1)S(1)}, bf16[2,384,768]{2,1,0:T(8,128)(2,1)S(1)}, u32[]{:S(2)}, u32[]{:S(2)}) collective-permute-start(bf16[2,384,768]{2,1,0:T(8,128)(2,1)S(1)} %get-tuple-element.681), channel_id=1, source_target_pairs={{0,4},{2,6},{4,0},{6,2},{8,12},{10,14},{12,8},{14,10},{16,20},{18,... | collective-permute-start | bytes 3538952 | tf_op jit(solution)/shard_map/ppermute | solution.py:1027
  266.8 20.4 %collective-permute-start.52 = (bf16[2,192,768]{2,1,0:T(8,128)(2,1)S(1)}, bf16[2,192,768]{2,1,0:T(8,128)(2,1)S(1)}, u32[]{:S(2)}, u32[]{:S(2)}) collective-permute-start(bf16[2,192,768]{2,1,0:T(8,128)(2,1)S(1)} %copy-done.56), channel_id=1, source_target_pairs={{0,1},{1,0},{2,3},{3,2},{4,5},{5,4},{6,7},{7,6},{8,9},{9,8},{10,11... | collective-permute-start | bytes 1769480 | tf_op jit(solution)/shard_map/ppermute | solution.py:1027
  304.7 18.3 %collective-permute-start.59 = (bf16[1,384,768]{2,1,0:T(8,128)(2,1)S(1)}, bf16[1,384,768]{2,1,0:T(8,128)(2,1)S(1)}, u32[]{:S(2)}, u32[]{:S(2)}) collective-permute-start(bf16[1,384,768]{2,1,0:T(8,128)(2,1)S(1)} %get-tuple-element.710), channel_id=1, source_target_pairs={{0,1},{1,0},{2,3},{3,2},{4,5},{5,4},{6,7},{7,6},{8,9},{9,8},{10,11... | collective-permute-start | bytes 1769480 | tf_op jit(solution)/shard_map/ppermute | solution.py:1027
  304.7 18.3 %collective-permute-start.60 = (bf16[1,192,768]{2,1,0:T(8,128)(2,1)S(1)}, bf16[1,192,768]{2,1,0:T(8,128)(2,1)S(1)}, u32[]{:S(2)}, u32[]{:S(2)}) collective-permute-start(bf16[1,192,768]{2,1,0:T(8,128)(2,1)S(1)} %get-tuple-element.694), channel_id=1, source_target_pairs={{0,4},{2,6},{4,0},{6,2},{8,12},{10,14},{12,8},{14,10},{16,20},{18,... | collective-permute-start | bytes 884744 | tf_op jit(solution)/shard_map/ppermute | solution.py:1027
  308.7 35.3 %collective-permute-start.58 = (bf16[2,384,768]{2,1,0:T(8,128)(2,1)}, bf16[2,384,768]{2,1,0:T(8,128)(2,1)}, u32[]{:S(2)}, u32[]{:S(2)}) collective-permute-start(bf16[2,384,768]{2,1,0:T(8,128)(2,1)} %get-tuple-element.719), channel_id=1, source_target_pairs={{0,1},{1,0},{2,3},{3,2},{4,5},{5,4},{6,7},{7,6},{8,9},{9,8},{10,11... | collective-permute-start | bytes 3538952 | tf_op jit(solution)/shard_map/ppermute | solution.py:1027
  335.0 21.3 %collective-permute-start.69 = (bf16[1,384,768]{2,1,0:T(8,128)(2,1)}, bf16[1,384,768]{2,1,0:T(8,128)(2,1)}, u32[]{:S(2)}, u32[]{:S(2)}) collective-permute-start(bf16[1,384,768]{2,1,0:T(8,128)(2,1)} %get-tuple-element.749), channel_id=1, source_target_pairs={{0,1},{1,0},{2,3},{3,2},{4,5},{5,4},{6,7},{7,6},{8,9},{9,8},{10,11... | collective-permute-start | bytes 1769480 | tf_op jit(solution)/shard_map/ppermute | solution.py:1027
  339.8 29.0 %collective-permute-start.66 = (bf16[1,384,768]{2,1,0:T(8,128)(2,1)S(1)}, bf16[1,384,768]{2,1,0:T(8,128)(2,1)S(1)}, u32[]{:S(2)}, u32[]{:S(2)}) collective-permute-start(bf16[1,384,768]{2,1,0:T(8,128)(2,1)S(1)} %get-tuple-element.754), channel_id=1, source_target_pairs={{0,1},{1,0},{2,3},{3,2},{4,5},{5,4},{6,7},{7,6},{8,9},{9,8},{10,11... | collective-permute-start | bytes 1769480 | tf_op jit(solution)/shard_map/ppermute | solution.py:1027
  341.5 16.0 %collective-permute-start.68 = (bf16[1,288,768]{2,1,0:T(8,128)(2,1)S(1)}, bf16[1,288,768]{2,1,0:T(8,128)(2,1)S(1)}, u32[]{:S(2)}, u32[]{:S(2)}) collective-permute-start(bf16[1,288,768]{2,1,0:T(8,128)(2,1)S(1)} %get-tuple-element.759), channel_id=1, source_target_pairs={{0,8},{2,10},{4,12},{6,14},{8,0},{10,2},{12,4},{14,6},{16,24},{18,... | collective-permute-start | bytes 1327112 | tf_op jit(solution)/shard_map/ppermute | solution.py:1027
  345.4 17.3 %collective-permute-start.67 = (bf16[1,384,768]{2,1,0:T(8,128)(2,1)S(1)}, bf16[1,384,768]{2,1,0:T(8,128)(2,1)S(1)}, u32[]{:S(2)}, u32[]{:S(2)}) collective-permute-start(bf16[1,384,768]{2,1,0:T(8,128)(2,1)S(1)} %get-tuple-element.762), channel_id=1, source_target_pairs={{0,4},{2,6},{4,0},{6,2},{8,12},{10,14},{12,8},{14,10},{16,20},{18,... | collective-permute-start | bytes 1769480 | tf_op jit(solution)/shard_map/ppermute | solution.py:1027
  357.6 21.3 %collective-permute-start.74 = (bf16[288,768]{1,0:T(8,128)(2,1)S(1)}, bf16[288,768]{1,0:T(8,128)(2,1)S(1)}, u32[]{:S(2)}, u32[]{:S(2)}) collective-permute-start(bf16[288,768]{1,0:T(8,128)(2,1)S(1)} %add_convert_fusion.1), channel_id=1, source_target_pairs={{0,16},{2,18},{4,20},{6,22},{8,24},{10,26},{12,28},{14,30},{16,0},... | collective-permute-start | bytes 1327112 | tf_op jit(solution)/shard_map/ppermute | solution.py:1027
  362.9 16.2 %collective-permute-start.73 = (bf16[1,192,768]{2,1,0:T(8,128)(2,1)S(1)}, bf16[1,192,768]{2,1,0:T(8,128)(2,1)S(1)}, u32[]{:S(2)}, u32[]{:S(2)}) collective-permute-start(bf16[1,192,768]{2,1,0:T(8,128)(2,1)S(1)} %get-tuple-element.784), channel_id=1, source_target_pairs={{0,8},{2,10},{4,12},{6,14},{8,0},{10,2},{12,4},{14,6},{16,24},{18,... | collective-permute-start | bytes 884744 | tf_op jit(solution)/shard_map/ppermute | solution.py:1027
  389.5 48.5 %collective-permute-start.82 = (bf16[576,768]{1,0:T(8,128)(2,1)S(1)}, bf16[576,768]{1,0:T(8,128)(2,1)S(1)}, u32[]{:S(2)}, u32[]{:S(2)}) collective-permute-start(bf16[576,768]{1,0:T(8,128)(2,1)S(1)} %bitcast.137), channel_id=1, source_target_pairs={{0,8},{2,10},{4,12},{6,14},{8,0},{10,2},{12,4},{14,6},{16,24},{18,... | collective-permute-start | bytes 2654216 | tf_op jit(solution)/shard_map/ppermute | solution.py:1027
  404.2 31.7 %collective-permute-start.77 = (bf16[288,768]{1,0:T(8,128)(2,1)S(1)}, bf16[288,768]{1,0:T(8,128)(2,1)S(1)}, u32[]{:S(2)}, u32[]{:S(2)}) collective-permute-start(bf16[288,768]{1,0:T(8,128)(2,1)S(1)} %add_convert_fusion.own_ref), channel_id=1, source_target_pairs={{0,8},{2,10},{4,12},{6,14},{8,0},{10,2},{12,4},{14,6},{16,24},{18,... | collective-permute-start | bytes 1327112 | tf_op jit(solution)/shard_map/ppermute | solution.py:1027
  404.9 30.9 %collective-permute-start.78 = (bf16[1,96,768]{2,1,0:T(8,128)(2,1)S(1)}, bf16[1,96,768]{2,1,0:T(8,128)(2,1)S(1)}, u32[]{:S(2)}, u32[]{:S(2)}) collective-permute-start(bf16[1,96,768]{2,1,0:T(8,128)(2,1)S(1)} %get-tuple-element.795), channel_id=1, source_target_pairs={{0,8},{2,10},{4,12},{6,14},{8,0},{10,2},{12,4},{14,6},{16,24},{18,... | collective-permute-start | bytes 442376 | tf_op jit(solution)/shard_map/ppermute | solution.py:1027
  411.5 26.4 %collective-permute-start.76 = (f32[32,768]{1,0:T(8,128)S(1)}, f32[32,768]{1,0:T(8,128)S(1)}, u32[]{:S(2)}, u32[]{:S(2)}) collective-permute-start(f32[32,768]{1,0:T(8,128)S(1)} %add.94), channel_id=1, source_target_pairs={{0,8},{2,10},{4,12},{6,14},{8,0},{10,2},{12,4},{14,6},{16,24},{18,... | collective-permute-start | bytes 294920 | tf_op jit(solution)/shard_map/ppermute | solution.py:1027
  438.1 57.8 %collective-permute-start.90 = (bf16[1152,768]{1,0:T(8,128)(2,1)S(1)}, bf16[1152,768]{1,0:T(8,128)(2,1)S(1)}, u32[]{:S(2)}, u32[]{:S(2)}) collective-permute-start(bf16[1152,768]{1,0:T(8,128)(2,1)S(1)} %bitcast.121), channel_id=1, source_target_pairs={{0,4},{2,6},{4,0},{6,2},{8,12},{10,14},{12,8},{14,10},{16,20},{18,... | collective-permute-start | bytes 5308424 | tf_op jit(solution)/shard_map/ppermute | solution.py:1027
  438.2 57.4 %collective-permute-start.86 = (bf16[576,768]{1,0:T(8,128)(2,1)S(1)}, bf16[576,768]{1,0:T(8,128)(2,1)S(1)}, u32[]{:S(2)}, u32[]{:S(2)}) collective-permute-start(bf16[576,768]{1,0:T(8,128)(2,1)S(1)} %bitcast.135), channel_id=1, source_target_pairs={{0,4},{2,6},{4,0},{6,2},{8,12},{10,14},{12,8},{14,10},{16,20},{18,... | collective-permute-start | bytes 2654216 | tf_op jit(solution)/shard_map/ppermute | solution.py:1027
  440.8 20.1 %collective-permute-start.80 = (bf16[192,768]{1,0:T(8,128)(2,1)S(1)}, bf16[192,768]{1,0:T(8,128)(2,1)S(1)}, u32[]{:S(2)}, u32[]{:S(2)}) collective-permute-start(bf16[192,768]{1,0:T(8,128)(2,1)S(1)} %add_convert_fusion.3), channel_id=1, source_target_pairs={{0,16},{2,18},{4,20},{6,22},{8,24},{10,26},{12,28},{14,30},{16,0},... | collective-permute-start | bytes 884744 | tf_op jit(solution)/shard_map/ppermute | solution.py:1027
  442.4 53.3 %collective-permute-start.85 = (bf16[96,768]{1,0:T(8,128)(2,1)S(1)}, bf16[96,768]{1,0:T(8,128)(2,1)S(1)}, u32[]{:S(2)}, u32[]{:S(2)}) collective-permute-start(bf16[96,768]{1,0:T(8,128)(2,1)S(1)} %add_convert_fusion.7), channel_id=1, source_target_pairs={{0,16},{2,18},{4,20},{6,22},{8,24},{10,26},{12,28},{14,30},{16,0},... | collective-permute-start | bytes 442376 | tf_op jit(solution)/shard_map/ppermute | solution.py:1027
  443.9 25.4 %collective-permute-start.79 = (f32[32,768]{1,0:T(8,128)S(1)}, f32[32,768]{1,0:T(8,128)S(1)}, u32[]{:S(2)}, u32[]{:S(2)}) collective-permute-start(f32[32,768]{1,0:T(8,128)S(1)} %add.96), channel_id=1, source_target_pairs={{0,16},{2,18},{4,20},{6,22},{8,24},{10,26},{12,28},{14,30},{16,0},... | collective-permute-start | bytes 294920 | tf_op jit(solution)/shard_map/ppermute | solution.py:1027
  460.8 34.9 %collective-permute-start.84 = (bf16[96,768]{1,0:T(8,128)(2,1)S(1)}, bf16[96,768]{1,0:T(8,128)(2,1)S(1)}, u32[]{:S(2)}, u32[]{:S(2)}) collective-permute-start(bf16[96,768]{1,0:T(8,128)(2,1)S(1)} %add_convert_fusion.6), channel_id=1, source_target_pairs={{0,16},{2,18},{4,20},{6,22},{8,24},{10,26},{12,28},{14,30},{16,0},... | collective-permute-start | bytes 442376 | tf_op jit(solution)/shard_map/ppermute | solution.py:1027
  469.3 26.5 %collective-permute-start.91 = (bf16[192,768]{1,0:T(8,128)(2,1)S(1)}, bf16[192,768]{1,0:T(8,128)(2,1)S(1)}, u32[]{:S(2)}, u32[]{:S(2)}) collective-permute-start(bf16[192,768]{1,0:T(8,128)(2,1)S(1)} %add_convert_fusion.2.own_ref), channel_id=1, source_target_pairs={{0,8},{2,10},{4,12},{6,14},{8,0},{10,2},{12,4},{14,6},{16,24},{18,... | collective-permute-start | bytes 884744 | tf_op jit(solution)/shard_map/ppermute | solution.py:1027
  496.1 22.2 %collective-permute-start.94 = (bf16[2304,768]{1,0:T(8,128)(2,1)S(1)}, bf16[2304,768]{1,0:T(8,128)(2,1)S(1)}, u32[]{:S(2)}, u32[]{:S(2)}) collective-permute-start(bf16[2304,768]{1,0:T(8,128)(2,1)S(1)} %bitcast.105), channel_id=1, source_target_pairs={{0,2},{2,0},{4,6},{6,4},{8,10},{10,8},{12,14},{14,12},{16,18},{18,... | collective-permute-start | bytes 10616840 | tf_op jit(solution)/shard_map/ppermute | solution.py:1027
  498.8 16.6 %collective-permute-start.95 = (bf16[384,768]{1,0:T(8,128)(2,1)S(1)}, bf16[384,768]{1,0:T(8,128)(2,1)S(1)}, u32[]{:S(2)}, u32[]{:S(2)}) collective-permute-start(bf16[384,768]{1,0:T(8,128)(2,1)S(1)} %bitcast.140), channel_id=1, source_target_pairs={{0,4},{2,6},{4,0},{6,2},{8,12},{10,14},{12,8},{14,10},{16,20},{18,... | collective-permute-start | bytes 1769480 | tf_op jit(solution)/shard_map/ppermute | solution.py:1027
  498.8 13.6 %collective-permute-start.88 = (bf16[96,768]{1,0:T(8,128)(2,1)S(1)}, bf16[96,768]{1,0:T(8,128)(2,1)S(1)}, u32[]{:S(2)}, u32[]{:S(2)}) collective-permute-start(bf16[96,768]{1,0:T(8,128)(2,1)S(1)} %add_convert_fusion.5.own_ref), channel_id=1, source_target_pairs={{0,8},{2,10},{4,12},{6,14},{8,0},{10,2},{12,4},{14,6},{16,24},{18,... | collective-permute-start | bytes 442376 | tf_op jit(solution)/shard_map/ppermute | solution.py:1027
  500.0 15.4 %collective-permute-start.83 = (f32[32,768]{1,0:T(8,128)S(1)}, f32[32,768]{1,0:T(8,128)S(1)}, u32[]{:S(2)}, u32[]{:S(2)}) collective-permute-start(f32[32,768]{1,0:T(8,128)S(1)} %add.99), channel_id=1, source_target_pairs={{0,4},{2,6},{4,0},{6,2},{8,12},{10,14},{12,8},{14,10},{16,20},{18,... | collective-permute-start | bytes 294920 | tf_op jit(solution)/shard_map/ppermute | solution.py:1027
  515.5 17.2 %collective-permute-start.98 = (bf16[768,768]{1,0:T(8,128)(2,1)S(1)}, bf16[768,768]{1,0:T(8,128)(2,1)S(1)}, u32[]{:S(2)}, u32[]{:S(2)}) collective-permute-start(bf16[768,768]{1,0:T(8,128)(2,1)S(1)} %bitcast.125), channel_id=1, source_target_pairs={{0,2},{2,0},{4,6},{6,4},{8,10},{10,8},{12,14},{14,12},{16,18},{18,... | collective-permute-start | bytes 3538952 | tf_op jit(solution)/shard_map/ppermute | solution.py:1027
  516.9 11.2 %collective-permute-start.93 = (bf16[192,768]{1,0:T(8,128)(2,1)S(1)}, bf16[192,768]{1,0:T(8,128)(2,1)S(1)}, u32[]{:S(2)}, u32[]{:S(2)}) collective-permute-start(bf16[192,768]{1,0:T(8,128)(2,1)S(1)} %bitcast.161), channel_id=1, source_target_pairs={{0,4},{2,6},{4,0},{6,2},{8,12},{10,14},{12,8},{14,10},{16,20},{18,... | collective-permute-start | bytes 884744 | tf_op jit(solution)/shard_map/ppermute | solution.py:1027
  516.9 14.9 %collective-permute-start.92 = (bf16[192,768]{1,0:T(8,128)(2,1)S(1)}, bf16[192,768]{1,0:T(8,128)(2,1)S(1)}, u32[]{:S(2)}, u32[]{:S(2)}) collective-permute-start(bf16[192,768]{1,0:T(8,128)(2,1)S(1)} %bitcast.159), channel_id=1, source_target_pairs={{0,4},{2,6},{4,0},{6,2},{8,12},{10,14},{12,8},{14,10},{16,20},{18,... | collective-permute-start | bytes 884744 | tf_op jit(solution)/shard_map/ppermute | solution.py:1027
  (155 other events, 987.4 us)
Sparse Core Ops, SparseCore 0:
  258.3 89.5 reduce-scatter.1

commit v5 on v2

--- a/solution.py
+++ b/solution.py
@@ -1351,46 +1351,46 @@
     third.step()
     first.step()
     second.step()
-    order.hold(part)
-    gathered = lax.all_gather(after(part, *order.last), "wide", axis_index_groups=groups, tiled=True)
-    fourth = Reduce(order, [two], late=(2,))
+    fourth = Reduce(order, [two])
     fourth.step()
     minor_step()
     third.step()
     first.step()
     second.step()
+    order.hold(part)
+    gathered = lax.all_gather(after(part, *order.last), "wide", axis_index_groups=groups, tiled=True)
+    fourth.step()
+    third.step()
+    first.step()
     minor_step()
     fourth.step()
+    second.step()
+    third.step()
     minor_step()
-    third.step()
     first.step()
     fourth.step()
     second.step()
     minor_step()
-    first.step()
-    third.step()
-    fourth.step()
-    order.hold(gathered)
-    other = swap(after(gathered, *order.last), "wide", 1)
     first.finish(done)
-    second.step()
     third.step()
     fourth.step()
     minor_step()
+    second.step()
+    order.hold(gathered)
+    other = swap(after(gathered, *order.last), "wide", 1)
+    third.step()
+    fourth.step()
+    second.finish(done)
     own, got = gathered.reshape(1, -1, width), other.reshape(1, -1, width)
     for which, term in enumerate((term_down1, term_up1, term_qkv1)):
         term.finish(done, own, got, which * (own.shape[1] // 3), own.shape[1] // 3)
-    fourth.step()
-    second.step()
-    third.step()
     for each in (first, second, third, fourth):
         while not each.closed:
             each.step()
     while minor_stages:
         minor_step()
+    third.finish(done)
     fourth.finish(done)
-    second.finish(done)
-    third.finish(done)
     small = order.run(lambda x: small_gradients(x, place, width, shares, up1.blocks), minor)
 
     return (

time: 546 us -> 542 us (level)
  waiting for transfers between devices: 137 us -> 129 us
  starting transfers between devices: 87.1 us -> 93.4 us
    ppermute x96, waiting for transfers between devices: 137 us -> 129 us  [swap(): lax.ppermute(values, axis, [(source, source ^ mask) for source in range(s...]
    ppermute x96, starting transfers between devices: 87 us -> 93.4 us  [swap(): lax.ppermute(values, axis, [(source, source ^ mask) for source in range(s...]
    unnamed x226 -> x212, local copies, waits for them, and re-layouts: 39.4 us -> 38.3 us
  transfers between devices with their start and end apart: 98 -> 98, of which waited for: 29 -> 31; matrix products, arithmetic and copies ran while one was open for 3% -> 3% of each run, Pallas kernels for 38% -> 39%
where the time goes in v5:
time: 542 us; the launch traced here: 532 us
  Pallas kernels  238 us (44%)
  waiting for transfers between devices  129 us (24%)
  starting transfers between devices  93.4 us (17%)
  local copies, waits for them, and re-layouts  51.6 us (10%)
  between operations  15.8 us (3%)
    pallas_call x13, Pallas kernels, call(): pl.pallas_call(body, grid=grid, in_specs=[spec for _, spec in ins], out_s...  158 us
    ppermute x96, waiting for transfers between devices, swap(): lax.ppermute(values, axis, [(source, source ^ mask) for source in range(s...  129 us
    ppermute x96, starting transfers between devices, swap(): lax.ppermute(values, axis, [(source, source ^ mask) for source in range(s...  93.4 us
    pallas_call x49, Pallas kernels, picked(): pl.pallas_call(body, grid_spec=pltpu.PrefetchScalarGridSpec(num_scalar_pr...  71.5 us
    unnamed x212, local copies, waits for them, and re-layouts  38.3 us
  transfers between devices with their start and end apart: 98, of which 31 were waited for; matrix products, arithmetic and copies ran while one was open for 3% of the time, Pallas kernels for 39%

profile of v5, /device:TPU:1, one launch (start us, length us, event | category | flops | bytes accessed | tf_op | source)
XLA Modules:
  0.0 532.5 jit_solution(12388189362018923362)
XLA Ops:
  34.9 5.9 %collective-permute-done.1.refs_3_ = bf16[1,96,2304]{2,1,0:T(8,128)(2,1)} collective-permute-done((bf16[1,96,2304]{2,1,0:T(8,128)(2,1)}, bf16[1,96,2304]{2,1,0:T(8,128)(2,1)}, u32[]{:S(2)}, u32[]{:S(2)}) %collective-permute-start.1) | collective-permute-done | bytes 442400 | tf_op jit(solution)/shard_map/ppermute | solution.py:1021
  40.8 3.0 collective-permute-start.3
  48.1 5.1 project_qkv.1
  54.7 8.7 %attend.2 = (bf16[2,336,768]{2,1,0:T(8,128)(2,1)S(1)}, f32[2,6,8,336]{3,2,1,0:T(8,128)S(1)}) custom-call(s32[2]{0:T(128)S(1)} %multiply_add_fusion.length_ref.refs_23_, bf16[3,2,336,768]{3,2,1,0:T(8,128)(2,1)S(1)} %bitcast.170, bf16[3,2,336,768]{3,2,1,0:T(8,128)(2,1)S(1)} %bitcast.171, bf16[3,2,336,768]{3,2,1,0:T(8,128)(2,1)S(1)} %bitcast.172), custom_call_target="tpu_custom_call" | custom-call | flops 3000000000 | tf_op jit(solution)/shard_map/attend/pallas_call | solution.py:69
  75.0 20.6 %feed_forward.2 = (f32[672,768]{1,0:T(8,128)S(1)}, bf16[672,768]{1,0:T(8,128)(2,1)S(1)}, bf16[672,3072]{1,0:T(8,128)(2,1)S(1)}, bf16[672,3072]{1,0:T(8,128)(2,1)}, bf16[672,768]{1,0:T(8,128)(2,1)S(1)}) custom-call(s32[2]{0:T(128)S(1)} %pad_add_fusion.refs_0_, bf16[2,384,768]{2,1,0:T(8,128)(2,1)} %refs_11_.7, bf16[1,96,3840]{2,1,0:T(8,128)(2,1)} %copy-done.74, ...), custom_call_target="tpu_custom_call" | custom-call | flops 6899999744 | tf_op jit(solution)/shard_map/feed_forward/pallas_call | solution.py:69
  104.1 8.2 %join_qkv.1 = (f32[672,768]{1,0:T(8,128)S(1)}, bf16[672,768]{1,0:T(8,128)(2,1)S(1)}, bf16[3,672,768]{2,1,0:T(8,128)(2,1)S(1)}) custom-call(s32[2]{0:T(128)S(1)} %pad_add_fusion.refs_0_, bf16[768,768]{1,0:T(8,128)(2,1)} %refs_6_.10, bf16[1,192,768]{2,1,0:T(8,128)(2,1)} %copy-done.98, bf16[1,192,768]{2,1,0:T(8,128)(2,1)} %copy-done.99, ...), custom_call_target="tpu_custom_call" | custom-call | flops 3300000000 | tf_op jit(solution)/shard_map/join_qkv/pallas_call | solution.py:69
  112.4 8.7 %attend.3 = (bf16[2,336,768]{2,1,0:T(8,128)(2,1)S(1)}, f32[2,6,8,336]{3,2,1,0:T(8,128)S(1)}) custom-call(s32[2]{0:T(128)S(1)} %multiply_add_fusion.length_ref.refs_23_, bf16[3,2,336,768]{3,2,1,0:T(8,128)(2,1)S(1)} %bitcast.176, bf16[3,2,336,768]{3,2,1,0:T(8,128)(2,1)S(1)} %bitcast.177, bf16[3,2,336,768]{3,2,1,0:T(8,128)(2,1)S(1)} %bitcast.178), custom_call_target="tpu_custom_call" | custom-call | flops 3000000000 | tf_op jit(solution)/shard_map/attend/pallas_call | solution.py:69
  122.5 3.1 collective-permute-done.27.refs_14_.refs_4_
  128.4 21.0 %feed_forward.3 = (f32[672,768]{1,0:T(8,128)S(1)}, bf16[672,768]{1,0:T(8,128)(2,1)S(1)}, bf16[672,3072]{1,0:T(8,128)(2,1)S(1)}, bf16[672,3072]{1,0:T(8,128)(2,1)}, bf16[672,768]{1,0:T(8,128)(2,1)}) custom-call(s32[2]{0:T(128)S(1)} %pad_add_fusion.refs_0_, bf16[2,384,768]{2,1,0:T(8,128)(2,1)} %refs_11_.7, bf16[1,96,3840]{2,1,0:T(8,128)(2,1)} %copy-done.78, ...), custom_call_target="tpu_custom_call" | custom-call | flops 6899999744 | tf_op jit(solution)/shard_map/feed_forward/pallas_call | solution.py:69
  150.7 4.1 down_term.4
  158.0 3.1 down_term.5
  165.0 18.3 %feed_forward_back.2 = (bf16[672,3072]{1,0:T(8,128)(2,1)}, f32[672,768]{1,0:T(8,128)S(1)}, bf16[672,768]{1,0:T(8,128)(2,1)S(1)}, bf16[672,768]{1,0:T(8,128)(2,1)S(1)}, f32[8,768]{1,0:T(8,128)S(1)}) custom-call(s32[2]{0:T(128)S(1)} %pad_add_fusion.refs_0_, bf16[2,1536,768]{2,1,0:T(8,128)(2,1)} %refs_1_.15, bf16[1,384,768]{2,1,0:T(8,128)(2,1)} %copy-done.88, ...), custom_call_target="tpu_custom_call" | custom-call | flops 6300000256 | tf_op jit(solution)/shard_map/feed_forward_back/pallas_call | solution.py:69
  183.3 3.6 copy-done.5
  186.9 2.7 up_term.4
  190.9 2.7 up_term.5
  198.7 2.7 add_into.3.rest_0_
  202.7 13.9 %attend_back.2 = bf16[3,2,336,768]{3,2,1,0:T(8,128)(2,1)S(1)} custom-call(s32[2]{0:T(128)S(1)} %multiply_add_fusion.length_ref.refs_23_, bf16[3,2,336,768]{3,2,1,0:T(8,128)(2,1)S(1)} %bitcast.179, bf16[3,2,336,768]{3,2,1,0:T(8,128)(2,1)S(1)} %bitcast.180, bf16[3,2,336,768]{3,2,1,0:T(8,128)(2,1)S(1)} %bitcast.181, bf16[2,336,768]{2,1,0:T(8,128)(2,1)S(1)} %bitcast.157, ...), custom_call_target="tpu_custom_call" | custom-call | flops 4499999744 | tf_op jit(solution)/shard_map/attend_back/pallas_call | solution.py:69
  227.4 2.7 add_into.4.rest_0_
  231.7 11.9 %project_back.2 = (bf16[672,768]{1,0:T(8,128)(2,1)S(1)}, f32[672,768]{1,0:T(8,128)S(1)}, bf16[672,768]{1,0:T(8,128)(2,1)S(1)}, f32[672,768]{1,0:T(8,128)}, f32[8,768]{1,0:T(8,128)S(1)}) custom-call(s32[2]{0:T(128)S(1)} %pad_add_fusion.refs_0_, bf16[2,384,2304]{2,1,0:T(8,128)(2,1)} %refs_1_.16, bf16[1,96,2304]{2,1,0:T(8,128)(2,1)} %collective-permute-done.10.refs_7_.refs_2_, ...), custom_call_target="tpu_custom_call" | custom-call | flops 3900000000 | tf_op jit(solution)/shard_map/project_back/pallas_call | solution.py:69
  250.0 2.7 down_term.6
  252.8 2.7 down_term.7
  267.1 19.6 %feed_forward_back.3 = (bf16[672,3072]{1,0:T(8,128)(2,1)}, f32[672,768]{1,0:T(8,128)S(1)}, bf16[672,768]{1,0:T(8,128)(2,1)S(1)}, bf16[672,768]{1,0:T(8,128)(2,1)S(1)}, f32[8,768]{1,0:T(8,128)S(1)}) custom-call(s32[2]{0:T(128)S(1)} %pad_add_fusion.refs_0_, bf16[2,1536,768]{2,1,0:T(8,128)(2,1)} %refs_1_.15, bf16[1,384,768]{2,1,0:T(8,128)(2,1)} %copy-done.84, ...), custom_call_target="tpu_custom_call" | custom-call | flops 6300000256 | tf_op jit(solution)/shard_map/feed_forward_back/pallas_call | solution.py:69
  290.9 2.7 up_term.6
  295.2 2.7 up_term.7
  297.9 5.1 collective-permute-done.57
  308.9 13.9 %attend_back.3 = bf16[3,2,336,768]{3,2,1,0:T(8,128)(2,1)S(1)} custom-call(s32[2]{0:T(128)S(1)} %multiply_add_fusion.length_ref.refs_23_, bf16[3,2,336,768]{3,2,1,0:T(8,128)(2,1)S(1)} %bitcast.173, bf16[3,2,336,768]{3,2,1,0:T(8,128)(2,1)S(1)} %bitcast.174, bf16[3,2,336,768]{3,2,1,0:T(8,128)(2,1)S(1)} %bitcast.175, bf16[2,336,768]{2,1,0:T(8,128)(2,1)S(1)} %bitcast.156, ...), custom_call_target="tpu_custom_call" | custom-call | flops 4499999744 | tf_op jit(solution)/shard_map/attend_back/pallas_call | solution.py:69
  322.9 3.6 qkv_out_term.6
  341.2 2.7 collective-permute-start.68
  345.5 8.4 %project_back.3 = (f32[672,768]{1,0:T(8,128)}, f32[8,768]{1,0:T(8,128)S(1)}) custom-call(s32[2]{0:T(128)S(1)} %pad_add_fusion.refs_0_, bf16[2,384,2304]{2,1,0:T(8,128)(2,1)} %refs_1_.16, bf16[1,96,2304]{2,1,0:T(8,128)(2,1)} %collective-permute-done.refs_2_, bf16[1,96,2304]{2,1,0:T(8,128)(2,1)} %collective-permute-done.1.refs_3_, ...), custom_call_target="tpu_custom_call" | custom-call | flops 2700000000 | tf_op jit(solution)/shard_map/project_back/pallas_call | solution.py:69
  357.3 2.6 collective-permute-start.71
  364.5 3.9 collective-permute-done.66
  370.7 7.2 %collective-permute-done.71 = bf16[288,768]{1,0:T(8,128)(2,1)S(1)} collective-permute-done((bf16[288,768]{1,0:T(8,128)(2,1)S(1)}, bf16[288,768]{1,0:T(8,128)(2,1)S(1)}, u32[]{:S(2)}, u32[]{:S(2)}) %collective-permute-start.71) | collective-permute-done | bytes 442400 | tf_op jit(solution)/shard_map/ppermute | solution.py:1021
  378.1 4.0 collective-permute-start.75
  383.6 4.7 collective-permute-done.75
  388.4 12.8 %collective-permute-done.74 = bf16[1,96,768]{2,1,0:T(8,128)(2,1)S(1)} collective-permute-done((bf16[1,96,768]{2,1,0:T(8,128)(2,1)S(1)}, bf16[1,96,768]{2,1,0:T(8,128)(2,1)S(1)}, u32[]{:S(2)}, u32[]{:S(2)}) %collective-permute-start.74) | collective-permute-done | bytes 147488 | tf_op jit(solution)/shard_map/ppermute | solution.py:1021
  401.5 11.2 %collective-permute-start.70 = (f32[32,768]{1,0:T(8,128)S(1)}, f32[32,768]{1,0:T(8,128)S(1)}, u32[]{:S(2)}, u32[]{:S(2)}) collective-permute-start(f32[32,768]{1,0:T(8,128)S(1)} %add.90), channel_id=1, source_target_pairs={{0,2},{2,0},{4,6},{6,4},{8,10},{10,8},{12,14},{14,12},{16,18},{18,... | collective-permute-start | bytes 294920 | tf_op jit(solution)/shard_map/ppermute | solution.py:1021
  412.6 4.6 collective-permute-start.79
  417.4 29.8 %collective-permute-done.79 = bf16[192,768]{1,0:T(8,128)(2,1)S(1)} collective-permute-done((bf16[192,768]{1,0:T(8,128)(2,1)S(1)}, bf16[192,768]{1,0:T(8,128)(2,1)S(1)}, u32[]{:S(2)}, u32[]{:S(2)}) %collective-permute-start.79) | collective-permute-done | bytes 294944 | tf_op jit(solution)/shard_map/ppermute | solution.py:1021
  447.3 9.9 %collective-permute-done.78 = bf16[96,768]{1,0:T(8,128)(2,1)S(1)} collective-permute-done((bf16[96,768]{1,0:T(8,128)(2,1)S(1)}, bf16[96,768]{1,0:T(8,128)(2,1)S(1)}, u32[]{:S(2)}, u32[]{:S(2)}) %collective-permute-start.78) | collective-permute-done | bytes 147488 | tf_op jit(solution)/shard_map/ppermute | solution.py:1021
  458.1 3.0 collective-permute-start.82
  461.0 10.9 %collective-permute-done.83 = bf16[96,768]{1,0:T(8,128)(2,1)S(1)} collective-permute-done((bf16[96,768]{1,0:T(8,128)(2,1)S(1)}, bf16[96,768]{1,0:T(8,128)(2,1)S(1)}, u32[]{:S(2)}, u32[]{:S(2)}) %collective-permute-start.83) | collective-permute-done | bytes 147488 | tf_op jit(solution)/shard_map/ppermute | solution.py:1021
  484.9 2.6 collective-permute-done.86.got_ref
  487.5 3.7 collective-permute-done.85
  494.4 6.7 %collective-permute-done.90.got_ref = bf16[192,768]{1,0:T(8,128)(2,1)S(1)} collective-permute-done((bf16[192,768]{1,0:T(8,128)(2,1)S(1)}, bf16[192,768]{1,0:T(8,128)(2,1)S(1)}, u32[]{:S(2)}, u32[]{:S(2)}) %collective-permute-start.90) | collective-permute-done | bytes 294944 | tf_op jit(solution)/shard_map/ppermute | solution.py:1021
  503.3 4.1 collective-permute-done.89.got_ref
  508.8 2.6 finish_columns.2.rest_0_
  514.8 2.6 finish_columns.3
  517.4 3.3 finish_qkv_out.2
  (462 shorter events, 172.3 us)
Async XLA Ops:
  7.2 370.9 %reduce-scatter.2.cloned.1.call-start = ((), (), s32[]{:S(2)}) async-start(), calls=%async_computation.1 | async-start | bytes 3981312 | tf_op jit(solution)/shard_map/reduce_scatter | solution.py:1307
  8.3 22.6 %collective-permute-start = (bf16[1,96,2304]{2,1,0:T(8,128)(2,1)S(1)}, bf16[1,96,2304]{2,1,0:T(8,128)(2,1)}, u32[]{:S(2)}, u32[]{:S(2)}) collective-permute-start(bf16[1,96,2304]{2,1,0:T(8,128)(2,1)S(1)} %constant_dynamic-slice_fusion.3), channel_id=1, source_target_pairs={{0,1},{1,0},{2,3},{3,2},{4,5},{5,4},{6,7},{7,6},{8,9},{9,8},{10,11... | collective-permute-start | bytes 1327112 | tf_op jit(solution)/shard_map/ppermute | solution.py:1021
  14.5 17.9 %collective-permute-start.4 = (bf16[1,32,384]{2,1,0:T(8,128)(2,1)S(1)}, bf16[1,32,384]{2,1,0:T(8,128)(2,1)S(1)}, u32[]{:S(2)}, u32[]{:S(2)}) collective-permute-start(bf16[1,32,384]{2,1,0:T(8,128)(2,1)S(1)} %convert_bitcast_fusion), channel_id=1, source_target_pairs={{0,1},{1,0},{2,3},{3,2},{4,5},{5,4},{6,7},{7,6},{8,9},{9,8},{10,11... | collective-permute-start | bytes 73736 | tf_op jit(solution)/shard_map/ppermute | solution.py:1021
  17.6 27.6 %collective-permute-start.5 = (bf16[1,96,3840]{2,1,0:T(8,128)(2,1)}, bf16[1,96,3840]{2,1,0:T(8,128)(2,1)S(1)}, u32[]{:S(2)}, u32[]{:S(2)}) collective-permute-start(bf16[1,96,3840]{2,1,0:T(8,128)(2,1)} %maximum_bitcast_fusion), channel_id=1, source_target_pairs={{0,1},{1,0},{2,3},{3,2},{4,5},{5,4},{6,7},{7,6},{8,9},{9,8},{10,11... | collective-permute-start | bytes 2211848 | tf_op jit(solution)/shard_map/ppermute | solution.py:1021
  20.9 32.4 %collective-permute-start.8 = (bf16[1,384,768]{2,1,0:T(8,128)(2,1)}, bf16[1,384,768]{2,1,0:T(8,128)(2,1)S(1)}, u32[]{:S(2)}, u32[]{:S(2)}) collective-permute-start(bf16[1,384,768]{2,1,0:T(8,128)(2,1)} %constant_dynamic-slice_fusion.2), channel_id=1, source_target_pairs={{0,1},{1,0},{2,3},{3,2},{4,5},{5,4},{6,7},{7,6},{8,9},{9,8},{10,11... | collective-permute-start | bytes 1769480 | tf_op jit(solution)/shard_map/ppermute | solution.py:1021
  24.5 40.6 %collective-permute-start.10 = (bf16[1,96,2304]{2,1,0:T(8,128)(2,1)}, bf16[1,96,2304]{2,1,0:T(8,128)(2,1)}, u32[]{:S(2)}, u32[]{:S(2)}) collective-permute-start(bf16[1,96,2304]{2,1,0:T(8,128)(2,1)} %constant_dynamic-slice_fusion.1), channel_id=1, source_target_pairs={{0,1},{1,0},{2,3},{3,2},{4,5},{5,4},{6,7},{7,6},{8,9},{9,8},{10,11... | collective-permute-start | bytes 1327112 | tf_op jit(solution)/shard_map/ppermute | solution.py:1021
  32.5 14.1 %collective-permute-start.2 = (bf16[1,96,2304]{2,1,0:T(8,128)(2,1)}, bf16[1,96,2304]{2,1,0:T(8,128)(2,1)S(1)}, u32[]{:S(2)}, u32[]{:S(2)}) collective-permute-start(bf16[1,96,2304]{2,1,0:T(8,128)(2,1)} %collective-permute-done.refs_2_), channel_id=1, source_target_pairs={{0,2},{2,0},{4,6},{6,4},{8,10},{10,8},{12,14},{14,12},{16,18},{18,... | collective-permute-start | bytes 1327112 | tf_op jit(solution)/shard_map/ppermute | solution.py:1021
  45.2 21.1 %collective-permute-start.7 = (bf16[1,96,3840]{2,1,0:T(8,128)(2,1)S(1)}, bf16[1,96,3840]{2,1,0:T(8,128)(2,1)S(1)}, u32[]{:S(2)}, u32[]{:S(2)}) collective-permute-start(bf16[1,96,3840]{2,1,0:T(8,128)(2,1)S(1)} %collective-permute-done.5.refs_2_.refs_7_.refs_12_), channel_id=1, source_target_pairs={{0,4},{2,6},{4,0},{6,2},{8,12},{10,14},{12,8},{14,10},{16,20},{18,... | collective-permute-start | bytes 2211848 | tf_op jit(solution)/shard_map/ppermute | solution.py:1021
  46.6 18.5 %collective-permute-start.9 = (bf16[1,192,768]{2,1,0:T(8,128)(2,1)}, bf16[1,192,768]{2,1,0:T(8,128)(2,1)S(1)}, u32[]{:S(2)}, u32[]{:S(2)}) collective-permute-start(bf16[1,192,768]{2,1,0:T(8,128)(2,1)} %dynamic-slice_bitcast_fusion.2), channel_id=1, source_target_pairs={{0,1},{1,0},{2,3},{3,2},{4,5},{5,4},{6,7},{7,6},{8,9},{9,8},{10,11... | collective-permute-start | bytes 884744 | tf_op jit(solution)/shard_map/ppermute | solution.py:1021
  53.4 14.7 %collective-permute-start.13 = (bf16[1,384,768]{2,1,0:T(8,128)(2,1)S(1)}, bf16[1,384,768]{2,1,0:T(8,128)(2,1)S(1)}, u32[]{:S(2)}, u32[]{:S(2)}) collective-permute-start(bf16[1,384,768]{2,1,0:T(8,128)(2,1)S(1)} %collective-permute-done.8.refs_12_.refs_2_), channel_id=1, source_target_pairs={{0,8},{2,10},{4,12},{6,14},{8,0},{10,2},{12,4},{14,6},{16,24},{18,... | collective-permute-start | bytes 1769480 | tf_op jit(solution)/shard_map/ppermute | solution.py:1021
  69.2 31.6 %collective-permute-start.23 = (bf16[1,384,768]{2,1,0:T(8,128)(2,1)S(1)}, bf16[1,384,768]{2,1,0:T(8,128)(2,1)S(1)}, u32[]{:S(2)}, u32[]{:S(2)}) collective-permute-start(bf16[1,384,768]{2,1,0:T(8,128)(2,1)S(1)} %copy-done.92), channel_id=1, source_target_pairs={{0,1},{1,0},{2,3},{3,2},{4,5},{5,4},{6,7},{7,6},{8,9},{9,8},{10,11... | collective-permute-start | bytes 1769480 | tf_op jit(solution)/shard_map/ppermute | solution.py:1021
  70.1 29.9 %collective-permute-start.6 = (bf16[1,96,3840]{2,1,0:T(8,128)(2,1)S(1)}, bf16[1,96,3840]{2,1,0:T(8,128)(2,1)S(1)}, u32[]{:S(2)}, u32[]{:S(2)}) collective-permute-start(bf16[1,96,3840]{2,1,0:T(8,128)(2,1)S(1)} %copy-done.83), channel_id=1, source_target_pairs={{0,1},{1,0},{2,3},{3,2},{4,5},{5,4},{6,7},{7,6},{8,9},{9,8},{10,11... | collective-permute-start | bytes 2211848 | tf_op jit(solution)/shard_map/ppermute | solution.py:1021
  71.6 24.1 %collective-permute-start.20 = (bf16[1,96,2304]{2,1,0:T(8,128)(2,1)}, bf16[1,96,2304]{2,1,0:T(8,128)(2,1)S(1)}, u32[]{:S(2)}, u32[]{:S(2)}) collective-permute-start(bf16[1,96,2304]{2,1,0:T(8,128)(2,1)} %collective-permute-done.10.refs_7_.refs_2_), channel_id=1, source_target_pairs={{0,4},{2,6},{4,0},{6,2},{8,12},{10,14},{12,8},{14,10},{16,20},{18,... | collective-permute-start | bytes 1327112 | tf_op jit(solution)/shard_map/ppermute | solution.py:1021
  72.8 24.2 %collective-permute-start.17 = (bf16[1,192,768]{2,1,0:T(8,128)(2,1)S(1)}, bf16[1,192,768]{2,1,0:T(8,128)(2,1)S(1)}, u32[]{:S(2)}, u32[]{:S(2)}) collective-permute-start(bf16[1,192,768]{2,1,0:T(8,128)(2,1)S(1)} %collective-permute-done.9.refs_2_.refs_7_), channel_id=1, source_target_pairs={{0,8},{2,10},{4,12},{6,14},{8,0},{10,2},{12,4},{14,6},{16,24},{18,... | collective-permute-start | bytes 884744 | tf_op jit(solution)/shard_map/ppermute | solution.py:1021
  100.8 21.0 %collective-permute-start.16 = (bf16[1,96,3840]{2,1,0:T(8,128)(2,1)S(1)}, bf16[1,96,3840]{2,1,0:T(8,128)(2,1)S(1)}, u32[]{:S(2)}, u32[]{:S(2)}) collective-permute-start(bf16[1,96,3840]{2,1,0:T(8,128)(2,1)S(1)} %collective-permute-done.6.refs_2_.refs_7_.refs_12_), channel_id=1, source_target_pairs={{0,4},{2,6},{4,0},{6,2},{8,12},{10,14},{12,8},{14,10},{16,20},{18,... | collective-permute-start | bytes 2211848 | tf_op jit(solution)/shard_map/ppermute | solution.py:1021
  101.1 21.3 %collective-permute-start.26 = (bf16[1,384,768]{2,1,0:T(8,128)(2,1)S(1)}, bf16[1,384,768]{2,1,0:T(8,128)(2,1)S(1)}, u32[]{:S(2)}, u32[]{:S(2)}) collective-permute-start(bf16[1,384,768]{2,1,0:T(8,128)(2,1)S(1)} %collective-permute-done.23.refs_12_.refs_2_), channel_id=1, source_target_pairs={{0,8},{2,10},{4,12},{6,14},{8,0},{10,2},{12,4},{14,6},{16,24},{18,... | collective-permute-start | bytes 1769480 | tf_op jit(solution)/shard_map/ppermute | solution.py:1021
  164.2 33.5 %collective-permute-start.33 = (bf16[2,384,768]{2,1,0:T(8,128)(2,1)S(1)}, bf16[2,384,768]{2,1,0:T(8,128)(2,1)S(1)}, u32[]{:S(2)}, u32[]{:S(2)}) collective-permute-start(bf16[2,384,768]{2,1,0:T(8,128)(2,1)S(1)} %get-tuple-element.551), channel_id=1, source_target_pairs={{0,1},{1,0},{2,3},{3,2},{4,5},{5,4},{6,7},{7,6},{8,9},{9,8},{10,11... | collective-permute-start | bytes 3538952 | tf_op jit(solution)/shard_map/ppermute | solution.py:1021
  197.0 30.4 %collective-permute-start.38 = (bf16[2,384,768]{2,1,0:T(8,128)(2,1)}, bf16[2,384,768]{2,1,0:T(8,128)(2,1)}, u32[]{:S(2)}, u32[]{:S(2)}) collective-permute-start(bf16[2,384,768]{2,1,0:T(8,128)(2,1)} %get-tuple-element.582), channel_id=1, source_target_pairs={{0,1},{1,0},{2,3},{3,2},{4,5},{5,4},{6,7},{7,6},{8,9},{9,8},{10,11... | collective-permute-start | bytes 3538952 | tf_op jit(solution)/shard_map/ppermute | solution.py:1021
  226.5 29.0 %collective-permute-start.51 = (bf16[2,384,768]{2,1,0:T(8,128)(2,1)}, bf16[2,384,768]{2,1,0:T(8,128)(2,1)}, u32[]{:S(2)}, u32[]{:S(2)}) collective-permute-start(bf16[2,384,768]{2,1,0:T(8,128)(2,1)} %get-tuple-element.617), channel_id=1, source_target_pairs={{0,1},{1,0},{2,3},{3,2},{4,5},{5,4},{6,7},{7,6},{8,9},{9,8},{10,11... | collective-permute-start | bytes 3538952 | tf_op jit(solution)/shard_map/ppermute | solution.py:1021
  258.1 233.2 %all-gather.2.cloned.1.call-start = ((), (), s32[]{:S(2)}) async-start(), calls=%async_computation.2 | async-start | bytes 3981312 | tf_op jit(solution)/shard_map/all_gather | solution.py:1361
  265.2 37.8 %collective-permute-start.57 = (bf16[2,384,768]{2,1,0:T(8,128)(2,1)S(1)}, bf16[2,384,768]{2,1,0:T(8,128)(2,1)S(1)}, u32[]{:S(2)}, u32[]{:S(2)}) collective-permute-start(bf16[2,384,768]{2,1,0:T(8,128)(2,1)S(1)} %get-tuple-element.677), channel_id=1, source_target_pairs={{0,4},{2,6},{4,0},{6,2},{8,12},{10,14},{12,8},{14,10},{16,20},{18,... | collective-permute-start | bytes 3538952 | tf_op jit(solution)/shard_map/ppermute | solution.py:1021
  266.5 20.3 %collective-permute-start.52 = (bf16[2,192,768]{2,1,0:T(8,128)(2,1)S(1)}, bf16[2,192,768]{2,1,0:T(8,128)(2,1)S(1)}, u32[]{:S(2)}, u32[]{:S(2)}) collective-permute-start(bf16[2,192,768]{2,1,0:T(8,128)(2,1)S(1)} %copy-done.54), channel_id=1, source_target_pairs={{0,1},{1,0},{2,3},{3,2},{4,5},{5,4},{6,7},{7,6},{8,9},{9,8},{10,11... | collective-permute-start | bytes 1769480 | tf_op jit(solution)/shard_map/ppermute | solution.py:1021
  304.4 18.5 %collective-permute-start.59 = (bf16[1,384,768]{2,1,0:T(8,128)(2,1)S(1)}, bf16[1,384,768]{2,1,0:T(8,128)(2,1)S(1)}, u32[]{:S(2)}, u32[]{:S(2)}) collective-permute-start(bf16[1,384,768]{2,1,0:T(8,128)(2,1)S(1)} %get-tuple-element.706), channel_id=1, source_target_pairs={{0,1},{1,0},{2,3},{3,2},{4,5},{5,4},{6,7},{7,6},{8,9},{9,8},{10,11... | collective-permute-start | bytes 1769480 | tf_op jit(solution)/shard_map/ppermute | solution.py:1021
  304.5 18.4 %collective-permute-start.60 = (bf16[1,192,768]{2,1,0:T(8,128)(2,1)S(1)}, bf16[1,192,768]{2,1,0:T(8,128)(2,1)S(1)}, u32[]{:S(2)}, u32[]{:S(2)}) collective-permute-start(bf16[1,192,768]{2,1,0:T(8,128)(2,1)S(1)} %get-tuple-element.690), channel_id=1, source_target_pairs={{0,4},{2,6},{4,0},{6,2},{8,12},{10,14},{12,8},{14,10},{16,20},{18,... | collective-permute-start | bytes 884744 | tf_op jit(solution)/shard_map/ppermute | solution.py:1021
  308.5 35.4 %collective-permute-start.58 = (bf16[2,384,768]{2,1,0:T(8,128)(2,1)}, bf16[2,384,768]{2,1,0:T(8,128)(2,1)}, u32[]{:S(2)}, u32[]{:S(2)}) collective-permute-start(bf16[2,384,768]{2,1,0:T(8,128)(2,1)} %get-tuple-element.715), channel_id=1, source_target_pairs={{0,1},{1,0},{2,3},{3,2},{4,5},{5,4},{6,7},{7,6},{8,9},{9,8},{10,11... | collective-permute-start | bytes 3538952 | tf_op jit(solution)/shard_map/ppermute | solution.py:1021
  334.8 21.2 %collective-permute-start.69 = (bf16[1,384,768]{2,1,0:T(8,128)(2,1)}, bf16[1,384,768]{2,1,0:T(8,128)(2,1)}, u32[]{:S(2)}, u32[]{:S(2)}) collective-permute-start(bf16[1,384,768]{2,1,0:T(8,128)(2,1)} %get-tuple-element.745), channel_id=1, source_target_pairs={{0,1},{1,0},{2,3},{3,2},{4,5},{5,4},{6,7},{7,6},{8,9},{9,8},{10,11... | collective-permute-start | bytes 1769480 | tf_op jit(solution)/shard_map/ppermute | solution.py:1021
  339.7 28.7 %collective-permute-start.66 = (bf16[1,384,768]{2,1,0:T(8,128)(2,1)S(1)}, bf16[1,384,768]{2,1,0:T(8,128)(2,1)S(1)}, u32[]{:S(2)}, u32[]{:S(2)}) collective-permute-start(bf16[1,384,768]{2,1,0:T(8,128)(2,1)S(1)} %get-tuple-element.750), channel_id=1, source_target_pairs={{0,1},{1,0},{2,3},{3,2},{4,5},{5,4},{6,7},{7,6},{8,9},{9,8},{10,11... | collective-permute-start | bytes 1769480 | tf_op jit(solution)/shard_map/ppermute | solution.py:1021
  341.2 16.0 %collective-permute-start.68 = (bf16[1,288,768]{2,1,0:T(8,128)(2,1)S(1)}, bf16[1,288,768]{2,1,0:T(8,128)(2,1)S(1)}, u32[]{:S(2)}, u32[]{:S(2)}) collective-permute-start(bf16[1,288,768]{2,1,0:T(8,128)(2,1)S(1)} %get-tuple-element.755), channel_id=1, source_target_pairs={{0,8},{2,10},{4,12},{6,14},{8,0},{10,2},{12,4},{14,6},{16,24},{18,... | collective-permute-start | bytes 1327112 | tf_op jit(solution)/shard_map/ppermute | solution.py:1021
  345.3 17.0 %collective-permute-start.67 = (bf16[1,384,768]{2,1,0:T(8,128)(2,1)S(1)}, bf16[1,384,768]{2,1,0:T(8,128)(2,1)S(1)}, u32[]{:S(2)}, u32[]{:S(2)}) collective-permute-start(bf16[1,384,768]{2,1,0:T(8,128)(2,1)S(1)} %get-tuple-element.758), channel_id=1, source_target_pairs={{0,4},{2,6},{4,0},{6,2},{8,12},{10,14},{12,8},{14,10},{16,20},{18,... | collective-permute-start | bytes 1769480 | tf_op jit(solution)/shard_map/ppermute | solution.py:1021
  357.3 20.6 %collective-permute-start.71 = (bf16[288,768]{1,0:T(8,128)(2,1)S(1)}, bf16[288,768]{1,0:T(8,128)(2,1)S(1)}, u32[]{:S(2)}, u32[]{:S(2)}) collective-permute-start(bf16[288,768]{1,0:T(8,128)(2,1)S(1)} %add_convert_fusion.1), channel_id=1, source_target_pairs={{0,16},{2,18},{4,20},{6,22},{8,24},{10,26},{12,28},{14,30},{16,0},... | collective-permute-start | bytes 1327112 | tf_op jit(solution)/shard_map/ppermute | solution.py:1021
  362.6 15.4 %collective-permute-start.76 = (bf16[1,192,768]{2,1,0:T(8,128)(2,1)S(1)}, bf16[1,192,768]{2,1,0:T(8,128)(2,1)S(1)}, u32[]{:S(2)}, u32[]{:S(2)}) collective-permute-start(bf16[1,192,768]{2,1,0:T(8,128)(2,1)S(1)} %get-tuple-element.780), channel_id=1, source_target_pairs={{0,8},{2,10},{4,12},{6,14},{8,0},{10,2},{12,4},{14,6},{16,24},{18,... | collective-permute-start | bytes 884744 | tf_op jit(solution)/shard_map/ppermute | solution.py:1021
  382.1 19.1 %collective-permute-start.73 = (bf16[288,768]{1,0:T(8,128)(2,1)S(1)}, bf16[288,768]{1,0:T(8,128)(2,1)S(1)}, u32[]{:S(2)}, u32[]{:S(2)}) collective-permute-start(bf16[288,768]{1,0:T(8,128)(2,1)S(1)} %add_convert_fusion.own_ref), channel_id=1, source_target_pairs={{0,8},{2,10},{4,12},{6,14},{8,0},{10,2},{12,4},{14,6},{16,24},{18,... | collective-permute-start | bytes 1327112 | tf_op jit(solution)/shard_map/ppermute | solution.py:1021
  382.6 18.6 %collective-permute-start.74 = (bf16[1,96,768]{2,1,0:T(8,128)(2,1)S(1)}, bf16[1,96,768]{2,1,0:T(8,128)(2,1)S(1)}, u32[]{:S(2)}, u32[]{:S(2)}) collective-permute-start(bf16[1,96,768]{2,1,0:T(8,128)(2,1)S(1)} %get-tuple-element.789), channel_id=1, source_target_pairs={{0,8},{2,10},{4,12},{6,14},{8,0},{10,2},{12,4},{14,6},{16,24},{18,... | collective-permute-start | bytes 442376 | tf_op jit(solution)/shard_map/ppermute | solution.py:1021
  401.3 56.0 %collective-permute-start.84 = (bf16[576,768]{1,0:T(8,128)(2,1)S(1)}, bf16[576,768]{1,0:T(8,128)(2,1)S(1)}, u32[]{:S(2)}, u32[]{:S(2)}) collective-permute-start(bf16[576,768]{1,0:T(8,128)(2,1)S(1)} %bitcast.128), channel_id=1, source_target_pairs={{0,4},{2,6},{4,0},{6,2},{8,12},{10,14},{12,8},{14,10},{16,20},{18,... | collective-permute-start | bytes 2654216 | tf_op jit(solution)/shard_map/ppermute | solution.py:1021
  401.4 16.0 %collective-permute-start.80 = (bf16[1,96,768]{2,1,0:T(8,128)(2,1)S(1)}, bf16[1,96,768]{2,1,0:T(8,128)(2,1)S(1)}, u32[]{:S(2)}, u32[]{:S(2)}) collective-permute-start(bf16[1,96,768]{2,1,0:T(8,128)(2,1)S(1)} %get-tuple-element.799), channel_id=1, source_target_pairs={{0,8},{2,10},{4,12},{6,14},{8,0},{10,2},{12,4},{14,6},{16,24},{18,... | collective-permute-start | bytes 442376 | tf_op jit(solution)/shard_map/ppermute | solution.py:1021
  401.5 15.8 %collective-permute-start.70 = (f32[32,768]{1,0:T(8,128)S(1)}, f32[32,768]{1,0:T(8,128)S(1)}, u32[]{:S(2)}, u32[]{:S(2)}) collective-permute-start(f32[32,768]{1,0:T(8,128)S(1)} %add.90), channel_id=1, source_target_pairs={{0,2},{2,0},{4,6},{6,4},{8,10},{10,8},{12,14},{14,12},{16,18},{18,... | collective-permute-start | bytes 294920 | tf_op jit(solution)/shard_map/ppermute | solution.py:1021
  412.6 34.6 %collective-permute-start.79 = (bf16[192,768]{1,0:T(8,128)(2,1)S(1)}, bf16[192,768]{1,0:T(8,128)(2,1)S(1)}, u32[]{:S(2)}, u32[]{:S(2)}) collective-permute-start(bf16[192,768]{1,0:T(8,128)(2,1)S(1)} %add_convert_fusion.3), channel_id=1, source_target_pairs={{0,16},{2,18},{4,20},{6,22},{8,24},{10,26},{12,28},{14,30},{16,0},... | collective-permute-start | bytes 884744 | tf_op jit(solution)/shard_map/ppermute | solution.py:1021
  417.2 40.0 %collective-permute-start.78 = (bf16[96,768]{1,0:T(8,128)(2,1)S(1)}, bf16[96,768]{1,0:T(8,128)(2,1)S(1)}, u32[]{:S(2)}, u32[]{:S(2)}) collective-permute-start(bf16[96,768]{1,0:T(8,128)(2,1)S(1)} %add_convert_fusion.7), channel_id=1, source_target_pairs={{0,16},{2,18},{4,20},{6,22},{8,24},{10,26},{12,28},{14,30},{16,0},... | collective-permute-start | bytes 442376 | tf_op jit(solution)/shard_map/ppermute | solution.py:1021
  417.3 40.0 %collective-permute-start.77 = (f32[32,768]{1,0:T(8,128)S(1)}, f32[32,768]{1,0:T(8,128)S(1)}, u32[]{:S(2)}, u32[]{:S(2)}) collective-permute-start(f32[32,768]{1,0:T(8,128)S(1)} %add.94), channel_id=1, source_target_pairs={{0,8},{2,10},{4,12},{6,14},{8,0},{10,2},{12,4},{14,6},{16,24},{18,... | collective-permute-start | bytes 294920 | tf_op jit(solution)/shard_map/ppermute | solution.py:1021
  457.4 23.3 %collective-permute-start.88 = (bf16[1152,768]{1,0:T(8,128)(2,1)S(1)}, bf16[1152,768]{1,0:T(8,128)(2,1)S(1)}, u32[]{:S(2)}, u32[]{:S(2)}) collective-permute-start(bf16[1152,768]{1,0:T(8,128)(2,1)S(1)} %bitcast.113), channel_id=1, source_target_pairs={{0,2},{2,0},{4,6},{6,4},{8,10},{10,8},{12,14},{14,12},{16,18},{18,... | collective-permute-start | bytes 5308424 | tf_op jit(solution)/shard_map/ppermute | solution.py:1021
  458.1 13.9 %collective-permute-start.83 = (bf16[96,768]{1,0:T(8,128)(2,1)S(1)}, bf16[96,768]{1,0:T(8,128)(2,1)S(1)}, u32[]{:S(2)}, u32[]{:S(2)}) collective-permute-start(bf16[96,768]{1,0:T(8,128)(2,1)S(1)} %add_convert_fusion.6), channel_id=1, source_target_pairs={{0,16},{2,18},{4,20},{6,22},{8,24},{10,26},{12,28},{14,30},{16,0},... | collective-permute-start | bytes 442376 | tf_op jit(solution)/shard_map/ppermute | solution.py:1021
  458.1 15.8 %collective-permute-start.82 = (bf16[192,768]{1,0:T(8,128)(2,1)S(1)}, bf16[192,768]{1,0:T(8,128)(2,1)S(1)}, u32[]{:S(2)}, u32[]{:S(2)}) collective-permute-start(bf16[192,768]{1,0:T(8,128)(2,1)S(1)} %add_convert_fusion.2.own_ref), channel_id=1, source_target_pairs={{0,8},{2,10},{4,12},{6,14},{8,0},{10,2},{12,4},{14,6},{16,24},{18,... | collective-permute-start | bytes 884744 | tf_op jit(solution)/shard_map/ppermute | solution.py:1021
  473.9 17.3 %collective-permute-start.91 = (bf16[384,768]{1,0:T(8,128)(2,1)S(1)}, bf16[384,768]{1,0:T(8,128)(2,1)S(1)}, u32[]{:S(2)}, u32[]{:S(2)}) collective-permute-start(bf16[384,768]{1,0:T(8,128)(2,1)S(1)} %bitcast.131), channel_id=1, source_target_pairs={{0,4},{2,6},{4,0},{6,2},{8,12},{10,14},{12,8},{14,10},{16,20},{18,... | collective-permute-start | bytes 1769480 | tf_op jit(solution)/shard_map/ppermute | solution.py:1021
  491.3 20.0 %collective-permute-start.94 = (bf16[2304,768]{1,0:T(8,128)(2,1)}, bf16[2304,768]{1,0:T(8,128)(2,1)S(1)}, u32[]{:S(2)}, u32[]{:S(2)}) collective-permute-start(bf16[2304,768]{1,0:T(8,128)(2,1)} %all-gather.2.cloned.1.call-done), channel_id=1, source_target_pairs={{0,2},{2,0},{4,6},{6,4},{8,10},{10,8},{12,14},{14,12},{16,18},{18,... | collective-permute-start | bytes 10616840 | tf_op jit(solution)/shard_map/ppermute | solution.py:1021
  492.8 15.9 %collective-permute-start.95 = (bf16[768,768]{1,0:T(8,128)(2,1)S(1)}, bf16[768,768]{1,0:T(8,128)(2,1)S(1)}, u32[]{:S(2)}, u32[]{:S(2)}) collective-permute-start(bf16[768,768]{1,0:T(8,128)(2,1)S(1)} %bitcast.118), channel_id=1, source_target_pairs={{0,2},{2,0},{4,6},{6,4},{8,10},{10,8},{12,14},{14,12},{16,18},{18,... | collective-permute-start | bytes 3538952 | tf_op jit(solution)/shard_map/ppermute | solution.py:1021
  494.4 13.0 %collective-permute-start.89 = (bf16[192,768]{1,0:T(8,128)(2,1)S(1)}, bf16[192,768]{1,0:T(8,128)(2,1)S(1)}, u32[]{:S(2)}, u32[]{:S(2)}) collective-permute-start(bf16[192,768]{1,0:T(8,128)(2,1)S(1)} %bitcast.148), channel_id=1, source_target_pairs={{0,4},{2,6},{4,0},{6,2},{8,12},{10,14},{12,8},{14,10},{16,20},{18,... | collective-permute-start | bytes 884744 | tf_op jit(solution)/shard_map/ppermute | solution.py:1021
  501.1 19.7 %collective-permute-start.93 = (bf16[384,768]{1,0:T(8,128)(2,1)S(1)}, bf16[384,768]{1,0:T(8,128)(2,1)S(1)}, u32[]{:S(2)}, u32[]{:S(2)}) collective-permute-start(bf16[384,768]{1,0:T(8,128)(2,1)S(1)} %bitcast.130), channel_id=1, source_target_pairs={{0,2},{2,0},{4,6},{6,4},{8,10},{10,8},{12,14},{14,12},{16,18},{18,... | collective-permute-start | bytes 1769480 | tf_op jit(solution)/shard_map/ppermute | solution.py:1021
  507.4 14.8 %collective-permute-start.92 = (bf16[384,768]{1,0:T(8,128)(2,1)S(1)}, bf16[384,768]{1,0:T(8,128)(2,1)S(1)}, u32[]{:S(2)}, u32[]{:S(2)}) collective-permute-start(bf16[384,768]{1,0:T(8,128)(2,1)S(1)} %bitcast.133), channel_id=1, source_target_pairs={{0,2},{2,0},{4,6},{6,4},{8,10},{10,8},{12,14},{14,12},{16,18},{18,... | collective-permute-start | bytes 1769480 | tf_op jit(solution)/shard_map/ppermute | solution.py:1021
  (153 other events, 976.8 us)
Sparse Core Ops, SparseCore 0:
  258.2 89.3 reduce-scatter.1
  378.2 93.9 all-gather.1

commit v6 on v5

--- a/solution.py
+++ b/solution.py
@@ -667,6 +667,10 @@
     )(which, *[array for array, _ in ins])
 
 
+def far(array):
+    return pltpu.with_memory_space_constraint(array, pltpu.HBM)
+
+
 def quarters(rows, width, narrow_rows):
     shape = (lax.axis_size("narrow") // 2 * narrow_rows, width)
     return [(shape, low, pl.BlockSpec(shape, lambda g, core: (0, 0)))] * 4
@@ -692,7 +696,7 @@
         (2,),
         [
             (left, pl.BlockSpec((rows, width), lambda g, core: (0, 0))),
-            (right, pl.BlockSpec((rows, width), lambda g, core: (0, core[0] * 2 + g))),
+            (far(right), pl.BlockSpec((rows, width), lambda g, core: (0, core[0] * 2 + g))),
         ],
         quarters(rows, width, part),
         "up_term",
@@ -768,7 +772,7 @@
         core,
         (2,),
         [
-            (left, pl.BlockSpec((rows, width), lambda g, core: (0, g * 2 + core[0] if direct else g))),
+            (far(left), pl.BlockSpec((rows, width), lambda g, core: (0, g * 2 + core[0] if direct else g))),
             (right, pl.BlockSpec((rows, width), lambda g, core: (0, 0))),
         ],
         quarters(rows, width, part // 2),
@@ -1370,20 +1374,20 @@
     first.step()
     fourth.step()
     second.step()
+    order.hold(gathered)
+    other = swap(after(gathered, *order.last), "wide", 1)
     minor_step()
     first.finish(done)
     third.step()
     fourth.step()
-    minor_step()
-    second.step()
-    order.hold(gathered)
-    other = swap(after(gathered, *order.last), "wide", 1)
-    third.step()
-    fourth.step()
-    second.finish(done)
     own, got = gathered.reshape(1, -1, width), other.reshape(1, -1, width)
     for which, term in enumerate((term_down1, term_up1, term_qkv1)):
         term.finish(done, own, got, which * (own.shape[1] // 3), own.shape[1] // 3)
+    minor_step()
+    second.step()
+    third.step()
+    second.finish(done)
+    fourth.step()
     for each in (first, second, third, fourth):
         while not each.closed:
             each.step()

time: 542 us -> 541 us (level)
  Pallas kernels: 238 us -> 249 us
  local copies, waits for them, and re-layouts: 51.6 us -> 44.3 us
    pallas_call x49, Pallas kernels: 71.5 us -> 82.5 us  [picked(): pl.pallas_call(body, grid_spec=pltpu.PrefetchScalarGridSpec(num_scalar_pr...]
    unnamed x212 -> x204, local copies, waits for them, and re-layouts: 38.3 us -> 31 us
  transfers between devices with their start and end apart: 98 -> 98, of which waited for: 31 -> 31; matrix products, arithmetic and copies ran while one was open for 3% -> 3% of each run, Pallas kernels for 39% -> 40%
where the time goes in v6:
time: 541 us; the launch traced here: 531 us
  Pallas kernels  249 us (46%)
  waiting for transfers between devices  128 us (24%)
  starting transfers between devices  89.1 us (16%)
  local copies, waits for them, and re-layouts  44.3 us (8%)
  between operations  15.9 us (3%)
    pallas_call x13, Pallas kernels, call(): pl.pallas_call(body, grid=grid, in_specs=[spec for _, spec in ins], out_s...  158 us
    ppermute x96, waiting for transfers between devices, swap(): lax.ppermute(values, axis, [(source, source ^ mask) for source in range(s...  128 us
    ppermute x96, starting transfers between devices, swap(): lax.ppermute(values, axis, [(source, source ^ mask) for source in range(s...  89 us
    pallas_call x49, Pallas kernels, picked(): pl.pallas_call(body, grid_spec=pltpu.PrefetchScalarGridSpec(num_scalar_pr...  82.5 us
    unnamed x204, local copies, waits for them, and re-layouts  31 us
  transfers between devices with their start and end apart: 98, of which 31 were waited for; matrix products, arithmetic and copies ran while one was open for 3% of the time, Pallas kernels for 40%

profile of v6, /device:TPU:1, one launch (start us, length us, event | category | flops | bytes accessed | tf_op | source)
XLA Modules:
  0.0 530.7 jit_solution(5282179026148525839)
XLA Ops:
  34.9 5.9 %collective-permute-done.1.refs_3_ = bf16[1,96,2304]{2,1,0:T(8,128)(2,1)} collective-permute-done((bf16[1,96,2304]{2,1,0:T(8,128)(2,1)}, bf16[1,96,2304]{2,1,0:T(8,128)(2,1)}, u32[]{:S(2)}, u32[]{:S(2)}) %collective-permute-start.1) | collective-permute-done | bytes 442400 | tf_op jit(solution)/shard_map/ppermute | solution.py:1025
  40.8 3.0 collective-permute-start.3
  48.2 5.1 project_qkv.1
  54.7 8.7 %attend.2 = (bf16[2,336,768]{2,1,0:T(8,128)(2,1)S(1)}, f32[2,6,8,336]{3,2,1,0:T(8,128)S(1)}) custom-call(s32[2]{0:T(128)S(1)} %multiply_add_fusion.length_ref.refs_23_, bf16[3,2,336,768]{3,2,1,0:T(8,128)(2,1)S(1)} %bitcast.170, bf16[3,2,336,768]{3,2,1,0:T(8,128)(2,1)S(1)} %bitcast.171, bf16[3,2,336,768]{3,2,1,0:T(8,128)(2,1)S(1)} %bitcast.172), custom_call_target="tpu_custom_call" | custom-call | flops 3000000000 | tf_op jit(solution)/shard_map/attend/pallas_call | solution.py:69
  75.0 20.6 %feed_forward.2 = (f32[672,768]{1,0:T(8,128)S(1)}, bf16[672,768]{1,0:T(8,128)(2,1)S(1)}, bf16[672,3072]{1,0:T(8,128)(2,1)S(1)}, bf16[672,3072]{1,0:T(8,128)(2,1)}, bf16[672,768]{1,0:T(8,128)(2,1)S(1)}) custom-call(s32[2]{0:T(128)S(1)} %pad_add_fusion.refs_0_, bf16[2,384,768]{2,1,0:T(8,128)(2,1)} %refs_11_.7, bf16[1,96,3840]{2,1,0:T(8,128)(2,1)} %copy-done.70, ...), custom_call_target="tpu_custom_call" | custom-call | flops 6899999744 | tf_op jit(solution)/shard_map/feed_forward/pallas_call | solution.py:69
  97.5 2.6 collective-permute-done.6.refs_2_.refs_7_.refs_12_
  104.1 8.1 %join_qkv.1 = (f32[672,768]{1,0:T(8,128)S(1)}, bf16[672,768]{1,0:T(8,128)(2,1)S(1)}, bf16[3,672,768]{2,1,0:T(8,128)(2,1)S(1)}) custom-call(s32[2]{0:T(128)S(1)} %pad_add_fusion.refs_0_, bf16[768,768]{1,0:T(8,128)(2,1)} %refs_6_.10, bf16[1,192,768]{2,1,0:T(8,128)(2,1)} %copy-done.94, bf16[1,192,768]{2,1,0:T(8,128)(2,1)} %copy-done.95, ...), custom_call_target="tpu_custom_call" | custom-call | flops 3300000000 | tf_op jit(solution)/shard_map/join_qkv/pallas_call | solution.py:69
  112.3 8.7 %attend.3 = (bf16[2,336,768]{2,1,0:T(8,128)(2,1)S(1)}, f32[2,6,8,336]{3,2,1,0:T(8,128)S(1)}) custom-call(s32[2]{0:T(128)S(1)} %multiply_add_fusion.length_ref.refs_23_, bf16[3,2,336,768]{3,2,1,0:T(8,128)(2,1)S(1)} %bitcast.176, bf16[3,2,336,768]{3,2,1,0:T(8,128)(2,1)S(1)} %bitcast.177, bf16[3,2,336,768]{3,2,1,0:T(8,128)(2,1)S(1)} %bitcast.178), custom_call_target="tpu_custom_call" | custom-call | flops 3000000000 | tf_op jit(solution)/shard_map/attend/pallas_call | solution.py:69
  122.4 3.1 collective-permute-done.27.refs_14_.refs_4_
  128.3 21.0 %feed_forward.3 = (f32[672,768]{1,0:T(8,128)S(1)}, bf16[672,768]{1,0:T(8,128)(2,1)S(1)}, bf16[672,3072]{1,0:T(8,128)(2,1)S(1)}, bf16[672,3072]{1,0:T(8,128)(2,1)}, bf16[672,768]{1,0:T(8,128)(2,1)}) custom-call(s32[2]{0:T(128)S(1)} %pad_add_fusion.refs_0_, bf16[2,384,768]{2,1,0:T(8,128)(2,1)} %refs_11_.7, bf16[1,96,3840]{2,1,0:T(8,128)(2,1)} %copy-done.74, ...), custom_call_target="tpu_custom_call" | custom-call | flops 6899999744 | tf_op jit(solution)/shard_map/feed_forward/pallas_call | solution.py:69
  151.3 5.9 %down_term.4 = (bf16[384,768]{1,0:T(8,128)(2,1)}, bf16[384,768]{1,0:T(8,128)(2,1)}, bf16[384,768]{1,0:T(8,128)(2,1)}, bf16[384,768]{1,0:T(8,128)(2,1)}) custom-call(s32[1]{0:T(128)S(6)} %sub.70.core_ref, bf16[672,3072]{1,0:T(8,128)(2,1)} %copy-done.3, bf16[672,768]{1,0:T(8,128)(2,1)S(1)} %broadcast_select_fusion.r_ref.refs_16_.refs_17_), custom_call_target="tpu_custom_call" | custom-call | flops 1050000000 | tf_op jit(solution)/shard_map/down_term/pallas_call | solution.py:654
  158.3 4.1 down_term.5
  166.3 18.3 %feed_forward_back.2 = (bf16[672,3072]{1,0:T(8,128)(2,1)}, f32[672,768]{1,0:T(8,128)S(1)}, bf16[672,768]{1,0:T(8,128)(2,1)S(1)}, bf16[672,768]{1,0:T(8,128)(2,1)S(1)}, f32[8,768]{1,0:T(8,128)S(1)}) custom-call(s32[2]{0:T(128)S(1)} %pad_add_fusion.refs_0_, bf16[2,1536,768]{2,1,0:T(8,128)(2,1)} %refs_1_.15, bf16[1,384,768]{2,1,0:T(8,128)(2,1)} %copy-done.84, ...), custom_call_target="tpu_custom_call" | custom-call | flops 6300000256 | tf_op jit(solution)/shard_map/feed_forward_back/pallas_call | solution.py:69
  184.6 4.6 up_term.4
  190.5 3.8 up_term.5
  198.6 2.7 add_into.3.rest_0_
  202.6 13.9 %attend_back.2 = bf16[3,2,336,768]{3,2,1,0:T(8,128)(2,1)S(1)} custom-call(s32[2]{0:T(128)S(1)} %multiply_add_fusion.length_ref.refs_23_, bf16[3,2,336,768]{3,2,1,0:T(8,128)(2,1)S(1)} %bitcast.179, bf16[3,2,336,768]{3,2,1,0:T(8,128)(2,1)S(1)} %bitcast.180, bf16[3,2,336,768]{3,2,1,0:T(8,128)(2,1)S(1)} %bitcast.181, bf16[2,336,768]{2,1,0:T(8,128)(2,1)S(1)} %bitcast.157, ...), custom_call_target="tpu_custom_call" | custom-call | flops 4499999744 | tf_op jit(solution)/shard_map/attend_back/pallas_call | solution.py:69
  216.6 2.6 qkv_out_term.4
  227.3 2.7 add_into.4.rest_0_
  231.6 11.9 %project_back.2 = (bf16[672,768]{1,0:T(8,128)(2,1)S(1)}, f32[672,768]{1,0:T(8,128)S(1)}, bf16[672,768]{1,0:T(8,128)(2,1)S(1)}, f32[672,768]{1,0:T(8,128)}, f32[8,768]{1,0:T(8,128)S(1)}) custom-call(s32[2]{0:T(128)S(1)} %pad_add_fusion.refs_0_, bf16[2,384,2304]{2,1,0:T(8,128)(2,1)} %refs_1_.16, bf16[1,96,2304]{2,1,0:T(8,128)(2,1)} %collective-permute-done.10.refs_7_.refs_2_, ...), custom_call_target="tpu_custom_call" | custom-call | flops 3900000000 | tf_op jit(solution)/shard_map/project_back/pallas_call | solution.py:69
  249.9 3.8 down_term.6
  253.8 4.6 down_term.7
  258.4 2.6 add_into.5
  270.1 19.6 %feed_forward_back.3 = (bf16[672,3072]{1,0:T(8,128)(2,1)}, f32[672,768]{1,0:T(8,128)S(1)}, bf16[672,768]{1,0:T(8,128)(2,1)S(1)}, bf16[672,768]{1,0:T(8,128)(2,1)S(1)}, f32[8,768]{1,0:T(8,128)S(1)}) custom-call(s32[2]{0:T(128)S(1)} %pad_add_fusion.refs_0_, bf16[2,1536,768]{2,1,0:T(8,128)(2,1)} %refs_1_.15, bf16[1,384,768]{2,1,0:T(8,128)(2,1)} %copy-done.80, ...), custom_call_target="tpu_custom_call" | custom-call | flops 6300000256 | tf_op jit(solution)/shard_map/feed_forward_back/pallas_call | solution.py:69
  291.6 3.8 up_term.6
  297.0 3.8 up_term.7
  300.7 5.2 collective-permute-done.57
  311.7 13.9 %attend_back.3 = bf16[3,2,336,768]{3,2,1,0:T(8,128)(2,1)S(1)} custom-call(s32[2]{0:T(128)S(1)} %multiply_add_fusion.length_ref.refs_23_, bf16[3,2,336,768]{3,2,1,0:T(8,128)(2,1)S(1)} %bitcast.173, bf16[3,2,336,768]{3,2,1,0:T(8,128)(2,1)S(1)} %bitcast.174, bf16[3,2,336,768]{3,2,1,0:T(8,128)(2,1)S(1)} %bitcast.175, bf16[2,336,768]{2,1,0:T(8,128)(2,1)S(1)} %bitcast.156, ...), custom_call_target="tpu_custom_call" | custom-call | flops 4499999744 | tf_op jit(solution)/shard_map/attend_back/pallas_call | solution.py:69
  325.7 3.6 qkv_out_term.6
  344.0 2.8 collective-permute-start.68
  348.3 8.4 %project_back.3 = (f32[672,768]{1,0:T(8,128)}, f32[8,768]{1,0:T(8,128)S(1)}) custom-call(s32[2]{0:T(128)S(1)} %pad_add_fusion.refs_0_, bf16[2,384,2304]{2,1,0:T(8,128)(2,1)} %refs_1_.16, bf16[1,96,2304]{2,1,0:T(8,128)(2,1)} %collective-permute-done.refs_2_, bf16[1,96,2304]{2,1,0:T(8,128)(2,1)} %collective-permute-done.1.refs_3_, ...), custom_call_target="tpu_custom_call" | custom-call | flops 2700000000 | tf_op jit(solution)/shard_map/project_back/pallas_call | solution.py:69
  360.2 2.6 collective-permute-start.71
  367.4 4.0 collective-permute-done.66
  373.6 7.0 %collective-permute-done.71 = bf16[288,768]{1,0:T(8,128)(2,1)S(1)} collective-permute-done((bf16[288,768]{1,0:T(8,128)(2,1)S(1)}, bf16[288,768]{1,0:T(8,128)(2,1)S(1)}, u32[]{:S(2)}, u32[]{:S(2)}) %collective-permute-start.71) | collective-permute-done | bytes 442400 | tf_op jit(solution)/shard_map/ppermute | solution.py:1025
  380.9 4.1 collective-permute-start.75
  386.5 4.7 collective-permute-done.75
  391.2 12.8 %collective-permute-done.74 = bf16[1,96,768]{2,1,0:T(8,128)(2,1)S(1)} collective-permute-done((bf16[1,96,768]{2,1,0:T(8,128)(2,1)S(1)}, bf16[1,96,768]{2,1,0:T(8,128)(2,1)S(1)}, u32[]{:S(2)}, u32[]{:S(2)}) %collective-permute-start.74) | collective-permute-done | bytes 147488 | tf_op jit(solution)/shard_map/ppermute | solution.py:1025
  404.3 11.4 %collective-permute-start.70 = (f32[32,768]{1,0:T(8,128)S(1)}, f32[32,768]{1,0:T(8,128)S(1)}, u32[]{:S(2)}, u32[]{:S(2)}) collective-permute-start(f32[32,768]{1,0:T(8,128)S(1)} %add.90), channel_id=1, source_target_pairs={{0,2},{2,0},{4,6},{6,4},{8,10},{10,8},{12,14},{14,12},{16,18},{18,... | collective-permute-start | bytes 294920 | tf_op jit(solution)/shard_map/ppermute | solution.py:1025
  415.6 4.5 collective-permute-start.79
  422.7 30.5 %collective-permute-done.79 = bf16[192,768]{1,0:T(8,128)(2,1)S(1)} collective-permute-done((bf16[192,768]{1,0:T(8,128)(2,1)S(1)}, bf16[192,768]{1,0:T(8,128)(2,1)S(1)}, u32[]{:S(2)}, u32[]{:S(2)}) %collective-permute-start.79) | collective-permute-done | bytes 294944 | tf_op jit(solution)/shard_map/ppermute | solution.py:1025
  453.4 8.6 %collective-permute-done.78 = bf16[96,768]{1,0:T(8,128)(2,1)S(1)} collective-permute-done((bf16[96,768]{1,0:T(8,128)(2,1)S(1)}, bf16[96,768]{1,0:T(8,128)(2,1)S(1)}, u32[]{:S(2)}, u32[]{:S(2)}) %collective-permute-start.78) | collective-permute-done | bytes 147488 | tf_op jit(solution)/shard_map/ppermute | solution.py:1025
  462.2 9.7 %collective-permute-done.83 = bf16[96,768]{1,0:T(8,128)(2,1)S(1)} collective-permute-done((bf16[96,768]{1,0:T(8,128)(2,1)S(1)}, bf16[96,768]{1,0:T(8,128)(2,1)S(1)}, u32[]{:S(2)}, u32[]{:S(2)}) %collective-permute-start.83) | collective-permute-done | bytes 147488 | tf_op jit(solution)/shard_map/ppermute | solution.py:1025
  471.9 6.2 %collective-permute-done.82.got_ref = bf16[192,768]{1,0:T(8,128)(2,1)S(1)} collective-permute-done((bf16[192,768]{1,0:T(8,128)(2,1)S(1)}, bf16[192,768]{1,0:T(8,128)(2,1)S(1)}, u32[]{:S(2)}, u32[]{:S(2)}) %collective-permute-start.82) | collective-permute-done | bytes 294944 | tf_op jit(solution)/shard_map/ppermute | solution.py:1025
  482.9 5.1 collective-permute-done.81
  496.4 2.6 finish_columns.2.rest_0_
  499.0 3.3 finish_qkv_out.2
  504.4 7.1 %collective-permute-done.93.got_ref = bf16[192,768]{1,0:T(8,128)(2,1)S(1)} collective-permute-done((bf16[192,768]{1,0:T(8,128)(2,1)S(1)}, bf16[192,768]{1,0:T(8,128)(2,1)S(1)}, u32[]{:S(2)}, u32[]{:S(2)}) %collective-permute-start.93) | collective-permute-done | bytes 294944 | tf_op jit(solution)/shard_map/ppermute | solution.py:1025
  513.0 2.6 finish_columns.3
  (454 shorter events, 158.8 us)
Async XLA Ops:
  7.2 373.7 %reduce-scatter.2.cloned.1.call-start = ((), (), s32[]{:S(2)}) async-start(), calls=%async_computation.1 | async-start | bytes 3981312 | tf_op jit(solution)/shard_map/reduce_scatter | solution.py:1311
  8.3 22.6 %collective-permute-start = (bf16[1,96,2304]{2,1,0:T(8,128)(2,1)S(1)}, bf16[1,96,2304]{2,1,0:T(8,128)(2,1)}, u32[]{:S(2)}, u32[]{:S(2)}) collective-permute-start(bf16[1,96,2304]{2,1,0:T(8,128)(2,1)S(1)} %constant_dynamic-slice_fusion.3), channel_id=1, source_target_pairs={{0,1},{1,0},{2,3},{3,2},{4,5},{5,4},{6,7},{7,6},{8,9},{9,8},{10,11... | collective-permute-start | bytes 1327112 | tf_op jit(solution)/shard_map/ppermute | solution.py:1025
  14.5 17.9 %collective-permute-start.4 = (bf16[1,32,384]{2,1,0:T(8,128)(2,1)S(1)}, bf16[1,32,384]{2,1,0:T(8,128)(2,1)S(1)}, u32[]{:S(2)}, u32[]{:S(2)}) collective-permute-start(bf16[1,32,384]{2,1,0:T(8,128)(2,1)S(1)} %convert_bitcast_fusion), channel_id=1, source_target_pairs={{0,1},{1,0},{2,3},{3,2},{4,5},{5,4},{6,7},{7,6},{8,9},{9,8},{10,11... | collective-permute-start | bytes 73736 | tf_op jit(solution)/shard_map/ppermute | solution.py:1025
  17.6 27.6 %collective-permute-start.5 = (bf16[1,96,3840]{2,1,0:T(8,128)(2,1)}, bf16[1,96,3840]{2,1,0:T(8,128)(2,1)S(1)}, u32[]{:S(2)}, u32[]{:S(2)}) collective-permute-start(bf16[1,96,3840]{2,1,0:T(8,128)(2,1)} %maximum_bitcast_fusion), channel_id=1, source_target_pairs={{0,1},{1,0},{2,3},{3,2},{4,5},{5,4},{6,7},{7,6},{8,9},{9,8},{10,11... | collective-permute-start | bytes 2211848 | tf_op jit(solution)/shard_map/ppermute | solution.py:1025
  20.9 32.4 %collective-permute-start.8 = (bf16[1,384,768]{2,1,0:T(8,128)(2,1)}, bf16[1,384,768]{2,1,0:T(8,128)(2,1)S(1)}, u32[]{:S(2)}, u32[]{:S(2)}) collective-permute-start(bf16[1,384,768]{2,1,0:T(8,128)(2,1)} %constant_dynamic-slice_fusion.2), channel_id=1, source_target_pairs={{0,1},{1,0},{2,3},{3,2},{4,5},{5,4},{6,7},{7,6},{8,9},{9,8},{10,11... | collective-permute-start | bytes 1769480 | tf_op jit(solution)/shard_map/ppermute | solution.py:1025
  24.5 40.6 %collective-permute-start.10 = (bf16[1,96,2304]{2,1,0:T(8,128)(2,1)}, bf16[1,96,2304]{2,1,0:T(8,128)(2,1)}, u32[]{:S(2)}, u32[]{:S(2)}) collective-permute-start(bf16[1,96,2304]{2,1,0:T(8,128)(2,1)} %constant_dynamic-slice_fusion.1), channel_id=1, source_target_pairs={{0,1},{1,0},{2,3},{3,2},{4,5},{5,4},{6,7},{7,6},{8,9},{9,8},{10,11... | collective-permute-start | bytes 1327112 | tf_op jit(solution)/shard_map/ppermute | solution.py:1025
  32.5 14.1 %collective-permute-start.2 = (bf16[1,96,2304]{2,1,0:T(8,128)(2,1)}, bf16[1,96,2304]{2,1,0:T(8,128)(2,1)S(1)}, u32[]{:S(2)}, u32[]{:S(2)}) collective-permute-start(bf16[1,96,2304]{2,1,0:T(8,128)(2,1)} %collective-permute-done.refs_2_), channel_id=1, source_target_pairs={{0,2},{2,0},{4,6},{6,4},{8,10},{10,8},{12,14},{14,12},{16,18},{18,... | collective-permute-start | bytes 1327112 | tf_op jit(solution)/shard_map/ppermute | solution.py:1025
  45.2 21.1 %collective-permute-start.7 = (bf16[1,96,3840]{2,1,0:T(8,128)(2,1)S(1)}, bf16[1,96,3840]{2,1,0:T(8,128)(2,1)S(1)}, u32[]{:S(2)}, u32[]{:S(2)}) collective-permute-start(bf16[1,96,3840]{2,1,0:T(8,128)(2,1)S(1)} %collective-permute-done.5.refs_2_.refs_7_.refs_12_), channel_id=1, source_target_pairs={{0,4},{2,6},{4,0},{6,2},{8,12},{10,14},{12,8},{14,10},{16,20},{18,... | collective-permute-start | bytes 2211848 | tf_op jit(solution)/shard_map/ppermute | solution.py:1025
  46.6 18.5 %collective-permute-start.9 = (bf16[1,192,768]{2,1,0:T(8,128)(2,1)}, bf16[1,192,768]{2,1,0:T(8,128)(2,1)S(1)}, u32[]{:S(2)}, u32[]{:S(2)}) collective-permute-start(bf16[1,192,768]{2,1,0:T(8,128)(2,1)} %dynamic-slice_bitcast_fusion.2), channel_id=1, source_target_pairs={{0,1},{1,0},{2,3},{3,2},{4,5},{5,4},{6,7},{7,6},{8,9},{9,8},{10,11... | collective-permute-start | bytes 884744 | tf_op jit(solution)/shard_map/ppermute | solution.py:1025
  53.4 14.7 %collective-permute-start.13 = (bf16[1,384,768]{2,1,0:T(8,128)(2,1)S(1)}, bf16[1,384,768]{2,1,0:T(8,128)(2,1)S(1)}, u32[]{:S(2)}, u32[]{:S(2)}) collective-permute-start(bf16[1,384,768]{2,1,0:T(8,128)(2,1)S(1)} %collective-permute-done.8.refs_12_.refs_2_), channel_id=1, source_target_pairs={{0,8},{2,10},{4,12},{6,14},{8,0},{10,2},{12,4},{14,6},{16,24},{18,... | collective-permute-start | bytes 1769480 | tf_op jit(solution)/shard_map/ppermute | solution.py:1025
  69.2 31.6 %collective-permute-start.23 = (bf16[1,384,768]{2,1,0:T(8,128)(2,1)S(1)}, bf16[1,384,768]{2,1,0:T(8,128)(2,1)S(1)}, u32[]{:S(2)}, u32[]{:S(2)}) collective-permute-start(bf16[1,384,768]{2,1,0:T(8,128)(2,1)S(1)} %copy-done.88), channel_id=1, source_target_pairs={{0,1},{1,0},{2,3},{3,2},{4,5},{5,4},{6,7},{7,6},{8,9},{9,8},{10,11... | collective-permute-start | bytes 1769480 | tf_op jit(solution)/shard_map/ppermute | solution.py:1025
  70.1 29.9 %collective-permute-start.6 = (bf16[1,96,3840]{2,1,0:T(8,128)(2,1)S(1)}, bf16[1,96,3840]{2,1,0:T(8,128)(2,1)S(1)}, u32[]{:S(2)}, u32[]{:S(2)}) collective-permute-start(bf16[1,96,3840]{2,1,0:T(8,128)(2,1)S(1)} %copy-done.79), channel_id=1, source_target_pairs={{0,1},{1,0},{2,3},{3,2},{4,5},{5,4},{6,7},{7,6},{8,9},{9,8},{10,11... | collective-permute-start | bytes 2211848 | tf_op jit(solution)/shard_map/ppermute | solution.py:1025
  71.6 24.1 %collective-permute-start.20 = (bf16[1,96,2304]{2,1,0:T(8,128)(2,1)}, bf16[1,96,2304]{2,1,0:T(8,128)(2,1)S(1)}, u32[]{:S(2)}, u32[]{:S(2)}) collective-permute-start(bf16[1,96,2304]{2,1,0:T(8,128)(2,1)} %collective-permute-done.10.refs_7_.refs_2_), channel_id=1, source_target_pairs={{0,4},{2,6},{4,0},{6,2},{8,12},{10,14},{12,8},{14,10},{16,20},{18,... | collective-permute-start | bytes 1327112 | tf_op jit(solution)/shard_map/ppermute | solution.py:1025
  72.8 24.2 %collective-permute-start.17 = (bf16[1,192,768]{2,1,0:T(8,128)(2,1)S(1)}, bf16[1,192,768]{2,1,0:T(8,128)(2,1)S(1)}, u32[]{:S(2)}, u32[]{:S(2)}) collective-permute-start(bf16[1,192,768]{2,1,0:T(8,128)(2,1)S(1)} %collective-permute-done.9.refs_2_.refs_7_), channel_id=1, source_target_pairs={{0,8},{2,10},{4,12},{6,14},{8,0},{10,2},{12,4},{14,6},{16,24},{18,... | collective-permute-start | bytes 884744 | tf_op jit(solution)/shard_map/ppermute | solution.py:1025
  100.8 20.9 %collective-permute-start.16 = (bf16[1,96,3840]{2,1,0:T(8,128)(2,1)S(1)}, bf16[1,96,3840]{2,1,0:T(8,128)(2,1)S(1)}, u32[]{:S(2)}, u32[]{:S(2)}) collective-permute-start(bf16[1,96,3840]{2,1,0:T(8,128)(2,1)S(1)} %collective-permute-done.6.refs_2_.refs_7_.refs_12_), channel_id=1, source_target_pairs={{0,4},{2,6},{4,0},{6,2},{8,12},{10,14},{12,8},{14,10},{16,20},{18,... | collective-permute-start | bytes 2211848 | tf_op jit(solution)/shard_map/ppermute | solution.py:1025
  101.1 21.2 %collective-permute-start.26 = (bf16[1,384,768]{2,1,0:T(8,128)(2,1)S(1)}, bf16[1,384,768]{2,1,0:T(8,128)(2,1)S(1)}, u32[]{:S(2)}, u32[]{:S(2)}) collective-permute-start(bf16[1,384,768]{2,1,0:T(8,128)(2,1)S(1)} %collective-permute-done.23.refs_12_.refs_2_), channel_id=1, source_target_pairs={{0,8},{2,10},{4,12},{6,14},{8,0},{10,2},{12,4},{14,6},{16,24},{18,... | collective-permute-start | bytes 1769480 | tf_op jit(solution)/shard_map/ppermute | solution.py:1025
  165.5 32.1 %collective-permute-start.33 = (bf16[2,384,768]{2,1,0:T(8,128)(2,1)S(1)}, bf16[2,384,768]{2,1,0:T(8,128)(2,1)S(1)}, u32[]{:S(2)}, u32[]{:S(2)}) collective-permute-start(bf16[2,384,768]{2,1,0:T(8,128)(2,1)S(1)} %get-tuple-element.551), channel_id=1, source_target_pairs={{0,1},{1,0},{2,3},{3,2},{4,5},{5,4},{6,7},{7,6},{8,9},{9,8},{10,11... | collective-permute-start | bytes 3538952 | tf_op jit(solution)/shard_map/ppermute | solution.py:1025
  196.9 30.4 %collective-permute-start.38 = (bf16[2,384,768]{2,1,0:T(8,128)(2,1)}, bf16[2,384,768]{2,1,0:T(8,128)(2,1)}, u32[]{:S(2)}, u32[]{:S(2)}) collective-permute-start(bf16[2,384,768]{2,1,0:T(8,128)(2,1)} %get-tuple-element.582), channel_id=1, source_target_pairs={{0,1},{1,0},{2,3},{3,2},{4,5},{5,4},{6,7},{7,6},{8,9},{9,8},{10,11... | collective-permute-start | bytes 3538952 | tf_op jit(solution)/shard_map/ppermute | solution.py:1025
  226.5 31.8 %collective-permute-start.51 = (bf16[2,384,768]{2,1,0:T(8,128)(2,1)}, bf16[2,384,768]{2,1,0:T(8,128)(2,1)}, u32[]{:S(2)}, u32[]{:S(2)}) collective-permute-start(bf16[2,384,768]{2,1,0:T(8,128)(2,1)} %get-tuple-element.617), channel_id=1, source_target_pairs={{0,1},{1,0},{2,3},{3,2},{4,5},{5,4},{6,7},{7,6},{8,9},{9,8},{10,11... | collective-permute-start | bytes 3538952 | tf_op jit(solution)/shard_map/ppermute | solution.py:1025
  261.0 217.2 %all-gather.2.cloned.1.call-start = ((), (), s32[]{:S(2)}) async-start(), calls=%async_computation.2 | async-start | bytes 3981312 | tf_op jit(solution)/shard_map/all_gather | solution.py:1365
  268.0 37.9 %collective-permute-start.57 = (bf16[2,384,768]{2,1,0:T(8,128)(2,1)S(1)}, bf16[2,384,768]{2,1,0:T(8,128)(2,1)S(1)}, u32[]{:S(2)}, u32[]{:S(2)}) collective-permute-start(bf16[2,384,768]{2,1,0:T(8,128)(2,1)S(1)} %get-tuple-element.677), channel_id=1, source_target_pairs={{0,4},{2,6},{4,0},{6,2},{8,12},{10,14},{12,8},{14,10},{16,20},{18,... | collective-permute-start | bytes 3538952 | tf_op jit(solution)/shard_map/ppermute | solution.py:1025
  269.3 20.3 %collective-permute-start.52 = (bf16[2,192,768]{2,1,0:T(8,128)(2,1)S(1)}, bf16[2,192,768]{2,1,0:T(8,128)(2,1)S(1)}, u32[]{:S(2)}, u32[]{:S(2)}) collective-permute-start(bf16[2,192,768]{2,1,0:T(8,128)(2,1)S(1)} %copy-done.50), channel_id=1, source_target_pairs={{0,1},{1,0},{2,3},{3,2},{4,5},{5,4},{6,7},{7,6},{8,9},{9,8},{10,11... | collective-permute-start | bytes 1769480 | tf_op jit(solution)/shard_map/ppermute | solution.py:1025
  295.4 12.1 %collective-permute-start.53 = (bf16[384,768]{1,0:T(8,128)(2,1)S(1)}, bf16[384,768]{1,0:T(8,128)(2,1)S(1)}, u32[]{:S(2)}, u32[]{:S(2)}) collective-permute-start(bf16[384,768]{1,0:T(8,128)(2,1)S(1)} %get-tuple-element.693), channel_id=1, source_target_pairs={{0,2},{2,0},{4,6},{6,4},{8,10},{10,8},{12,14},{14,12},{16,18},{18,... | collective-permute-start | bytes 1769480 | tf_op jit(solution)/shard_map/ppermute | solution.py:1025
  296.4 12.5 %collective-permute-start.54 = (bf16[384,768]{1,0:T(8,128)(2,1)S(1)}, bf16[384,768]{1,0:T(8,128)(2,1)S(1)}, u32[]{:S(2)}, u32[]{:S(2)}) collective-permute-start(bf16[384,768]{1,0:T(8,128)(2,1)S(1)} %get-tuple-element.700), channel_id=1, source_target_pairs={{0,2},{2,0},{4,6},{6,4},{8,10},{10,8},{12,14},{14,12},{16,18},{18,... | collective-permute-start | bytes 1769480 | tf_op jit(solution)/shard_map/ppermute | solution.py:1025
  296.5 12.4 %collective-permute-start.55 = (bf16[384,768]{1,0:T(8,128)(2,1)S(1)}, bf16[384,768]{1,0:T(8,128)(2,1)S(1)}, u32[]{:S(2)}, u32[]{:S(2)}) collective-permute-start(bf16[384,768]{1,0:T(8,128)(2,1)S(1)} %get-tuple-element.701), channel_id=1, source_target_pairs={{0,2},{2,0},{4,6},{6,4},{8,10},{10,8},{12,14},{14,12},{16,18},{18,... | collective-permute-start | bytes 1769480 | tf_op jit(solution)/shard_map/ppermute | solution.py:1025
  307.3 18.3 %collective-permute-start.59 = (bf16[1,384,768]{2,1,0:T(8,128)(2,1)S(1)}, bf16[1,384,768]{2,1,0:T(8,128)(2,1)S(1)}, u32[]{:S(2)}, u32[]{:S(2)}) collective-permute-start(bf16[1,384,768]{2,1,0:T(8,128)(2,1)S(1)} %get-tuple-element.706), channel_id=1, source_target_pairs={{0,1},{1,0},{2,3},{3,2},{4,5},{5,4},{6,7},{7,6},{8,9},{9,8},{10,11... | collective-permute-start | bytes 1769480 | tf_op jit(solution)/shard_map/ppermute | solution.py:1025
  307.5 18.1 %collective-permute-start.60 = (bf16[1,192,768]{2,1,0:T(8,128)(2,1)S(1)}, bf16[1,192,768]{2,1,0:T(8,128)(2,1)S(1)}, u32[]{:S(2)}, u32[]{:S(2)}) collective-permute-start(bf16[1,192,768]{2,1,0:T(8,128)(2,1)S(1)} %get-tuple-element.690), channel_id=1, source_target_pairs={{0,4},{2,6},{4,0},{6,2},{8,12},{10,14},{12,8},{14,10},{16,20},{18,... | collective-permute-start | bytes 884744 | tf_op jit(solution)/shard_map/ppermute | solution.py:1025
  311.4 35.3 %collective-permute-start.58 = (bf16[2,384,768]{2,1,0:T(8,128)(2,1)}, bf16[2,384,768]{2,1,0:T(8,128)(2,1)}, u32[]{:S(2)}, u32[]{:S(2)}) collective-permute-start(bf16[2,384,768]{2,1,0:T(8,128)(2,1)} %get-tuple-element.715), channel_id=1, source_target_pairs={{0,1},{1,0},{2,3},{3,2},{4,5},{5,4},{6,7},{7,6},{8,9},{9,8},{10,11... | collective-permute-start | bytes 3538952 | tf_op jit(solution)/shard_map/ppermute | solution.py:1025
  337.6 21.3 %collective-permute-start.69 = (bf16[1,384,768]{2,1,0:T(8,128)(2,1)}, bf16[1,384,768]{2,1,0:T(8,128)(2,1)}, u32[]{:S(2)}, u32[]{:S(2)}) collective-permute-start(bf16[1,384,768]{2,1,0:T(8,128)(2,1)} %get-tuple-element.745), channel_id=1, source_target_pairs={{0,1},{1,0},{2,3},{3,2},{4,5},{5,4},{6,7},{7,6},{8,9},{9,8},{10,11... | collective-permute-start | bytes 1769480 | tf_op jit(solution)/shard_map/ppermute | solution.py:1025
  342.7 28.7 %collective-permute-start.66 = (bf16[1,384,768]{2,1,0:T(8,128)(2,1)S(1)}, bf16[1,384,768]{2,1,0:T(8,128)(2,1)S(1)}, u32[]{:S(2)}, u32[]{:S(2)}) collective-permute-start(bf16[1,384,768]{2,1,0:T(8,128)(2,1)S(1)} %get-tuple-element.750), channel_id=1, source_target_pairs={{0,1},{1,0},{2,3},{3,2},{4,5},{5,4},{6,7},{7,6},{8,9},{9,8},{10,11... | collective-permute-start | bytes 1769480 | tf_op jit(solution)/shard_map/ppermute | solution.py:1025
  344.0 16.1 %collective-permute-start.68 = (bf16[1,288,768]{2,1,0:T(8,128)(2,1)S(1)}, bf16[1,288,768]{2,1,0:T(8,128)(2,1)S(1)}, u32[]{:S(2)}, u32[]{:S(2)}) collective-permute-start(bf16[1,288,768]{2,1,0:T(8,128)(2,1)S(1)} %get-tuple-element.755), channel_id=1, source_target_pairs={{0,8},{2,10},{4,12},{6,14},{8,0},{10,2},{12,4},{14,6},{16,24},{18,... | collective-permute-start | bytes 1327112 | tf_op jit(solution)/shard_map/ppermute | solution.py:1025
  348.2 17.1 %collective-permute-start.67 = (bf16[1,384,768]{2,1,0:T(8,128)(2,1)S(1)}, bf16[1,384,768]{2,1,0:T(8,128)(2,1)S(1)}, u32[]{:S(2)}, u32[]{:S(2)}) collective-permute-start(bf16[1,384,768]{2,1,0:T(8,128)(2,1)S(1)} %get-tuple-element.758), channel_id=1, source_target_pairs={{0,4},{2,6},{4,0},{6,2},{8,12},{10,14},{12,8},{14,10},{16,20},{18,... | collective-permute-start | bytes 1769480 | tf_op jit(solution)/shard_map/ppermute | solution.py:1025
  360.2 20.4 %collective-permute-start.71 = (bf16[288,768]{1,0:T(8,128)(2,1)S(1)}, bf16[288,768]{1,0:T(8,128)(2,1)S(1)}, u32[]{:S(2)}, u32[]{:S(2)}) collective-permute-start(bf16[288,768]{1,0:T(8,128)(2,1)S(1)} %add_convert_fusion.1), channel_id=1, source_target_pairs={{0,16},{2,18},{4,20},{6,22},{8,24},{10,26},{12,28},{14,30},{16,0},... | collective-permute-start | bytes 1327112 | tf_op jit(solution)/shard_map/ppermute | solution.py:1025
  365.4 15.3 %collective-permute-start.76 = (bf16[1,192,768]{2,1,0:T(8,128)(2,1)S(1)}, bf16[1,192,768]{2,1,0:T(8,128)(2,1)S(1)}, u32[]{:S(2)}, u32[]{:S(2)}) collective-permute-start(bf16[1,192,768]{2,1,0:T(8,128)(2,1)S(1)} %get-tuple-element.780), channel_id=1, source_target_pairs={{0,8},{2,10},{4,12},{6,14},{8,0},{10,2},{12,4},{14,6},{16,24},{18,... | collective-permute-start | bytes 884744 | tf_op jit(solution)/shard_map/ppermute | solution.py:1025
  385.0 19.1 %collective-permute-start.73 = (bf16[288,768]{1,0:T(8,128)(2,1)S(1)}, bf16[288,768]{1,0:T(8,128)(2,1)S(1)}, u32[]{:S(2)}, u32[]{:S(2)}) collective-permute-start(bf16[288,768]{1,0:T(8,128)(2,1)S(1)} %add_convert_fusion.own_ref), channel_id=1, source_target_pairs={{0,8},{2,10},{4,12},{6,14},{8,0},{10,2},{12,4},{14,6},{16,24},{18,... | collective-permute-start | bytes 1327112 | tf_op jit(solution)/shard_map/ppermute | solution.py:1025
  385.5 18.5 %collective-permute-start.74 = (bf16[1,96,768]{2,1,0:T(8,128)(2,1)S(1)}, bf16[1,96,768]{2,1,0:T(8,128)(2,1)S(1)}, u32[]{:S(2)}, u32[]{:S(2)}) collective-permute-start(bf16[1,96,768]{2,1,0:T(8,128)(2,1)S(1)} %get-tuple-element.789), channel_id=1, source_target_pairs={{0,8},{2,10},{4,12},{6,14},{8,0},{10,2},{12,4},{14,6},{16,24},{18,... | collective-permute-start | bytes 442376 | tf_op jit(solution)/shard_map/ppermute | solution.py:1025
  404.1 57.9 %collective-permute-start.84 = (bf16[576,768]{1,0:T(8,128)(2,1)S(1)}, bf16[576,768]{1,0:T(8,128)(2,1)S(1)}, u32[]{:S(2)}, u32[]{:S(2)}) collective-permute-start(bf16[576,768]{1,0:T(8,128)(2,1)S(1)} %bitcast.128), channel_id=1, source_target_pairs={{0,4},{2,6},{4,0},{6,2},{8,12},{10,14},{12,8},{14,10},{16,20},{18,... | collective-permute-start | bytes 2654216 | tf_op jit(solution)/shard_map/ppermute | solution.py:1025
  404.2 16.1 %collective-permute-start.80 = (bf16[1,96,768]{2,1,0:T(8,128)(2,1)S(1)}, bf16[1,96,768]{2,1,0:T(8,128)(2,1)S(1)}, u32[]{:S(2)}, u32[]{:S(2)}) collective-permute-start(bf16[1,96,768]{2,1,0:T(8,128)(2,1)S(1)} %get-tuple-element.799), channel_id=1, source_target_pairs={{0,8},{2,10},{4,12},{6,14},{8,0},{10,2},{12,4},{14,6},{16,24},{18,... | collective-permute-start | bytes 442376 | tf_op jit(solution)/shard_map/ppermute | solution.py:1025
  404.3 15.9 %collective-permute-start.70 = (f32[32,768]{1,0:T(8,128)S(1)}, f32[32,768]{1,0:T(8,128)S(1)}, u32[]{:S(2)}, u32[]{:S(2)}) collective-permute-start(f32[32,768]{1,0:T(8,128)S(1)} %add.90), channel_id=1, source_target_pairs={{0,2},{2,0},{4,6},{6,4},{8,10},{10,8},{12,14},{14,12},{16,18},{18,... | collective-permute-start | bytes 294920 | tf_op jit(solution)/shard_map/ppermute | solution.py:1025
  415.6 37.6 %collective-permute-start.79 = (bf16[192,768]{1,0:T(8,128)(2,1)S(1)}, bf16[192,768]{1,0:T(8,128)(2,1)S(1)}, u32[]{:S(2)}, u32[]{:S(2)}) collective-permute-start(bf16[192,768]{1,0:T(8,128)(2,1)S(1)} %add_convert_fusion.3), channel_id=1, source_target_pairs={{0,16},{2,18},{4,20},{6,22},{8,24},{10,26},{12,28},{14,30},{16,0},... | collective-permute-start | bytes 884744 | tf_op jit(solution)/shard_map/ppermute | solution.py:1025
  420.1 41.8 %collective-permute-start.78 = (bf16[96,768]{1,0:T(8,128)(2,1)S(1)}, bf16[96,768]{1,0:T(8,128)(2,1)S(1)}, u32[]{:S(2)}, u32[]{:S(2)}) collective-permute-start(bf16[96,768]{1,0:T(8,128)(2,1)S(1)} %add_convert_fusion.7), channel_id=1, source_target_pairs={{0,16},{2,18},{4,20},{6,22},{8,24},{10,26},{12,28},{14,30},{16,0},... | collective-permute-start | bytes 442376 | tf_op jit(solution)/shard_map/ppermute | solution.py:1025
  420.2 41.8 %collective-permute-start.77 = (f32[32,768]{1,0:T(8,128)S(1)}, f32[32,768]{1,0:T(8,128)S(1)}, u32[]{:S(2)}, u32[]{:S(2)}) collective-permute-start(f32[32,768]{1,0:T(8,128)S(1)} %add.94), channel_id=1, source_target_pairs={{0,8},{2,10},{4,12},{6,14},{8,0},{10,2},{12,4},{14,6},{16,24},{18,... | collective-permute-start | bytes 294920 | tf_op jit(solution)/shard_map/ppermute | solution.py:1025
  420.3 51.5 %collective-permute-start.83 = (bf16[96,768]{1,0:T(8,128)(2,1)S(1)}, bf16[96,768]{1,0:T(8,128)(2,1)S(1)}, u32[]{:S(2)}, u32[]{:S(2)}) collective-permute-start(bf16[96,768]{1,0:T(8,128)(2,1)S(1)} %add_convert_fusion.6), channel_id=1, source_target_pairs={{0,16},{2,18},{4,20},{6,22},{8,24},{10,26},{12,28},{14,30},{16,0},... | collective-permute-start | bytes 442376 | tf_op jit(solution)/shard_map/ppermute | solution.py:1025
  453.3 24.8 %collective-permute-start.82 = (bf16[192,768]{1,0:T(8,128)(2,1)S(1)}, bf16[192,768]{1,0:T(8,128)(2,1)S(1)}, u32[]{:S(2)}, u32[]{:S(2)}) collective-permute-start(bf16[192,768]{1,0:T(8,128)(2,1)S(1)} %add_convert_fusion.2.own_ref), channel_id=1, source_target_pairs={{0,8},{2,10},{4,12},{6,14},{8,0},{10,2},{12,4},{14,6},{16,24},{18,... | collective-permute-start | bytes 884744 | tf_op jit(solution)/shard_map/ppermute | solution.py:1025
  478.2 14.7 %collective-permute-start.86 = (bf16[2304,768]{1,0:T(8,128)(2,1)}, bf16[2304,768]{1,0:T(8,128)(2,1)S(1)}, u32[]{:S(2)}, u32[]{:S(2)}) collective-permute-start(bf16[2304,768]{1,0:T(8,128)(2,1)} %all-gather.2.cloned.1.call-done), channel_id=1, source_target_pairs={{0,2},{2,0},{4,6},{6,4},{8,10},{10,8},{12,14},{14,12},{16,18},{18,... | collective-permute-start | bytes 10616840 | tf_op jit(solution)/shard_map/ppermute | solution.py:1025
  478.8 23.6 %collective-permute-start.91 = (bf16[384,768]{1,0:T(8,128)(2,1)S(1)}, bf16[384,768]{1,0:T(8,128)(2,1)S(1)}, u32[]{:S(2)}, u32[]{:S(2)}) collective-permute-start(bf16[384,768]{1,0:T(8,128)(2,1)S(1)} %bitcast.131), channel_id=1, source_target_pairs={{0,4},{2,6},{4,0},{6,2},{8,12},{10,14},{12,8},{14,10},{16,20},{18,... | collective-permute-start | bytes 1769480 | tf_op jit(solution)/shard_map/ppermute | solution.py:1025
  488.1 14.3 %collective-permute-start.85 = (f32[32,768]{1,0:T(8,128)S(1)}, f32[32,768]{1,0:T(8,128)S(1)}, u32[]{:S(2)}, u32[]{:S(2)}) collective-permute-start(f32[32,768]{1,0:T(8,128)S(1)} %add.100), channel_id=1, source_target_pairs={{0,4},{2,6},{4,0},{6,2},{8,12},{10,14},{12,8},{14,10},{16,20},{18,... | collective-permute-start | bytes 294920 | tf_op jit(solution)/shard_map/ppermute | solution.py:1025
  504.3 13.6 %collective-permute-start.90 = (bf16[192,768]{1,0:T(8,128)(2,1)S(1)}, bf16[192,768]{1,0:T(8,128)(2,1)S(1)}, u32[]{:S(2)}, u32[]{:S(2)}) collective-permute-start(bf16[192,768]{1,0:T(8,128)(2,1)S(1)} %bitcast.148), channel_id=1, source_target_pairs={{0,4},{2,6},{4,0},{6,2},{8,12},{10,14},{12,8},{14,10},{16,20},{18,... | collective-permute-start | bytes 884744 | tf_op jit(solution)/shard_map/ppermute | solution.py:1025
  (149 other events, 957.9 us)
Sparse Core Ops, SparseCore 0:
  261.1 89.4 reduce-scatter.1
  381.0 94.2 all-gather.1

commit v7 on v6

--- a/solution.py
+++ b/solution.py
@@ -772,7 +772,7 @@
         core,
         (2,),
         [
-            (far(left), pl.BlockSpec((rows, width), lambda g, core: (0, g * 2 + core[0] if direct else g))),
+            (left, pl.BlockSpec((rows, width), lambda g, core: (0, g * 2 + core[0] if direct else g))),
             (right, pl.BlockSpec((rows, width), lambda g, core: (0, 0))),
         ],
         quarters(rows, width, part // 2),
@@ -932,7 +932,7 @@
         place = layer if kind == "down" else 0
         shape = (2 if kind == "down" else 1, 2 * rows, columns)
         out = (shape, full, pl.BlockSpec((1, rows, columns), lambda g, core: (place, g, 0)))
-        return picked(body, core, (2,), ins, [out], "finish_rows", 3, aliases)
+        return picked(body, core, (2,), ins, [out], "finish_rows", 0, aliases)
     steps = 4 if half is None else 2
     rows = rows // 2 if half is None else rows
 
@@ -965,7 +965,7 @@
 
     if kind == "up":
         outs = [((2, rows, 4 * columns), full, pl.BlockSpec((1, rows, columns), lambda g, core: (layer, 0, block(g))))]
-        return picked(body, core, (steps,), ins, outs, "finish_columns", 3, aliases)
+        return picked(body, core, (steps,), ins, outs, "finish_columns", 0, aliases)
 
     def spot(step):
         return block(step if half == 0 else jnp.minimum(step, steps - 2))
@@ -977,8 +977,8 @@
     if half == 0:
         kept = targets[1:]
         ins, outs, aliases = ins[:3] if targets else ins, outs[:1], {2: 0} if targets else {}
-        return (picked(body, core, (steps,), ins, outs, "finish_qkv", 3, aliases)[0], *kept)
-    return picked(body, core, (steps,), ins, outs, "finish_qkv_out", 3, aliases)
+        return (picked(body, core, (steps,), ins, outs, "finish_qkv", 0, aliases)[0], *kept)
+    return picked(body, core, (steps,), ins, outs, "finish_qkv_out", 0, aliases)
 
 
 def small_gradients(total, me, width, shares, blocks):

time: 541 us -> 536 us (level)
  Pallas kernels: 249 us -> 243 us
    pallas_call x49, Pallas kernels: 82.5 us -> 76.7 us  [picked(): pl.pallas_call(body, grid_spec=pltpu.PrefetchScalarGridSpec(num_scalar_pr...]
    unnamed x204 -> x208, local copies, waits for them, and re-layouts: 31 us -> 32.5 us
where the time goes in v7:
time: 536 us; the launch traced here: 526 us
  Pallas kernels  243 us (45%)
  waiting for transfers between devices  128 us (24%)
  starting transfers between devices  89 us (17%)
  local copies, waits for them, and re-layouts  45.8 us (9%)
  between operations  15.9 us (3%)
    pallas_call x13, Pallas kernels, call(): pl.pallas_call(body, grid=grid, in_specs=[spec for _, spec in ins], out_s...  158 us
    ppermute x96, waiting for transfers between devices, swap(): lax.ppermute(values, axis, [(source, source ^ mask) for source in range(s...  128 us
    ppermute x96, starting transfers between devices, swap(): lax.ppermute(values, axis, [(source, source ^ mask) for source in range(s...  88.9 us
    pallas_call x49, Pallas kernels, picked(): pl.pallas_call(body, grid_spec=pltpu.PrefetchScalarGridSpec(num_scalar_pr...  76.7 us
    unnamed x208, local copies, waits for them, and re-layouts  32.5 us
  transfers between devices with their start and end apart: 98, of which 31 were waited for; matrix products, arithmetic and copies ran while one was open for 3% of the time, Pallas kernels for 40%

profile of v7, /device:TPU:1, one launch (start us, length us, event | category | flops | bytes accessed | tf_op | source)
XLA Modules:
  0.0 526.2 jit_solution(8433965090244104908)
XLA Ops:
  34.9 5.9 %collective-permute-done.1.refs_3_ = bf16[1,96,2304]{2,1,0:T(8,128)(2,1)} collective-permute-done((bf16[1,96,2304]{2,1,0:T(8,128)(2,1)}, bf16[1,96,2304]{2,1,0:T(8,128)(2,1)}, u32[]{:S(2)}, u32[]{:S(2)}) %collective-permute-start.1) | collective-permute-done | bytes 442400 | tf_op jit(solution)/shard_map/ppermute | solution.py:1025
  40.8 3.0 collective-permute-start.3
  48.1 5.1 project_qkv.1
  54.7 8.7 %attend.2 = (bf16[2,336,768]{2,1,0:T(8,128)(2,1)S(1)}, f32[2,6,8,336]{3,2,1,0:T(8,128)S(1)}) custom-call(s32[2]{0:T(128)S(1)} %multiply_add_fusion.length_ref.refs_23_, bf16[3,2,336,768]{3,2,1,0:T(8,128)(2,1)S(1)} %bitcast.170, bf16[3,2,336,768]{3,2,1,0:T(8,128)(2,1)S(1)} %bitcast.171, bf16[3,2,336,768]{3,2,1,0:T(8,128)(2,1)S(1)} %bitcast.172), custom_call_target="tpu_custom_call" | custom-call | flops 3000000000 | tf_op jit(solution)/shard_map/attend/pallas_call | solution.py:69
  75.0 20.6 %feed_forward.2 = (f32[672,768]{1,0:T(8,128)S(1)}, bf16[672,768]{1,0:T(8,128)(2,1)S(1)}, bf16[672,3072]{1,0:T(8,128)(2,1)S(1)}, bf16[672,3072]{1,0:T(8,128)(2,1)}, bf16[672,768]{1,0:T(8,128)(2,1)S(1)}) custom-call(s32[2]{0:T(128)S(1)} %pad_add_fusion.refs_0_, bf16[2,384,768]{2,1,0:T(8,128)(2,1)} %refs_11_.7, bf16[1,96,3840]{2,1,0:T(8,128)(2,1)} %copy-done.72, ...), custom_call_target="tpu_custom_call" | custom-call | flops 6899999744 | tf_op jit(solution)/shard_map/feed_forward/pallas_call | solution.py:69
  97.5 2.5 collective-permute-done.6.refs_2_.refs_7_.refs_12_
  104.0 8.2 %join_qkv.1 = (f32[672,768]{1,0:T(8,128)S(1)}, bf16[672,768]{1,0:T(8,128)(2,1)S(1)}, bf16[3,672,768]{2,1,0:T(8,128)(2,1)S(1)}) custom-call(s32[2]{0:T(128)S(1)} %pad_add_fusion.refs_0_, bf16[768,768]{1,0:T(8,128)(2,1)} %refs_6_.10, bf16[1,192,768]{2,1,0:T(8,128)(2,1)} %copy-done.96, bf16[1,192,768]{2,1,0:T(8,128)(2,1)} %copy-done.97, ...), custom_call_target="tpu_custom_call" | custom-call | flops 3300000000 | tf_op jit(solution)/shard_map/join_qkv/pallas_call | solution.py:69
  112.3 8.7 %attend.3 = (bf16[2,336,768]{2,1,0:T(8,128)(2,1)S(1)}, f32[2,6,8,336]{3,2,1,0:T(8,128)S(1)}) custom-call(s32[2]{0:T(128)S(1)} %multiply_add_fusion.length_ref.refs_23_, bf16[3,2,336,768]{3,2,1,0:T(8,128)(2,1)S(1)} %bitcast.176, bf16[3,2,336,768]{3,2,1,0:T(8,128)(2,1)S(1)} %bitcast.177, bf16[3,2,336,768]{3,2,1,0:T(8,128)(2,1)S(1)} %bitcast.178), custom_call_target="tpu_custom_call" | custom-call | flops 3000000000 | tf_op jit(solution)/shard_map/attend/pallas_call | solution.py:69
  122.4 3.1 collective-permute-done.27.refs_14_.refs_4_
  128.3 21.0 %feed_forward.3 = (f32[672,768]{1,0:T(8,128)S(1)}, bf16[672,768]{1,0:T(8,128)(2,1)S(1)}, bf16[672,3072]{1,0:T(8,128)(2,1)S(1)}, bf16[672,3072]{1,0:T(8,128)(2,1)}, bf16[672,768]{1,0:T(8,128)(2,1)}) custom-call(s32[2]{0:T(128)S(1)} %pad_add_fusion.refs_0_, bf16[2,384,768]{2,1,0:T(8,128)(2,1)} %refs_11_.7, bf16[1,96,3840]{2,1,0:T(8,128)(2,1)} %copy-done.76, ...), custom_call_target="tpu_custom_call" | custom-call | flops 6899999744 | tf_op jit(solution)/shard_map/feed_forward/pallas_call | solution.py:69
  150.7 4.1 down_term.4
  158.0 3.1 down_term.5
  164.9 18.3 %feed_forward_back.2 = (bf16[672,3072]{1,0:T(8,128)(2,1)}, f32[672,768]{1,0:T(8,128)S(1)}, bf16[672,768]{1,0:T(8,128)(2,1)S(1)}, bf16[672,768]{1,0:T(8,128)(2,1)S(1)}, f32[8,768]{1,0:T(8,128)S(1)}) custom-call(s32[2]{0:T(128)S(1)} %pad_add_fusion.refs_0_, bf16[2,1536,768]{2,1,0:T(8,128)(2,1)} %refs_1_.15, bf16[1,384,768]{2,1,0:T(8,128)(2,1)} %copy-done.86, ...), custom_call_target="tpu_custom_call" | custom-call | flops 6300000256 | tf_op jit(solution)/shard_map/feed_forward_back/pallas_call | solution.py:69
  183.2 4.6 up_term.4
  189.1 3.8 up_term.5
  197.2 2.7 add_into.3.rest_0_
  201.2 13.9 %attend_back.2 = bf16[3,2,336,768]{3,2,1,0:T(8,128)(2,1)S(1)} custom-call(s32[2]{0:T(128)S(1)} %multiply_add_fusion.length_ref.refs_23_, bf16[3,2,336,768]{3,2,1,0:T(8,128)(2,1)S(1)} %bitcast.179, bf16[3,2,336,768]{3,2,1,0:T(8,128)(2,1)S(1)} %bitcast.180, bf16[3,2,336,768]{3,2,1,0:T(8,128)(2,1)S(1)} %bitcast.181, bf16[2,336,768]{2,1,0:T(8,128)(2,1)S(1)} %bitcast.157, ...), custom_call_target="tpu_custom_call" | custom-call | flops 4499999744 | tf_op jit(solution)/shard_map/attend_back/pallas_call | solution.py:69
  215.2 2.6 qkv_out_term.4
  225.9 2.7 add_into.4.rest_0_
  230.2 11.9 %project_back.2 = (bf16[672,768]{1,0:T(8,128)(2,1)S(1)}, f32[672,768]{1,0:T(8,128)S(1)}, bf16[672,768]{1,0:T(8,128)(2,1)S(1)}, f32[672,768]{1,0:T(8,128)}, f32[8,768]{1,0:T(8,128)S(1)}) custom-call(s32[2]{0:T(128)S(1)} %pad_add_fusion.refs_0_, bf16[2,384,2304]{2,1,0:T(8,128)(2,1)} %refs_1_.16, bf16[1,96,2304]{2,1,0:T(8,128)(2,1)} %collective-permute-done.10.refs_7_.refs_2_, ...), custom_call_target="tpu_custom_call" | custom-call | flops 3900000000 | tf_op jit(solution)/shard_map/project_back/pallas_call | solution.py:69
  248.6 2.7 down_term.6
  251.3 2.7 down_term.7
  254.1 2.6 add_into.5
  265.7 19.6 %feed_forward_back.3 = (bf16[672,3072]{1,0:T(8,128)(2,1)}, f32[672,768]{1,0:T(8,128)S(1)}, bf16[672,768]{1,0:T(8,128)(2,1)S(1)}, bf16[672,768]{1,0:T(8,128)(2,1)S(1)}, f32[8,768]{1,0:T(8,128)S(1)}) custom-call(s32[2]{0:T(128)S(1)} %pad_add_fusion.refs_0_, bf16[2,1536,768]{2,1,0:T(8,128)(2,1)} %refs_1_.15, bf16[1,384,768]{2,1,0:T(8,128)(2,1)} %copy-done.82, ...), custom_call_target="tpu_custom_call" | custom-call | flops 6300000256 | tf_op jit(solution)/shard_map/feed_forward_back/pallas_call | solution.py:69
  287.3 3.8 up_term.6
  292.7 3.8 up_term.7
  296.4 5.2 collective-permute-done.57
  307.4 13.9 %attend_back.3 = bf16[3,2,336,768]{3,2,1,0:T(8,128)(2,1)S(1)} custom-call(s32[2]{0:T(128)S(1)} %multiply_add_fusion.length_ref.refs_23_, bf16[3,2,336,768]{3,2,1,0:T(8,128)(2,1)S(1)} %bitcast.173, bf16[3,2,336,768]{3,2,1,0:T(8,128)(2,1)S(1)} %bitcast.174, bf16[3,2,336,768]{3,2,1,0:T(8,128)(2,1)S(1)} %bitcast.175, bf16[2,336,768]{2,1,0:T(8,128)(2,1)S(1)} %bitcast.156, ...), custom_call_target="tpu_custom_call" | custom-call | flops 4499999744 | tf_op jit(solution)/shard_map/attend_back/pallas_call | solution.py:69
  321.4 3.6 qkv_out_term.6
  339.7 2.7 collective-permute-start.68
  344.0 8.4 %project_back.3 = (f32[672,768]{1,0:T(8,128)}, f32[8,768]{1,0:T(8,128)S(1)}) custom-call(s32[2]{0:T(128)S(1)} %pad_add_fusion.refs_0_, bf16[2,384,2304]{2,1,0:T(8,128)(2,1)} %refs_1_.16, bf16[1,96,2304]{2,1,0:T(8,128)(2,1)} %collective-permute-done.refs_2_, bf16[1,96,2304]{2,1,0:T(8,128)(2,1)} %collective-permute-done.1.refs_3_, ...), custom_call_target="tpu_custom_call" | custom-call | flops 2700000000 | tf_op jit(solution)/shard_map/project_back/pallas_call | solution.py:69
  355.8 2.6 collective-permute-start.71
  363.1 3.9 collective-permute-done.66
  369.3 7.0 %collective-permute-done.71 = bf16[288,768]{1,0:T(8,128)(2,1)S(1)} collective-permute-done((bf16[288,768]{1,0:T(8,128)(2,1)S(1)}, bf16[288,768]{1,0:T(8,128)(2,1)S(1)}, u32[]{:S(2)}, u32[]{:S(2)}) %collective-permute-start.71) | collective-permute-done | bytes 442400 | tf_op jit(solution)/shard_map/ppermute | solution.py:1025
  376.6 4.1 collective-permute-start.75
  382.1 4.7 collective-permute-done.75
  386.9 12.9 %collective-permute-done.74 = bf16[1,96,768]{2,1,0:T(8,128)(2,1)S(1)} collective-permute-done((bf16[1,96,768]{2,1,0:T(8,128)(2,1)S(1)}, bf16[1,96,768]{2,1,0:T(8,128)(2,1)S(1)}, u32[]{:S(2)}, u32[]{:S(2)}) %collective-permute-start.74) | collective-permute-done | bytes 147488 | tf_op jit(solution)/shard_map/ppermute | solution.py:1025
  400.1 11.2 %collective-permute-start.70 = (f32[32,768]{1,0:T(8,128)S(1)}, f32[32,768]{1,0:T(8,128)S(1)}, u32[]{:S(2)}, u32[]{:S(2)}) collective-permute-start(f32[32,768]{1,0:T(8,128)S(1)} %add.90), channel_id=1, source_target_pairs={{0,2},{2,0},{4,6},{6,4},{8,10},{10,8},{12,14},{14,12},{16,18},{18,... | collective-permute-start | bytes 294920 | tf_op jit(solution)/shard_map/ppermute | solution.py:1025
  411.3 4.5 collective-permute-start.79
  418.3 30.5 %collective-permute-done.79 = bf16[192,768]{1,0:T(8,128)(2,1)S(1)} collective-permute-done((bf16[192,768]{1,0:T(8,128)(2,1)S(1)}, bf16[192,768]{1,0:T(8,128)(2,1)S(1)}, u32[]{:S(2)}, u32[]{:S(2)}) %collective-permute-start.79) | collective-permute-done | bytes 294944 | tf_op jit(solution)/shard_map/ppermute | solution.py:1025
  449.0 8.6 %collective-permute-done.78 = bf16[96,768]{1,0:T(8,128)(2,1)S(1)} collective-permute-done((bf16[96,768]{1,0:T(8,128)(2,1)S(1)}, bf16[96,768]{1,0:T(8,128)(2,1)S(1)}, u32[]{:S(2)}, u32[]{:S(2)}) %collective-permute-start.78) | collective-permute-done | bytes 147488 | tf_op jit(solution)/shard_map/ppermute | solution.py:1025
  457.8 9.7 %collective-permute-done.83 = bf16[96,768]{1,0:T(8,128)(2,1)S(1)} collective-permute-done((bf16[96,768]{1,0:T(8,128)(2,1)S(1)}, bf16[96,768]{1,0:T(8,128)(2,1)S(1)}, u32[]{:S(2)}, u32[]{:S(2)}) %collective-permute-start.83) | collective-permute-done | bytes 147488 | tf_op jit(solution)/shard_map/ppermute | solution.py:1025
  467.5 6.3 %collective-permute-done.82.got_ref = bf16[192,768]{1,0:T(8,128)(2,1)S(1)} collective-permute-done((bf16[192,768]{1,0:T(8,128)(2,1)S(1)}, bf16[192,768]{1,0:T(8,128)(2,1)S(1)}, u32[]{:S(2)}, u32[]{:S(2)}) %collective-permute-start.82) | collective-permute-done | bytes 294944 | tf_op jit(solution)/shard_map/ppermute | solution.py:1025
  478.5 5.1 collective-permute-done.81
  492.0 2.6 finish_columns.2.rest_0_
  494.6 3.3 finish_qkv_out.2
  500.0 7.1 %collective-permute-done.93.got_ref = bf16[192,768]{1,0:T(8,128)(2,1)S(1)} collective-permute-done((bf16[192,768]{1,0:T(8,128)(2,1)S(1)}, bf16[192,768]{1,0:T(8,128)(2,1)S(1)}, u32[]{:S(2)}, u32[]{:S(2)}) %collective-permute-start.93) | collective-permute-done | bytes 294944 | tf_op jit(solution)/shard_map/ppermute | solution.py:1025
  508.5 2.6 finish_columns.3
  (458 shorter events, 160.4 us)
Async XLA Ops:
  7.2 369.3 %reduce-scatter.2.cloned.1.call-start = ((), (), s32[]{:S(2)}) async-start(), calls=%async_computation.1 | async-start | bytes 3981312 | tf_op jit(solution)/shard_map/reduce_scatter | solution.py:1311
  8.3 22.6 %collective-permute-start = (bf16[1,96,2304]{2,1,0:T(8,128)(2,1)S(1)}, bf16[1,96,2304]{2,1,0:T(8,128)(2,1)}, u32[]{:S(2)}, u32[]{:S(2)}) collective-permute-start(bf16[1,96,2304]{2,1,0:T(8,128)(2,1)S(1)} %constant_dynamic-slice_fusion.3), channel_id=1, source_target_pairs={{0,1},{1,0},{2,3},{3,2},{4,5},{5,4},{6,7},{7,6},{8,9},{9,8},{10,11... | collective-permute-start | bytes 1327112 | tf_op jit(solution)/shard_map/ppermute | solution.py:1025
  14.5 17.9 %collective-permute-start.4 = (bf16[1,32,384]{2,1,0:T(8,128)(2,1)S(1)}, bf16[1,32,384]{2,1,0:T(8,128)(2,1)S(1)}, u32[]{:S(2)}, u32[]{:S(2)}) collective-permute-start(bf16[1,32,384]{2,1,0:T(8,128)(2,1)S(1)} %convert_bitcast_fusion), channel_id=1, source_target_pairs={{0,1},{1,0},{2,3},{3,2},{4,5},{5,4},{6,7},{7,6},{8,9},{9,8},{10,11... | collective-permute-start | bytes 73736 | tf_op jit(solution)/shard_map/ppermute | solution.py:1025
  17.6 27.6 %collective-permute-start.5 = (bf16[1,96,3840]{2,1,0:T(8,128)(2,1)}, bf16[1,96,3840]{2,1,0:T(8,128)(2,1)S(1)}, u32[]{:S(2)}, u32[]{:S(2)}) collective-permute-start(bf16[1,96,3840]{2,1,0:T(8,128)(2,1)} %maximum_bitcast_fusion), channel_id=1, source_target_pairs={{0,1},{1,0},{2,3},{3,2},{4,5},{5,4},{6,7},{7,6},{8,9},{9,8},{10,11... | collective-permute-start | bytes 2211848 | tf_op jit(solution)/shard_map/ppermute | solution.py:1025
  20.9 32.4 %collective-permute-start.8 = (bf16[1,384,768]{2,1,0:T(8,128)(2,1)}, bf16[1,384,768]{2,1,0:T(8,128)(2,1)S(1)}, u32[]{:S(2)}, u32[]{:S(2)}) collective-permute-start(bf16[1,384,768]{2,1,0:T(8,128)(2,1)} %constant_dynamic-slice_fusion.2), channel_id=1, source_target_pairs={{0,1},{1,0},{2,3},{3,2},{4,5},{5,4},{6,7},{7,6},{8,9},{9,8},{10,11... | collective-permute-start | bytes 1769480 | tf_op jit(solution)/shard_map/ppermute | solution.py:1025
  24.5 40.6 %collective-permute-start.10 = (bf16[1,96,2304]{2,1,0:T(8,128)(2,1)}, bf16[1,96,2304]{2,1,0:T(8,128)(2,1)}, u32[]{:S(2)}, u32[]{:S(2)}) collective-permute-start(bf16[1,96,2304]{2,1,0:T(8,128)(2,1)} %constant_dynamic-slice_fusion.1), channel_id=1, source_target_pairs={{0,1},{1,0},{2,3},{3,2},{4,5},{5,4},{6,7},{7,6},{8,9},{9,8},{10,11... | collective-permute-start | bytes 1327112 | tf_op jit(solution)/shard_map/ppermute | solution.py:1025
  32.5 14.1 %collective-permute-start.2 = (bf16[1,96,2304]{2,1,0:T(8,128)(2,1)}, bf16[1,96,2304]{2,1,0:T(8,128)(2,1)S(1)}, u32[]{:S(2)}, u32[]{:S(2)}) collective-permute-start(bf16[1,96,2304]{2,1,0:T(8,128)(2,1)} %collective-permute-done.refs_2_), channel_id=1, source_target_pairs={{0,2},{2,0},{4,6},{6,4},{8,10},{10,8},{12,14},{14,12},{16,18},{18,... | collective-permute-start | bytes 1327112 | tf_op jit(solution)/shard_map/ppermute | solution.py:1025
  45.2 21.1 %collective-permute-start.7 = (bf16[1,96,3840]{2,1,0:T(8,128)(2,1)S(1)}, bf16[1,96,3840]{2,1,0:T(8,128)(2,1)S(1)}, u32[]{:S(2)}, u32[]{:S(2)}) collective-permute-start(bf16[1,96,3840]{2,1,0:T(8,128)(2,1)S(1)} %collective-permute-done.5.refs_2_.refs_7_.refs_12_), channel_id=1, source_target_pairs={{0,4},{2,6},{4,0},{6,2},{8,12},{10,14},{12,8},{14,10},{16,20},{18,... | collective-permute-start | bytes 2211848 | tf_op jit(solution)/shard_map/ppermute | solution.py:1025
  46.6 18.5 %collective-permute-start.9 = (bf16[1,192,768]{2,1,0:T(8,128)(2,1)}, bf16[1,192,768]{2,1,0:T(8,128)(2,1)S(1)}, u32[]{:S(2)}, u32[]{:S(2)}) collective-permute-start(bf16[1,192,768]{2,1,0:T(8,128)(2,1)} %dynamic-slice_bitcast_fusion.2), channel_id=1, source_target_pairs={{0,1},{1,0},{2,3},{3,2},{4,5},{5,4},{6,7},{7,6},{8,9},{9,8},{10,11... | collective-permute-start | bytes 884744 | tf_op jit(solution)/shard_map/ppermute | solution.py:1025
  53.3 14.7 %collective-permute-start.13 = (bf16[1,384,768]{2,1,0:T(8,128)(2,1)S(1)}, bf16[1,384,768]{2,1,0:T(8,128)(2,1)S(1)}, u32[]{:S(2)}, u32[]{:S(2)}) collective-permute-start(bf16[1,384,768]{2,1,0:T(8,128)(2,1)S(1)} %collective-permute-done.8.refs_12_.refs_2_), channel_id=1, source_target_pairs={{0,8},{2,10},{4,12},{6,14},{8,0},{10,2},{12,4},{14,6},{16,24},{18,... | collective-permute-start | bytes 1769480 | tf_op jit(solution)/shard_map/ppermute | solution.py:1025
  69.2 31.6 %collective-permute-start.23 = (bf16[1,384,768]{2,1,0:T(8,128)(2,1)S(1)}, bf16[1,384,768]{2,1,0:T(8,128)(2,1)S(1)}, u32[]{:S(2)}, u32[]{:S(2)}) collective-permute-start(bf16[1,384,768]{2,1,0:T(8,128)(2,1)S(1)} %copy-done.90), channel_id=1, source_target_pairs={{0,1},{1,0},{2,3},{3,2},{4,5},{5,4},{6,7},{7,6},{8,9},{9,8},{10,11... | collective-permute-start | bytes 1769480 | tf_op jit(solution)/shard_map/ppermute | solution.py:1025
  70.1 29.9 %collective-permute-start.6 = (bf16[1,96,3840]{2,1,0:T(8,128)(2,1)S(1)}, bf16[1,96,3840]{2,1,0:T(8,128)(2,1)S(1)}, u32[]{:S(2)}, u32[]{:S(2)}) collective-permute-start(bf16[1,96,3840]{2,1,0:T(8,128)(2,1)S(1)} %copy-done.81), channel_id=1, source_target_pairs={{0,1},{1,0},{2,3},{3,2},{4,5},{5,4},{6,7},{7,6},{8,9},{9,8},{10,11... | collective-permute-start | bytes 2211848 | tf_op jit(solution)/shard_map/ppermute | solution.py:1025
  71.6 24.1 %collective-permute-start.20 = (bf16[1,96,2304]{2,1,0:T(8,128)(2,1)}, bf16[1,96,2304]{2,1,0:T(8,128)(2,1)S(1)}, u32[]{:S(2)}, u32[]{:S(2)}) collective-permute-start(bf16[1,96,2304]{2,1,0:T(8,128)(2,1)} %collective-permute-done.10.refs_7_.refs_2_), channel_id=1, source_target_pairs={{0,4},{2,6},{4,0},{6,2},{8,12},{10,14},{12,8},{14,10},{16,20},{18,... | collective-permute-start | bytes 1327112 | tf_op jit(solution)/shard_map/ppermute | solution.py:1025
  72.8 24.2 %collective-permute-start.17 = (bf16[1,192,768]{2,1,0:T(8,128)(2,1)S(1)}, bf16[1,192,768]{2,1,0:T(8,128)(2,1)S(1)}, u32[]{:S(2)}, u32[]{:S(2)}) collective-permute-start(bf16[1,192,768]{2,1,0:T(8,128)(2,1)S(1)} %collective-permute-done.9.refs_2_.refs_7_), channel_id=1, source_target_pairs={{0,8},{2,10},{4,12},{6,14},{8,0},{10,2},{12,4},{14,6},{16,24},{18,... | collective-permute-start | bytes 884744 | tf_op jit(solution)/shard_map/ppermute | solution.py:1025
  100.8 20.9 %collective-permute-start.16 = (bf16[1,96,3840]{2,1,0:T(8,128)(2,1)S(1)}, bf16[1,96,3840]{2,1,0:T(8,128)(2,1)S(1)}, u32[]{:S(2)}, u32[]{:S(2)}) collective-permute-start(bf16[1,96,3840]{2,1,0:T(8,128)(2,1)S(1)} %collective-permute-done.6.refs_2_.refs_7_.refs_12_), channel_id=1, source_target_pairs={{0,4},{2,6},{4,0},{6,2},{8,12},{10,14},{12,8},{14,10},{16,20},{18,... | collective-permute-start | bytes 2211848 | tf_op jit(solution)/shard_map/ppermute | solution.py:1025
  101.1 21.2 %collective-permute-start.26 = (bf16[1,384,768]{2,1,0:T(8,128)(2,1)S(1)}, bf16[1,384,768]{2,1,0:T(8,128)(2,1)S(1)}, u32[]{:S(2)}, u32[]{:S(2)}) collective-permute-start(bf16[1,384,768]{2,1,0:T(8,128)(2,1)S(1)} %collective-permute-done.23.refs_12_.refs_2_), channel_id=1, source_target_pairs={{0,8},{2,10},{4,12},{6,14},{8,0},{10,2},{12,4},{14,6},{16,24},{18,... | collective-permute-start | bytes 1769480 | tf_op jit(solution)/shard_map/ppermute | solution.py:1025
  164.1 32.1 %collective-permute-start.33 = (bf16[2,384,768]{2,1,0:T(8,128)(2,1)S(1)}, bf16[2,384,768]{2,1,0:T(8,128)(2,1)S(1)}, u32[]{:S(2)}, u32[]{:S(2)}) collective-permute-start(bf16[2,384,768]{2,1,0:T(8,128)(2,1)S(1)} %get-tuple-element.551), channel_id=1, source_target_pairs={{0,1},{1,0},{2,3},{3,2},{4,5},{5,4},{6,7},{7,6},{8,9},{9,8},{10,11... | collective-permute-start | bytes 3538952 | tf_op jit(solution)/shard_map/ppermute | solution.py:1025
  195.5 30.4 %collective-permute-start.38 = (bf16[2,384,768]{2,1,0:T(8,128)(2,1)}, bf16[2,384,768]{2,1,0:T(8,128)(2,1)}, u32[]{:S(2)}, u32[]{:S(2)}) collective-permute-start(bf16[2,384,768]{2,1,0:T(8,128)(2,1)} %get-tuple-element.582), channel_id=1, source_target_pairs={{0,1},{1,0},{2,3},{3,2},{4,5},{5,4},{6,7},{7,6},{8,9},{9,8},{10,11... | collective-permute-start | bytes 3538952 | tf_op jit(solution)/shard_map/ppermute | solution.py:1025
  225.1 28.9 %collective-permute-start.51 = (bf16[2,384,768]{2,1,0:T(8,128)(2,1)}, bf16[2,384,768]{2,1,0:T(8,128)(2,1)}, u32[]{:S(2)}, u32[]{:S(2)}) collective-permute-start(bf16[2,384,768]{2,1,0:T(8,128)(2,1)} %get-tuple-element.617), channel_id=1, source_target_pairs={{0,1},{1,0},{2,3},{3,2},{4,5},{5,4},{6,7},{7,6},{8,9},{9,8},{10,11... | collective-permute-start | bytes 3538952 | tf_op jit(solution)/shard_map/ppermute | solution.py:1025
  256.7 217.1 %all-gather.2.cloned.1.call-start = ((), (), s32[]{:S(2)}) async-start(), calls=%async_computation.2 | async-start | bytes 3981312 | tf_op jit(solution)/shard_map/all_gather | solution.py:1365
  263.7 37.9 %collective-permute-start.57 = (bf16[2,384,768]{2,1,0:T(8,128)(2,1)S(1)}, bf16[2,384,768]{2,1,0:T(8,128)(2,1)S(1)}, u32[]{:S(2)}, u32[]{:S(2)}) collective-permute-start(bf16[2,384,768]{2,1,0:T(8,128)(2,1)S(1)} %get-tuple-element.677), channel_id=1, source_target_pairs={{0,4},{2,6},{4,0},{6,2},{8,12},{10,14},{12,8},{14,10},{16,20},{18,... | collective-permute-start | bytes 3538952 | tf_op jit(solution)/shard_map/ppermute | solution.py:1025
  265.0 20.3 %collective-permute-start.52 = (bf16[2,192,768]{2,1,0:T(8,128)(2,1)S(1)}, bf16[2,192,768]{2,1,0:T(8,128)(2,1)S(1)}, u32[]{:S(2)}, u32[]{:S(2)}) collective-permute-start(bf16[2,192,768]{2,1,0:T(8,128)(2,1)S(1)} %copy-done.52), channel_id=1, source_target_pairs={{0,1},{1,0},{2,3},{3,2},{4,5},{5,4},{6,7},{7,6},{8,9},{9,8},{10,11... | collective-permute-start | bytes 1769480 | tf_op jit(solution)/shard_map/ppermute | solution.py:1025
  292.1 12.4 %collective-permute-start.54 = (bf16[384,768]{1,0:T(8,128)(2,1)S(1)}, bf16[384,768]{1,0:T(8,128)(2,1)S(1)}, u32[]{:S(2)}, u32[]{:S(2)}) collective-permute-start(bf16[384,768]{1,0:T(8,128)(2,1)S(1)} %get-tuple-element.700), channel_id=1, source_target_pairs={{0,2},{2,0},{4,6},{6,4},{8,10},{10,8},{12,14},{14,12},{16,18},{18,... | collective-permute-start | bytes 1769480 | tf_op jit(solution)/shard_map/ppermute | solution.py:1025
  292.2 12.3 %collective-permute-start.55 = (bf16[384,768]{1,0:T(8,128)(2,1)S(1)}, bf16[384,768]{1,0:T(8,128)(2,1)S(1)}, u32[]{:S(2)}, u32[]{:S(2)}) collective-permute-start(bf16[384,768]{1,0:T(8,128)(2,1)S(1)} %get-tuple-element.701), channel_id=1, source_target_pairs={{0,2},{2,0},{4,6},{6,4},{8,10},{10,8},{12,14},{14,12},{16,18},{18,... | collective-permute-start | bytes 1769480 | tf_op jit(solution)/shard_map/ppermute | solution.py:1025
  302.9 18.4 %collective-permute-start.59 = (bf16[1,384,768]{2,1,0:T(8,128)(2,1)S(1)}, bf16[1,384,768]{2,1,0:T(8,128)(2,1)S(1)}, u32[]{:S(2)}, u32[]{:S(2)}) collective-permute-start(bf16[1,384,768]{2,1,0:T(8,128)(2,1)S(1)} %get-tuple-element.706), channel_id=1, source_target_pairs={{0,1},{1,0},{2,3},{3,2},{4,5},{5,4},{6,7},{7,6},{8,9},{9,8},{10,11... | collective-permute-start | bytes 1769480 | tf_op jit(solution)/shard_map/ppermute | solution.py:1025
  302.9 18.4 %collective-permute-start.60 = (bf16[1,192,768]{2,1,0:T(8,128)(2,1)S(1)}, bf16[1,192,768]{2,1,0:T(8,128)(2,1)S(1)}, u32[]{:S(2)}, u32[]{:S(2)}) collective-permute-start(bf16[1,192,768]{2,1,0:T(8,128)(2,1)S(1)} %get-tuple-element.690), channel_id=1, source_target_pairs={{0,4},{2,6},{4,0},{6,2},{8,12},{10,14},{12,8},{14,10},{16,20},{18,... | collective-permute-start | bytes 884744 | tf_op jit(solution)/shard_map/ppermute | solution.py:1025
  307.0 35.4 %collective-permute-start.58 = (bf16[2,384,768]{2,1,0:T(8,128)(2,1)}, bf16[2,384,768]{2,1,0:T(8,128)(2,1)}, u32[]{:S(2)}, u32[]{:S(2)}) collective-permute-start(bf16[2,384,768]{2,1,0:T(8,128)(2,1)} %get-tuple-element.715), channel_id=1, source_target_pairs={{0,1},{1,0},{2,3},{3,2},{4,5},{5,4},{6,7},{7,6},{8,9},{9,8},{10,11... | collective-permute-start | bytes 3538952 | tf_op jit(solution)/shard_map/ppermute | solution.py:1025
  333.3 21.2 %collective-permute-start.69 = (bf16[1,384,768]{2,1,0:T(8,128)(2,1)}, bf16[1,384,768]{2,1,0:T(8,128)(2,1)}, u32[]{:S(2)}, u32[]{:S(2)}) collective-permute-start(bf16[1,384,768]{2,1,0:T(8,128)(2,1)} %get-tuple-element.745), channel_id=1, source_target_pairs={{0,1},{1,0},{2,3},{3,2},{4,5},{5,4},{6,7},{7,6},{8,9},{9,8},{10,11... | collective-permute-start | bytes 1769480 | tf_op jit(solution)/shard_map/ppermute | solution.py:1025
  338.3 28.8 %collective-permute-start.66 = (bf16[1,384,768]{2,1,0:T(8,128)(2,1)S(1)}, bf16[1,384,768]{2,1,0:T(8,128)(2,1)S(1)}, u32[]{:S(2)}, u32[]{:S(2)}) collective-permute-start(bf16[1,384,768]{2,1,0:T(8,128)(2,1)S(1)} %get-tuple-element.750), channel_id=1, source_target_pairs={{0,1},{1,0},{2,3},{3,2},{4,5},{5,4},{6,7},{7,6},{8,9},{9,8},{10,11... | collective-permute-start | bytes 1769480 | tf_op jit(solution)/shard_map/ppermute | solution.py:1025
  339.7 16.0 %collective-permute-start.68 = (bf16[1,288,768]{2,1,0:T(8,128)(2,1)S(1)}, bf16[1,288,768]{2,1,0:T(8,128)(2,1)S(1)}, u32[]{:S(2)}, u32[]{:S(2)}) collective-permute-start(bf16[1,288,768]{2,1,0:T(8,128)(2,1)S(1)} %get-tuple-element.755), channel_id=1, source_target_pairs={{0,8},{2,10},{4,12},{6,14},{8,0},{10,2},{12,4},{14,6},{16,24},{18,... | collective-permute-start | bytes 1327112 | tf_op jit(solution)/shard_map/ppermute | solution.py:1025
  343.9 17.0 %collective-permute-start.67 = (bf16[1,384,768]{2,1,0:T(8,128)(2,1)S(1)}, bf16[1,384,768]{2,1,0:T(8,128)(2,1)S(1)}, u32[]{:S(2)}, u32[]{:S(2)}) collective-permute-start(bf16[1,384,768]{2,1,0:T(8,128)(2,1)S(1)} %get-tuple-element.758), channel_id=1, source_target_pairs={{0,4},{2,6},{4,0},{6,2},{8,12},{10,14},{12,8},{14,10},{16,20},{18,... | collective-permute-start | bytes 1769480 | tf_op jit(solution)/shard_map/ppermute | solution.py:1025
  355.8 20.5 %collective-permute-start.71 = (bf16[288,768]{1,0:T(8,128)(2,1)S(1)}, bf16[288,768]{1,0:T(8,128)(2,1)S(1)}, u32[]{:S(2)}, u32[]{:S(2)}) collective-permute-start(bf16[288,768]{1,0:T(8,128)(2,1)S(1)} %add_convert_fusion.1), channel_id=1, source_target_pairs={{0,16},{2,18},{4,20},{6,22},{8,24},{10,26},{12,28},{14,30},{16,0},... | collective-permute-start | bytes 1327112 | tf_op jit(solution)/shard_map/ppermute | solution.py:1025
  361.1 15.4 %collective-permute-start.76 = (bf16[1,192,768]{2,1,0:T(8,128)(2,1)S(1)}, bf16[1,192,768]{2,1,0:T(8,128)(2,1)S(1)}, u32[]{:S(2)}, u32[]{:S(2)}) collective-permute-start(bf16[1,192,768]{2,1,0:T(8,128)(2,1)S(1)} %get-tuple-element.780), channel_id=1, source_target_pairs={{0,8},{2,10},{4,12},{6,14},{8,0},{10,2},{12,4},{14,6},{16,24},{18,... | collective-permute-start | bytes 884744 | tf_op jit(solution)/shard_map/ppermute | solution.py:1025
  380.6 19.2 %collective-permute-start.73 = (bf16[288,768]{1,0:T(8,128)(2,1)S(1)}, bf16[288,768]{1,0:T(8,128)(2,1)S(1)}, u32[]{:S(2)}, u32[]{:S(2)}) collective-permute-start(bf16[288,768]{1,0:T(8,128)(2,1)S(1)} %add_convert_fusion.own_ref), channel_id=1, source_target_pairs={{0,8},{2,10},{4,12},{6,14},{8,0},{10,2},{12,4},{14,6},{16,24},{18,... | collective-permute-start | bytes 1327112 | tf_op jit(solution)/shard_map/ppermute | solution.py:1025
  381.1 18.8 %collective-permute-start.74 = (bf16[1,96,768]{2,1,0:T(8,128)(2,1)S(1)}, bf16[1,96,768]{2,1,0:T(8,128)(2,1)S(1)}, u32[]{:S(2)}, u32[]{:S(2)}) collective-permute-start(bf16[1,96,768]{2,1,0:T(8,128)(2,1)S(1)} %get-tuple-element.789), channel_id=1, source_target_pairs={{0,8},{2,10},{4,12},{6,14},{8,0},{10,2},{12,4},{14,6},{16,24},{18,... | collective-permute-start | bytes 442376 | tf_op jit(solution)/shard_map/ppermute | solution.py:1025
  399.9 57.7 %collective-permute-start.84 = (bf16[576,768]{1,0:T(8,128)(2,1)S(1)}, bf16[576,768]{1,0:T(8,128)(2,1)S(1)}, u32[]{:S(2)}, u32[]{:S(2)}) collective-permute-start(bf16[576,768]{1,0:T(8,128)(2,1)S(1)} %bitcast.128), channel_id=1, source_target_pairs={{0,4},{2,6},{4,0},{6,2},{8,12},{10,14},{12,8},{14,10},{16,20},{18,... | collective-permute-start | bytes 2654216 | tf_op jit(solution)/shard_map/ppermute | solution.py:1025
  400.0 15.8 %collective-permute-start.80 = (bf16[1,96,768]{2,1,0:T(8,128)(2,1)S(1)}, bf16[1,96,768]{2,1,0:T(8,128)(2,1)S(1)}, u32[]{:S(2)}, u32[]{:S(2)}) collective-permute-start(bf16[1,96,768]{2,1,0:T(8,128)(2,1)S(1)} %get-tuple-element.799), channel_id=1, source_target_pairs={{0,8},{2,10},{4,12},{6,14},{8,0},{10,2},{12,4},{14,6},{16,24},{18,... | collective-permute-start | bytes 442376 | tf_op jit(solution)/shard_map/ppermute | solution.py:1025
  400.1 15.7 %collective-permute-start.70 = (f32[32,768]{1,0:T(8,128)S(1)}, f32[32,768]{1,0:T(8,128)S(1)}, u32[]{:S(2)}, u32[]{:S(2)}) collective-permute-start(f32[32,768]{1,0:T(8,128)S(1)} %add.90), channel_id=1, source_target_pairs={{0,2},{2,0},{4,6},{6,4},{8,10},{10,8},{12,14},{14,12},{16,18},{18,... | collective-permute-start | bytes 294920 | tf_op jit(solution)/shard_map/ppermute | solution.py:1025
  411.3 37.5 %collective-permute-start.79 = (bf16[192,768]{1,0:T(8,128)(2,1)S(1)}, bf16[192,768]{1,0:T(8,128)(2,1)S(1)}, u32[]{:S(2)}, u32[]{:S(2)}) collective-permute-start(bf16[192,768]{1,0:T(8,128)(2,1)S(1)} %add_convert_fusion.3), channel_id=1, source_target_pairs={{0,16},{2,18},{4,20},{6,22},{8,24},{10,26},{12,28},{14,30},{16,0},... | collective-permute-start | bytes 884744 | tf_op jit(solution)/shard_map/ppermute | solution.py:1025
  415.7 41.8 %collective-permute-start.78 = (bf16[96,768]{1,0:T(8,128)(2,1)S(1)}, bf16[96,768]{1,0:T(8,128)(2,1)S(1)}, u32[]{:S(2)}, u32[]{:S(2)}) collective-permute-start(bf16[96,768]{1,0:T(8,128)(2,1)S(1)} %add_convert_fusion.7), channel_id=1, source_target_pairs={{0,16},{2,18},{4,20},{6,22},{8,24},{10,26},{12,28},{14,30},{16,0},... | collective-permute-start | bytes 442376 | tf_op jit(solution)/shard_map/ppermute | solution.py:1025
  415.8 41.8 %collective-permute-start.77 = (f32[32,768]{1,0:T(8,128)S(1)}, f32[32,768]{1,0:T(8,128)S(1)}, u32[]{:S(2)}, u32[]{:S(2)}) collective-permute-start(f32[32,768]{1,0:T(8,128)S(1)} %add.94), channel_id=1, source_target_pairs={{0,8},{2,10},{4,12},{6,14},{8,0},{10,2},{12,4},{14,6},{16,24},{18,... | collective-permute-start | bytes 294920 | tf_op jit(solution)/shard_map/ppermute | solution.py:1025
  415.9 51.5 %collective-permute-start.83 = (bf16[96,768]{1,0:T(8,128)(2,1)S(1)}, bf16[96,768]{1,0:T(8,128)(2,1)S(1)}, u32[]{:S(2)}, u32[]{:S(2)}) collective-permute-start(bf16[96,768]{1,0:T(8,128)(2,1)S(1)} %add_convert_fusion.6), channel_id=1, source_target_pairs={{0,16},{2,18},{4,20},{6,22},{8,24},{10,26},{12,28},{14,30},{16,0},... | collective-permute-start | bytes 442376 | tf_op jit(solution)/shard_map/ppermute | solution.py:1025
  448.9 24.8 %collective-permute-start.82 = (bf16[192,768]{1,0:T(8,128)(2,1)S(1)}, bf16[192,768]{1,0:T(8,128)(2,1)S(1)}, u32[]{:S(2)}, u32[]{:S(2)}) collective-permute-start(bf16[192,768]{1,0:T(8,128)(2,1)S(1)} %add_convert_fusion.2.own_ref), channel_id=1, source_target_pairs={{0,8},{2,10},{4,12},{6,14},{8,0},{10,2},{12,4},{14,6},{16,24},{18,... | collective-permute-start | bytes 884744 | tf_op jit(solution)/shard_map/ppermute | solution.py:1025
  473.8 14.7 %collective-permute-start.86 = (bf16[2304,768]{1,0:T(8,128)(2,1)}, bf16[2304,768]{1,0:T(8,128)(2,1)S(1)}, u32[]{:S(2)}, u32[]{:S(2)}) collective-permute-start(bf16[2304,768]{1,0:T(8,128)(2,1)} %all-gather.2.cloned.1.call-done), channel_id=1, source_target_pairs={{0,2},{2,0},{4,6},{6,4},{8,10},{10,8},{12,14},{14,12},{16,18},{18,... | collective-permute-start | bytes 10616840 | tf_op jit(solution)/shard_map/ppermute | solution.py:1025
  474.4 23.6 %collective-permute-start.91 = (bf16[384,768]{1,0:T(8,128)(2,1)S(1)}, bf16[384,768]{1,0:T(8,128)(2,1)S(1)}, u32[]{:S(2)}, u32[]{:S(2)}) collective-permute-start(bf16[384,768]{1,0:T(8,128)(2,1)S(1)} %bitcast.131), channel_id=1, source_target_pairs={{0,4},{2,6},{4,0},{6,2},{8,12},{10,14},{12,8},{14,10},{16,20},{18,... | collective-permute-start | bytes 1769480 | tf_op jit(solution)/shard_map/ppermute | solution.py:1025
  476.3 12.1 %collective-permute-start.89 = (bf16[96,768]{1,0:T(8,128)(2,1)S(1)}, bf16[96,768]{1,0:T(8,128)(2,1)S(1)}, u32[]{:S(2)}, u32[]{:S(2)}) collective-permute-start(bf16[96,768]{1,0:T(8,128)(2,1)S(1)} %add_convert_fusion.5.own_ref), channel_id=1, source_target_pairs={{0,8},{2,10},{4,12},{6,14},{8,0},{10,2},{12,4},{14,6},{16,24},{18,... | collective-permute-start | bytes 442376 | tf_op jit(solution)/shard_map/ppermute | solution.py:1025
  483.6 14.3 %collective-permute-start.85 = (f32[32,768]{1,0:T(8,128)S(1)}, f32[32,768]{1,0:T(8,128)S(1)}, u32[]{:S(2)}, u32[]{:S(2)}) collective-permute-start(f32[32,768]{1,0:T(8,128)S(1)} %add.100), channel_id=1, source_target_pairs={{0,4},{2,6},{4,0},{6,2},{8,12},{10,14},{12,8},{14,10},{16,20},{18,... | collective-permute-start | bytes 294920 | tf_op jit(solution)/shard_map/ppermute | solution.py:1025
  499.9 13.6 %collective-permute-start.90 = (bf16[192,768]{1,0:T(8,128)(2,1)S(1)}, bf16[192,768]{1,0:T(8,128)(2,1)S(1)}, u32[]{:S(2)}, u32[]{:S(2)}) collective-permute-start(bf16[192,768]{1,0:T(8,128)(2,1)S(1)} %bitcast.148), channel_id=1, source_target_pairs={{0,4},{2,6},{4,0},{6,2},{8,12},{10,14},{12,8},{14,10},{16,20},{18,... | collective-permute-start | bytes 884744 | tf_op jit(solution)/shard_map/ppermute | solution.py:1025
  (151 other events, 958.5 us)
Sparse Core Ops, SparseCore 0:
  256.8 89.3 reduce-scatter.1
  376.7 94.1 all-gather.1
